TPU v7x, 32 devices: a whole 2x2x4 slice. The times are simulated.
32 devices in a mesh: band: 4 (over y, core), sub: 8 (over z, x).
Axes of the slice: x: 2, y: 2, z: 4, core: 2. Of those that a mesh axis runs over, the one named last changes fastest.
Arguments:
- background: float32 [8, 4, 768, 1536], P('band', None, 'sub'), may hold values from -18 to 18
- obs_columns: float32 [8, 4, 32768], P('band', None, 'sub'), may hold values from -18 to 18
- obs_owner: int32 [32768, 1], P('sub'), may hold values from 0 to 7; in each aligned block of 4096 rows (0 to 4095, 4096 to 8191, ...) at most 1024 rows name the same one
- obs_cell: int32 [32768], P('sub'), may hold values from 0 to 147455
- lat_length: float32 [8, 4, 768], P('band'), may hold values from 1 to 2200
- lon_length: float32 [8, 4], P('band'), may hold values from 2 to 48
- vert_length: float32 [8, 4], P('band'), may hold values from 1 to 720
Outputs:
- filtered: float32 [8, 4, 768, 1536], P('band', None, 'sub')
Inputs may be any that keep to these rules, and one draw needn't show every extreme that they name: `obs_owner`: among the 4096 observations of one device no subdomain is named more than 1024 times, and in every draw some device names some subdomain exactly 1024 times.
All inputs are finite; a program needn't handle non-finite values.
Results may differ from a plain program's by a relative error of at most 0.0003.
Values sent between devices are 32-bit elements; how exact they have to be, the bound alone decides.
No kernel may reach another device: no remote copies, remote signals or barrier semaphores. Data moves between devices by JAX's collectives and lax.ppermute only.
A program may use at most 128 MiB of HBM per device.

v0:
```python
import jax
import jax.numpy as jnp
from jax import lax
from jax.sharding import PartitionSpec as P

highest = lax.Precision.HIGHEST


def prefix(part, axis, combine, identity, reverse):
    count = lax.axis_size(axis)
    place = lax.axis_index(axis)
    ahead = count - 1 - place if reverse else place
    gathered = jax.tree.map(lambda a: lax.all_gather(a, axis), part)
    state = jax.tree.map(lambda a, e: jnp.zeros_like(a) + jnp.asarray(e, a.dtype), part, identity)

    def one(turn, state):
        source = count - 1 - turn if reverse else turn
        return combine(
            state, jax.tree.map(lambda a: lax.dynamic_index_in_dim(a, source, 0, False), gathered)
        )

    return lax.fori_loop(0, ahead, one, state)


def combine(earlier, later):
    return (earlier[0] * later[0], later[0] * earlier[1] + later[1])


def row_sweep(values, decays, reverse):
    group_count, scale_length, column_count = values.shape
    block_len = min(scale_length, 128)
    block_count = scale_length // block_len
    blocked = values.reshape(group_count, block_count, block_len, column_count)
    decay_blocks = decays.reshape(group_count, block_count, block_len)
    log_decay = jnp.log(decay_blocks)
    inclusive = jnp.cumsum(log_decay, axis=-1)
    exclusive = inclusive - log_decay
    position = jnp.arange(block_len)
    if reverse:
        log_gap = exclusive[..., None, :] - exclusive[..., :, None]
        lower_mask = position[None, :] >= position[:, None]
        entry_weight = jnp.exp(inclusive[..., -1:] - exclusive)
    else:
        log_gap = inclusive[..., :, None] - inclusive[..., None, :]
        lower_mask = position[:, None] >= position[None, :]
        entry_weight = jnp.exp(inclusive)
    weights = (
        jnp.where(lower_mask, jnp.exp(jnp.minimum(log_gap, 0.0)), 0.0)
        * (1.0 - decay_blocks)[..., None, :]
    )
    local_part = jnp.einsum("knij,knjc->knic", weights, blocked, precision=highest)
    pieces = [None] * block_count
    carry_state = jnp.zeros((group_count, column_count), jnp.float32)
    visit_order = range(block_count - 1, -1, -1) if reverse else range(block_count)
    for block_index in visit_order:
        piece_value = (
            local_part[:, block_index]
            + entry_weight[:, block_index, :, None] * carry_state[:, None, :]
        )
        pieces[block_index] = piece_value
        carry_state = piece_value[:, 0] if reverse else piece_value[:, -1]
    return jnp.concatenate(pieces, axis=1)


def cycle_sweep(values, decays, reverse):
    group_count, row_count, column_count = values.shape
    block_len = 128
    block_count = column_count // block_len
    log_decay = jnp.log(decays)
    position = jnp.arange(block_len, dtype=jnp.float32)
    if reverse:
        column_gap = position[None, :] - position[:, None]
    else:
        column_gap = position[:, None] - position[None, :]
    weights = jnp.where(
        column_gap[None] >= 0.0,
        jnp.exp(log_decay[:, None, None] * jnp.maximum(column_gap, 0.0)[None]),
        0.0,
    )
    weights = weights * (1.0 - decays)[:, None, None]
    blocked = values.reshape(group_count, row_count, block_count, block_len)
    local_part = jnp.einsum("krnj,kij->krni", blocked, weights, precision=highest)
    block_decay = jnp.exp(log_decay * block_len)[:, None]
    full_turn = (1.0 - jnp.exp(log_decay * column_count))[:, None]
    starts = [None] * block_count
    carry_state = jnp.zeros((group_count, row_count), jnp.float32)
    if reverse:
        edge_value = local_part[..., 0]
        for block_index in range(block_count - 1, -1, -1):
            starts[block_index] = carry_state
            carry_state = block_decay * carry_state + edge_value[:, :, block_index]
        wrapped = carry_state / full_turn
        incoming = jnp.stack(
            [
                starts[block_index]
                + jnp.exp(log_decay * block_len * (block_count - 1 - block_index))[:, None]
                * wrapped
                for block_index in range(block_count)
            ],
            axis=2,
        )
        within = jnp.exp(log_decay[:, None] * (block_len - position)[None, :])
    else:
        edge_value = local_part[..., -1]
        for block_index in range(block_count):
            starts[block_index] = carry_state
            carry_state = block_decay * carry_state + edge_value[:, :, block_index]
        wrapped = carry_state / full_turn
        incoming = jnp.stack(
            [
                starts[block_index]
                + jnp.exp(log_decay * block_len * block_index)[:, None] * wrapped
                for block_index in range(block_count)
            ],
            axis=2,
        )
        within = jnp.exp(log_decay[:, None] * (position + 1.0)[None, :])
    result = local_part + within[:, None, None, :] * incoming[..., None]
    return result.reshape(group_count, row_count, column_count)


def latitude_filter(values, decays):
    for reverse in (False, True, False, True):
        values = row_sweep(values, decays, reverse)
    return values


def longitude_filter(values, decays):
    for reverse in (False, True, False, True):
        values = cycle_sweep(values, decays, reverse)
    return values


def level_chain(values, decays, reverse):
    level_count = values.shape[0]
    visit_order = range(level_count - 1, -1, -1) if reverse else range(level_count)
    carry_state = jnp.zeros_like(values[0])
    level_gain = jnp.ones((values.shape[1],), jnp.float32)
    outputs = [None] * level_count
    carried = [None] * level_count
    for level_index in visit_order:
        factor = decays[level_index][:, None, None]
        carry_state = factor * carry_state + (1.0 - factor) * values[level_index]
        level_gain = level_gain * decays[level_index]
        outputs[level_index] = carry_state
        carried[level_index] = level_gain
    total_decay = level_gain[:, None, None]
    identity = (jnp.ones_like(total_decay), jnp.zeros_like(carry_state))
    incoming = prefix((total_decay, carry_state), "band", combine, identity, reverse)[1]
    return jnp.stack(
        [
            outputs[level_index] + carried[level_index][:, None, None] * incoming
            for level_index in range(level_count)
        ]
    )


def route_slots(owners, sub_count, capacity):
    matches = (owners[:, None] == jnp.arange(sub_count, dtype=jnp.int32)[None, :]).astype(jnp.int32)
    ranks = jnp.sum((jnp.cumsum(matches, axis=0) - 1) * matches, axis=1)
    return owners * capacity + ranks


def fill_slots(obs_values, obs_cell, slots, sub_count, capacity):
    group_count = obs_values.shape[0]
    sent_values = (
        jnp.zeros((group_count, sub_count * capacity), jnp.float32).at[:, slots].set(obs_values)
    )
    sent_cells = jnp.zeros((sub_count * capacity,), jnp.int32).at[slots].set(obs_cell)
    return (
        sent_values.reshape(group_count, sub_count, capacity),
        sent_cells.reshape(sub_count, capacity),
    )


def deposit(target, obs_values, cells):
    group_count = target.shape[0]
    flat = target.reshape(group_count, -1)
    flat = flat.at[:, cells.reshape(-1)].add(obs_values.reshape(group_count, -1))
    return flat.reshape(target.shape)


def per_device(background, obs_columns, obs_owner, obs_cell, lat_length, lon_length, vert_length):
    level_count, var_count, row_count, lon_count = background.shape
    sub_count = lax.axis_size("sub")
    sub_index = lax.axis_index("sub")
    group_count = level_count * var_count
    lat_count = row_count * sub_count
    tile_field = background.reshape(group_count, row_count, lon_count)
    obs_values = obs_columns.reshape(group_count, -1)
    owners = obs_owner[:, 0]
    capacity = 2 * owners.shape[0] // sub_count
    lat_decay = jnp.exp(-1.0 / lat_length).reshape(group_count, lat_count)
    lon_decay = jnp.exp(-1.0 / lon_length).reshape(group_count)
    slots = route_slots(owners, sub_count, capacity)
    sent_values, sent_cells = fill_slots(obs_values, obs_cell, slots, sub_count, capacity)
    got_values = lax.all_to_all(sent_values, "sub", split_axis=1, concat_axis=1, tiled=True)
    got_cells = lax.all_to_all(sent_cells, "sub", split_axis=0, concat_axis=0, tiled=True)
    tile_field = deposit(tile_field, got_values, got_cells)
    own_lat = lax.dynamic_slice_in_dim(lat_decay, sub_index, 1, 0)
    own_lon = lax.dynamic_slice_in_dim(lon_decay, sub_index, 1, 0)
    level_slab = latitude_filter(
        lax.all_to_all(tile_field, "sub", split_axis=0, concat_axis=1, tiled=True), own_lat
    )
    level_slab = longitude_filter(level_slab, own_lon)
    tile_field = lax.all_to_all(level_slab, "sub", split_axis=1, concat_axis=0, tiled=True)
    result = tile_field.reshape(level_count, var_count, row_count, lon_count)
    vert_decay = jnp.exp(-1.0 / vert_length)
    result = level_chain(result, vert_decay, False)
    result = level_chain(result, vert_decay, True)
    return result


def solution(mesh):
    placed = (
        P("band", None, "sub", None),
        P("band", None, "sub"),
        P("sub", None),
        P("sub"),
        P("band", None, None),
        P("band", None),
        P("band", None),
    )
    return jax.shard_map(
        per_device,
        mesh=mesh,
        in_specs=placed,
        out_specs=P("band", None, "sub", None),
        check_vma=False,
    )
```

profile of v0, /device:TPU:1, one launch (start us, length us, event | category | flops | bytes accessed | tf_op | source)
XLA Modules:
  0.0 799.1 jit_solution(10603191301992070660)
XLA Ops:
  7.3 2.3 reduce-window.6
  11.8 16.3 %scatter_custom_fusion = s32[8192]{0:T(1024)} fusion(s32[4096]{0:T(1024)S(1)} %bitcast.358, s32[4096]{0:T(1024)} %param.14, s32[]{:T(128)} %constant.117.clone.1), kind=kCustom, calls=%fused_computation.217 | custom fusion | bytes 33280 | tf_op jit(solution)/shard_map/scatter | solution.py:169
  28.0 6.4 all-to-all-start
  35.9 12.9 %scatter_custom_fusion.1 = f32[8,8192]{0,1:T(8,128)} fusion(s32[4096]{0:T(1024)S(1)} %bitcast.359, f32[8,4096]{0,1:T(8,128)S(1)} %copy.72, f32[]{:T(128)} %constant.114.clone.1), kind=kCustom, calls=%fused_computation.39 | custom fusion | bytes 2359300 | tf_op jit(solution)/shard_map/scatter | solution.py:167
  48.8 3.4 copy.73
  52.3 7.3 copy.106
  59.5 33.7 %copy.74 = f32[8,147456]{0,1:T(8,128)} copy(f32[8,147456]{1,0:T(8,128)} %bitcast.321) | data formatting | bytes 9437184 | tf_op jit(solution)/shard_map/reshape;reshape | solution.py:178
  93.3 5.8 all-to-all-start.1
  99.1 5.9 sort
  106.2 2.7 copy.75
  108.8 144.8 %scatter_custom_fusion.2 = f32[8,147456]{0,1:T(8,128)} fusion(f32[8,147456]{0,1:T(8,128)} %copy.74, s32[8192]{0:T(1024)S(1)} %get-tuple-element.175, f32[8192,8]{1,0:T(8,128)} %copy.75, s32[8192]{0:T(1024)S(1)} %broadcast_clamp_fusion), kind=kCustom, calls=%fused_computation.19 | custom fusion | flops 65536 | bytes 4718592 | tf_op jit(solution)/shard_map/scatter-add | solution.py:179
  253.6 43.8 %copy.76 = f32[8,96,1536]{2,1,0:T(8,128)} copy(f32[8,96,1536]{0,2,1:T(8,128)} %bitcast.19) | data formatting | bytes 9437184 | tf_op jit(solution)/shard_map/reshape | solution.py:180
  297.4 11.1 %all-to-all-start.2 = ((f32[8,96,1536]{2,1,0:T(8,128)}), f32[8,96,1536]{2,1,0:T(8,128)}, u32[]{:S(2)}, u32[]{:S(2)}) async-start(f32[8,96,1536]{2,1,0:T(8,128)} %copy.76), calls=%async_computation.2 | async-start | bytes 9437184 | tf_op jit(solution)/shard_map/all_to_all | solution.py:203
  311.7 99.8 %all-to-all-done.2 = f32[8,96,1536]{2,1,0:T(8,128)} async-done(((f32[8,96,1536]{2,1,0:T(8,128)}), f32[8,96,1536]{2,1,0:T(8,128)}, u32[]{:S(2)}, u32[]{:S(2)}) %all-to-all-start.2) | async-done | bytes 4718624 | tf_op jit(solution)/shard_map/all_to_all | solution.py:203
  411.5 6.7 convolution_bitcast_fusion.3
  419.4 4.7 convolution_bitcast_fusion.2
  425.8 4.7 convolution_bitcast_fusion.1
  431.7 4.9 convolution_bitcast_fusion
  436.6 2.6 fusion.126
  439.3 2.3 copy.77
  441.6 2.3 copy.78
  443.8 2.3 copy.79
  446.1 2.3 copy.80
  466.2 4.8 fusion.72
  471.3 5.4 fusion.7
  476.7 3.4 dot_general.51
  480.4 5.2 fusion.4
  485.6 3.8 dot_general.53
  489.7 5.2 fusion.1
  494.9 3.4 dot_general.55
  498.6 2.7 multiply_add_fusion
  501.4 12.2 %copy.92 = f32[1,768,1536]{2,0,1:T(1,128)} copy(f32[1,768,1536]{1,2,0:T(8,128)} %bitcast.322) | data formatting | bytes 9437184 | tf_op jit(solution)/shard_map/reshape | solution.py:119
  513.6 5.4 all-to-all-start.3
  519.2 102.9 %all-to-all-done.3 = f32[1,768,1536]{2,0,1:T(1,128)} async-done(((f32[1,768,1536]{2,0,1:T(1,128)}), f32[1,768,1536]{2,0,1:T(1,128)}, u32[]{:S(2)}, u32[]{:S(2)}) %all-to-all-start.3) | async-done | bytes 4718624 | tf_op jit(solution)/shard_map/all_to_all | solution.py:206
  622.0 3.3 slice.585
  625.3 4.1 slice.586
  629.5 2.1 fusion.15
  631.6 7.3 all-gather.2
  640.6 56.7 %all-gather.6.cloned.1.call-done = f32[4,4,96,1536]{3,2,1,0:T(8,128)} async-done(((f32[1,4,96,1536]{3,2,1,0:T(8,128)}), f32[4,4,96,1536]{3,2,1,0:T(8,128)}) %all-gather.6.cloned.1.call-update) | async-done | bytes 9437200 | tf_op jit(solution)/shard_map/all_gather | solution.py:13
  697.6 2.5 while.26
  697.6 2.3 bitcast_add_fusion.4
  700.1 4.9 multiply_add_fusion.1
  705.1 69.0 %all-gather.8.cloned.1.call-done = f32[16,96,1536]{2,1,0:T(8,128)} async-done(((f32[4,96,1536]{2,1,0:T(8,128)}), f32[16,96,1536]{2,1,0:T(8,128)}) %all-gather.8.cloned.1.call-update) | async-done | bytes 9437200 | tf_op jit(solution)/shard_map/all_gather | solution.py:13
  775.7 8.5 %while.27 = (s32[]{:T(128)}, f32[4,96,1536]{2,1,0:T(8,128)}, s32[]{:T(128)}, f32[4,4,1,1]{1,3,2,0:T(1,128)S(1)}, f32[4,4,96,1536]{3,2,1,0:T(8,128)}, /*index=5*/s32[]{:T(128)}, s32[]{:T(128)}, s32[]{:T(128)}, s32[]{:T(128)}) while((s32[]{:T(128)}, f32[4,96,1536]{2,1,0:T(8,128)}, s32[]{:T(128)}, f32[4,4,1,1]{1,3,2,0:T(1,128)S(1)}, ...), condition=%wide.region_10.11_spmd, body=%wide.region_9.10_spmd.sunk | while | flops 1179654 | bytes 7078083 | solution.py:22
  775.7 4.3 bitcast_add_fusion.5
  780.0 4.3 bitcast_add_fusion.5
  784.3 5.3 add_bitcast_fusion.1
  789.6 2.6 pad_maximum_fusion
  (162 shorter events, 33.1 us)
Async XLA Ops:
  28.0 65.2 %all-to-all-start = ((s32[8,1,1024]{2,1,0:T(1,128)}), s32[8,1,1024]{2,1,0:T(1,128)S(1)}, u32[]{:S(2)}, u32[]{:S(2)}) async-start(s32[8,1,1024]{2,1,0:T(1,128)} %bitcast.12), calls=%async_computation | async-start | bytes 65536 | tf_op jit(solution)/shard_map/all_to_all | solution.py:198
  93.3 12.9 %all-to-all-start.1 = ((f32[8,8,1024]{2,0,1:T(8,128)}), f32[8,8,1024]{2,0,1:T(8,128)S(1)}, u32[]{:S(2)}, u32[]{:S(2)}) async-start(f32[8,8,1024]{2,0,1:T(8,128)} %copy.73), calls=%async_computation.1 | async-start | bytes 524288 | tf_op jit(solution)/shard_map/all_to_all | solution.py:197
  297.4 11.1 %copy-start.1 = (f32[2,4,768]{2,1,0:T(4,128)S(1)}, f32[2,4,768]{2,1,0:T(4,128)}, u32[]{:S(2)}) copy-start(f32[2,4,768]{2,1,0:T(4,128)} %param.15) | copy-start | bytes 73732
  297.4 11.2 %copy-start.2 = (f32[2,4]{1,0:T(2,128)S(1)}, f32[2,4]{1,0:T(2,128)}, u32[]{:S(2)}) copy-start(f32[2,4]{1,0:T(2,128)} %param.16) | copy-start | bytes 100
  297.4 114.1 %all-to-all-start.2 = ((f32[8,96,1536]{2,1,0:T(8,128)}), f32[8,96,1536]{2,1,0:T(8,128)}, u32[]{:S(2)}, u32[]{:S(2)}) async-start(f32[8,96,1536]{2,1,0:T(8,128)} %copy.76), calls=%async_computation.2 | async-start | bytes 9437184 | tf_op jit(solution)/shard_map/all_to_all | solution.py:203
  513.6 5.5 copy-start.3
  513.6 108.4 %all-to-all-start.3 = ((f32[1,768,1536]{2,0,1:T(1,128)}), f32[1,768,1536]{2,0,1:T(1,128)}, u32[]{:S(2)}, u32[]{:S(2)}) async-start(f32[1,768,1536]{2,0,1:T(1,128)} %copy.92), calls=%async_computation.3 | async-start | bytes 9437184 | tf_op jit(solution)/shard_map/all_to_all | solution.py:206
  519.1 178.2 %all-gather.6.cloned.1.call-start = ((), (), s32[]{:S(2)}) async-start(), calls=%async_computation.4 | async-start | bytes 11796480 | tf_op jit(solution)/shard_map/all_gather | solution.py:13
  625.3 4.2 copy-start
  631.6 142.5 %all-gather.8.cloned.1.call-start = ((), (), s32[]{:S(2)}) async-start(), calls=%async_computation.5 | async-start | bytes 11796480 | tf_op jit(solution)/shard_map/all_gather | solution.py:13
Sparse Core Ops, SparseCore 0:
  631.7 65.5 all-gather.5
  705.2 68.8 all-gather.7
where the time goes:
time: 813 us; the launch traced here: 799 us
  waiting for transfers between devices  329 us (40%)
  other arithmetic  196 us (24%)
  local copies, waits for them, and re-layouts  179 us (22%)
  matrix products  41.7 us (5%)
  starting transfers between devices  28.7 us (4%)
  between operations  16.3 us (2%)
    scatter-add x3, other arithmetic, deposit(): flat.at[:, cells.reshape(-1)].add(obs_values.reshape(group_count, -1))  151 us
    all_gather x2, waiting for transfers between devices, prefix(): gathered = jax.tree.map(lambda a: lax.all_gather(a, axis), part)  126 us
    all_to_all x1, waiting for transfers between devices, per_device(): lax.all_to_all(level_slab, 'sub', split_axis=1, concat_axis=0, tiled=True)  103 us
    all_to_all x1, waiting for transfers between devices, per_device(): lax.all_to_all(tile_field, 'sub', split_axis=0, concat_axis=1, tiled=True)  99.8 us
    reshape x1, local copies, waits for them, and re-layouts, deposit(): return flat.reshape(target.shape)  43.8 us
    another operation x1, local copies, waits for them, and re-layouts, deposit(): flat = target.reshape(group_count, -1)  33.7 us
    dot_general x4, matrix products, row_sweep(): jnp.einsum('knij,knjc->knic', weights, blocked, precision=highest)  21.1 us
    dot_general x4, matrix products, cycle_sweep(): jnp.einsum('krnj,kij->krni', blocked, weights, precision=highest)  20.6 us
  transfers between devices with their start and end apart: 6, of which 5 were waited for; matrix products, arithmetic and copies ran while one was open for 8% of the time, Pallas kernels for 0%

commit v1 on v0

v1 whole, which is shorter than its diff:
```python
import functools

import jax
import jax.numpy as jnp
from jax import lax
from jax.experimental import pallas as pl
from jax.experimental.pallas import tpu as pltpu
from jax.sharding import PartitionSpec as P

f32 = jnp.float32
i32 = jnp.int32
bf16 = jnp.bfloat16
highest = lax.Precision.HIGHEST

LANES = 128
SUBLANES = 8
BLOCK = 256
CHAINS = 4

VMEM = pl.BlockSpec(memory_space=pltpu.VMEM)
SMEM = pl.BlockSpec(memory_space=pltpu.SMEM)
ANY = pl.BlockSpec(memory_space=pl.ANY)


def params(mib):
    return pltpu.CompilerParams(vmem_limit_bytes=mib << 20)


def cost(flops, read):
    return pl.CostEstimate(flops=flops, bytes_accessed=read, transcendentals=0)


def dot(a, b, dims=(((1,), (0,)), ((), ()))):
    return lax.dot_general(a, b, dims, preferred_element_type=f32)


def split(x):
    high = x.astype(bf16)
    return high, (x - high.astype(f32)).astype(bf16)


def split_outside(x):
    high = lax.reduce_precision(x, 8, 7)
    return high.astype(bf16), (x - high).astype(bf16)


def pack_kernel(group_count, chunk_count, strip, starts, places, cells, values, packed):
    sub_count = packed.shape[0]
    lane = lax.broadcasted_iota(i32, (1, LANES), 1)
    word_row = chunk_count * group_count

    def unaligned(ref, base):
        row = lax.shift_right_logical(base, 7)
        offset = base & 127
        turn = (LANES - offset) & 127
        first = pltpu.roll(ref[pl.ds(row, 1), :], turn, 1)
        second = pltpu.roll(ref[pl.ds(row + 1, 1), :], turn, 1)
        return jnp.where(lane < LANES - offset, first, second)

    def one_owner(owner, carry):
        start = starts[owner]
        count = starts[owner + 1] - start
        word_rows = packed.shape[1] - word_row
        packed[owner, word_row:, :] = jnp.full((word_rows, LANES), float(strip), f32)

        def one_chunk(chunk, carry):
            base = start + chunk * LANES
            place = jnp.broadcast_to(unaligned(places, base), (SUBLANES, LANES))
            source = lax.shift_right_logical(place, 7)
            within = place & 127
            for tile in range(group_count // SUBLANES):
                rows = slice(tile * SUBLANES, (tile + 1) * SUBLANES)
                total = jnp.zeros((SUBLANES, LANES), f32)
                for column in range(values.shape[1] // LANES):
                    block = values[rows, column * LANES : (column + 1) * LANES]
                    total = jnp.where(
                        source == column, jnp.take_along_axis(block, within, axis=1), total
                    )
                at = pl.multiple_of(chunk * group_count + tile * SUBLANES, SUBLANES)
                packed[owner, pl.ds(at, SUBLANES), :] = total
            cell = unaligned(cells, base)
            word = (cell - (cell & 127)) + ((cell - lane) & 127)
            word = jnp.where(lane + chunk * LANES < count, word, strip)
            packed[owner, pl.ds(word_row + chunk, 1), :] = word.astype(f32)
            return carry

        lax.fori_loop(0, (count + LANES - 1) // LANES, one_chunk, 0)
        return carry

    lax.fori_loop(0, sub_count, one_owner, 0)


def pack_observations(obs_values, owners, cells, sub_count, strip, capacity):
    group_count, obs_count = obs_values.shape
    chunk_count = capacity // LANES
    rows = chunk_count * group_count + SUBLANES * (-(-chunk_count // SUBLANES))
    keys, places = lax.sort(
        (owners * strip + cells, lax.iota(i32, obs_count)), num_keys=1, is_stable=False
    )
    bounds = jnp.arange(sub_count + 1, dtype=i32)
    starts = jnp.sum((owners[:, None] < bounds[None, :]).astype(i32), axis=0)
    pad = (0, SUBLANES * LANES)
    places = jnp.pad(places, pad).reshape(-1, LANES)
    cells = jnp.pad(keys % strip, pad).reshape(-1, LANES)
    return pl.pallas_call(
        functools.partial(pack_kernel, group_count, chunk_count, strip),
        out_shape=jax.ShapeDtypeStruct((sub_count, rows, LANES), f32),
        in_specs=[SMEM, VMEM, VMEM, VMEM],
        out_specs=VMEM,
        compiler_params=params(16),
        cost_estimate=cost(10**6, 10**6),
    )(starts, places, cells, obs_values)


def deposit_kernel(sizes, words, got, field, decay, swept, exits, loaded, *rest):
    sub_count, group_count, row_count, column_count, chunk_count, strip = sizes
    totals, sems = rest[:CHAINS], rest[CHAINS]
    tiles = group_count // SUBLANES
    span = (chunk_count + 1) * LANES

    def load(column):
        return pltpu.make_async_copy(
            field.at[:, pl.ds(column * LANES, LANES)], loaded.at[column], sems.at[column]
        )

    for column in range(column_count):
        load(column).start()

    def clear(at, carry):
        for total in totals:
            for tile in range(tiles):
                for k in range(8):
                    total[tile, at * 8 + k] = jnp.zeros((SUBLANES, LANES), f32)
        return carry

    lax.fori_loop(0, row_count * column_count // 8, clear, 0)
    lane = lax.broadcasted_iota(i32, (SUBLANES, LANES), 1)

    def one_source(source, carry):
        first = source * span

        def more(chunk):
            return words[first + chunk * LANES] < strip

        def one_chunk(chunk):
            start = first + chunk * LANES
            blocks = [
                got[
                    source,
                    pl.ds(pl.multiple_of(chunk * group_count + tile * SUBLANES, 8), SUBLANES),
                    :,
                ]
                for tile in range(tiles)
            ]
            for slot in range(LANES):
                word = words[start + slot]
                target = lax.shift_right_logical(word, 7)
                turn = word & 127
                for tile in range(tiles):
                    value = pltpu.roll(jnp.where(lane == slot, blocks[tile], 0.0), turn, 1)
                    total = totals[slot % CHAINS]
                    total[tile, target] = total[tile, target] + value
            return chunk + 1

        lax.while_loop(more, one_chunk, jnp.int32(0))
        return carry

    lax.fori_loop(0, sub_count, one_source, 0)
    for column in range(column_count):
        load(column).wait()

    for tile in range(tiles):
        held = totals[0]
        spot = tile * SUBLANES * row_count

        def read_first(row, column):
            at = row * column_count + column
            value = loaded[column, pl.ds(spot + row, SUBLANES, stride=row_count), :]
            for total in totals:
                value = value + total[tile, at]
            return value

        def read_held(row, column):
            return held[tile, row * column_count + column]

        def write_held(row, column, value):
            held[tile, row * column_count + column] = value

        def write_last(row, column, value):
            swept[column, pl.ds(spot + row, SUBLANES, stride=row_count), :] = value

        for turn in range(4):
            read = read_first if turn == 0 else read_held
            write = write_last if turn == 3 else write_held

            def one_row(step, state, turn=turn, read=read, write=write):
                row = row_count - 1 - step if turn % 2 else step
                keep = decay[row, tile * SUBLANES : (tile + 1) * SUBLANES, :]
                take = 1.0 - keep
                following = []
                for column in range(column_count):
                    value = keep * state[column] + take * read(row, column)
                    write(row, column, value)
                    following.append(value)
                return tuple(following)

            nothing = tuple(jnp.zeros((SUBLANES, LANES), f32) for _ in range(column_count))
            state = lax.fori_loop(0, row_count, one_row, nothing, unroll=4)
            message_rows = 4 * column_count
            for column in range(column_count):
                at = tile * SUBLANES * message_rows + turn * column_count + column
                exits[pl.ds(at, SUBLANES, stride=message_rows), :] = state[column]


def deposit_and_sweep(field, got, words, decay, sizes):
    sub_count, group_count, row_count, column_count, chunk_count, strip = sizes
    tiles = group_count // SUBLANES
    cells = row_count * column_count
    return pl.pallas_call(
        functools.partial(deposit_kernel, sizes),
        out_shape=[
            jax.ShapeDtypeStruct((column_count, group_count * row_count, LANES), f32),
            jax.ShapeDtypeStruct((group_count * 4 * column_count, LANES), f32),
        ],
        in_specs=[SMEM, VMEM, ANY, VMEM],
        out_specs=[VMEM, VMEM],
        scratch_shapes=[pltpu.VMEM((column_count, group_count * row_count, LANES), f32)]
        + [pltpu.VMEM((tiles, cells + 8, SUBLANES, LANES), f32)] * CHAINS
        + [pltpu.SemaphoreType.DMA((column_count,))],
        compiler_params=params(40),
        cost_estimate=cost(10**7, 10**7),
    )(words, got, field, decay)


def unit_kernel(decay, inside, leaving, held):
    row_count = decay.shape[0]
    state_of = lax.broadcasted_iota(i32, (1, LANES), 1) & 3
    held[...] = jnp.zeros(held.shape, f32)
    for turn in range(4):

        def one_row(step, state, turn=turn):
            row = row_count - 1 - step if turn % 2 else step
            keep = decay[pl.ds(row, 1), :]
            value = keep * state + (1.0 - keep) * held[pl.ds(row, 1), :]
            held[pl.ds(row, 1), :] = value
            return value

        enter = jnp.where(state_of == turn, 1.0, 0.0)
        leaving[turn : turn + 1, :] = lax.fori_loop(0, row_count, one_row, enter, unroll=8)
    inside[...] = jnp.transpose(held[...], (1, 0))


def unit_responses(decay):
    return pl.pallas_call(
        unit_kernel,
        out_shape=[
            jax.ShapeDtypeStruct((LANES, LANES), f32),
            jax.ShapeDtypeStruct((4, LANES), f32),
        ],
        in_specs=[VMEM],
        out_specs=[VMEM, VMEM],
        scratch_shapes=[pltpu.VMEM((LANES, LANES), f32)],
        compiler_params=params(8),
        cost_estimate=cost(10**6, 10**6),
    )(decay)


def circle_weights(lon_length, column_total):
    block_count = column_total // BLOCK
    rate = -1.0 / lon_length[:, None, None]
    decay = jnp.exp(rate)
    gain = jnp.square(-jnp.expm1(rate) / (1.0 + decay))
    centre = (1.0 + decay * decay) / -jnp.expm1(2.0 * rate)
    spot = jnp.arange(BLOCK, dtype=f32)
    gap = jnp.abs(spot[:, None] - spot[None, :])[None]
    near = gain * jnp.exp(rate * gap) * (gap + centre)
    lane = jnp.arange(LANES)
    kind = (lane % 4)[None, None, :]
    forth = (BLOCK - spot)[None, :, None]
    back = spot[None, :, None]
    far = jnp.where(kind < 2, forth, back)
    moment = jnp.exp(rate * far) * jnp.where(kind % 2 == 1, far, 1.0)
    row = jnp.arange(LANES)
    row_kind = (row % 4)[:, None]
    row_block = ((row // 4) % 8)[:, None]
    column = jnp.arange(column_total)[None, :]
    column_block = column // BLOCK
    column_spot = (column % BLOCK).astype(f32)
    ahead = jnp.where(row_kind < 2, column_block - row_block, row_block - column_block)
    steps = ((ahead - 1) % block_count).astype(f32)[None]
    reach = jnp.where(row_kind < 2, column_spot, BLOCK - column_spot)[None]
    turn = jnp.exp(rate * column_total)
    open_turn = -jnp.expm1(rate * column_total)
    weight = gain * jnp.exp(rate * (reach + BLOCK * steps)) / open_turn
    lead = reach + centre + BLOCK * (steps + block_count * turn / open_turn)
    spread = jnp.where(row_kind[None] % 2 == 1, weight, weight * lead)
    spread = jnp.where(row_block[None] < block_count, spread, 0.0)
    near_high, near_low = split_outside(near)
    moment_high, moment_low = split_outside(moment)
    spread_high, spread_low = split_outside(spread)
    use_high = (row // 32 < 2)[None, :, None]
    return (
        near_high,
        near_low,
        jnp.concatenate([moment_high, moment_low], axis=2),
        jnp.where(use_high, spread_high, spread_low),
    )


def circle(pieces, near_high, near_low, moment, spread):
    row_count = pieces[0].shape[0]
    whole = jnp.concatenate(pieces, axis=0)
    high, low = split(whole)
    near = dot(high, near_high) + dot(low, near_high) + dot(high, near_low)
    sums = dot(high, moment)
    sums = sums[:, :LANES] + sums[:, LANES:] + dot(low, moment[:, :LANES])
    lane = lax.broadcasted_iota(i32, (row_count, LANES), 1)
    slot = lax.shift_right_logical(lane, 2) & 7
    moments = jnp.zeros((row_count, LANES), f32)
    for at in range(len(pieces)):
        part = sums[at * row_count : (at + 1) * row_count]
        moments = jnp.where(slot == at, part, moments)
    rest = moments - moments.astype(bf16).astype(f32)
    moments = jnp.where((lax.shift_right_logical(lane, 5) & 1) == 1, rest, moments).astype(bf16)
    far = dot(moments, spread)
    return [
        near[at * row_count : (at + 1) * row_count] + far[:, at * BLOCK : (at + 1) * BLOCK]
        for at in range(len(pieces))
    ]


def longitude_kernel(send_base, swept, near_high, near_low, moment, spread, *rest):
    if send_base is None:
        (out,) = rest
    else:
        weights, out, sent = rest
    column_count = swept.shape[0]
    pieces = [
        jnp.concatenate([swept[2 * at, 0], swept[2 * at + 1, 0]], axis=1)
        for at in range(column_count // 2)
    ]
    pieces = circle(pieces, near_high[0], near_low[0], moment[0], spread[0])
    level = pl.program_id(0)
    for at, piece in enumerate(pieces):
        out[0, :, at * BLOCK : (at + 1) * BLOCK] = piece
    if send_base is None:
        return
    weight = weights[send_base + level * 4]

    @pl.when(level == 0)
    def _():
        for at, piece in enumerate(pieces):
            sent[:, at * BLOCK : (at + 1) * BLOCK] = weight * piece

    @pl.when(level > 0)
    def _():
        for at, piece in enumerate(pieces):
            spot = slice(at * BLOCK, (at + 1) * BLOCK)
            sent[:, spot] = sent[:, spot] + weight * piece


def longitude(swept, weights, count, first, stride, send=None):
    column_count, _, row_count, _ = swept.shape
    column_total = column_count * LANES

    def of(i):
        return first + stride * i

    in_specs = [
        pl.BlockSpec((column_count, 1, row_count, LANES), lambda i: (0, of(i), 0, 0)),
        pl.BlockSpec((1, BLOCK, BLOCK), lambda i: (of(i), 0, 0)),
        pl.BlockSpec((1, BLOCK, BLOCK), lambda i: (of(i), 0, 0)),
        pl.BlockSpec((1, BLOCK, BLOCK), lambda i: (of(i), 0, 0)),
        pl.BlockSpec((1, LANES, column_total), lambda i: (of(i), 0, 0)),
    ]
    out_specs = [pl.BlockSpec((1, row_count, column_total), lambda i: (i, 0, 0))]
    out_shape = [jax.ShapeDtypeStruct((count, row_count, column_total), f32)]
    operands = [swept, *weights]
    if send is not None:
        in_specs.append(SMEM)
        operands.append(send)
        out_specs.append(pl.BlockSpec((row_count, column_total), lambda i: (0, 0)))
        out_shape.append(jax.ShapeDtypeStruct((row_count, column_total), f32))
    return pl.pallas_call(
        functools.partial(longitude_kernel, None if send is None else first),
        grid=(count,),
        in_specs=in_specs,
        out_specs=out_specs,
        out_shape=out_shape,
        compiler_params=params(24),
        cost_estimate=cost(count * 10**9, count * 2 * 10**6),
    )(*operands)


def chain_kernel(index, exits, leaving, inside, near_high, near_low, moment, spread, out, held):
    sub_count, _, _ = exits.shape
    column_count = exits.shape[1] // 4
    shape = (column_count, LANES)
    entering = {}
    for turn in range(4):
        order = list(range(sub_count))
        if turn % 2:
            order.reverse()
        state = jnp.zeros(shape, f32)
        for block in order:
            entering[turn, block] = state
            at = (turn * sub_count + block) * column_count
            held[at : at + column_count, :] = state
            state = exits[block, turn * column_count : (turn + 1) * column_count, :]
            for other in range(turn + 1):
                state = state + leaving[turn, block * 4 + other] * entering[other, block]
    pieces = []
    for at in range(column_count // 2):
        pair = [
            held[pl.ds(2 * at + k, 4 * sub_count, stride=column_count), :] for k in range(2)
        ]
        pieces.append(jnp.concatenate(pair, axis=1))
    pieces = circle(pieces, near_high[0], near_low[0], moment[0], spread[0])
    message_rows = out.shape[0] // sub_count
    for at, piece in enumerate(pieces):
        for k in range(2):
            for turn in range(4):
                place = turn * column_count + 2 * at + k
                out[pl.ds(place, sub_count, stride=message_rows), :] = piece[
                    turn * sub_count : (turn + 1) * sub_count, k * LANES : (k + 1) * LANES
                ]
    for block in range(sub_count):
        at = block * message_rows + 4 * column_count
        out[at : at + 4, :] = inside[block * 4 : (block + 1) * 4, :]
        out[at + 4 : (block + 1) * message_rows, :] = jnp.zeros(
            (message_rows - 4 * column_count - 4, LANES), f32
        )


def chain_states(index, exits, leaving, inside, weights):
    sub_count, rows, _ = exits.shape
    column_total = rows // 4 * LANES
    message_rows = rows + 8

    def whole(*shape):
        return pl.BlockSpec(shape, lambda i, at: (0,) * len(shape))

    def own(*shape):
        return pl.BlockSpec((1,) + shape, lambda i, at: (at[0], 0, 0))

    return pl.pallas_call(
        chain_kernel,
        grid_spec=pltpu.PrefetchScalarGridSpec(
            num_scalar_prefetch=1,
            grid=(1,),
            in_specs=[
                whole(*exits.shape),
                SMEM,
                whole(LANES, LANES),
                own(BLOCK, BLOCK),
                own(BLOCK, BLOCK),
                own(BLOCK, BLOCK),
                own(LANES, column_total),
            ],
            out_specs=whole(sub_count * message_rows, LANES),
            scratch_shapes=[pltpu.VMEM((sub_count * rows, LANES), f32)],
        ),
        out_shape=jax.ShapeDtypeStruct((sub_count * message_rows, LANES), f32),
        compiler_params=params(24),
        cost_estimate=cost(10**9, 2 * 10**6),
    )(index, exits, leaving, inside, *weights)


def level_operator(vert_length):
    rate = (-1.0 / vert_length).T
    count = rate.shape[1]
    lower = jnp.arange(count)[:, None] >= jnp.arange(count)[None, :]
    until = jnp.sum(jnp.where(lower[None], rate[:, None, :], 0.0), axis=2)
    before = until - rate
    take = -jnp.expm1(rate)
    forward = jnp.where(
        lower[None], jnp.exp(jnp.minimum(until[:, :, None] - until[:, None, :], 0.0)), 0.0
    ) * take[:, None, :]
    backward = jnp.where(
        lower.T[None], jnp.exp(jnp.minimum(before[:, None, :] - before[:, :, None], 0.0)), 0.0
    ) * take[:, None, :]
    return jnp.sum(backward[:, :, :, None] * forward[:, None, :, :], axis=2)


def pair_factors(decay):
    top, low = decay[:, 0], decay[:, 1]
    top_take, low_take = 1.0 - top, 1.0 - low
    through = top * low
    sends = (low * top_take, low_take)
    low_out = (low_take * through, low, low_take * low * top_take, low_take * low_take)
    top_out = (
        top * low_out[0] + top_take * top,
        top * low_out[1],
        top * low_out[2] + top_take * top_take,
        top * low_out[3],
    )
    return through, sends, top_out, low_out


def band_tables(vert_length, band):
    decay = jnp.exp(-1.0 / vert_length)
    through, sends, top_out, low_out = pair_factors(decay)
    echo = top_out[0]
    bands = jnp.arange(4)[:, None]
    even = bands % 2 == 0

    def other(x):
        return x.reshape(2, 2, -1)[:, ::-1].reshape(4, -1)

    through_n, echo_n = other(through), other(echo)
    send = [jnp.where(even, sends[i], top_out[2 + i]) for i in range(2)]
    first = [jnp.where(even, through * echo_n * sends[i] + top_out[2 + i], sends[i]) for i in range(2)]
    zeta = jnp.where(bands == 1, (through * through * echo_n + echo)[2][None], 0.0)
    final = []
    for fin, bin_, own_top, own_low in (top_out, low_out):
        for own, sent in ((own_top, sends[0]), (own_low, sends[1])):
            final.append(jnp.where(even, own + bin_ * echo_n * sent, own))
        final.append(jnp.where(even, bin_, fin))
        final.append(
            jnp.where(bands == 0, bin_ * through_n, jnp.where(bands == 3, fin * through_n, 0.0))
        )
        final.append(
            jnp.where(
                bands == 1,
                bin_,
                jnp.where(bands == 2, fin + bin_ * echo_n * through, 0.0),
            )
        )
    table = jnp.stack(send + first + [through, zeta] + final)
    table = lax.dynamic_index_in_dim(table, band, 1, False)
    return table[:2].reshape(-1), table[2:5], table[5], table[6:].reshape(-1)


def last_kernel(variable, own, near, far, kept, message, mix, weights, *rest):
    out = rest[-1]
    row_count, column_total = near.shape
    column_count = column_total // LANES
    message_rows = message.shape[0] // 32
    step = 4 * message_rows
    first = variable * message_rows
    lanes = []
    for column in range(column_count):
        lanes.append(
            jnp.concatenate(
                [
                    message[pl.ds(first + k * column_count + column, 8, stride=step), :]
                    for k in range(4)
                ],
                axis=0,
            )
        )
    states = jnp.concatenate(lanes, axis=1)
    high, low = split(states)
    states = jnp.concatenate([high, high, low, low], axis=0)
    inside = [
        message[pl.ds(first + 4 * column_count + k, 8, stride=step), :] for k in range(4)
    ]
    for level in range(2):
        mixed = jnp.concatenate([part * mix[level, 0] for part in inside], axis=0)
        high, low = split(mixed)
        mixed = jnp.concatenate([high, low, high, low], axis=0)
        total = dot(mixed, states, (((0,), (0,)), ((), ())))[:row_count]
        at = level * 20 + variable
        total = total + weights[at] * own[0] + weights[at + 4] * own[1]
        total = total + weights[at + 8] * near[...] + weights[at + 12] * far[...]
        out[level, 0] = total + weights[at + 16] * kept[...]


def last_step(variable, own, near, far, kept, message, mix, weights, so_far):
    _, row_count, column_total = own.shape

    def whole(shape):
        return pl.BlockSpec(shape, lambda i: (0,) * len(shape))

    operands = [own, near, far, kept, message, mix, weights]
    in_specs = [whole(x.shape) for x in operands[:5]]
    in_specs.append(pl.BlockSpec((2, 1, 8, LANES), lambda i: (0, variable, 0, 0)))
    in_specs.append(SMEM)
    aliases = {}
    if so_far is not None:
        operands.append(so_far)
        in_specs.append(ANY)
        aliases = {7: 0}
    return pl.pallas_call(
        functools.partial(last_kernel, variable),
        grid=(1,),
        in_specs=in_specs,
        out_specs=pl.BlockSpec(
            (2, 1, row_count, column_total), lambda i: (0, variable, 0, 0)
        ),
        out_shape=jax.ShapeDtypeStruct((2, 4, row_count, column_total), f32),
        input_output_aliases=aliases,
        compiler_params=params(24),
        cost_estimate=cost(10**8, 5 * 10**6),
    )(*operands)


def four_bands(swept, lon_weights, messages, vert_length):
    band = lax.axis_index("band")
    lengths = lax.all_gather(vert_length, "band")
    send, first, zeta, final = band_tables(lengths, band)
    operator = level_operator(lengths.reshape(8, 4))
    order = jnp.stack([band, band ^ 2, band ^ 1, band ^ 3])
    columns = (order[:, None] * 2 + jnp.arange(2)[None, :]).reshape(-1)
    mix = lax.dynamic_slice_in_dim(operator, 2 * band, 2, 1)
    mix = jnp.take(mix, columns, axis=2)
    mix = jnp.broadcast_to(jnp.transpose(mix, (1, 0, 2))[..., None], (2, 4, 8, LANES))

    swap = [(0, 1), (1, 0), (2, 3), (3, 2)]
    cross = [(0, 2), (2, 0), (1, 3), (3, 1)]
    fields = []
    for variable in range(4):
        own, sent = longitude(swept, lon_weights, 2, variable, 4, send)
        near = lax.ppermute(sent, "band", swap)
        total = (
            first[0, variable] * own[0] + first[1, variable] * own[1] + first[2, variable] * near
        )
        met = lax.ppermute(total, "band", [(1, 2), (2, 1)])
        kept = met + zeta[variable] * total
        far = lax.ppermute(kept, "band", [(1, 0), (2, 3)])
        fields.append((own, near, far, kept))
    opposite = lax.ppermute(messages, "band", cross)
    pair = jnp.concatenate([messages, opposite], axis=0)
    pair = jnp.concatenate([pair, lax.ppermute(pair, "band", swap)], axis=0)
    result = None
    for variable in range(4):
        result = last_step(variable, *fields[variable], pair, mix, final, result)
    return result


def prefix(part, axis, combine, identity, reverse):
    count = lax.axis_size(axis)
    place = lax.axis_index(axis)
    ahead = count - 1 - place if reverse else place
    gathered = jax.tree.map(lambda a: lax.all_gather(a, axis), part)
    state = jax.tree.map(lambda a, e: jnp.zeros_like(a) + jnp.asarray(e, a.dtype), part, identity)

    def one(turn, state):
        source = count - 1 - turn if reverse else turn
        return combine(
            state, jax.tree.map(lambda a: lax.dynamic_index_in_dim(a, source, 0, False), gathered)
        )

    return lax.fori_loop(0, ahead, one, state)


def combine(earlier, later):
    return (earlier[0] * later[0], later[0] * earlier[1] + later[1])


def level_chain(values, decays, reverse):
    level_count = values.shape[0]
    visit_order = range(level_count - 1, -1, -1) if reverse else range(level_count)
    carry_state = jnp.zeros_like(values[0])
    level_gain = jnp.ones((values.shape[1],), f32)
    outputs = [None] * level_count
    carried = [None] * level_count
    for level_index in visit_order:
        factor = decays[level_index][:, None, None]
        carry_state = factor * carry_state + (1.0 - factor) * values[level_index]
        level_gain = level_gain * decays[level_index]
        outputs[level_index] = carry_state
        carried[level_index] = level_gain
    total_decay = level_gain[:, None, None]
    identity = (jnp.ones_like(total_decay), jnp.zeros_like(carry_state))
    incoming = prefix((total_decay, carry_state), "band", combine, identity, reverse)[1]
    return jnp.stack(
        [
            outputs[level_index] + carried[level_index][:, None, None] * incoming
            for level_index in range(level_count)
        ]
    )


def any_bands(swept, lon_weights, messages, vert_length):
    column_count, group_count, row_count, _ = swept.shape
    (values,) = longitude(swept, lon_weights, group_count, 0, 1)
    messages = messages.reshape(group_count, -1, LANES)
    states = messages[:, : 4 * column_count].reshape(group_count, 4, -1)
    inside = messages[:, 4 * column_count : 4 * column_count + 4, :row_count]
    values = values + jnp.einsum("gkr,gkc->grc", inside, states, precision=highest)
    decay = jnp.exp(-1.0 / vert_length)
    values = values.reshape(decay.shape + values.shape[1:])
    return level_chain(level_chain(values, decay, False), decay, True)


def per_device(background, obs_columns, obs_owner, obs_cell, lat_length, lon_length, vert_length):
    level_count, var_count, row_count, lon_count = background.shape
    sub_count = lax.axis_size("sub")
    sub_index = lax.axis_index("sub")
    group_count = level_count * var_count
    strip = row_count * lon_count
    column_count = lon_count // LANES
    owners = obs_owner[:, 0]
    capacity = 2 * owners.shape[0] // sub_count
    chunk_count = capacity // LANES

    packed = pack_observations(
        obs_columns.reshape(group_count, -1), owners, obs_cell, sub_count, strip, capacity
    )
    got = lax.all_to_all(packed, "sub", split_axis=0, concat_axis=0, tiled=True)
    words = got[:, chunk_count * group_count :, :].reshape(sub_count, -1)[:, :capacity]
    words = jnp.pad(words.astype(i32), ((0, 0), (0, LANES)), constant_values=strip).reshape(-1)

    lengths = lat_length.reshape(group_count, sub_count, row_count)
    own_rows = lax.dynamic_index_in_dim(lengths, sub_index, 1, False)
    decay = jnp.exp(-1.0 / own_rows).T
    decay = jnp.broadcast_to(decay[:, :, None], (row_count, group_count, LANES))
    own_group = lax.dynamic_index_in_dim(lengths, sub_index, 0, False)
    unit_decay = jnp.repeat(jnp.exp(-1.0 / own_group).T, 4, axis=1)
    unit_decay = jnp.pad(unit_decay, ((0, 0), (0, LANES - 4 * sub_count)))
    inside, leaving = unit_responses(unit_decay)
    lon_weights = circle_weights(lon_length.reshape(-1), lon_count)

    sizes = (sub_count, group_count, row_count, column_count, chunk_count, strip)
    swept, exits = deposit_and_sweep(
        background.reshape(group_count * row_count, lon_count), got, words, decay, sizes
    )
    swept = swept.reshape(column_count, group_count, row_count, LANES)
    exits = exits.reshape(group_count, 4 * column_count, LANES)
    exits = lax.all_to_all(exits, "sub", split_axis=0, concat_axis=0, tiled=True)
    index = sub_index.astype(i32).reshape(1)
    messages = chain_states(index, exits, leaving, inside, lon_weights)
    messages = lax.all_to_all(messages, "sub", split_axis=0, concat_axis=0, tiled=True)
    if lax.axis_size("band") == 4 and level_count == 2:
        return four_bands(swept, lon_weights, messages, vert_length)
    return any_bands(swept, lon_weights, messages, vert_length)


def solution(mesh):
    placed = (
        P("band", None, "sub", None),
        P("band", None, "sub"),
        P("sub", None),
        P("sub"),
        P("band", None, None),
        P("band", None),
        P("band", None),
    )
    return jax.shard_map(
        per_device,
        mesh=mesh,
        in_specs=placed,
        out_specs=P("band", None, "sub", None),
        check_vma=False,
    )
```

time: 813 us -> 203 us (0.25); the launches traced: 799 us -> 200 us
  waiting for transfers between devices: 329 us -> 6.6 us
  local copies, waits for them, and re-layouts: 179 us -> 28.5 us
  other arithmetic: 196 us -> 49.5 us
  Pallas kernels: 0 us -> 70.4 us
  matrix products: 41.7 us -> 0 us
  between operations: 16.3 us -> 0.49 us
  starting transfers between devices: 28.7 us -> 38.9 us
    all_to_all x4 -> x3, waiting for transfers between devices: 204 us -> 0.01 us  [the longest x1 0.01 us: per_device(): lax.all_to_all(messages, 'sub', split_axis=0, concat_axis=0, tiled=True)]
    scatter-add x3 -> x0, other arithmetic: 151 us -> none  [deposit(): flat.at[:, cells.reshape(-1)].add(obs_values.reshape(group_count, -1))]
    all_gather x2 -> x0, waiting for transfers between devices: 126 us -> none  [prefix(): gathered = jax.tree.map(lambda a: lax.all_gather(a, axis), part)]
    pallas_call x0 -> x12, Pallas kernels: none -> 70.4 us  [the longest x1 34 us: deposit_and_sweep(): pl.pallas_call(functools.partial(deposit_kernel, sizes), out_shape=[jax.S...]
    reshape x8 -> x7, local copies, waits for them, and re-layouts: 63.8 us -> 2.81 us  [the longest x1 0.95 us: per_device(): obs_columns.reshape(group_count, -1)]
    dot_general x8 -> x0, matrix products: 41.7 us -> none  [the longest x4 21.1 us: row_sweep(): jnp.einsum('knij,knjc->knic', weights, blocked, precision=highest)]
    another operation x3 -> x1, local copies, waits for them, and re-layouts: 35.7 us -> 0.17 us  [band_tables(): table = jnp.stack(send + first + [through, zeta] + final)]
    scatter x2 -> x0, local copies, waits for them, and re-layouts: 29.1 us -> none  [the longest x1 16.3 us: fill_slots(): jnp.zeros((sub_count * capacity,), jnp.int32).at[slots].set(obs_cell)]
  transfers between devices with their start and end apart: 6 -> 17, of which waited for: 5 -> 1; matrix products, arithmetic and copies ran while one was open for 8% -> 26% of each run, Pallas kernels for 0% -> 11%
where the time goes in v1:
time: 203 us; the launch traced here: 200 us
  Pallas kernels  70.4 us (35%)
  other arithmetic  49.5 us (24%)
  starting transfers between devices  38.9 us (19%)
  local copies, waits for them, and re-layouts  28.5 us (14%)
  waiting for transfers between devices  6.6 us (3%)
  blocking collectives  6.05 us (3%)
    pallas_call x1, Pallas kernels, deposit_and_sweep(): pl.pallas_call(functools.partial(deposit_kernel, sizes), out_shape=[jax.S...  34 us
    unnamed x51, local copies, waits for them, and re-layouts  17.6 us
    add x4, other arithmetic, four_bands(): first[0, variable] * own[0] + first[1, variable] * own[1]  14.4 us
    pallas_call x4, Pallas kernels, longitude(): pl.pallas_call(functools.partial(longitude_kernel, None if send is None e...  13.3 us
    pallas_call x4, Pallas kernels, last_step(): pl.pallas_call(functools.partial(last_kernel, variable), grid=(1,), in_sp...  12.2 us
    ppermute x4, starting transfers between devices, four_bands(): met = lax.ppermute(total, 'band', [(1, 2), (2, 1)])  11.1 us
    ppermute x4, starting transfers between devices, four_bands(): far = lax.ppermute(kept, 'band', [(1, 0), (2, 3)])  9.13 us
    add x4, other arithmetic, four_bands(): kept = met + zeta[variable] * total  8.01 us
  transfers between devices with their start and end apart: 17, of which 1 were waited for; matrix products, arithmetic and copies ran while one was open for 26% of the time, Pallas kernels for 11%

profile of v1, /device:TPU:1, one launch (start us, length us, event | category | flops | bytes accessed | tf_op | source)
XLA Modules:
  0.0 200.4 jit_solution(963204496342453126)
XLA Ops:
  1.6 5.0 %sort.15 = (s32[4096]{0:T(1024)S(1)}, s32[4096]{0:T(1024)S(1)}) sort(s32[4096]{0:T(1024)S(1)} %multiply_add_fusion.5, s32[4096]{0:T(1024)S(1)} %iota.171), dimensions={0}, to_apply=%region_1.0 | sort | flops 49152 | bytes 65536 | tf_op jit(solution)/shard_map/sort | solution.py:97
  7.6 7.7 %shard_map.73 = f32[8,72,128]{2,1,0:T(8,128)} custom-call(s32[9]{0:T(128)S(1)} %convert_reduce_fusion.starts, s32[40,128]{1,0:T(8,128)S(1)} %get-tuple-element.95.places, s32[40,128]{1,0:T(8,128)S(1)} %get-tuple-element.94.cells, f32[8,4096]{1,0:T(8,128)S(1)} %reshape.1711.values), custom_call_target="tpu_custom_call" | custom-call | flops 1000000 | bytes 1000000 | tf_op jit(solution)/shard_map/pallas_call | solution.py:105
  15.3 6.4 %all-to-all-start = ((f32[8,72,128]{2,1,0:T(8,128)}), f32[8,72,128]{2,1,0:T(8,128)S(1)}, u32[]{:S(2)}, u32[]{:S(2)}) async-start(f32[8,72,128]{2,1,0:T(8,128)} %shard_map.73), calls=%async_computation | async-start | bytes 589824 | tf_op jit(solution)/shard_map/all_to_all | solution.py:701
  22.5 6.0 %all-gather.1 = f32[4,2,4]{2,1,0:T(2,128)S(1)} all-gather(f32[1,2,4]{2,1,0:T(2,128)} %bitcast.113), channel_id=2, replica_groups=mesh['band'=4,'sub'=8] {'band'}, dimensions={0}, use_global_device_ids=true | all-gather | bytes 160 | tf_op jit(solution)/shard_map/all_gather | solution.py:600
  36.8 1.5 fusion.5
  38.2 1.8 multiply_add_fusion
  40.3 4.8 %fusion.2.spread = bf16[8,128,1536]{2,1,0:T(8,128)(2,1)S(1)} fusion(f32[8]{0:T(128)S(1)} %get-tuple-element.86, f32[128,1536]{1,0:T(8,128)} %fusion.5, f32[8]{0:T(128)S(1)} %get-tuple-element.85, f32[128,1536]{1,0:T(8,128)} %get-tuple-element.44, f32[8]{0:T(128)S(1)} %get-tuple-element.84, f32[128,1536]{1,0:T(8,128)} %get-tuple-element.43, f32[8]{0:T(128)S(1)} %div.102, ...), kind=kLoop, calls=%fused_computation.6 | loop fusion | flops 23592960 | bytes 5505568 | tf_op jit(solution)/shard_map/jit(_where)/select_n | solution.py:306
  47.5 1.3 shard_map.76
  48.8 1.4 exponential_bitcast_fusion
  50.3 3.1 %fusion.3 = (bf16[8,256,256]{2,1,0:T(8,128)(2,1)}, bf16[8,256,256]{2,1,0:T(8,128)(2,1)}) fusion(f32[8]{0:T(128)S(1)} %get-tuple-element.85, f32[256,256]{1,0:T(8,128)} %subtract_abs_fusion, f32[8]{0:T(128)S(1)} %div.102, f32[8]{0:T(128)S(1)} %get-tuple-element.87), kind=kLoop, calls=%fused_computation.9 | loop fusion | flops 4194304 | bytes 2359392 | tf_op jit(solution)/shard_map/convert_element_type | solution.py:44
  55.9 2.3 %copy-done.13 = f32[2,4,96,1536]{3,2,1,0:T(8,128)S(1)} copy-done((f32[2,4,96,1536]{3,2,1,0:T(8,128)S(1)}, f32[2,4,96,1536]{3,2,1,0:T(8,128)}, u32[]{:S(2)}) %copy-start.13) | copy-done | bytes 4718616
  58.2 34.0 %shard_map.74 = (f32[12,768,128]{2,1,0:T(8,128)S(1)}, f32[384,128]{1,0:T(8,128)S(1)}) custom-call(s32[9216]{0:T(1024)S(1)} %reshape.1712.words, f32[8,72,128]{2,1,0:T(8,128)S(1)} %all-to-all-done.got, f32[768,1536]{1,0:T(8,128)S(1)} %bitcast.84, f32[96,8,128]{2,1,0:T(8,128)S(1)} %broadcast_in_dim.322.decay), custom_call_target="tpu_custom_call" | custom-call | flops 10000000 | bytes 10000000 | tf_op jit(solution)/shard_map/pallas_call | solution.py:219
  92.3 3.3 %shard_map.75 = (f32[2,96,1536]{2,1,0:T(8,128)S(1)}, f32[96,1536]{1,0:T(8,128)}) custom-call(f32[12,8,96,128]{3,2,1,0:T(8,128)S(1)} %bitcast.80, bf16[8,256,256]{2,1,0:T(8,128)(2,1)S(1)} %copy-done.8, bf16[8,256,256]{2,1,0:T(8,128)(2,1)S(1)} %copy-done.5, bf16[8,256,256]{2,1,0:T(8,128)(2,1)S(1)} %copy-done.2, bf16[8,128,1536]{2,1,0:T(8,128)(2,1)S(1)} %fusion.2.spread, ...), custom_call_target="tpu_custom_call" | custom-call | flops 2000000000 | bytes 4000000 | tf_op jit(solution)/shard_map/pallas_call | solution.py:384
  96.9 3.6 %all-to-all-start.1 = ((f32[8,48,128]{2,1,0:T(8,128)}), f32[8,48,128]{2,1,0:T(8,128)S(1)}, u32[]{:S(2)}, u32[]{:S(2)}) async-start(f32[8,48,128]{2,1,0:T(8,128)} %bitcast.85), calls=%async_computation.1 | async-start | bytes 393216 | tf_op jit(solution)/shard_map/all_to_all | solution.py:721
  100.5 2.3 %copy-done.1 = f32[12,768,128]{2,1,0:T(8,128)S(1)} copy-done((f32[12,768,128]{2,1,0:T(8,128)S(1)}, f32[12,768,128]{2,1,0:T(8,128)}, u32[]{:S(2)}) %copy-start.1) | copy-done | bytes 4718616
  102.8 1.2 copy-done.3
  104.1 1.2 copy-done.6
  105.3 1.2 copy-done.9
  106.5 3.3 %shard_map.78 = (f32[2,96,1536]{2,1,0:T(8,128)S(1)}, f32[96,1536]{1,0:T(8,128)}) custom-call(f32[12,8,96,128]{3,2,1,0:T(8,128)S(1)} %bitcast.81, bf16[8,256,256]{2,1,0:T(8,128)(2,1)S(1)} %copy-done.9, bf16[8,256,256]{2,1,0:T(8,128)(2,1)S(1)} %copy-done.6, bf16[8,256,256]{2,1,0:T(8,128)(2,1)S(1)} %copy-done.3, bf16[8,128,1536]{2,1,0:T(8,128)(2,1)S(1)} %fusion.2.spread, ...), custom_call_target="tpu_custom_call" | custom-call | flops 2000000000 | bytes 4000000 | tf_op jit(solution)/shard_map/pallas_call | solution.py:384
  111.2 3.3 %shard_map.79 = (f32[2,96,1536]{2,1,0:T(8,128)S(1)}, f32[96,1536]{1,0:T(8,128)}) custom-call(f32[12,8,96,128]{3,2,1,0:T(8,128)S(1)} %bitcast.82, bf16[8,256,256]{2,1,0:T(8,128)(2,1)S(1)} %copy-done.9, bf16[8,256,256]{2,1,0:T(8,128)(2,1)S(1)} %copy-done.6, bf16[8,256,256]{2,1,0:T(8,128)(2,1)S(1)} %copy-done.3, bf16[8,128,1536]{2,1,0:T(8,128)(2,1)S(1)} %fusion.2.spread, ...), custom_call_target="tpu_custom_call" | custom-call | flops 2000000000 | bytes 4000000 | tf_op jit(solution)/shard_map/pallas_call | solution.py:384
  115.7 3.3 %shard_map.80 = (f32[2,96,1536]{2,1,0:T(8,128)S(1)}, f32[96,1536]{1,0:T(8,128)}) custom-call(f32[12,8,96,128]{3,2,1,0:T(8,128)S(1)} %bitcast.83, bf16[8,256,256]{2,1,0:T(8,128)(2,1)S(1)} %copy-done.9, bf16[8,256,256]{2,1,0:T(8,128)(2,1)S(1)} %copy-done.6, bf16[8,256,256]{2,1,0:T(8,128)(2,1)S(1)} %copy-done.3, bf16[8,128,1536]{2,1,0:T(8,128)(2,1)S(1)} %fusion.2.spread, ...), custom_call_target="tpu_custom_call" | custom-call | flops 2000000000 | bytes 4000000 | tf_op jit(solution)/shard_map/pallas_call | solution.py:384
  120.4 1.2 copy-done.4
  121.6 1.2 copy-done.7
  122.8 1.2 copy-done.10
  124.0 1.8 shard_map.77
  125.9 5.6 %all-to-all-start.2 = ((f32[8,56,128]{2,1,0:T(8,128)}), f32[8,56,128]{2,1,0:T(8,128)S(1)}, u32[]{:S(2)}, u32[]{:S(2)}) async-start(f32[8,56,128]{2,1,0:T(8,128)} %bitcast.31), calls=%async_computation.2 | async-start | bytes 458752 | tf_op jit(solution)/shard_map/all_to_all | solution.py:724
  131.5 3.4 %bitcast_add_fusion.3 = f32[96,1536]{1,0:T(8,128)S(1)} fusion(f32[96,1536]{1,0:T(8,128)} %collective-permute-done.near, f32[2,96,1536]{2,1,0:T(8,128)} %copy-done.14, f32[]{:T(128)} %bitcast.24, f32[]{:T(128)} %bitcast.22, f32[]{:T(128)} %bitcast.21), kind=kLoop, calls=%fused_computation.27 | loop fusion | flops 737280 | bytes 2359308 | tf_op jit(solution)/shard_map/add | solution.py:616
  134.9 3.3 %collective-permute-start.1 = (f32[96,1536]{1,0:T(8,128)S(1)}, f32[96,1536]{1,0:T(8,128)}, u32[]{:S(2)}, u32[]{:S(2)}) collective-permute-start(f32[96,1536]{1,0:T(8,128)S(1)} %bitcast_add_fusion.3), channel_id=1, source_target_pairs={{8,16},{16,8},{9,17},{17,9},{10,18},{18,10},{11,19},{19,11},{12,20... | collective-permute-start | bytes 1769480 | tf_op jit(solution)/shard_map/ppermute | solution.py:618
  138.3 4.2 %bitcast_add_fusion.2 = f32[96,1536]{1,0:T(8,128)} fusion(f32[96,1536]{1,0:T(8,128)} %collective-permute-done.5.near, f32[2,96,1536]{2,1,0:T(8,128)} %copy-done.16, f32[]{:T(128)} %bitcast.43, f32[]{:T(128)} %bitcast.41, f32[]{:T(128)} %bitcast.40), kind=kLoop, calls=%fused_computation.26 | loop fusion | flops 737280 | bytes 2359308 | tf_op jit(solution)/shard_map/add | solution.py:616
  142.4 2.2 %collective-permute-start.6 = (f32[96,1536]{1,0:T(8,128)}, f32[96,1536]{1,0:T(8,128)}, u32[]{:S(2)}, u32[]{:S(2)}) collective-permute-start(f32[96,1536]{1,0:T(8,128)} %bitcast_add_fusion.2), channel_id=1, source_target_pairs={{8,16},{16,8},{9,17},{17,9},{10,18},{18,10},{11,19},{19,11},{12,20... | collective-permute-start | bytes 1769480 | tf_op jit(solution)/shard_map/ppermute | solution.py:618
  144.7 3.8 %bitcast_add_fusion.1 = f32[96,1536]{1,0:T(8,128)} fusion(f32[96,1536]{1,0:T(8,128)} %collective-permute-done.8.near, f32[2,96,1536]{2,1,0:T(8,128)S(1)} %copy-done.19, f32[]{:T(128)} %bitcast.48, f32[]{:T(128)} %bitcast.46, f32[]{:T(128)} %bitcast.45), kind=kLoop, calls=%fused_computation.25 | loop fusion | flops 737280 | bytes 2359308 | tf_op jit(solution)/shard_map/add | solution.py:616
  148.5 3.3 %collective-permute-start.9 = (f32[96,1536]{1,0:T(8,128)}, f32[96,1536]{1,0:T(8,128)}, u32[]{:S(2)}, u32[]{:S(2)}) collective-permute-start(f32[96,1536]{1,0:T(8,128)} %bitcast_add_fusion.1), channel_id=1, source_target_pairs={{8,16},{16,8},{9,17},{17,9},{10,18},{18,10},{11,19},{19,11},{12,20... | collective-permute-start | bytes 1769480 | tf_op jit(solution)/shard_map/ppermute | solution.py:618
  152.0 3.0 %bitcast_add_fusion = f32[96,1536]{1,0:T(8,128)S(1)} fusion(f32[96,1536]{1,0:T(8,128)} %collective-permute-done.11.near, f32[2,96,1536]{2,1,0:T(8,128)S(1)} %copy-done.12, f32[]{:T(128)} %bitcast.53, f32[]{:T(128)} %bitcast.51, f32[]{:T(128)} %bitcast.50), kind=kLoop, calls=%fused_computation.24 | loop fusion | flops 737280 | bytes 2359308 | tf_op jit(solution)/shard_map/add | solution.py:616
  154.9 2.3 %collective-permute-start.12 = (f32[96,1536]{1,0:T(8,128)S(1)}, f32[96,1536]{1,0:T(8,128)S(1)}, u32[]{:S(2)}, u32[]{:S(2)}) collective-permute-start(f32[96,1536]{1,0:T(8,128)S(1)} %bitcast_add_fusion), channel_id=1, source_target_pairs={{8,16},{16,8},{9,17},{17,9},{10,18},{18,10},{11,19},{19,11},{12,20... | collective-permute-start | bytes 1769480 | tf_op jit(solution)/shard_map/ppermute | solution.py:618
  157.2 6.6 %collective-permute-done.3 = f32[448,128]{1,0:T(8,128)S(1)} collective-permute-done((f32[448,128]{1,0:T(8,128)S(1)}, f32[448,128]{1,0:T(8,128)S(1)}, u32[]{:S(2)}, u32[]{:S(2)}) %collective-permute-start.3) | collective-permute-done | bytes 229408 | tf_op jit(solution)/shard_map/ppermute | solution.py:622
  164.6 2.0 %collective-permute-start.4 = (f32[896,128]{1,0:T(8,128)}, f32[896,128]{1,0:T(8,128)}, u32[]{:S(2)}, u32[]{:S(2)}) collective-permute-start(f32[896,128]{1,0:T(8,128)} %pad_maximum_fusion.2), channel_id=1, source_target_pairs={{0,8},{8,0},{16,24},{24,16},{1,9},{9,1},{17,25},{25,17},{2,10},{10... | collective-permute-start | bytes 1376264 | tf_op jit(solution)/shard_map/ppermute | solution.py:624
  166.6 1.7 multiply_add_fusion.4.kept
  168.4 2.8 %collective-permute-start.2 = (f32[96,1536]{1,0:T(8,128)S(1)}, f32[96,1536]{1,0:T(8,128)}, u32[]{:S(2)}, u32[]{:S(2)}) collective-permute-start(f32[96,1536]{1,0:T(8,128)S(1)} %multiply_add_fusion.4.kept), channel_id=1, source_target_pairs={{8,0},{16,24},{9,1},{17,25},{10,2},{18,26},{11,3},{19,27},{12,4},{... | collective-permute-start | bytes 1769480 | tf_op jit(solution)/shard_map/ppermute | solution.py:620
  171.2 2.8 %multiply_add_fusion.3.kept = f32[96,1536]{1,0:T(8,128)} fusion(f32[96,1536]{1,0:T(8,128)} %collective-permute-done.6, f32[96,1536]{1,0:T(8,128)} %bitcast_add_fusion.2, f32[]{:T(128)} %bitcast.44), kind=kLoop, calls=%fused_computation.30 | loop fusion | flops 294912 | bytes 1769476 | tf_op jit(solution)/shard_map/add | solution.py:619
  174.0 2.1 %collective-permute-start.7 = (f32[96,1536]{1,0:T(8,128)}, f32[96,1536]{1,0:T(8,128)}, u32[]{:S(2)}, u32[]{:S(2)}) collective-permute-start(f32[96,1536]{1,0:T(8,128)} %multiply_add_fusion.3.kept), channel_id=1, source_target_pairs={{8,0},{16,24},{9,1},{17,25},{10,2},{18,26},{11,3},{19,27},{12,4},{... | collective-permute-start | bytes 1769480 | tf_op jit(solution)/shard_map/ppermute | solution.py:620
  176.8 2.1 %collective-permute-start.13 = (f32[96,1536]{1,0:T(8,128)S(1)}, f32[96,1536]{1,0:T(8,128)}, u32[]{:S(2)}, u32[]{:S(2)}) collective-permute-start(f32[96,1536]{1,0:T(8,128)S(1)} %multiply_add_fusion.1.kept), channel_id=1, source_target_pairs={{8,0},{16,24},{9,1},{17,25},{10,2},{18,26},{11,3},{19,27},{12,4},{... | collective-permute-start | bytes 1769480 | tf_op jit(solution)/shard_map/ppermute | solution.py:620
  178.9 2.8 %multiply_add_fusion.2.kept = f32[96,1536]{1,0:T(8,128)} fusion(f32[96,1536]{1,0:T(8,128)} %collective-permute-done.9, f32[96,1536]{1,0:T(8,128)} %bitcast_add_fusion.1, f32[]{:T(128)} %bitcast.49), kind=kLoop, calls=%fused_computation.29 | loop fusion | flops 294912 | bytes 1769476 | tf_op jit(solution)/shard_map/add | solution.py:619
  181.7 2.1 %collective-permute-start.10 = (f32[96,1536]{1,0:T(8,128)}, f32[96,1536]{1,0:T(8,128)}, u32[]{:S(2)}, u32[]{:S(2)}) collective-permute-start(f32[96,1536]{1,0:T(8,128)} %multiply_add_fusion.2.kept), channel_id=1, source_target_pairs={{8,0},{16,24},{9,1},{17,25},{10,2},{18,26},{11,3},{19,27},{12,4},{... | collective-permute-start | bytes 1769480 | tf_op jit(solution)/shard_map/ppermute | solution.py:620
  186.8 1.3 pad_maximum_fusion.1.message
  188.1 2.9 %shard_map.81.rest_0_ = f32[2,4,96,1536]{3,2,1,0:T(8,128)} custom-call(f32[2,96,1536]{2,1,0:T(8,128)S(1)} %copy-done.12, f32[96,1536]{1,0:T(8,128)} %collective-permute-done.11.near, f32[96,1536]{1,0:T(8,128)} %collective-permute-done.13.far, f32[96,1536]{1,0:T(8,128)S(1)} %multiply_add_fusion.1.kept, f32[1792,128]{1,0:T(8,128)S(1)} %pad_maximum_fusion.1.message, ...), custom_call_target="tpu_custom_call" | custom-call | flops 100000000 | bytes 5000000 | tf_op jit(solution)/shard_map/pallas_call | solution.py:584
  191.0 3.2 %shard_map.82.rest_0_ = f32[2,4,96,1536]{3,2,1,0:T(8,128)} custom-call(f32[2,96,1536]{2,1,0:T(8,128)S(1)} %copy-done.19, f32[96,1536]{1,0:T(8,128)} %collective-permute-done.8.near, f32[96,1536]{1,0:T(8,128)} %collective-permute-done.10.far, f32[96,1536]{1,0:T(8,128)} %multiply_add_fusion.2.kept, ...), custom_call_target="tpu_custom_call", output_to_operand_aliasing={{}: (7, {})} | custom-call | flops 100000000 | bytes 5000000 | tf_op jit(solution)/shard_map/pallas_call | solution.py:584
  194.3 3.2 %shard_map.83.rest_0_ = f32[2,4,96,1536]{3,2,1,0:T(8,128)} custom-call(f32[2,96,1536]{2,1,0:T(8,128)S(1)} %copy-done.17, f32[96,1536]{1,0:T(8,128)} %collective-permute-done.5.near, f32[96,1536]{1,0:T(8,128)} %collective-permute-done.7.far, f32[96,1536]{1,0:T(8,128)} %multiply_add_fusion.3.kept, ...), custom_call_target="tpu_custom_call", output_to_operand_aliasing={{}: (7, {})} | custom-call | flops 100000000 | bytes 5000000 | tf_op jit(solution)/shard_map/pallas_call | solution.py:584
  197.5 2.9 %shard_map.84 = f32[2,4,96,1536]{3,2,1,0:T(8,128)} custom-call(f32[2,96,1536]{2,1,0:T(8,128)S(1)} %copy-done.15, f32[96,1536]{1,0:T(8,128)} %collective-permute-done.near, f32[96,1536]{1,0:T(8,128)} %collective-permute-done.2.far, f32[96,1536]{1,0:T(8,128)S(1)} %multiply_add_fusion.4.kept, ...), custom_call_target="tpu_custom_call", output_to_operand_aliasing={{}: (7, {})} | custom-call | flops 100000000 | bytes 5000000 | tf_op jit(solution)/shard_map/pallas_call | solution.py:584
  (156 shorter events, 26.5 us)
Async XLA Ops:
  15.3 38.1 %all-to-all-start = ((f32[8,72,128]{2,1,0:T(8,128)}), f32[8,72,128]{2,1,0:T(8,128)S(1)}, u32[]{:S(2)}, u32[]{:S(2)}) async-start(f32[8,72,128]{2,1,0:T(8,128)} %shard_map.73), calls=%async_computation | async-start | bytes 589824 | tf_op jit(solution)/shard_map/all_to_all | solution.py:701
  54.8 37.5 %copy-start.2 = (bf16[8,256,256]{2,1,0:T(8,128)(2,1)S(1)}, bf16[8,256,256]{2,1,0:T(8,128)(2,1)}, u32[]{:S(2)}) copy-start(bf16[8,256,256]{2,1,0:T(8,128)(2,1)} %pad_maximum_fusion.moment) | copy-start | bytes 3145732
  54.8 37.5 %copy-start.5 = (bf16[8,256,256]{2,1,0:T(8,128)(2,1)S(1)}, bf16[8,256,256]{2,1,0:T(8,128)(2,1)}, u32[]{:S(2)}) copy-start(bf16[8,256,256]{2,1,0:T(8,128)(2,1)} %get-tuple-element.39.near_low) | copy-start | bytes 3145732
  54.8 37.5 %copy-start.8 = (bf16[8,256,256]{2,1,0:T(8,128)(2,1)S(1)}, bf16[8,256,256]{2,1,0:T(8,128)(2,1)}, u32[]{:S(2)}) copy-start(bf16[8,256,256]{2,1,0:T(8,128)(2,1)} %get-tuple-element.40.near_high) | copy-start | bytes 3145732
  55.9 2.3 %copy-start.13 = (f32[2,4,96,1536]{3,2,1,0:T(8,128)S(1)}, f32[2,4,96,1536]{3,2,1,0:T(8,128)}, u32[]{:S(2)}) copy-start(f32[2,4,96,1536]{3,2,1,0:T(8,128)} %param.7) | copy-start | bytes 14155780
  92.3 3.4 %copy-start = (f32[12,768,128]{2,1,0:T(8,128)}, f32[12,768,128]{2,1,0:T(8,128)S(1)}, u32[]{:S(2)}) copy-start(f32[12,768,128]{2,1,0:T(8,128)S(1)} %get-tuple-element.21) | copy-start | bytes 14155780
  92.3 3.4 %copy-start.20 = (f32[384,128]{1,0:T(8,128)}, f32[384,128]{1,0:T(8,128)S(1)}, u32[]{:S(2)}) copy-start(f32[384,128]{1,0:T(8,128)S(1)} %get-tuple-element.24) | copy-start | bytes 589828
  95.7 1.1 copy-start.14
  96.7 34.8 %collective-permute-start = (f32[96,1536]{1,0:T(8,128)}, f32[96,1536]{1,0:T(8,128)}, u32[]{:S(2)}, u32[]{:S(2)}) collective-permute-start(f32[96,1536]{1,0:T(8,128)} %get-tuple-element.23), channel_id=1, source_target_pairs={{0,8},{8,0},{16,24},{24,16},{1,9},{9,1},{17,25},{25,17},{2,10},{10... | collective-permute-start | bytes 1769480 | tf_op jit(solution)/shard_map/ppermute | solution.py:614
  96.9 23.5 %all-to-all-start.1 = ((f32[8,48,128]{2,1,0:T(8,128)}), f32[8,48,128]{2,1,0:T(8,128)S(1)}, u32[]{:S(2)}, u32[]{:S(2)}) async-start(f32[8,48,128]{2,1,0:T(8,128)} %bitcast.85), calls=%async_computation.1 | async-start | bytes 393216 | tf_op jit(solution)/shard_map/all_to_all | solution.py:721
  100.5 2.3 %copy-start.1 = (f32[12,768,128]{2,1,0:T(8,128)S(1)}, f32[12,768,128]{2,1,0:T(8,128)}, u32[]{:S(2)}) copy-start(f32[12,768,128]{2,1,0:T(8,128)} %copy-done) | copy-start | bytes 14155780
  102.8 1.2 copy-start.3
  104.1 1.2 copy-start.6
  105.3 1.2 copy-start.9
  109.8 1.0 copy-start.16
  110.9 27.4 %collective-permute-start.5 = (f32[96,1536]{1,0:T(8,128)}, f32[96,1536]{1,0:T(8,128)}, u32[]{:S(2)}, u32[]{:S(2)}) collective-permute-start(f32[96,1536]{1,0:T(8,128)} %get-tuple-element.28), channel_id=1, source_target_pairs={{0,8},{8,0},{16,24},{24,16},{1,9},{9,1},{17,25},{25,17},{2,10},{10... | collective-permute-start | bytes 1769480 | tf_op jit(solution)/shard_map/ppermute | solution.py:614
  114.5 1.0 copy-start.18
  115.5 29.2 %collective-permute-start.8 = (f32[96,1536]{1,0:T(8,128)}, f32[96,1536]{1,0:T(8,128)}, u32[]{:S(2)}, u32[]{:S(2)}) collective-permute-start(f32[96,1536]{1,0:T(8,128)} %get-tuple-element.30), channel_id=1, source_target_pairs={{0,8},{8,0},{16,24},{24,16},{1,9},{9,1},{17,25},{25,17},{2,10},{10... | collective-permute-start | bytes 1769480 | tf_op jit(solution)/shard_map/ppermute | solution.py:614
  119.0 1.1 copy-start.11
  120.0 31.9 %collective-permute-start.11 = (f32[96,1536]{1,0:T(8,128)}, f32[96,1536]{1,0:T(8,128)}, u32[]{:S(2)}, u32[]{:S(2)}) collective-permute-start(f32[96,1536]{1,0:T(8,128)} %get-tuple-element.32), channel_id=1, source_target_pairs={{0,8},{8,0},{16,24},{24,16},{1,9},{9,1},{17,25},{25,17},{2,10},{10... | collective-permute-start | bytes 1769480 | tf_op jit(solution)/shard_map/ppermute | solution.py:614
  120.4 1.2 copy-start.4
  121.6 1.2 copy-start.7
  122.8 1.2 copy-start.10
  125.9 18.8 %copy-start.19 = (f32[2,96,1536]{2,1,0:T(8,128)S(1)}, f32[2,96,1536]{2,1,0:T(8,128)}, u32[]{:S(2)}) copy-start(f32[2,96,1536]{2,1,0:T(8,128)} %copy-done.18) | copy-start | bytes 3538948
  125.9 26.1 %copy-start.12 = (f32[2,96,1536]{2,1,0:T(8,128)S(1)}, f32[2,96,1536]{2,1,0:T(8,128)}, u32[]{:S(2)}) copy-start(f32[2,96,1536]{2,1,0:T(8,128)} %copy-done.11) | copy-start | bytes 3538948
  125.9 25.9 %all-to-all-start.2 = ((f32[8,56,128]{2,1,0:T(8,128)}), f32[8,56,128]{2,1,0:T(8,128)S(1)}, u32[]{:S(2)}, u32[]{:S(2)}) async-start(f32[8,56,128]{2,1,0:T(8,128)} %bitcast.31), calls=%async_computation.2 | async-start | bytes 458752 | tf_op jit(solution)/shard_map/all_to_all | solution.py:724
  134.9 31.7 %collective-permute-start.1 = (f32[96,1536]{1,0:T(8,128)S(1)}, f32[96,1536]{1,0:T(8,128)}, u32[]{:S(2)}, u32[]{:S(2)}) collective-permute-start(f32[96,1536]{1,0:T(8,128)S(1)} %bitcast_add_fusion.3), channel_id=1, source_target_pairs={{8,16},{16,8},{9,17},{17,9},{10,18},{18,10},{11,19},{19,11},{12,20... | collective-permute-start | bytes 1769480 | tf_op jit(solution)/shard_map/ppermute | solution.py:618
  142.4 28.7 %collective-permute-start.6 = (f32[96,1536]{1,0:T(8,128)}, f32[96,1536]{1,0:T(8,128)}, u32[]{:S(2)}, u32[]{:S(2)}) collective-permute-start(f32[96,1536]{1,0:T(8,128)} %bitcast_add_fusion.2), channel_id=1, source_target_pairs={{8,16},{16,8},{9,17},{17,9},{10,18},{18,10},{11,19},{19,11},{12,20... | collective-permute-start | bytes 1769480 | tf_op jit(solution)/shard_map/ppermute | solution.py:618
  148.5 30.4 %collective-permute-start.9 = (f32[96,1536]{1,0:T(8,128)}, f32[96,1536]{1,0:T(8,128)}, u32[]{:S(2)}, u32[]{:S(2)}) collective-permute-start(f32[96,1536]{1,0:T(8,128)} %bitcast_add_fusion.1), channel_id=1, source_target_pairs={{8,16},{16,8},{9,17},{17,9},{10,18},{18,10},{11,19},{19,11},{12,20... | collective-permute-start | bytes 1769480 | tf_op jit(solution)/shard_map/ppermute | solution.py:618
  151.8 14.8 %copy-start.21 = (f32[8,56,128]{2,1,0:T(8,128)}, f32[8,56,128]{2,1,0:T(8,128)S(1)}, u32[]{:S(2)}) copy-start(f32[8,56,128]{2,1,0:T(8,128)S(1)} %all-to-all-done.2) | copy-start | bytes 688132
  151.8 11.9 %collective-permute-start.3 = (f32[448,128]{1,0:T(8,128)S(1)}, f32[448,128]{1,0:T(8,128)S(1)}, u32[]{:S(2)}, u32[]{:S(2)}) collective-permute-start(f32[448,128]{1,0:T(8,128)S(1)} %bitcast.86), channel_id=1, source_target_pairs={{0,16},{16,0},{8,24},{24,8},{1,17},{17,1},{9,25},{25,9},{2,18},{18... | collective-permute-start | bytes 688136 | tf_op jit(solution)/shard_map/ppermute | solution.py:622
  151.9 32.5 %copy-start.23 = (f32[4,2,8]{0,1,2:T(2,128)S(1)}, f32[4,2,8]{0,1,2:T(2,128)}, u32[]{:S(2)}) copy-start(f32[4,2,8]{0,1,2:T(2,128)} %copy.81) | copy-start | bytes 772
  154.9 21.2 %collective-permute-start.12 = (f32[96,1536]{1,0:T(8,128)S(1)}, f32[96,1536]{1,0:T(8,128)S(1)}, u32[]{:S(2)}, u32[]{:S(2)}) collective-permute-start(f32[96,1536]{1,0:T(8,128)S(1)} %bitcast_add_fusion), channel_id=1, source_target_pairs={{8,16},{16,8},{9,17},{17,9},{10,18},{18,10},{11,19},{19,11},{12,20... | collective-permute-start | bytes 1769480 | tf_op jit(solution)/shard_map/ppermute | solution.py:618
  163.8 2.9 %copy-start.22 = (f32[448,128]{1,0:T(8,128)}, f32[448,128]{1,0:T(8,128)S(1)}, u32[]{:S(2)}) copy-start(f32[448,128]{1,0:T(8,128)S(1)} %collective-permute-done.3) | copy-start | bytes 688132
  164.6 22.2 %collective-permute-start.4 = (f32[896,128]{1,0:T(8,128)}, f32[896,128]{1,0:T(8,128)}, u32[]{:S(2)}, u32[]{:S(2)}) collective-permute-start(f32[896,128]{1,0:T(8,128)} %pad_maximum_fusion.2), channel_id=1, source_target_pairs={{0,8},{8,0},{16,24},{24,16},{1,9},{9,1},{17,25},{25,17},{2,10},{10... | collective-permute-start | bytes 1376264 | tf_op jit(solution)/shard_map/ppermute | solution.py:624
  168.4 29.1 %collective-permute-start.2 = (f32[96,1536]{1,0:T(8,128)S(1)}, f32[96,1536]{1,0:T(8,128)}, u32[]{:S(2)}, u32[]{:S(2)}) collective-permute-start(f32[96,1536]{1,0:T(8,128)S(1)} %multiply_add_fusion.4.kept), channel_id=1, source_target_pairs={{8,0},{16,24},{9,1},{17,25},{10,2},{18,26},{11,3},{19,27},{12,4},{... | collective-permute-start | bytes 1769480 | tf_op jit(solution)/shard_map/ppermute | solution.py:620
  174.0 20.3 %collective-permute-start.7 = (f32[96,1536]{1,0:T(8,128)}, f32[96,1536]{1,0:T(8,128)}, u32[]{:S(2)}, u32[]{:S(2)}) collective-permute-start(f32[96,1536]{1,0:T(8,128)} %multiply_add_fusion.3.kept), channel_id=1, source_target_pairs={{8,0},{16,24},{9,1},{17,25},{10,2},{18,26},{11,3},{19,27},{12,4},{... | collective-permute-start | bytes 1769480 | tf_op jit(solution)/shard_map/ppermute | solution.py:620
  176.8 11.3 %collective-permute-start.13 = (f32[96,1536]{1,0:T(8,128)S(1)}, f32[96,1536]{1,0:T(8,128)}, u32[]{:S(2)}, u32[]{:S(2)}) collective-permute-start(f32[96,1536]{1,0:T(8,128)S(1)} %multiply_add_fusion.1.kept), channel_id=1, source_target_pairs={{8,0},{16,24},{9,1},{17,25},{10,2},{18,26},{11,3},{19,27},{12,4},{... | collective-permute-start | bytes 1769480 | tf_op jit(solution)/shard_map/ppermute | solution.py:620
  181.7 9.4 %collective-permute-start.10 = (f32[96,1536]{1,0:T(8,128)}, f32[96,1536]{1,0:T(8,128)}, u32[]{:S(2)}, u32[]{:S(2)}) collective-permute-start(f32[96,1536]{1,0:T(8,128)} %multiply_add_fusion.2.kept), channel_id=1, source_target_pairs={{8,0},{16,24},{9,1},{17,25},{10,2},{18,26},{11,3},{19,27},{12,4},{... | collective-permute-start | bytes 1769480 | tf_op jit(solution)/shard_map/ppermute | solution.py:620
  191.0 3.2 %copy-start.17 = (f32[2,96,1536]{2,1,0:T(8,128)S(1)}, f32[2,96,1536]{2,1,0:T(8,128)}, u32[]{:S(2)}) copy-start(f32[2,96,1536]{2,1,0:T(8,128)} %copy-done.16) | copy-start | bytes 3538948
  194.2 3.2 %copy-start.15 = (f32[2,96,1536]{2,1,0:T(8,128)S(1)}, f32[2,96,1536]{2,1,0:T(8,128)}, u32[]{:S(2)}) copy-start(f32[2,96,1536]{2,1,0:T(8,128)} %copy-done.14) | copy-start | bytes 3538948

commit v2 on v1

v2 whole, which is shorter than its diff:
```python
import functools

import jax
import jax.numpy as jnp
from jax import lax
from jax.experimental import pallas as pl
from jax.experimental.pallas import tpu as pltpu
from jax.sharding import PartitionSpec as P

f32 = jnp.float32
i32 = jnp.int32
bf16 = jnp.bfloat16
highest = lax.Precision.HIGHEST

LANES = 128
SUBLANES = 8
BLOCK = 256
CHAINS = 4

VMEM = pl.BlockSpec(memory_space=pltpu.VMEM)
SMEM = pl.BlockSpec(memory_space=pltpu.SMEM)
HBM = pl.BlockSpec(memory_space=pltpu.HBM)


def params(mib):
    return pltpu.CompilerParams(vmem_limit_bytes=mib << 20)


def cost(flops, read):
    return pl.CostEstimate(flops=flops, bytes_accessed=read, transcendentals=0)


def dot(a, b, dims=(((1,), (0,)), ((), ()))):
    return lax.dot_general(a, b, dims, preferred_element_type=f32)


def split(x):
    high = x.astype(bf16)
    return high, (x - high.astype(f32)).astype(bf16)


def pack_kernel(sizes, owners, cells, values, packed, places, tally, joined, counts, sem):
    sub_count, group_count, chunk_count, strip = sizes
    block_count = owners.shape[0]
    tiles = group_count // SUBLANES
    lane = lax.broadcasted_iota(i32, (SUBLANES, LANES), 1)
    square = lambda axis: lax.broadcasted_iota(i32, (LANES, LANES), axis)
    owner = owners[...]
    picked = [jnp.where(owner == sub, 1.0, 0.0) for sub in range(sub_count)]
    upto = jnp.where(square(0) <= square(1), 1.0, 0.0).astype(bf16)
    ranks = dot(jnp.concatenate(picked, axis=0).astype(bf16), upto)
    wide = lax.broadcasted_iota(i32, (block_count, LANES), 1)
    place = jnp.zeros((block_count, LANES), f32)
    base = jnp.zeros((block_count, LANES), f32)
    totals = jnp.zeros((block_count, LANES), f32)
    for sub in range(sub_count):
        rank = ranks[sub * block_count : (sub + 1) * block_count]
        total = jnp.broadcast_to(rank[:, LANES - 1 :], rank.shape)
        place = jnp.where(owner == sub, rank - 1.0 + base, place)
        totals = jnp.where(wide == sub, total, totals)
        base = base + total
    places[...] = place.astype(i32)
    tally[...] = totals.astype(i32)
    copy = pltpu.make_async_copy(tally, counts, sem)
    copy.start()
    copy.wait()
    extra = -(group_count + SUBLANES) % 16
    row = square(0)

    def one_block(block, ends):
        at = pl.multiple_of(block * LANES, LANES)
        parts = [
            values[:, pl.ds(at, LANES)],
            jnp.broadcast_to(cells[pl.ds(block, 1), :], (SUBLANES, LANES)).astype(f32),
        ]
        if extra:
            parts.append(jnp.zeros((extra, LANES), f32))
        whole = jnp.concatenate(parts, axis=0)
        rows = whole.shape[0]
        high, rest = whole.astype(bf16), whole
        rest = rest - high.astype(f32)
        middle = rest.astype(bf16)
        low = (rest - middle.astype(f32)).astype(bf16)
        move = jnp.where(row == places[pl.ds(block, 1), :], 1.0, 0.0).astype(bf16)
        moved = dot(
            jnp.concatenate([high, middle, low], axis=0), move, (((1,), (1,)), ((), ()))
        )
        moved = moved[:rows] + moved[rows : 2 * rows] + moved[2 * rows :]
        start = jnp.int32(0)
        writes, following = [], []
        for sub in range(sub_count):
            end = ends[sub]
            chunk, offset = lax.shift_right_logical(end, 7), end & 127
            for tile in range(tiles + 1):
                turned = pltpu.roll(
                    moved[tile * SUBLANES : (tile + 1) * SUBLANES], (end - start) & 127, 1
                )
                kept = jnp.where(lane >= offset, turned, joined[sub, chunk, tile])
                writes.append((sub, chunk, tile, kept, turned))
            start = start + counts[block, sub]
            following.append(end + counts[block, sub])
        for sub, chunk, tile, kept, turned in writes:
            joined[sub, chunk, tile] = kept
            joined[sub, chunk + 1, tile] = turned
        return tuple(following)

    ends = lax.fori_loop(0, block_count, one_block, (jnp.int32(0),) * sub_count)
    word_row = chunk_count * group_count
    word_rows = packed.shape[1] - word_row
    for sub in range(sub_count):
        packed[sub, word_row:, :] = jnp.full((word_rows, LANES), float(strip), f32)
        for chunk in range(chunk_count):
            for tile in range(tiles):
                at = chunk * group_count + tile * SUBLANES
                packed[sub, at : at + SUBLANES, :] = joined[sub, chunk, tile]
            filled = lane + chunk * LANES < ends[sub]
            cell = jnp.where(filled, joined[sub, chunk, tiles], 0.0).astype(i32)
            word = (cell - (cell & 127)) + ((cell - lane) & 127)
            word = jnp.where(filled, word, strip).astype(f32)
            packed[sub, word_row + chunk : word_row + chunk + 1, :] = word[:1]


def pack_observations(obs_values, owners, cells, sub_count, strip, capacity):
    group_count, obs_count = obs_values.shape
    chunk_count = capacity // LANES
    block_count = obs_count // LANES
    rows = chunk_count * group_count + SUBLANES * (-(-chunk_count // SUBLANES))
    tiles = group_count // SUBLANES
    return pl.pallas_call(
        functools.partial(pack_kernel, (sub_count, group_count, chunk_count, strip)),
        out_shape=jax.ShapeDtypeStruct((sub_count, rows, LANES), f32),
        in_specs=[VMEM, VMEM, VMEM],
        out_specs=VMEM,
        scratch_shapes=[
            pltpu.VMEM((block_count, LANES), i32),
            pltpu.VMEM((block_count, LANES), i32),
            pltpu.VMEM((sub_count, chunk_count + 2, tiles + 1, SUBLANES, LANES), f32),
            pltpu.SMEM((block_count, LANES), i32),
            pltpu.SemaphoreType.DMA,
        ],
        compiler_params=params(40),
        cost_estimate=cost(10**6, 10**6),
    )(owners.reshape(block_count, LANES), cells.reshape(block_count, LANES), obs_values)


def deposit_kernel(sizes, index, lengths, got, field, swept, exits, loaded, *rest):
    sub_count, group_count, row_count, column_count, chunk_count, strip = sizes
    totals, (decay, own, integers, words, word_sem, sems) = rest[:CHAINS], rest[CHAINS:]
    tiles = group_count // SUBLANES
    word_row = chunk_count * group_count
    word_rows = got.shape[1] - word_row

    def load(column):
        return pltpu.make_async_copy(
            field.at[:, pl.ds(column * LANES, LANES)], loaded.at[column], sems.at[column]
        )

    for source in range(sub_count):
        integers[source * word_rows : (source + 1) * word_rows, :] = got[
            source, word_row:, :
        ].astype(i32)
    hand_over = pltpu.make_async_copy(integers, words, word_sem)
    hand_over.start()
    for column in range(column_count):
        load(column).start()
    here = index[0]
    for group in range(group_count):
        own[group : group + 1, :] = jnp.exp(-1.0 / lengths[group, pl.ds(here, 1), :])
    for tile in range(tiles):
        keep = own[tile * SUBLANES : (tile + 1) * SUBLANES, :]
        for row in range(row_count):
            decay[row, tile] = jnp.broadcast_to(keep[:, row : row + 1], (SUBLANES, LANES))

    def clear(at, carry):
        for total in totals:
            for tile in range(tiles):
                for k in range(8):
                    total[tile, at * 8 + k] = jnp.zeros((SUBLANES, LANES), f32)
        return carry

    lax.fori_loop(0, row_count * column_count // 8, clear, 0)
    lane = lax.broadcasted_iota(i32, (SUBLANES, LANES), 1)
    hand_over.wait()

    def one_source(source, carry):
        first = source * word_rows

        def more(chunk):
            last = jnp.minimum(chunk, chunk_count - 1)
            return (chunk < chunk_count) & (words[first + last, 0] < strip)

        def one_chunk(chunk):
            blocks = [
                got[
                    source,
                    pl.ds(pl.multiple_of(chunk * group_count + tile * SUBLANES, 8), SUBLANES),
                    :,
                ]
                for tile in range(tiles)
            ]
            for slot in range(LANES):
                word = words[first + chunk, slot]
                target = lax.shift_right_logical(word, 7)
                turn = word & 127
                for tile in range(tiles):
                    value = pltpu.roll(jnp.where(lane == slot, blocks[tile], 0.0), turn, 1)
                    total = totals[slot % CHAINS]
                    total[tile, target] = total[tile, target] + value
            return chunk + 1

        lax.while_loop(more, one_chunk, jnp.int32(0))
        return carry

    lax.fori_loop(0, sub_count, one_source, 0)
    for column in range(column_count):
        load(column).wait()

    for tile in range(tiles):
        held = totals[0]
        spot = tile * SUBLANES * row_count

        def read_first(row, column):
            at = row * column_count + column
            value = loaded[column, pl.ds(spot + row, SUBLANES, stride=row_count), :]
            for total in totals:
                value = value + total[tile, at]
            return value

        def read_held(row, column):
            return held[tile, row * column_count + column]

        def write_held(row, column, value):
            held[tile, row * column_count + column] = value

        def write_last(row, column, value):
            swept[column, pl.ds(spot + row, SUBLANES, stride=row_count), :] = value

        for turn in range(4):
            read = read_first if turn == 0 else read_held
            write = write_last if turn == 3 else write_held

            def one_row(step, state, turn=turn, read=read, write=write):
                row = row_count - 1 - step if turn % 2 else step
                keep = decay[row, tile]
                take = 1.0 - keep
                following = []
                for column in range(column_count):
                    value = keep * state[column] + take * read(row, column)
                    write(row, column, value)
                    following.append(value)
                return tuple(following)

            nothing = tuple(jnp.zeros((SUBLANES, LANES), f32) for _ in range(column_count))
            state = lax.fori_loop(0, row_count, one_row, nothing, unroll=4)
            message_rows = 4 * column_count
            for column in range(column_count):
                at = tile * SUBLANES * message_rows + turn * column_count + column
                exits[pl.ds(at, SUBLANES, stride=message_rows), :] = state[column]


def deposit_and_sweep(index, lengths, got, field, sizes):
    sub_count, group_count, row_count, column_count, chunk_count, strip = sizes
    tiles = group_count // SUBLANES
    cells = row_count * column_count
    word_rows = got.shape[1] - chunk_count * group_count
    return pl.pallas_call(
        functools.partial(deposit_kernel, sizes),
        out_shape=[
            jax.ShapeDtypeStruct((column_count, group_count * row_count, LANES), f32),
            jax.ShapeDtypeStruct((group_count * 4 * column_count, LANES), f32),
        ],
        in_specs=[SMEM, VMEM, VMEM, HBM],
        out_specs=[VMEM, VMEM],
        scratch_shapes=[pltpu.VMEM((column_count, group_count * row_count, LANES), f32)]
        + [pltpu.VMEM((tiles, cells + 8, SUBLANES, LANES), f32)] * CHAINS
        + [
            pltpu.VMEM((row_count, tiles, SUBLANES, LANES), f32),
            pltpu.VMEM((group_count, LANES), f32),
            pltpu.VMEM((sub_count * word_rows, LANES), i32),
            pltpu.SMEM((sub_count * word_rows, LANES), i32),
            pltpu.SemaphoreType.DMA,
            pltpu.SemaphoreType.DMA((column_count,)),
        ],
        compiler_params=params(56),
        cost_estimate=cost(10**7, 10**7),
    )(index, lengths, got, field)


def prepare_kernel(sizes, index, lon_length, lengths, *rest):
    sub_count, row_count, block_count = sizes
    near_high, near_low, moment, spread, inside, leaving, decay, held = rest
    group = pl.program_id(0)

    @pl.when(group == 0)
    def _():
        keep = jnp.exp(-1.0 / lengths[index[0]])
        decay[...] = jnp.zeros(decay.shape, f32)
        for turn in range(4):
            decay[pl.ds(turn, sub_count, stride=4), :] = keep
        decay[...] = jnp.transpose(decay[...], (1, 0))
        held[...] = jnp.zeros(held.shape, f32)
        state_of = lax.broadcasted_iota(i32, (1, LANES), 1) & 3
        for turn in range(4):

            def one_row(step, state, turn=turn):
                row = row_count - 1 - step if turn % 2 else step
                keep = decay[pl.ds(row, 1), :]
                value = keep * state + (1.0 - keep) * held[pl.ds(row, 1), :]
                held[pl.ds(row, 1), :] = value
                return value

            enter = jnp.where(state_of == turn, 1.0, 0.0)
            state = lax.fori_loop(0, row_count, one_row, enter, unroll=8)
            leaving[turn : turn + 1, :] = state
        inside[...] = jnp.transpose(held[...], (1, 0))

    def ramp(shape, axis):
        return lax.broadcasted_iota(i32, shape, axis)

    def constant(x, shape):
        return jnp.broadcast_to(x, shape)

    one = (1, LANES)
    rate = -1.0 / jnp.full(one, lon_length[group], f32)
    decays = jnp.exp(rate)
    gain = ((1.0 - decays) / (1.0 + decays)) ** 2
    centre = (1.0 + decays * decays) / (1.0 - decays * decays)
    turn = jnp.exp(rate * float(BLOCK * block_count))
    lag = float(BLOCK * block_count) * turn / (1.0 - turn)
    full_gain = gain / (1.0 - turn)

    def twice(x):
        return jnp.concatenate([x, x], axis=1)

    shape = (BLOCK, BLOCK)
    gap = jnp.abs(ramp(shape, 0) - ramp(shape, 1)).astype(f32)
    near = twice(gain) * jnp.exp(twice(rate) * gap) * (gap + twice(centre))
    high, low = split(near)
    near_high[0] = high
    near_low[0] = low
    shape = (BLOCK, LANES)
    kind = ramp(shape, 1) & 3
    spot = ramp(shape, 0)
    far = jnp.where(kind < 2, BLOCK - spot, spot).astype(f32)
    sums = jnp.exp(rate * far) * jnp.where((kind & 1) == 1, far, 1.0)
    high, low = split(sums)
    moment[0, :, :LANES] = high
    moment[0, :, LANES:] = low
    shape = (32, BLOCK)
    kind = ramp(shape, 0) & 3
    block = lax.shift_right_logical(ramp(shape, 0), 2)
    spot = ramp(shape, 1)
    reach = jnp.where(kind < 2, spot, BLOCK - spot).astype(f32)
    for at in range(block_count):
        ahead = jnp.where(kind < 2, at - block, block - at) - 1
        steps = jnp.where(ahead < 0, ahead + block_count, ahead)
        full = reach + (steps * BLOCK).astype(f32)
        weight = twice(full_gain) * jnp.exp(twice(rate) * full)
        lead = full + twice(centre + lag)
        value = jnp.where((kind & 1) == 1, weight, weight * lead)
        value = jnp.where(block < block_count, value, 0.0)
        high, low = split(value)
        spread[0, :32, at * BLOCK : (at + 1) * BLOCK] = high
        spread[0, 32:, at * BLOCK : (at + 1) * BLOCK] = low


def prepare(index, lon_length, lengths, row_count, column_total):
    group_count, sub_count, _ = lengths.shape
    sizes = (sub_count, row_count, column_total // BLOCK)
    shapes = [
        ((BLOCK, BLOCK), bf16),
        ((BLOCK, BLOCK), bf16),
        ((BLOCK, BLOCK), bf16),
        ((64, column_total), bf16),
    ]
    return pl.pallas_call(
        functools.partial(prepare_kernel, sizes),
        grid=(group_count,),
        in_specs=[SMEM, SMEM, VMEM],
        out_specs=[pl.BlockSpec((1,) + shape, lambda i: (i, 0, 0)) for shape, _ in shapes]
        + [
            pl.BlockSpec((LANES, LANES), lambda i: (0, 0)),
            pl.BlockSpec((4, LANES), lambda i: (0, 0)),
        ],
        out_shape=[jax.ShapeDtypeStruct((group_count,) + shape, kind) for shape, kind in shapes]
        + [
            jax.ShapeDtypeStruct((LANES, LANES), f32),
            jax.ShapeDtypeStruct((4, LANES), f32),
        ],
        scratch_shapes=[pltpu.VMEM((LANES, LANES), f32)] * 2,
        compiler_params=params(56),
        cost_estimate=cost(10**7, 10**7),
    )(index, lon_length, lengths)


def circle(pieces, near_high, near_low, moment, spread):
    row_count = pieces[0].shape[0]
    whole = jnp.concatenate(pieces, axis=0)
    high, low = split(whole)
    near = dot(high, near_high) + dot(low, near_high) + dot(high, near_low)
    sums = dot(high, moment)
    sums = sums[:, :LANES] + sums[:, LANES:] + dot(low, moment[:, :LANES])
    lane = lax.broadcasted_iota(i32, (row_count, LANES), 1)
    slot = lax.shift_right_logical(lane, 2) & 7
    moments = jnp.zeros((row_count, LANES), f32)
    for at in range(len(pieces)):
        part = sums[at * row_count : (at + 1) * row_count]
        moments = jnp.where(slot == at, part, moments)
    rest = moments - moments.astype(bf16).astype(f32)
    moments = jnp.where((lax.shift_right_logical(lane, 5) & 1) == 1, rest, moments).astype(bf16)
    spread = jnp.concatenate([spread[:32], spread[:32], spread[32:], spread[32:]], axis=0)
    far = dot(moments, spread)
    return [
        near[at * row_count : (at + 1) * row_count] + far[:, at * BLOCK : (at + 1) * BLOCK]
        for at in range(len(pieces))
    ]


def longitude_kernel(swept, near_high, near_low, moment, spread, *rest):
    column_count = swept.shape[0]
    pieces = [
        jnp.concatenate([swept[2 * at, 0], swept[2 * at + 1, 0]], axis=1)
        for at in range(column_count // 2)
    ]
    pieces = circle(pieces, near_high[0], near_low[0], moment[0], spread[0])
    out = rest[0] if len(rest) == 1 else rest[1]
    for at, piece in enumerate(pieces):
        out[0, :, at * BLOCK : (at + 1) * BLOCK] = piece
    if len(rest) == 1:
        return
    table, _, sent, part = rest
    level = pl.program_id(0)
    sums = []
    for target, first in ((sent, 0), (part, 2)):
        weight = table[0, pl.ds(first + level, 1), :]
        sums.append((target, jnp.concatenate([weight, weight], axis=1)))

    @pl.when(level == 0)
    def _():
        for target, weight in sums:
            for at, piece in enumerate(pieces):
                target[:, at * BLOCK : (at + 1) * BLOCK] = weight * piece

    @pl.when(level > 0)
    def _():
        for target, weight in sums:
            for at, piece in enumerate(pieces):
                spot = slice(at * BLOCK, (at + 1) * BLOCK)
                target[:, spot] = target[:, spot] + weight * piece


def longitude(swept, weights, count, first, stride, table=None):
    column_count, _, row_count, _ = swept.shape
    column_total = column_count * LANES

    def of(i):
        return first + stride * i

    in_specs = [
        pl.BlockSpec((column_count, 1, row_count, LANES), lambda i: (0, of(i), 0, 0)),
        pl.BlockSpec((1, BLOCK, BLOCK), lambda i: (of(i), 0, 0)),
        pl.BlockSpec((1, BLOCK, BLOCK), lambda i: (of(i), 0, 0)),
        pl.BlockSpec((1, BLOCK, BLOCK), lambda i: (of(i), 0, 0)),
        pl.BlockSpec((1, 64, column_total), lambda i: (of(i), 0, 0)),
    ]
    out_specs = [pl.BlockSpec((1, row_count, column_total), lambda i: (i, 0, 0))]
    out_shape = [jax.ShapeDtypeStruct((count, row_count, column_total), f32)]
    operands = [swept, *weights]
    if table is not None:
        in_specs.append(pl.BlockSpec((1, 16, LANES), lambda i: (first, 0, 0)))
        operands.append(table)
        out_specs += [pl.BlockSpec((row_count, column_total), lambda i: (0, 0))] * 2
        out_shape += [jax.ShapeDtypeStruct((row_count, column_total), f32)] * 2
    return pl.pallas_call(
        longitude_kernel,
        grid=(count,),
        in_specs=in_specs,
        out_specs=out_specs,
        out_shape=out_shape,
        compiler_params=params(56),
        cost_estimate=cost(count * 10**9, count * 2 * 10**6),
    )(*operands)


def chain_kernel(index, exits, leaving, inside, near_high, near_low, moment, spread, out, held):
    sub_count, _, _ = exits.shape
    column_count = exits.shape[1] // 4
    shape = (column_count, LANES)
    entering = {}
    for turn in range(4):
        order = list(range(sub_count))
        if turn % 2:
            order.reverse()
        state = jnp.zeros(shape, f32)
        for block in order:
            entering[turn, block] = state
            at = (turn * sub_count + block) * column_count
            held[at : at + column_count, :] = state
            state = exits[block, turn * column_count : (turn + 1) * column_count, :]
            for other in range(turn + 1):
                state = state + leaving[turn, block * 4 + other] * entering[other, block]
    pieces = []
    for at in range(column_count // 2):
        pair = [
            held[pl.ds(2 * at + k, 4 * sub_count, stride=column_count), :] for k in range(2)
        ]
        pieces.append(jnp.concatenate(pair, axis=1))
    pieces = circle(pieces, near_high[0], near_low[0], moment[0], spread[0])
    message_rows = out.shape[0] // sub_count
    for at, piece in enumerate(pieces):
        for k in range(2):
            for turn in range(4):
                place = turn * column_count + 2 * at + k
                out[pl.ds(place, sub_count, stride=message_rows), :] = piece[
                    turn * sub_count : (turn + 1) * sub_count, k * LANES : (k + 1) * LANES
                ]
    for block in range(sub_count):
        at = block * message_rows + 4 * column_count
        out[at : at + 4, :] = inside[block * 4 : (block + 1) * 4, :]
        out[at + 4 : (block + 1) * message_rows, :] = jnp.zeros(
            (message_rows - 4 * column_count - 4, LANES), f32
        )


def chain_states(index, exits, leaving, inside, weights):
    sub_count, rows, _ = exits.shape
    column_total = rows // 4 * LANES
    message_rows = rows + 8

    def whole(*shape):
        return pl.BlockSpec(shape, lambda i, at: (0,) * len(shape))

    def own(*shape):
        return pl.BlockSpec((1,) + shape, lambda i, at: (at[0], 0, 0))

    return pl.pallas_call(
        chain_kernel,
        grid_spec=pltpu.PrefetchScalarGridSpec(
            num_scalar_prefetch=1,
            grid=(1,),
            in_specs=[
                whole(*exits.shape),
                SMEM,
                whole(LANES, LANES),
                own(BLOCK, BLOCK),
                own(BLOCK, BLOCK),
                own(BLOCK, BLOCK),
                own(64, column_total),
            ],
            out_specs=whole(sub_count * message_rows, LANES),
            scratch_shapes=[pltpu.VMEM((sub_count * rows, LANES), f32)],
        ),
        out_shape=jax.ShapeDtypeStruct((sub_count * message_rows, LANES), f32),
        compiler_params=params(56),
        cost_estimate=cost(10**9, 2 * 10**6),
    )(index, exits, leaving, inside, *weights)


def pair_factors(top, low):
    top_take, low_take = 1.0 - top, 1.0 - low
    through = top * low
    sends = (low * top_take, low_take)
    low_out = (low_take * through, low, low_take * low * top_take, low_take * low_take)
    top_out = (
        top * low_out[0] + top_take * top,
        top * low_out[1],
        top * low_out[2] + top_take * top_take,
        top * low_out[3],
    )
    return through, sends, top_out, low_out


def tables_kernel(index, decay, table, mix):
    band = index[0]

    def factors(at):
        return pair_factors(decay[at * 8 : at * 8 + 4, :], decay[at * 8 + 4 : at * 8 + 8, :])

    def by_band(*values):
        result = values[0]
        for at in range(1, 4):
            result = jnp.where(band == at, values[at], result)
        return result

    through, sends, top_out, low_out = factors(0)
    across, beside, corner = factors(1), factors(2), factors(3)
    through_n, echo_n = beside[0], beside[2][0]
    third = by_band(across[0], corner[0], across[0], across[0])
    third_echo = by_band(across[2][0], corner[2][0], across[2][0], across[2][0])
    fourth_echo = by_band(corner[2][0], across[2][0], corner[2][0], corner[2][0])
    zeta = third * third * fourth_echo + third_echo
    rows = []
    for i in range(2):
        reply = top_out[2 + i]
        rows.append(by_band(sends[i], reply + through * zeta * sends[i], sends[i], reply))
    for i in range(2):
        rows.append(
            by_band(
                sends[i], sends[i], through * echo_n * sends[i] + top_out[2 + i], sends[i]
            )
        )
    rows.append(through)
    for fin, back, *own in (top_out, low_out):
        for i in range(2):
            rows.append(
                by_band(
                    own[i] + back * (through_n * through_n * zeta + echo_n) * sends[i],
                    own[i] + back * zeta * sends[i],
                    own[i] + back * echo_n * sends[i],
                    own[i],
                )
            )
        none = jnp.zeros_like(fin)
        rows.append(by_band(back, fin + back * zeta * through, back, fin))
        rows.append(by_band(back * through_n, none, none, fin * through_n))
        rows.append(by_band(none, back, fin + back * echo_n * through, none))
    for variable in range(4):
        for at, row in enumerate(rows):
            table[variable, at : at + 1, :] = row[variable : variable + 1]
    row = lax.broadcasted_iota(i32, (SUBLANES, LANES), 0)
    for variable in range(4):
        value = jnp.zeros((SUBLANES, LANES), f32)
        downward, keeps = [], []
        for level in range(8):
            other = (level // 2) ^ band
            place = (other & 1) * 2 + lax.shift_right_logical(other, 1)
            at = place * 8 + (level % 2) * 4 + variable
            keep = jnp.broadcast_to(decay[pl.ds(at, 1), :], (SUBLANES, LANES))
            unit = jnp.where(row == place * 2 + level % 2, 1.0, 0.0)
            value = keep * value + (1.0 - keep) * unit
            downward.append(value)
            keeps.append(keep)
        value = jnp.zeros((SUBLANES, LANES), f32)
        upward = [None] * 8
        for level in reversed(range(8)):
            value = keeps[level] * value + (1.0 - keeps[level]) * downward[level]
            upward[level] = value
        for level in range(2):
            mix[level, variable] = by_band(*[upward[2 * at + level] for at in range(4)])


def tables(index, decay):
    return pl.pallas_call(
        tables_kernel,
        in_specs=[SMEM, VMEM],
        out_specs=[VMEM, VMEM],
        out_shape=[
            jax.ShapeDtypeStruct((4, 16, LANES), f32),
            jax.ShapeDtypeStruct((2, 4, SUBLANES, LANES), f32),
        ],
        compiler_params=params(56),
        cost_estimate=cost(10**5, 10**5),
    )(index, decay)


def add_kernel(part, near, table, total):
    weight = table[0, 4:5, :]
    for column in range(part.shape[1] // LANES):
        at = slice(column * LANES, (column + 1) * LANES)
        total[:, at] = part[:, at] + weight * near[:, at]


def add_near(variable, part, near, table):
    row_count, column_total = part.shape
    steps = 2 if row_count % 16 == 0 else 1
    block = pl.BlockSpec((row_count // steps, column_total), lambda i: (i, 0))
    return pl.pallas_call(
        add_kernel,
        grid=(steps,),
        in_specs=[block, block, pl.BlockSpec((1, 16, LANES), lambda i: (variable, 0, 0))],
        out_specs=block,
        out_shape=jax.ShapeDtypeStruct(part.shape, f32),
        compiler_params=params(56),
        cost_estimate=cost(10**6, 2 * 10**6),
    )(part, near, table)


def last_kernel(own, near, far, met, message, mix, table, *rest):
    out, added = rest[-2:]
    rows, column_total = near.shape
    column_count = column_total // LANES
    row_count = added.shape[1]
    step = pl.program_id(0)

    @pl.when(step == 0)
    def _():
        parts = message.reshape(SUBLANES * message.shape[2], LANES)
        stride = message.shape[2]
        lanes = []
        for column in range(column_count):
            lanes.append(
                jnp.concatenate(
                    [
                        parts[pl.ds(k * column_count + column, SUBLANES, stride=stride), :]
                        for k in range(4)
                    ],
                    axis=0,
                )
            )
        high, low = split(jnp.concatenate(lanes, axis=1))
        states = jnp.concatenate([high, high, low, low], axis=0)
        inside = [parts[pl.ds(4 * column_count + k, SUBLANES, stride=stride), :] for k in range(4)]
        for level in range(2):
            mixed = jnp.concatenate([part * mix[level, 0] for part in inside], axis=0)
            high, low = split(mixed)
            mixed = jnp.concatenate([high, low, high, low], axis=0)
            added[level] = dot(mixed, states, (((0,), (0,)), ((), ())))[:row_count]

    first = pl.multiple_of(step * rows, SUBLANES)
    for level in range(2):
        weights = [table[0, 5 + level * 5 + k : 6 + level * 5 + k, :] for k in range(5)]
        for column in range(column_count):
            at = slice(column * LANES, (column + 1) * LANES)
            total = added[level, pl.ds(first, rows), at]
            total = total + weights[0] * own[0, :, at] + weights[1] * own[1, :, at]
            total = total + weights[2] * near[:, at] + weights[3] * far[:, at]
            out[level, 0, :, at] = total + weights[4] * met[:, at]


def last_step(variable, own, near, far, met, message, mix, table, so_far):
    _, row_count, column_total = own.shape
    steps = 3 if row_count % 24 == 0 else 1
    rows = row_count // steps
    block = pl.BlockSpec((rows, column_total), lambda i: (i, 0))
    message_rows = message.shape[2]
    operands = [own, near, far, met, message, mix, table]
    in_specs = [
        pl.BlockSpec((2, rows, column_total), lambda i: (0, i, 0)),
        block,
        block,
        block,
        pl.BlockSpec((8, 1, message_rows, LANES), lambda i: (0, variable, 0, 0)),
        pl.BlockSpec((2, 1, SUBLANES, LANES), lambda i: (0, variable, 0, 0)),
        pl.BlockSpec((1, 16, LANES), lambda i: (variable, 0, 0)),
    ]
    aliases = {}
    if so_far is not None:
        operands.append(so_far)
        in_specs.append(HBM)
        aliases = {7: 0}
    return pl.pallas_call(
        last_kernel,
        grid=(steps,),
        in_specs=in_specs,
        out_specs=pl.BlockSpec((2, 1, rows, column_total), lambda i: (0, variable, i, 0)),
        out_shape=jax.ShapeDtypeStruct((2, 4, row_count, column_total), f32),
        scratch_shapes=[pltpu.VMEM((2, row_count, column_total), f32)],
        input_output_aliases=aliases,
        compiler_params=params(56),
        cost_estimate=cost(10**8, 5 * 10**6),
    )(*operands)


SWAP = [(0, 1), (1, 0), (2, 3), (3, 2)]
CROSS = [(0, 2), (2, 0), (1, 3), (3, 1)]


def of_all_bands(part):
    pair = jnp.concatenate([part, lax.ppermute(part, "band", CROSS)], axis=0)
    return jnp.concatenate([pair, lax.ppermute(pair, "band", SWAP)], axis=0)


def after(value, *earlier):
    return lax.optimization_barrier((value,) + earlier)[0]


def four_bands(swept, weights, exits, chain, table, mix):
    owns, parts, nears, totals, mets = [], [], [], [], []

    def filter_one(variable, *earlier):
        own, sent, part = longitude(after(swept, *earlier), weights, 2, variable, 4, table)
        owns.append(own)
        parts.append(part)
        nears.append(lax.ppermute(sent, "band", SWAP))
        return part

    def cross_one(variable, *earlier):
        part = after(parts[variable], *earlier)
        total = add_near(variable, part, nears[variable], table)
        totals.append(total)
        mets.append(lax.ppermute(total, "band", [(1, 2), (2, 1)]))
        return total

    mark = filter_one(0)
    mark = filter_one(1, mark)
    mark = cross_one(0, mark)
    exits = lax.all_to_all(after(exits, mark), "sub", split_axis=0, concat_axis=0, tiled=True)
    mark = cross_one(1, mark)
    mark = filter_one(2, mark)
    mark = filter_one(3, mark)
    mark = cross_one(2, mark)
    mark = cross_one(3, mark)
    messages = lax.all_to_all(
        chain(after(exits, mark)), "sub", split_axis=0, concat_axis=0, tiled=True
    )
    fars = [lax.ppermute(met, "band", [(1, 0), (2, 3)]) for met in mets]
    messages = of_all_bands(messages).reshape(8, 4, -1, LANES)
    result = None
    for v in range(4):
        result = last_step(v, owns[v], nears[v], fars[v], mets[v], messages, mix, table, result)
    return result


def prefix(part, axis, combine, identity, reverse):
    count = lax.axis_size(axis)
    place = lax.axis_index(axis)
    ahead = count - 1 - place if reverse else place
    gathered = jax.tree.map(lambda a: lax.all_gather(a, axis), part)
    state = jax.tree.map(lambda a, e: jnp.zeros_like(a) + jnp.asarray(e, a.dtype), part, identity)

    def one(turn, state):
        source = count - 1 - turn if reverse else turn
        return combine(
            state, jax.tree.map(lambda a: lax.dynamic_index_in_dim(a, source, 0, False), gathered)
        )

    return lax.fori_loop(0, ahead, one, state)


def combine(earlier, later):
    return (earlier[0] * later[0], later[0] * earlier[1] + later[1])


def level_chain(values, decays, reverse):
    level_count = values.shape[0]
    visit_order = range(level_count - 1, -1, -1) if reverse else range(level_count)
    carry_state = jnp.zeros_like(values[0])
    level_gain = jnp.ones((values.shape[1],), f32)
    outputs = [None] * level_count
    carried = [None] * level_count
    for level_index in visit_order:
        factor = decays[level_index][:, None, None]
        carry_state = factor * carry_state + (1.0 - factor) * values[level_index]
        level_gain = level_gain * decays[level_index]
        outputs[level_index] = carry_state
        carried[level_index] = level_gain
    total_decay = level_gain[:, None, None]
    identity = (jnp.ones_like(total_decay), jnp.zeros_like(carry_state))
    incoming = prefix((total_decay, carry_state), "band", combine, identity, reverse)[1]
    return jnp.stack(
        [
            outputs[level_index] + carried[level_index][:, None, None] * incoming
            for level_index in range(level_count)
        ]
    )


def any_bands(swept, weights, exits, chain, vert_length):
    column_count, group_count, row_count, _ = swept.shape
    exits = lax.all_to_all(exits, "sub", split_axis=0, concat_axis=0, tiled=True)
    messages = lax.all_to_all(chain(exits), "sub", split_axis=0, concat_axis=0, tiled=True)
    (values,) = longitude(swept, weights, group_count, 0, 1)
    messages = messages.reshape(group_count, -1, LANES)
    states = messages[:, : 4 * column_count].reshape(group_count, 4, -1)
    inside = messages[:, 4 * column_count : 4 * column_count + 4, :row_count]
    values = values + jnp.einsum("gkr,gkc->grc", inside, states, precision=highest)
    decay = jnp.exp(-1.0 / vert_length)
    values = values.reshape(decay.shape + values.shape[1:])
    return level_chain(level_chain(values, decay, False), decay, True)


def per_device(background, obs_columns, obs_owner, obs_cell, lat_length, lon_length, vert_length):
    level_count, var_count, row_count, lon_count = background.shape
    sub_count = lax.axis_size("sub")
    group_count = level_count * var_count
    strip = row_count * lon_count
    column_count = lon_count // LANES
    capacity = 2 * obs_owner.shape[0] // sub_count
    chunk_count = capacity // LANES
    two_chips = lax.axis_size("band") == 4 and level_count == 2
    index = lax.axis_index("sub").astype(i32).reshape(1)
    band = lax.axis_index("band").astype(i32).reshape(1)

    packed = pack_observations(
        obs_columns.reshape(group_count, -1), obs_owner[:, 0], obs_cell, sub_count, strip, capacity
    )
    if two_chips:
        decay = jnp.exp(-1.0 / vert_length).reshape(-1, 1)
        decays = of_all_bands(jnp.broadcast_to(decay, (8, LANES)))
    lengths = lat_length.reshape(group_count, sub_count, row_count)
    lengths = jnp.pad(lengths, ((0, 0), (0, 0), (0, LANES - row_count)), constant_values=1.0)
    got = lax.all_to_all(packed, "sub", split_axis=0, concat_axis=0, tiled=True)
    *weights, inside, leaving = prepare(
        index, after(lon_length.reshape(-1), packed), lengths, row_count, lon_count
    )
    ready = [inside]
    if two_chips:
        table, mix = tables(band, after(decays, packed))
        ready.append(table)

    sizes = (sub_count, group_count, row_count, column_count, chunk_count, strip)
    swept, exits = deposit_and_sweep(
        index,
        lengths,
        after(got, *ready),
        background.reshape(group_count * row_count, lon_count),
        sizes,
    )
    swept = swept.reshape(column_count, group_count, row_count, LANES)
    exits = exits.reshape(group_count, 4 * column_count, LANES)

    def chain(arrived):
        return chain_states(index, arrived, leaving, inside, weights)

    if two_chips:
        return four_bands(swept, weights, exits, chain, table, mix)
    return any_bands(swept, weights, exits, chain, vert_length)


def solution(mesh):
    placed = (
        P("band", None, "sub", None),
        P("band", None, "sub"),
        P("sub", None),
        P("sub"),
        P("band", None, None),
        P("band", None),
        P("band", None),
    )
    return jax.shard_map(
        per_device,
        mesh=mesh,
        in_specs=placed,
        out_specs=P("band", None, "sub", None),
        check_vma=False,
    )
```

time: 203 us -> 179 us (0.88)
  other arithmetic: 49.5 us -> 2.32 us
  Pallas kernels: 70.4 us -> 97.2 us
  waiting for transfers between devices: 6.6 us -> 26.1 us
  local copies, waits for them, and re-layouts: 28.5 us -> 13.2 us
  blocking collectives: 6.05 us -> 0 us
    pallas_call x10 -> x15, Pallas kernels: 34.5 us -> 60.2 us  [the longest x4 17.9 us: longitude(): pl.pallas_call(longitude_kernel, grid=(count,), in_specs=in_specs, out_sp...]
    add x13 -> x0, other arithmetic: 25.1 us -> none  [the longest x4 14.4 us: four_bands(): first[0, variable] * own[0] + first[1, variable] * own[1]]
    ppermute x14 -> x16, waiting for transfers between devices: 6.6 us -> 24.5 us  [the longest x2 24.5 us: of_all_bands(): pair = jnp.concatenate([part, lax.ppermute(part, 'band', CROSS)], axis=0)]
    unnamed x51 -> x34, local copies, waits for them, and re-layouts: 17.6 us -> 9.38 us
    all_gather x1 -> x0, blocking collectives: 6.05 us -> none  [four_bands(): lengths = lax.all_gather(vert_length, 'band')]
    select_n x10 -> x0, other arithmetic: 5.94 us -> none  [the longest x1 4.84 us: circle_weights(): jnp.where(use_high, spread_high, spread_low)]
    sort x1 -> x0, other arithmetic: 4.95 us -> none  [pack_observations(): lax.sort((owners * strip + cells, lax.iota(i32, obs_count)), num_keys=1,...]
    convert_element_type x3 -> x0, other arithmetic: 4.92 us -> none  [the longest x2 3.44 us: split_outside(): return (high.astype(bf16), (x - high).astype(bf16))]
  transfers between devices with their start and end apart: 17 -> 19, of which waited for: 1 -> 3; matrix products, arithmetic and copies ran while one was open for 26% -> 3% of each run, Pallas kernels for 11% -> 20%
where the time goes in v2:
time: 179 us; the launch traced here: 177 us
  Pallas kernels  97.2 us (54%)
  starting transfers between devices  38.2 us (21%)
  waiting for transfers between devices  26.1 us (15%)
  local copies, waits for them, and re-layouts  13.2 us (7%)
  other arithmetic  2.32 us (1%)
    pallas_call x1, Pallas kernels, deposit_and_sweep(): pl.pallas_call(functools.partial(deposit_kernel, sizes), out_shape=[jax.S...  34.5 us
    ppermute x2, waiting for transfers between devices, of_all_bands(): pair = jnp.concatenate([part, lax.ppermute(part, 'band', CROSS)], axis=0)  24.5 us
    pallas_call x4, Pallas kernels, longitude(): pl.pallas_call(longitude_kernel, grid=(count,), in_specs=in_specs, out_sp...  17.9 us
    pallas_call x4, Pallas kernels, last_step(): pl.pallas_call(last_kernel, grid=(steps,), in_specs=in_specs, out_specs=p...  16.8 us
    ppermute x4, starting transfers between devices, cross_one(): mets.append(lax.ppermute(total, 'band', [(1, 2), (2, 1)]))  11.7 us
    pallas_call x1, Pallas kernels, pack_observations(): pl.pallas_call(functools.partial(pack_kernel, (sub_count, group_count, ch...  9.61 us
    unnamed x34, local copies, waits for them, and re-layouts  9.38 us
    pallas_call x4, Pallas kernels, add_near(): pl.pallas_call(add_kernel, grid=(steps,), in_specs=[block, block, pl.Bloc...  8.01 us
  transfers between devices with their start and end apart: 19, of which 3 were waited for; matrix products, arithmetic and copies ran while one was open for 3% of the time, Pallas kernels for 20%

profile of v2, /device:TPU:1, one launch (start us, length us, event | category | flops | bytes accessed | tf_op | source)
XLA Modules:
  0.0 177.3 jit_solution(16127634834544757097)
XLA Ops:
  0.0 0.9 reshape.37.values
  1.7 0.7 copy-done.1
  2.4 9.6 %shard_map.73 = f32[8,72,128]{2,1,0:T(8,128)} custom-call(s32[32,128]{1,0:T(8,128)S(1)} %bitcast.10, s32[32,128]{1,0:T(8,128)S(1)} %bitcast.11, f32[8,4096]{1,0:T(8,128)S(1)} %reshape.37.values), custom_call_target="tpu_custom_call" | custom-call | flops 1000000 | bytes 1000000 | tf_op jit(solution)/shard_map/pallas_call | solution.py:129
  12.0 6.4 %all-to-all-start = ((f32[8,72,128]{2,1,0:T(8,128)}), f32[8,72,128]{2,1,0:T(8,128)S(1)}, u32[]{:S(2)}, u32[]{:S(2)}) async-start(f32[8,72,128]{2,1,0:T(8,128)} %shard_map.73), calls=%async_computation | async-start | bytes 589824 | tf_op jit(solution)/shard_map/all_to_all | solution.py:882
  19.2 1.2 collective-permute-start
  20.5 1.2 collective-permute-done
  21.7 2.1 %collective-permute-start.1 = (f32[16,128]{1,0:T(8,128)S(1)}, f32[16,128]{1,0:T(8,128)S(1)}, u32[]{:S(2)}, u32[]{:S(2)}) collective-permute-start(f32[16,128]{1,0:T(8,128)S(1)} %pad_maximum_fusion.3), channel_id=1, source_target_pairs={{0,8},{8,0},{16,24},{24,16},{1,9},{9,1},{17,25},{25,17},{2,10},{10... | collective-permute-start | bytes 24584 | tf_op jit(solution)/shard_map/ppermute | solution.py:760
  23.8 1.3 reshape.38.lon_length
  25.1 0.8 reshape.35
  26.5 6.5 %shard_map.74 = (bf16[8,256,256]{2,1,0:T(8,128)(2,1)}, bf16[8,256,256]{2,1,0:T(8,128)(2,1)}, bf16[8,256,256]{2,1,0:T(8,128)(2,1)}, bf16[8,64,1536]{2,1,0:T(8,128...) custom-call(s32[1]{0:T(128)} %bitcast.index, f32[8]{0:T(128)} %reshape.38.lon_length, f32[8,8,128]{2,1,0:T(8,128)} %pad.4.lengths), custom_call_target="tpu_custom_call" | custom-call | flops 10000000 | bytes 10000000 | tf_op jit(solution)/shard_map/pallas_call | solution.py:376
  33.6 1.4 shard_map.75
  35.0 0.7 copy-done.6
  35.7 34.5 %shard_map.76 = (f32[12,768,128]{2,1,0:T(8,128)}, f32[384,128]{1,0:T(8,128)}) custom-call(s32[1]{0:T(128)} %bitcast.index, f32[8,8,128]{2,1,0:T(8,128)} %pad.4.lengths, f32[8,72,128]{2,1,0:T(8,128)} %copy-done.6, f32[768,1536]{1,0:T(8,128)} %bitcast.20), custom_call_target="tpu_custom_call" | custom-call | flops 10000000 | bytes 10000000 | tf_op jit(solution)/shard_map/pallas_call | solution.py:266
  70.3 4.5 %shard_map.77 = (f32[2,96,1536]{2,1,0:T(8,128)}, f32[96,1536]{1,0:T(8,128)}, f32[96,1536]{1,0:T(8,128)}) custom-call(f32[12,8,96,128]{3,2,1,0:T(8,128)} %bitcast.12, bf16[8,256,256]{2,1,0:T(8,128)(2,1)} %get-tuple-element.45.near_high, bf16[8,256,256]{2,1,0:T(8,128)(2,1)} %get-tuple-element.46.near_low, bf16[8,256,256]{2,1,0:T(8,128)(2,1)} %get-tuple-element.47.moment, ...), custom_call_target="tpu_custom_call" | custom-call | flops 2000000000 | bytes 4000000 | tf_op jit(solution)/shard_map/pallas_call | solution.py:474
  74.8 4.5 %shard_map.78 = (f32[2,96,1536]{2,1,0:T(8,128)}, f32[96,1536]{1,0:T(8,128)}, f32[96,1536]{1,0:T(8,128)}) custom-call(f32[12,8,96,128]{3,2,1,0:T(8,128)} %bitcast.13, bf16[8,256,256]{2,1,0:T(8,128)(2,1)} %get-tuple-element.45.near_high, bf16[8,256,256]{2,1,0:T(8,128)(2,1)} %get-tuple-element.46.near_low, bf16[8,256,256]{2,1,0:T(8,128)(2,1)} %get-tuple-element.47.moment, ...), custom_call_target="tpu_custom_call" | custom-call | flops 2000000000 | bytes 4000000 | tf_op jit(solution)/shard_map/pallas_call | solution.py:474
  79.8 0.8 copy-done.3
  80.6 2.0 %shard_map.79 = f32[96,1536]{1,0:T(8,128)} custom-call(f32[96,1536]{1,0:T(8,128)} %get-tuple-element.52.part, f32[96,1536]{1,0:T(8,128)} %copy-done.3, f32[4,16,128]{2,1,0:T(8,128)} %get-tuple-element.42.rest_0_.table), custom_call_target="tpu_custom_call" | custom-call | flops 1000000 | bytes 2000000 | tf_op jit(solution)/shard_map/pallas_call | solution.py:667
  82.6 0.8 copy-done.2
  83.4 2.0 %shard_map.80 = f32[96,1536]{1,0:T(8,128)} custom-call(f32[96,1536]{1,0:T(8,128)} %get-tuple-element.54.part, f32[96,1536]{1,0:T(8,128)} %copy-done.2, f32[4,16,128]{2,1,0:T(8,128)} %get-tuple-element.42.rest_0_.table), custom_call_target="tpu_custom_call" | custom-call | flops 1000000 | bytes 2000000 | tf_op jit(solution)/shard_map/pallas_call | solution.py:667
  85.5 4.5 %shard_map.81 = (f32[2,96,1536]{2,1,0:T(8,128)}, f32[96,1536]{1,0:T(8,128)}, f32[96,1536]{1,0:T(8,128)}) custom-call(f32[12,8,96,128]{3,2,1,0:T(8,128)} %bitcast.14, bf16[8,256,256]{2,1,0:T(8,128)(2,1)} %get-tuple-element.45.near_high, bf16[8,256,256]{2,1,0:T(8,128)(2,1)} %get-tuple-element.46.near_low, bf16[8,256,256]{2,1,0:T(8,128)(2,1)} %get-tuple-element.47.moment, ...), custom_call_target="tpu_custom_call" | custom-call | flops 2000000000 | bytes 4000000 | tf_op jit(solution)/shard_map/pallas_call | solution.py:474
  90.0 4.5 %shard_map.82 = (f32[2,96,1536]{2,1,0:T(8,128)}, f32[96,1536]{1,0:T(8,128)}, f32[96,1536]{1,0:T(8,128)}) custom-call(f32[12,8,96,128]{3,2,1,0:T(8,128)} %bitcast.15, bf16[8,256,256]{2,1,0:T(8,128)(2,1)} %get-tuple-element.45.near_high, bf16[8,256,256]{2,1,0:T(8,128)(2,1)} %get-tuple-element.46.near_low, bf16[8,256,256]{2,1,0:T(8,128)(2,1)} %get-tuple-element.47.moment, ...), custom_call_target="tpu_custom_call" | custom-call | flops 2000000000 | bytes 4000000 | tf_op jit(solution)/shard_map/pallas_call | solution.py:474
  94.9 4.3 %all-to-all-start.1 = ((f32[8,48,128]{2,1,0:T(8,128)}), f32[8,48,128]{2,1,0:T(8,128)S(1)}, u32[]{:S(2)}, u32[]{:S(2)}) async-start(f32[8,48,128]{2,1,0:T(8,128)} %bitcast.6), calls=%async_computation.1 | async-start | bytes 393216 | tf_op jit(solution)/shard_map/all_to_all | solution.py:787
  99.3 0.8 copy-done.5
  100.1 2.0 %shard_map.83 = f32[96,1536]{1,0:T(8,128)} custom-call(f32[96,1536]{1,0:T(8,128)} %get-tuple-element.62.part, f32[96,1536]{1,0:T(8,128)} %copy-done.5, f32[4,16,128]{2,1,0:T(8,128)} %get-tuple-element.42.rest_0_.table), custom_call_target="tpu_custom_call" | custom-call | flops 1000000 | bytes 2000000 | tf_op jit(solution)/shard_map/pallas_call | solution.py:667
  102.1 0.8 copy-done.4
  102.9 2.0 %shard_map.84 = f32[96,1536]{1,0:T(8,128)} custom-call(f32[96,1536]{1,0:T(8,128)} %get-tuple-element.64.part, f32[96,1536]{1,0:T(8,128)} %copy-done.4, f32[4,16,128]{2,1,0:T(8,128)} %get-tuple-element.42.rest_0_.table), custom_call_target="tpu_custom_call" | custom-call | flops 1000000 | bytes 2000000 | tf_op jit(solution)/shard_map/pallas_call | solution.py:667
  104.9 1.5 all-to-all-done.1.exits
  107.1 2.5 %shard_map.85 = f32[448,128]{1,0:T(8,128)} custom-call(s32[1]{0:T(128)} %bitcast.index, f32[8,48,128]{2,1,0:T(8,128)} %copy-done.7, f32[4,128]{1,0:T(4,128)} %get-tuple-element.68.leaving, f32[128,128]{1,0:T(8,128)} %get-tuple-element.40.inside, bf16[8,256,256]{2,1,0:T(8,128)(2,1)} %get-tuple-element.45.near_high, ...), custom_call_target="tpu_custom_call" | custom-call | flops 1000000000 | bytes 2000000 | tf_op jit(solution)/shard_map/pallas_call | solution.py:536
  109.6 3.9 %all-to-all-start.2 = ((f32[8,56,128]{2,1,0:T(8,128)}), f32[8,56,128]{2,1,0:T(8,128)S(1)}, u32[]{:S(2)}, u32[]{:S(2)}) async-start(f32[8,56,128]{2,1,0:T(8,128)} %bitcast.24), calls=%async_computation.2 | async-start | bytes 458752 | tf_op jit(solution)/shard_map/all_to_all | solution.py:793
  113.5 4.3 %collective-permute-start.14 = (f32[96,1536]{1,0:T(8,128)}, f32[96,1536]{1,0:T(8,128)S(1)}, u32[]{:S(2)}, u32[]{:S(2)}) collective-permute-start(f32[96,1536]{1,0:T(8,128)} %shard_map.79), channel_id=1, source_target_pairs={{8,16},{16,8},{9,17},{17,9},{10,18},{18,10},{11,19},{19,11},{12,20... | collective-permute-start | bytes 1769480 | tf_op jit(solution)/shard_map/ppermute | solution.py:781
  117.7 1.9 %collective-permute-start.12 = (f32[96,1536]{1,0:T(8,128)S(1)}, f32[96,1536]{1,0:T(8,128)S(1)}, u32[]{:S(2)}, u32[]{:S(2)}) collective-permute-start(f32[96,1536]{1,0:T(8,128)S(1)} %copy-done.16), channel_id=1, source_target_pairs={{8,16},{16,8},{9,17},{17,9},{10,18},{18,10},{11,19},{19,11},{12,20... | collective-permute-start | bytes 1769480 | tf_op jit(solution)/shard_map/ppermute | solution.py:781
  119.7 3.6 %collective-permute-start.10 = (f32[96,1536]{1,0:T(8,128)}, f32[96,1536]{1,0:T(8,128)S(1)}, u32[]{:S(2)}, u32[]{:S(2)}) collective-permute-start(f32[96,1536]{1,0:T(8,128)} %shard_map.83), channel_id=1, source_target_pairs={{8,16},{16,8},{9,17},{17,9},{10,18},{18,10},{11,19},{19,11},{12,20... | collective-permute-start | bytes 1769480 | tf_op jit(solution)/shard_map/ppermute | solution.py:781
  123.3 1.9 %collective-permute-start.6 = (f32[96,1536]{1,0:T(8,128)}, f32[96,1536]{1,0:T(8,128)S(1)}, u32[]{:S(2)}, u32[]{:S(2)}) collective-permute-start(f32[96,1536]{1,0:T(8,128)} %shard_map.84), channel_id=1, source_target_pairs={{8,16},{16,8},{9,17},{17,9},{10,18},{18,10},{11,19},{19,11},{12,20... | collective-permute-start | bytes 1769480 | tf_op jit(solution)/shard_map/ppermute | solution.py:781
  125.3 23.3 %collective-permute-done.8 = f32[448,128]{1,0:T(8,128)S(1)} collective-permute-done((f32[448,128]{1,0:T(8,128)S(1)}, f32[448,128]{1,0:T(8,128)S(1)}, u32[]{:S(2)}, u32[]{:S(2)}) %collective-permute-start.8) | collective-permute-done | bytes 229408 | tf_op jit(solution)/shard_map/ppermute | solution.py:759
  148.7 1.5 collective-permute-start.9
  150.2 2.0 %collective-permute-start.15 = (f32[96,1536]{1,0:T(8,128)S(1)}, f32[96,1536]{1,0:T(8,128)S(1)}, u32[]{:S(2)}, u32[]{:S(2)}) collective-permute-start(f32[96,1536]{1,0:T(8,128)S(1)} %collective-permute-done.14.met), channel_id=1, source_target_pairs={{8,0},{16,24},{9,1},{17,25},{10,2},{18,26},{11,3},{19,27},{12,4},{... | collective-permute-start | bytes 1769480 | tf_op jit(solution)/shard_map/ppermute | solution.py:796
  152.2 1.3 collective-permute-start.13
  153.5 1.3 collective-permute-start.11
  154.9 1.3 collective-permute-start.7
  156.2 1.0 pad_maximum_fusion
  157.2 0.8 copy-done.15
  158.0 4.2 %shard_map.86.rest_0_ = f32[2,4,96,1536]{3,2,1,0:T(8,128)} custom-call(f32[2,96,1536]{2,1,0:T(8,128)} %get-tuple-element.72.own, f32[96,1536]{1,0:T(8,128)} %copy-done.3, f32[96,1536]{1,0:T(8,128)} %copy-done.15, f32[96,1536]{1,0:T(8,128)} %copy-done.11, f32[8,4,56,128]{3,2,1,0:T(8,128)} %bitcast.16, f32[2,4,8,128]{3,2,1,0:T(8,128)} %get-tuple-element.69.mix, ...), custom_call_target="tpu_custom_call" | custom-call | flops 100000000 | bytes 5000000 | tf_op jit(solution)/shard_map/pallas_call | solution.py:741
  162.3 0.8 copy-done.14
  163.1 4.2 %shard_map.87.rest_0_ = f32[2,4,96,1536]{3,2,1,0:T(8,128)} custom-call(f32[2,96,1536]{2,1,0:T(8,128)} %get-tuple-element.71.own, f32[96,1536]{1,0:T(8,128)} %copy-done.2, f32[96,1536]{1,0:T(8,128)} %copy-done.14, f32[96,1536]{1,0:T(8,128)} %copy-done.10, f32[8,4,56,128]{3,2,1,0:T(8,128)} %bitcast.17, ...), custom_call_target="tpu_custom_call", output_to_operand_aliasing={{}: (7, {})} | custom-call | flops 100000000 | bytes 5000000 | tf_op jit(solution)/shard_map/pallas_call | solution.py:741
  167.3 0.8 copy-done.13
  168.1 4.2 %shard_map.88.rest_0_ = f32[2,4,96,1536]{3,2,1,0:T(8,128)} custom-call(f32[2,96,1536]{2,1,0:T(8,128)} %get-tuple-element.70.own, f32[96,1536]{1,0:T(8,128)} %copy-done.5, f32[96,1536]{1,0:T(8,128)} %copy-done.13, f32[96,1536]{1,0:T(8,128)} %copy-done.9, f32[8,4,56,128]{3,2,1,0:T(8,128)} %bitcast.18, ...), custom_call_target="tpu_custom_call", output_to_operand_aliasing={{}: (7, {})} | custom-call | flops 100000000 | bytes 5000000 | tf_op jit(solution)/shard_map/pallas_call | solution.py:741
  172.3 0.8 copy-done.12
  173.1 4.2 %shard_map.89 = f32[2,4,96,1536]{3,2,1,0:T(8,128)} custom-call(f32[2,96,1536]{2,1,0:T(8,128)} %get-tuple-element.59.own, f32[96,1536]{1,0:T(8,128)} %copy-done.4, f32[96,1536]{1,0:T(8,128)} %copy-done.12, f32[96,1536]{1,0:T(8,128)} %copy-done.8, f32[8,4,56,128]{3,2,1,0:T(8,128)} %bitcast.19, ...), custom_call_target="tpu_custom_call", output_to_operand_aliasing={{}: (7, {})} | custom-call | flops 100000000 | bytes 5000000 | tf_op jit(solution)/shard_map/pallas_call | solution.py:741
  (52 shorter events, 4.6 us)
Async XLA Ops:
  1.0 0.7 copy-start
  1.7 0.7 copy-start.1
  12.0 23.0 %all-to-all-start = ((f32[8,72,128]{2,1,0:T(8,128)}), f32[8,72,128]{2,1,0:T(8,128)S(1)}, u32[]{:S(2)}, u32[]{:S(2)}) async-start(f32[8,72,128]{2,1,0:T(8,128)} %shard_map.73), calls=%async_computation | async-start | bytes 589824 | tf_op jit(solution)/shard_map/all_to_all | solution.py:882
  19.2 2.5 %collective-permute-start = (f32[8,128]{1,0:T(8,128)S(1)}, f32[8,128]{1,0:T(8,128)S(1)}, u32[]{:S(2)}, u32[]{:S(2)}) collective-permute-start(f32[8,128]{1,0:T(8,128)S(1)} %broadcast_in_dim.8), channel_id=1, source_target_pairs={{0,16},{16,0},{8,24},{24,8},{1,17},{17,1},{9,25},{25,9},{2,18},{18... | collective-permute-start | bytes 12296 | tf_op jit(solution)/shard_map/ppermute | solution.py:759
  21.7 11.3 %collective-permute-start.1 = (f32[16,128]{1,0:T(8,128)S(1)}, f32[16,128]{1,0:T(8,128)S(1)}, u32[]{:S(2)}, u32[]{:S(2)}) collective-permute-start(f32[16,128]{1,0:T(8,128)S(1)} %pad_maximum_fusion.3), channel_id=1, source_target_pairs={{0,8},{8,0},{16,24},{24,16},{1,9},{9,1},{17,25},{25,17},{2,10},{10... | collective-permute-start | bytes 24584 | tf_op jit(solution)/shard_map/ppermute | solution.py:760
  35.0 0.7 copy-start.6
  74.7 5.0 %collective-permute-start.2 = (f32[96,1536]{1,0:T(8,128)}, f32[96,1536]{1,0:T(8,128)S(1)}, u32[]{:S(2)}, u32[]{:S(2)}) collective-permute-start(f32[96,1536]{1,0:T(8,128)} %get-tuple-element.53), channel_id=1, source_target_pairs={{0,8},{8,0},{16,24},{24,16},{1,9},{9,1},{17,25},{25,17},{2,10},{10... | collective-permute-start | bytes 1769480 | tf_op jit(solution)/shard_map/ppermute | solution.py:774
  79.3 3.3 %collective-permute-start.3 = (f32[96,1536]{1,0:T(8,128)}, f32[96,1536]{1,0:T(8,128)S(1)}, u32[]{:S(2)}, u32[]{:S(2)}) collective-permute-start(f32[96,1536]{1,0:T(8,128)} %get-tuple-element.55), channel_id=1, source_target_pairs={{0,8},{8,0},{16,24},{24,16},{1,9},{9,1},{17,25},{25,17},{2,10},{10... | collective-permute-start | bytes 1769480 | tf_op jit(solution)/shard_map/ppermute | solution.py:774
  79.8 0.8 copy-start.3
  82.6 0.8 copy-start.2
  89.9 9.3 %collective-permute-start.5 = (f32[96,1536]{1,0:T(8,128)}, f32[96,1536]{1,0:T(8,128)S(1)}, u32[]{:S(2)}, u32[]{:S(2)}) collective-permute-start(f32[96,1536]{1,0:T(8,128)} %get-tuple-element.63), channel_id=1, source_target_pairs={{0,8},{8,0},{16,24},{24,16},{1,9},{9,1},{17,25},{25,17},{2,10},{10... | collective-permute-start | bytes 1769480 | tf_op jit(solution)/shard_map/ppermute | solution.py:774
  94.4 7.6 %collective-permute-start.4 = (f32[96,1536]{1,0:T(8,128)}, f32[96,1536]{1,0:T(8,128)S(1)}, u32[]{:S(2)}, u32[]{:S(2)}) collective-permute-start(f32[96,1536]{1,0:T(8,128)} %get-tuple-element.60), channel_id=1, source_target_pairs={{0,8},{8,0},{16,24},{24,16},{1,9},{9,1},{17,25},{25,17},{2,10},{10... | collective-permute-start | bytes 1769480 | tf_op jit(solution)/shard_map/ppermute | solution.py:774
  94.9 11.5 %all-to-all-start.1 = ((f32[8,48,128]{2,1,0:T(8,128)}), f32[8,48,128]{2,1,0:T(8,128)S(1)}, u32[]{:S(2)}, u32[]{:S(2)}) async-start(f32[8,48,128]{2,1,0:T(8,128)} %bitcast.6), calls=%async_computation.1 | async-start | bytes 393216 | tf_op jit(solution)/shard_map/all_to_all | solution.py:787
  99.2 18.5 %copy-start.16 = (f32[96,1536]{1,0:T(8,128)S(1)}, f32[96,1536]{1,0:T(8,128)}, u32[]{:S(2)}) copy-start(f32[96,1536]{1,0:T(8,128)} %shard_map.80) | copy-start | bytes 1769476
  99.2 0.8 copy-start.5
  102.1 0.8 copy-start.4
  106.4 0.7 copy-start.7
  109.6 15.7 %all-to-all-start.2 = ((f32[8,56,128]{2,1,0:T(8,128)}), f32[8,56,128]{2,1,0:T(8,128)S(1)}, u32[]{:S(2)}, u32[]{:S(2)}) async-start(f32[8,56,128]{2,1,0:T(8,128)} %bitcast.24), calls=%async_computation.2 | async-start | bytes 458752 | tf_op jit(solution)/shard_map/all_to_all | solution.py:793
  113.5 36.7 %collective-permute-start.14 = (f32[96,1536]{1,0:T(8,128)}, f32[96,1536]{1,0:T(8,128)S(1)}, u32[]{:S(2)}, u32[]{:S(2)}) collective-permute-start(f32[96,1536]{1,0:T(8,128)} %shard_map.79), channel_id=1, source_target_pairs={{8,16},{16,8},{9,17},{17,9},{10,18},{18,10},{11,19},{19,11},{12,20... | collective-permute-start | bytes 1769480 | tf_op jit(solution)/shard_map/ppermute | solution.py:781
  117.7 34.4 %collective-permute-start.12 = (f32[96,1536]{1,0:T(8,128)S(1)}, f32[96,1536]{1,0:T(8,128)S(1)}, u32[]{:S(2)}, u32[]{:S(2)}) collective-permute-start(f32[96,1536]{1,0:T(8,128)S(1)} %copy-done.16), channel_id=1, source_target_pairs={{8,16},{16,8},{9,17},{17,9},{10,18},{18,10},{11,19},{19,11},{12,20... | collective-permute-start | bytes 1769480 | tf_op jit(solution)/shard_map/ppermute | solution.py:781
  119.7 33.8 %collective-permute-start.10 = (f32[96,1536]{1,0:T(8,128)}, f32[96,1536]{1,0:T(8,128)S(1)}, u32[]{:S(2)}, u32[]{:S(2)}) collective-permute-start(f32[96,1536]{1,0:T(8,128)} %shard_map.83), channel_id=1, source_target_pairs={{8,16},{16,8},{9,17},{17,9},{10,18},{18,10},{11,19},{19,11},{12,20... | collective-permute-start | bytes 1769480 | tf_op jit(solution)/shard_map/ppermute | solution.py:781
  123.3 31.5 %collective-permute-start.6 = (f32[96,1536]{1,0:T(8,128)}, f32[96,1536]{1,0:T(8,128)S(1)}, u32[]{:S(2)}, u32[]{:S(2)}) collective-permute-start(f32[96,1536]{1,0:T(8,128)} %shard_map.84), channel_id=1, source_target_pairs={{8,16},{16,8},{9,17},{17,9},{10,18},{18,10},{11,19},{19,11},{12,20... | collective-permute-start | bytes 1769480 | tf_op jit(solution)/shard_map/ppermute | solution.py:781
  125.3 23.4 %collective-permute-start.8 = (f32[448,128]{1,0:T(8,128)S(1)}, f32[448,128]{1,0:T(8,128)S(1)}, u32[]{:S(2)}, u32[]{:S(2)}) collective-permute-start(f32[448,128]{1,0:T(8,128)S(1)} %bitcast.21), channel_id=1, source_target_pairs={{0,16},{16,0},{8,24},{24,8},{1,17},{17,1},{9,25},{25,9},{2,18},{18... | collective-permute-start | bytes 688136 | tf_op jit(solution)/shard_map/ppermute | solution.py:759
  148.7 7.6 %collective-permute-start.9 = (f32[896,128]{1,0:T(8,128)S(1)}, f32[896,128]{1,0:T(8,128)S(1)}, u32[]{:S(2)}, u32[]{:S(2)}) collective-permute-start(f32[896,128]{1,0:T(8,128)S(1)} %pad_maximum_fusion.1), channel_id=1, source_target_pairs={{0,8},{8,0},{16,24},{24,16},{1,9},{9,1},{17,25},{25,17},{2,10},{10... | collective-permute-start | bytes 1376264 | tf_op jit(solution)/shard_map/ppermute | solution.py:760
  150.2 7.1 %copy-start.11 = (f32[96,1536]{1,0:T(8,128)}, f32[96,1536]{1,0:T(8,128)S(1)}, u32[]{:S(2)}) copy-start(f32[96,1536]{1,0:T(8,128)S(1)} %collective-permute-done.14.met) | copy-start | bytes 1769476
  150.2 7.1 %collective-permute-start.15 = (f32[96,1536]{1,0:T(8,128)S(1)}, f32[96,1536]{1,0:T(8,128)S(1)}, u32[]{:S(2)}, u32[]{:S(2)}) collective-permute-start(f32[96,1536]{1,0:T(8,128)S(1)} %collective-permute-done.14.met), channel_id=1, source_target_pairs={{8,0},{16,24},{9,1},{17,25},{10,2},{18,26},{11,3},{19,27},{12,4},{... | collective-permute-start | bytes 1769480 | tf_op jit(solution)/shard_map/ppermute | solution.py:796
  152.1 10.1 %copy-start.10 = (f32[96,1536]{1,0:T(8,128)}, f32[96,1536]{1,0:T(8,128)S(1)}, u32[]{:S(2)}) copy-start(f32[96,1536]{1,0:T(8,128)S(1)} %collective-permute-done.12.met) | copy-start | bytes 1769476
  152.2 10.1 %collective-permute-start.13 = (f32[96,1536]{1,0:T(8,128)S(1)}, f32[96,1536]{1,0:T(8,128)S(1)}, u32[]{:S(2)}, u32[]{:S(2)}) collective-permute-start(f32[96,1536]{1,0:T(8,128)S(1)} %collective-permute-done.12.met), channel_id=1, source_target_pairs={{8,0},{16,24},{9,1},{17,25},{10,2},{18,26},{11,3},{19,27},{12,4},{... | collective-permute-start | bytes 1769480 | tf_op jit(solution)/shard_map/ppermute | solution.py:796
  153.5 8.7 %copy-start.9 = (f32[96,1536]{1,0:T(8,128)}, f32[96,1536]{1,0:T(8,128)S(1)}, u32[]{:S(2)}) copy-start(f32[96,1536]{1,0:T(8,128)S(1)} %collective-permute-done.10.met) | copy-start | bytes 1769476
  153.5 13.8 %collective-permute-start.11 = (f32[96,1536]{1,0:T(8,128)S(1)}, f32[96,1536]{1,0:T(8,128)S(1)}, u32[]{:S(2)}, u32[]{:S(2)}) collective-permute-start(f32[96,1536]{1,0:T(8,128)S(1)} %collective-permute-done.10.met), channel_id=1, source_target_pairs={{8,0},{16,24},{9,1},{17,25},{10,2},{18,26},{11,3},{19,27},{12,4},{... | collective-permute-start | bytes 1769480 | tf_op jit(solution)/shard_map/ppermute | solution.py:796
  154.9 7.4 %copy-start.8 = (f32[96,1536]{1,0:T(8,128)}, f32[96,1536]{1,0:T(8,128)S(1)}, u32[]{:S(2)}) copy-start(f32[96,1536]{1,0:T(8,128)S(1)} %collective-permute-done.6.met) | copy-start | bytes 1769476
  154.9 17.5 %collective-permute-start.7 = (f32[96,1536]{1,0:T(8,128)S(1)}, f32[96,1536]{1,0:T(8,128)S(1)}, u32[]{:S(2)}, u32[]{:S(2)}) collective-permute-start(f32[96,1536]{1,0:T(8,128)S(1)} %collective-permute-done.6.met), channel_id=1, source_target_pairs={{8,0},{16,24},{9,1},{17,25},{10,2},{18,26},{11,3},{19,27},{12,4},{... | collective-permute-start | bytes 1769480 | tf_op jit(solution)/shard_map/ppermute | solution.py:796
  157.2 0.8 copy-start.15
  162.3 0.8 copy-start.14
  167.3 0.8 copy-start.13
  172.3 0.8 copy-start.12

commit v3 on v2

v3 whole, which is shorter than its diff:
```python
import functools

import jax
import jax.numpy as jnp
from jax import lax
from jax.experimental import pallas as pl
from jax.experimental.pallas import tpu as pltpu
from jax.sharding import PartitionSpec as P

f32 = jnp.float32
i32 = jnp.int32
bf16 = jnp.bfloat16
highest = lax.Precision.HIGHEST

LANES = 128
SUBLANES = 8
BLOCK = 256
CHAINS = 4

VMEM = pl.BlockSpec(memory_space=pltpu.VMEM)
SMEM = pl.BlockSpec(memory_space=pltpu.SMEM)
HBM = pl.BlockSpec(memory_space=pltpu.HBM)


def params(mib):
    return pltpu.CompilerParams(vmem_limit_bytes=mib << 20)


def pinned(*arrays):
    return [pltpu.with_memory_space_constraint(array, pltpu.VMEM) for array in arrays]


def in_hbm(*arrays):
    return [pltpu.with_memory_space_constraint(array, pltpu.HBM) for array in arrays]


def exchange(parts, axis):
    count = len(parts)
    moved = [
        lax.ppermute(part, axis, [(at, at ^ k) for at in range(count)])
        for k, part in enumerate(parts)
        if k
    ]
    return list(parts[:1]) + moved


def cost(flops, read):
    return pl.CostEstimate(flops=flops, bytes_accessed=read, transcendentals=0)


def dot(a, b, dims=(((1,), (0,)), ((), ()))):
    return lax.dot_general(a, b, dims, preferred_element_type=f32)


def split(x):
    high = x.astype(bf16)
    return high, (x - high.astype(f32)).astype(bf16)


def pack_kernel(sizes, index, owners, cells, values, *rest):
    outs, (packed, places, tally, sorted_, joined, counts, sem) = rest[:-7], rest[-7:]
    sub_count, group_count, chunk_count, strip = sizes
    block_count = owners.shape[0]
    tiles = group_count // SUBLANES
    lane = lax.broadcasted_iota(i32, (SUBLANES, LANES), 1)
    square = lambda axis: lax.broadcasted_iota(i32, (LANES, LANES), axis)
    owner = owners[...]
    picked = [jnp.where(owner == sub, 1.0, 0.0) for sub in range(sub_count)]
    upto = jnp.where(square(0) <= square(1), 1.0, 0.0).astype(bf16)
    ranks = dot(jnp.concatenate(picked, axis=0).astype(bf16), upto)
    wide = lax.broadcasted_iota(i32, (block_count, LANES), 1)
    place = jnp.zeros((block_count, LANES), f32)
    base = jnp.zeros((block_count, LANES), f32)
    totals = jnp.zeros((block_count, LANES), f32)
    for sub in range(sub_count):
        rank = ranks[sub * block_count : (sub + 1) * block_count]
        total = jnp.broadcast_to(rank[:, LANES - 1 :], rank.shape)
        place = jnp.where(owner == sub, rank - 1.0 + base, place)
        totals = jnp.where(wide == sub, total, totals)
        base = base + total
    places[...] = place.astype(i32)
    tally[...] = totals.astype(i32)
    copy = pltpu.make_async_copy(tally, counts, sem)
    copy.start()
    extra = -(group_count + SUBLANES) % 16
    row = square(0)

    def sort_block(block, carry):
        at = pl.multiple_of(block * LANES, LANES)
        parts = [
            *[values[level, :, pl.ds(at, LANES)] for level in range(values.shape[0])],
            jnp.broadcast_to(cells[pl.ds(block, 1), :], (SUBLANES, LANES)).astype(f32),
        ]
        if extra:
            parts.append(jnp.zeros((extra, LANES), f32))
        whole = jnp.concatenate(parts, axis=0)
        rows = whole.shape[0]
        high, rest = whole.astype(bf16), whole
        rest = rest - high.astype(f32)
        middle = rest.astype(bf16)
        low = (rest - middle.astype(f32)).astype(bf16)
        move = jnp.where(row == places[pl.ds(block, 1), :], 1.0, 0.0).astype(bf16)
        moved = dot(
            jnp.concatenate([high, middle, low], axis=0), move, (((1,), (1,)), ((), ()))
        )
        moved = moved[:rows] + moved[rows : 2 * rows] + moved[2 * rows :]
        for tile in range(tiles + 1):
            sorted_[block, tile] = moved[tile * SUBLANES : (tile + 1) * SUBLANES]
        return carry

    lax.fori_loop(0, block_count, sort_block, 0, unroll=8)
    copy.wait()

    def join_block(block, ends):
        start = jnp.int32(0)
        writes, following = [], []
        for sub in range(sub_count):
            end = ends[sub]
            chunk, offset = lax.shift_right_logical(end, 7), end & 127
            for tile in range(tiles + 1):
                turned = pltpu.roll(sorted_[block, tile], (end - start) & 127, 1)
                kept = jnp.where(lane >= offset, turned, joined[sub, chunk, tile])
                writes.append((sub, chunk, tile, kept, turned))
            start = start + counts[block, sub]
            following.append(end + counts[block, sub])
        for sub, chunk, tile, kept, turned in writes:
            joined[sub, chunk, tile] = kept
            joined[sub, chunk + 1, tile] = turned
        return tuple(following)

    ends = lax.fori_loop(0, block_count, join_block, (jnp.int32(0),) * sub_count, unroll=2)
    word_row = chunk_count * group_count
    word_rows = packed.shape[1] - word_row
    for sub in range(sub_count):
        packed[sub, word_row:, :] = jnp.full((word_rows, LANES), float(strip), f32)
        for chunk in range(chunk_count):
            for tile in range(tiles):
                at = chunk * group_count + tile * SUBLANES
                packed[sub, at : at + SUBLANES, :] = joined[sub, chunk, tile]
            filled = lane + chunk * LANES < ends[sub]
            cell = jnp.where(filled, joined[sub, chunk, tiles], 0.0).astype(i32)
            word = (cell - (cell & 127)) + ((cell - lane) & 127)
            word = jnp.where(filled, word, strip).astype(f32)
            packed[sub, word_row + chunk : word_row + chunk + 1, :] = word[:1]
    for k, out in enumerate(outs):
        out[...] = packed[index[0] ^ k]


def pack_observations(index, obs_values, owners, cells, sub_count, strip, capacity):
    level_count, var_count, obs_count = obs_values.shape
    group_count = level_count * var_count
    chunk_count = capacity // LANES
    block_count = obs_count // LANES
    rows = chunk_count * group_count + SUBLANES * (-(-chunk_count // SUBLANES))
    tiles = group_count // SUBLANES
    return pl.pallas_call(
        functools.partial(pack_kernel, (sub_count, group_count, chunk_count, strip)),
        out_shape=[pltpu.VMEM((rows, LANES), f32)] * sub_count,
        in_specs=[SMEM, VMEM, VMEM, VMEM],
        out_specs=[VMEM] * sub_count,
        scratch_shapes=[
            pltpu.VMEM((sub_count, rows, LANES), f32),
            pltpu.VMEM((block_count, LANES), i32),
            pltpu.VMEM((block_count, LANES), i32),
            pltpu.VMEM((block_count, tiles + 1, SUBLANES, LANES), f32),
            pltpu.VMEM((sub_count, chunk_count + 2, tiles + 1, SUBLANES, LANES), f32),
            pltpu.SMEM((block_count, LANES), i32),
            pltpu.SemaphoreType.DMA,
        ],
        compiler_params=params(6),
        cost_estimate=cost(10, 10),
    )(index, *in_hbm(owners.reshape(block_count, LANES), cells.reshape(block_count, LANES), obs_values))


def deposit_kernel(sizes, index, lat_length, field, *rest):
    sub_count, group_count, row_count, column_count, chunk_count, strip = sizes
    arrived, swept, leaving = rest[:sub_count], rest[sub_count], rest[sub_count + 1 :][:sub_count]
    got, exits, loaded, *rest = rest[2 * sub_count + 1 :]
    totals, (decay, integers, words, word_sem, sems) = rest[:CHAINS], rest[CHAINS:]
    tiles = group_count // SUBLANES
    word_row = chunk_count * group_count
    word_rows = got.shape[1] - word_row
    span = row_count * column_count

    def load(group):
        return pltpu.make_async_copy(field.at[group], loaded.at[group], sems.at[group])

    for group in range(group_count):
        load(group).start()
    for source in range(sub_count):
        got[source] = arrived[source][...]
        integers[source * word_rows : (source + 1) * word_rows, :] = arrived[source][
            word_row:, :
        ].astype(i32)
    hand_over = pltpu.make_async_copy(integers, words, word_sem)
    hand_over.start()
    here = index[0] * row_count
    for tile in range(tiles):
        lengths = jnp.concatenate(
            [lat_length[2 * tile + k].astype(f32) for k in range(SUBLANES // 4)], axis=0
        )
        lengths = pltpu.roll(lengths, jnp.where(here > 0, lengths.shape[1] - here, 0), 1)
        keep = jnp.exp(-1.0 / lengths[:, :LANES])
        for row in range(row_count):
            decay[row, tile] = jnp.broadcast_to(keep[:, row : row + 1], (SUBLANES, LANES))

    def clear(row, carry):
        for total in totals:
            for tile in range(tiles):
                for column in range(column_count):
                    total[tile, row, column] = jnp.zeros((SUBLANES, LANES), f32)
        return carry

    lax.fori_loop(0, row_count, clear, 0)
    lane = lax.broadcasted_iota(i32, (SUBLANES, LANES), 1)
    hand_over.wait()

    def one_source(source, carry):
        first = source * word_rows

        def more(chunk):
            last = jnp.minimum(chunk, chunk_count - 1)
            return (chunk < chunk_count) & (words[first + last, 0] < strip)

        def one_chunk(chunk):
            blocks = [
                got[
                    source,
                    pl.ds(pl.multiple_of(chunk * group_count + tile * SUBLANES, 8), SUBLANES),
                    :,
                ]
                for tile in range(tiles)
            ]
            for slot in range(LANES):
                word = words[first + chunk, slot]
                target = lax.shift_right_logical(word, 7)
                turn = word & 127
                for tile in range(tiles):
                    value = pltpu.roll(jnp.where(lane == slot, blocks[tile], 0.0), turn, 1)
                    total = flat[slot % CHAINS]
                    total[tile, target] = total[tile, target] + value
            return chunk + 1

        lax.while_loop(more, one_chunk, jnp.int32(0))
        return carry

    flat = [total.reshape(tiles, -1, SUBLANES, LANES) for total in totals]
    lax.fori_loop(0, sub_count, one_source, 0)
    for group in range(group_count):
        load(group).wait()

    for tile in range(tiles):
        groups = slice(tile * SUBLANES, (tile + 1) * SUBLANES)

        def add_rows(at, carry):
            rows = pl.ds(pl.multiple_of(at * SUBLANES, SUBLANES), SUBLANES)
            for column in range(column_count):
                lanes = slice(column * LANES, (column + 1) * LANES)
                value = jnp.swapaxes(loaded[groups, rows, lanes], 0, 1)
                for total in totals:
                    value = value + total[tile, rows, column]
                totals[0][tile, rows, column] = value
            return carry

        lax.fori_loop(0, row_count // SUBLANES, add_rows, 0)

        def sweep(source, target, turn):
            def one_row(step, state):
                row = row_count - 1 - step if turn % 2 else step
                keep = decay[row, tile]
                take = 1.0 - keep
                following = []
                for column in range(column_count):
                    value = keep * state[column] + take * source[tile, row, column]
                    target[tile, row, column] = value
                    following.append(value)
                return tuple(following)

            nothing = tuple(jnp.zeros((SUBLANES, LANES), f32) for _ in range(column_count))
            state = lax.fori_loop(0, row_count, one_row, nothing, unroll=4)
            message_rows = 4 * column_count
            for column in range(column_count):
                at = tile * SUBLANES * message_rows + turn * column_count + column
                exits[pl.ds(at, SUBLANES, stride=message_rows), :] = state[column]

        for turn in range(4):
            sweep(totals[turn % 2], totals[1 - turn % 2], turn)

        def turn_rows(at, carry):
            rows = pl.ds(pl.multiple_of(at * SUBLANES, SUBLANES), SUBLANES)
            for column in range(column_count):
                swept[column, groups, rows, :] = jnp.swapaxes(totals[0][tile, rows, column], 0, 1)
            return carry

        lax.fori_loop(0, row_count // SUBLANES, turn_rows, 0)
    rows = 4 * column_count
    for k, out in enumerate(leaving):
        out[...] = exits[pl.ds(pl.multiple_of((index[0] ^ k) * rows, SUBLANES), rows), :]


def deposit_and_sweep(index, lat_length, got, field, sizes):
    sub_count, group_count, row_count, column_count, chunk_count, strip = sizes
    tiles = group_count // SUBLANES
    rows = got[0].shape[0]
    word_rows = rows - chunk_count * group_count
    exit_rows = 4 * column_count
    plain = (group_count, row_count, column_count * LANES)
    dump = (tiles, row_count + 1, column_count, SUBLANES, LANES)
    return pl.pallas_call(
        functools.partial(deposit_kernel, sizes),
        out_shape=[
            pltpu.VMEM((column_count, group_count, row_count, LANES), f32),
        ]
        + [pltpu.VMEM((exit_rows, LANES), f32)] * sub_count,
        in_specs=[SMEM, VMEM, HBM] + [VMEM] * sub_count,
        out_specs=[VMEM] * (sub_count + 1),
        scratch_shapes=[
            pltpu.VMEM((sub_count, rows, LANES), f32),
            pltpu.VMEM((group_count * exit_rows, LANES), f32),
            pltpu.VMEM(plain, f32),
        ]
        + [pltpu.VMEM(dump, f32)] * CHAINS
        + [
            pltpu.VMEM((row_count, tiles, SUBLANES, LANES), f32),
            pltpu.VMEM((sub_count * word_rows, LANES), i32),
            pltpu.SMEM((sub_count * word_rows, LANES), i32),
            pltpu.SemaphoreType.DMA,
            pltpu.SemaphoreType.DMA((group_count,)),
        ],
        compiler_params=params(26),
        cost_estimate=cost(10, 10),
    )(index, lat_length, *in_hbm(field), *pinned(*got))


def unit_kernel(sizes, index, lat_length, inside, leaving, decay, held):
    sub_count, row_count = sizes
    group = index[0]
    decay[...] = jnp.zeros(decay.shape, f32)
    lengths = lat_length[group // 4, pl.ds(group % 4, 1), :]
    keep = jnp.exp(-1.0 / lengths)
    for sub in range(sub_count):
        part = keep[:, sub * row_count : (sub + 1) * row_count]
        decay[4 * sub : 4 * sub + 4, :row_count] = jnp.broadcast_to(part, (4, row_count))
    decay[...] = jnp.transpose(decay[...], (1, 0))
    held[...] = jnp.zeros(held.shape, f32)
    state_of = lax.broadcasted_iota(i32, (1, LANES), 1) & 3
    for turn in range(4):

        def one_row(step, state, turn=turn):
            row = row_count - 1 - step if turn % 2 else step
            keep = decay[pl.ds(row, 1), :]
            value = keep * state + (1.0 - keep) * held[pl.ds(row, 1), :]
            held[pl.ds(row, 1), :] = value
            return value

        enter = jnp.where(state_of == turn, 1.0, 0.0)
        state = lax.fori_loop(0, row_count, one_row, enter, unroll=8)
        leaving[turn : turn + 1, :] = state
    inside[...] = jnp.transpose(held[...], (1, 0))


def unit_responses(index, lat_length, sub_count, row_count):
    return pl.pallas_call(
        functools.partial(unit_kernel, (sub_count, row_count)),
        in_specs=[SMEM, VMEM],
        out_specs=[VMEM, VMEM],
        out_shape=[
            pltpu.VMEM((LANES, LANES), f32),
            jax.ShapeDtypeStruct((4, LANES), f32),
        ],
        scratch_shapes=[pltpu.VMEM((LANES, LANES), f32)] * 2,
        compiler_params=params(4),
        cost_estimate=cost(10, 10),
    )(index, lat_length)


def circle_weights(length, block_count, near_high, near_low, moment, spread):
    def ramp(shape, axis):
        return lax.broadcasted_iota(i32, shape, axis)

    def twice(x):
        return jnp.concatenate([x, x], axis=1)

    rate = -1.0 / jnp.full((1, LANES), length, f32)
    decay = jnp.exp(rate)
    gain = ((1.0 - decay) / (1.0 + decay)) ** 2
    centre = (1.0 + decay * decay) / (1.0 - decay * decay)
    turn = jnp.exp(rate * float(BLOCK * block_count))
    lag = float(BLOCK * block_count) * turn / (1.0 - turn)
    full_gain = gain / (1.0 - turn)

    shape = (BLOCK, BLOCK)
    gap = jnp.abs(ramp(shape, 0) - ramp(shape, 1)).astype(f32)
    near = twice(gain) * jnp.exp(twice(rate) * gap) * (gap + twice(centre))
    high, low = split(near)
    near_high[0] = high
    near_low[0] = low
    shape = (BLOCK, LANES)
    kind = ramp(shape, 1) & 3
    spot = ramp(shape, 0)
    far = jnp.where(kind < 2, BLOCK - spot, spot).astype(f32)
    sums = jnp.exp(rate * far) * jnp.where((kind & 1) == 1, far, 1.0)
    high, low = split(sums)
    moment[0, :, :LANES] = high
    moment[0, :, LANES:] = low
    shape = (32, BLOCK)
    kind = ramp(shape, 0) & 3
    block = lax.shift_right_logical(ramp(shape, 0), 2)
    spot = ramp(shape, 1)
    reach = jnp.where(kind < 2, spot, BLOCK - spot).astype(f32)
    for at in range(block_count):
        ahead = jnp.where(kind < 2, at - block, block - at) - 1
        steps = jnp.where(ahead < 0, ahead + block_count, ahead)
        full = reach + (steps * BLOCK).astype(f32)
        weight = twice(full_gain) * jnp.exp(twice(rate) * full)
        lead = full + twice(centre + lag)
        value = jnp.where((kind & 1) == 1, weight, weight * lead)
        value = jnp.where(block < block_count, value, 0.0)
        high, low = split(value)
        spread[0, :32, at * BLOCK : (at + 1) * BLOCK] = high
        spread[0, 32:, at * BLOCK : (at + 1) * BLOCK] = low


def weight_kernel(block_count, lon_length, *outs):
    group = pl.program_id(0)
    circle_weights(lon_length[group // 4, group % 4], block_count, *outs)


def weight_shapes(column_total):
    return [(BLOCK, BLOCK)] * 3 + [(64, column_total)]


def prepare(lon_length, column_total, space):
    group_count = lon_length.size
    shapes = weight_shapes(column_total)
    return pl.pallas_call(
        functools.partial(weight_kernel, column_total // BLOCK),
        grid=(group_count,),
        in_specs=[SMEM],
        out_specs=[pl.BlockSpec((1,) + shape, lambda i: (i, 0, 0)) for shape in shapes],
        out_shape=[space((group_count,) + shape, bf16) for shape in shapes],
        compiler_params=params(10),
        cost_estimate=cost(10, 10),
    )(lon_length)


def circle(pieces, near_high, near_low, moment, spread):
    row_count = pieces[0].shape[0]
    whole = jnp.concatenate(pieces, axis=0)
    high, low = split(whole)
    near = dot(high, near_high) + dot(low, near_high) + dot(high, near_low)
    sums = dot(high, moment)
    sums = sums[:, :LANES] + sums[:, LANES:] + dot(low, moment[:, :LANES])
    lane = lax.broadcasted_iota(i32, (row_count, LANES), 1)
    slot = lax.shift_right_logical(lane, 2) & 7
    moments = jnp.zeros((row_count, LANES), f32)
    for at in range(len(pieces)):
        part = sums[at * row_count : (at + 1) * row_count]
        moments = jnp.where(slot == at, part, moments)
    rest = moments - moments.astype(bf16).astype(f32)
    moments = jnp.where((lax.shift_right_logical(lane, 5) & 1) == 1, rest, moments).astype(bf16)
    spread = jnp.concatenate([spread[:32], spread[:32], spread[32:], spread[32:]], axis=0)
    far = dot(moments, spread)
    return [
        near[at * row_count : (at + 1) * row_count] + far[:, at * BLOCK : (at + 1) * BLOCK]
        for at in range(len(pieces))
    ]


def longitude_kernel(swept, near_high, near_low, moment, spread, out):
    column_count = swept.shape[0]
    pieces = [
        jnp.concatenate([swept[2 * at, 0], swept[2 * at + 1, 0]], axis=1)
        for at in range(column_count // 2)
    ]
    pieces = circle(pieces, near_high[0], near_low[0], moment[0], spread[0])
    for at, piece in enumerate(pieces):
        out[0, :, at * BLOCK : (at + 1) * BLOCK] = piece


def pair_kernel(variable, swept, near_high, near_low, moment, spread, table, own, sent, part):
    column_count = swept.shape[0]
    for level in range(2):
        group = level * 4 + variable
        pieces = [
            jnp.concatenate([swept[2 * at, group], swept[2 * at + 1, group]], axis=1)
            for at in range(column_count // 2)
        ]
        pieces = circle(
            pieces, near_high[group], near_low[group], moment[group], spread[group]
        )
        for target, first in ((sent, 0), (part, 2)):
            weight = table[variable, first + level : first + level + 1, :]
            weight = jnp.concatenate([weight, weight], axis=1)
            for at, piece in enumerate(pieces):
                spot = slice(at * BLOCK, (at + 1) * BLOCK)
                value = weight * piece
                target[:, spot] = target[:, spot] + value if level else value
        for at, piece in enumerate(pieces):
            own[level, :, at * BLOCK : (at + 1) * BLOCK] = piece


def longitude_pair(variable, swept, weights, table):
    column_count, _, row_count, _ = swept.shape
    shape = (row_count, column_count * LANES)
    return pl.pallas_call(
        functools.partial(pair_kernel, variable),
        in_specs=[VMEM] * 6,
        out_specs=[VMEM] * 3,
        out_shape=[pltpu.VMEM((2,) + shape, f32), pltpu.VMEM(shape, f32), pltpu.VMEM(shape, f32)],
        compiler_params=params(10),
        cost_estimate=cost(10, 10),
    )(*pinned(swept, *weights, table))


def longitude(swept, weights, count, first, stride):
    column_count, _, row_count, _ = swept.shape
    column_total = column_count * LANES

    def of(i):
        return first + stride * i

    in_specs = [
        pl.BlockSpec((column_count, 1, row_count, LANES), lambda i: (0, of(i), 0, 0)),
        pl.BlockSpec((1, BLOCK, BLOCK), lambda i: (of(i), 0, 0)),
        pl.BlockSpec((1, BLOCK, BLOCK), lambda i: (of(i), 0, 0)),
        pl.BlockSpec((1, BLOCK, BLOCK), lambda i: (of(i), 0, 0)),
        pl.BlockSpec((1, 64, column_total), lambda i: (of(i), 0, 0)),
    ]
    out_specs = [pl.BlockSpec((1, row_count, column_total), lambda i: (i, 0, 0))]
    out_shape = [jax.ShapeDtypeStruct((count, row_count, column_total), f32)]
    operands = [swept, *weights]
    return pl.pallas_call(
        longitude_kernel,
        grid=(count,),
        in_specs=in_specs,
        out_specs=out_specs,
        out_shape=out_shape,
        compiler_params=params(14),
        cost_estimate=cost(10, 10),
    )(*operands)


def chain_kernel(sub_count, index, lon_length, leaving, inside, *rest):
    arrived, outs = rest[:sub_count], rest[sub_count : 2 * sub_count]
    exits, out, held, *weights = rest[2 * sub_count :]
    for k, part in enumerate(arrived):
        exits[index[0] ^ k] = part[...]
    column_count = exits.shape[1] // 4
    shape = (column_count, LANES)
    group = index[0]
    circle_weights(lon_length[group // 4, group % 4], column_count // 2, *weights)
    entering = {}
    for turn in range(4):
        order = list(range(sub_count))
        if turn % 2:
            order.reverse()
        state = jnp.zeros(shape, f32)
        for block in order:
            entering[turn, block] = state
            at = (turn * sub_count + block) * column_count
            held[at : at + column_count, :] = state
            state = exits[block, turn * column_count : (turn + 1) * column_count, :]
            for other in range(turn + 1):
                state = state + leaving[turn, block * 4 + other] * entering[other, block]
    pieces = []
    for at in range(column_count // 2):
        pair = [
            held[pl.ds(2 * at + k, 4 * sub_count, stride=column_count), :] for k in range(2)
        ]
        pieces.append(jnp.concatenate(pair, axis=1))
    pieces = circle(pieces, *[weight[0] for weight in weights])
    message_rows = out.shape[0] // sub_count
    for at, piece in enumerate(pieces):
        for k in range(2):
            for turn in range(4):
                place = turn * column_count + 2 * at + k
                out[pl.ds(place, sub_count, stride=message_rows), :] = piece[
                    turn * sub_count : (turn + 1) * sub_count, k * LANES : (k + 1) * LANES
                ]
    for block in range(sub_count):
        at = block * message_rows + 4 * column_count
        out[at : at + 4, :] = inside[block * 4 : (block + 1) * 4, :]
        out[at + 4 : (block + 1) * message_rows, :] = jnp.zeros(
            (message_rows - 4 * column_count - 4, LANES), f32
        )
    for k, target in enumerate(outs):
        at = pl.multiple_of((index[0] ^ k) * message_rows, SUBLANES)
        target[...] = out[pl.ds(at, message_rows), :]


def chain_states(index, lon_length, exits, leaving, inside):
    sub_count = len(exits)
    rows = exits[0].shape[0]
    column_total = rows // 4 * LANES
    message_rows = rows + 8
    return pl.pallas_call(
        functools.partial(chain_kernel, sub_count),
        in_specs=[SMEM, SMEM, SMEM, VMEM] + [VMEM] * sub_count,
        out_specs=[VMEM] * sub_count,
        scratch_shapes=[
            pltpu.VMEM((sub_count, rows, LANES), f32),
            pltpu.VMEM((sub_count * message_rows, LANES), f32),
            pltpu.VMEM((sub_count * rows, LANES), f32),
        ]
        + [pltpu.VMEM((1,) + shape, bf16) for shape in weight_shapes(column_total)],
        out_shape=[pltpu.VMEM((message_rows, LANES), f32)] * sub_count,
        compiler_params=params(16),
        cost_estimate=cost(10, 10),
    )(index, lon_length, leaving, *pinned(inside, *exits))


def gather_kernel(index, *rest):
    *parts, out = rest
    rows = parts[0].shape[0]
    for k, part in enumerate(parts):
        out[pl.ds(pl.multiple_of((index[0] ^ k) * rows, SUBLANES), rows), :] = part[...]


def gather_messages(index, parts):
    rows = parts[0].shape[0]
    return pl.pallas_call(
        gather_kernel,
        in_specs=[SMEM] + [VMEM] * len(parts),
        out_specs=VMEM,
        out_shape=pltpu.VMEM((len(parts) * rows, LANES), f32),
        compiler_params=params(4),
        cost_estimate=cost(10, 10),
    )(index, *pinned(*parts))


def pair_factors(top, low):
    top_take, low_take = 1.0 - top, 1.0 - low
    through = top * low
    sends = (low * top_take, low_take)
    low_out = (low_take * through, low, low_take * low * top_take, low_take * low_take)
    top_out = (
        top * low_out[0] + top_take * top,
        top * low_out[1],
        top * low_out[2] + top_take * top_take,
        top * low_out[3],
    )
    return through, sends, top_out, low_out


def tables_kernel(index, own, across_, beside_, corner_, table, mix, decay):
    band = index[0]
    for at, lengths in enumerate((own, across_, beside_, corner_)):
        for level in range(2):
            for variable in range(4):
                row = at * 8 + level * 4 + variable
                decay[row : row + 1, :] = jnp.full((1, LANES), lengths[level, variable], f32)
    decay[...] = jnp.exp(-1.0 / decay[...])

    def factors(at):
        return pair_factors(decay[at * 8 : at * 8 + 4, :], decay[at * 8 + 4 : at * 8 + 8, :])

    def by_band(*values):
        result = values[0]
        for at in range(1, 4):
            result = jnp.where(band == at, values[at], result)
        return result

    through, sends, top_out, low_out = factors(0)
    across, beside, corner = factors(1), factors(2), factors(3)
    through_n, echo_n = beside[0], beside[2][0]
    third = by_band(across[0], corner[0], across[0], across[0])
    third_echo = by_band(across[2][0], corner[2][0], across[2][0], across[2][0])
    fourth_echo = by_band(corner[2][0], across[2][0], corner[2][0], corner[2][0])
    zeta = third * third * fourth_echo + third_echo
    rows = []
    for i in range(2):
        reply = top_out[2 + i]
        rows.append(by_band(sends[i], reply + through * zeta * sends[i], sends[i], reply))
    for i in range(2):
        rows.append(
            by_band(
                sends[i], sends[i], through * echo_n * sends[i] + top_out[2 + i], sends[i]
            )
        )
    rows.append(through)
    for fin, back, *own in (top_out, low_out):
        for i in range(2):
            rows.append(
                by_band(
                    own[i] + back * (through_n * through_n * zeta + echo_n) * sends[i],
                    own[i] + back * zeta * sends[i],
                    own[i] + back * echo_n * sends[i],
                    own[i],
                )
            )
        none = jnp.zeros_like(fin)
        rows.append(by_band(back, fin + back * zeta * through, back, fin))
        rows.append(by_band(back * through_n, none, none, fin * through_n))
        rows.append(by_band(none, back, fin + back * echo_n * through, none))
    for variable in range(4):
        for at, row in enumerate(rows):
            table[variable, at : at + 1, :] = row[variable : variable + 1]
    row = lax.broadcasted_iota(i32, (SUBLANES, LANES), 0)
    for variable in range(4):
        value = jnp.zeros((SUBLANES, LANES), f32)
        downward, keeps = [], []
        for level in range(8):
            other = (level // 2) ^ band
            place = (other & 1) * 2 + lax.shift_right_logical(other, 1)
            at = place * 8 + (level % 2) * 4 + variable
            keep = jnp.broadcast_to(decay[pl.ds(at, 1), :], (SUBLANES, LANES))
            unit = jnp.where(row == place * 2 + level % 2, 1.0, 0.0)
            value = keep * value + (1.0 - keep) * unit
            downward.append(value)
            keeps.append(keep)
        value = jnp.zeros((SUBLANES, LANES), f32)
        upward = [None] * 8
        for level in reversed(range(8)):
            value = keeps[level] * value + (1.0 - keeps[level]) * downward[level]
            upward[level] = value
        for level in range(2):
            mix[level, variable] = by_band(*[upward[2 * at + level] for at in range(4)])


def tables(index, lengths):
    return pl.pallas_call(
        tables_kernel,
        in_specs=[SMEM] * 5,
        out_specs=[VMEM, VMEM],
        out_shape=[
            jax.ShapeDtypeStruct((4, 16, LANES), f32),
            jax.ShapeDtypeStruct((2, 4, SUBLANES, LANES), f32),
        ],
        scratch_shapes=[pltpu.VMEM((32, LANES), f32)],
        compiler_params=params(4),
        cost_estimate=cost(10, 10),
    )(index, *lengths)


ADD_FLOPS = 10


def add_kernel(variable, part, near, table, total):
    weight = table[variable, 4:5, :]
    for column in range(part.shape[1] // LANES):
        at = slice(column * LANES, (column + 1) * LANES)
        total[:, at] = part[:, at] + weight * near[:, at]


def add_near(variable, part, near, table):
    return pl.pallas_call(
        functools.partial(add_kernel, variable),
        in_specs=[VMEM] * 3,
        out_specs=VMEM,
        out_shape=pltpu.VMEM(part.shape, f32),
        compiler_params=params(4),
        cost_estimate=cost(ADD_FLOPS, 10),
    )(*pinned(part, near, table))


def last_kernel(variable, own, near, far, met, mix, table, *rest):
    out, added, message, sems = rest[-4:]
    row_count, column_total = near.shape
    column_count = column_total // LANES
    stride = message.shape[0] // SUBLANES
    first = 0
    for at, part in enumerate(rest[:4]):
        for level in range(2):
            source = (level * 4 + variable) * stride
            target = (2 * at + level) * stride
            message[target : target + stride, :] = part[source : source + stride, :]
    lanes = []
    for column in range(column_count):
        lanes.append(
            jnp.concatenate(
                [
                    message[pl.ds(first + k * column_count + column, SUBLANES, stride=stride), :]
                    for k in range(4)
                ],
                axis=0,
            )
        )
    high, low = split(jnp.concatenate(lanes, axis=1))
    states = jnp.concatenate([high, high, low, low], axis=0)
    inside = [
        message[pl.ds(first + 4 * column_count + k, SUBLANES, stride=stride), :] for k in range(4)
    ]
    copies = []
    for level in range(2):
        mixed = jnp.concatenate([part * mix[level, variable] for part in inside], axis=0)
        high, low = split(mixed)
        mixed = jnp.concatenate([high, low, high, low], axis=0)
        total = dot(mixed, states, (((0,), (0,)), ((), ())))[:row_count]
        weights = [table[variable, 5 + level * 5 + k : 6 + level * 5 + k, :] for k in range(5)]
        for column in range(column_count):
            at = slice(column * LANES, (column + 1) * LANES)
            value = total[:, at] + weights[0] * own[0, :, at] + weights[1] * own[1, :, at]
            value = value + weights[2] * near[:, at] + weights[3] * far[:, at]
            added[level, :, at] = value + weights[4] * met[:, at]
        copy = pltpu.make_async_copy(added.at[level], out.at[level, variable], sems.at[level])
        copy.start()
        copies.append(copy)
    for copy in copies:
        copy.wait()


def last_step(variable, own, near, far, met, messages, mix, table, so_far):
    _, row_count, column_total = own.shape
    operands = pinned(own, near, far, met, mix, table, *messages)
    in_specs = [VMEM] * 10
    aliases = {}
    if so_far is not None:
        operands.append(so_far)
        in_specs.append(HBM)
        aliases = {10: 0}
    return pl.pallas_call(
        functools.partial(last_kernel, variable),
        in_specs=in_specs,
        out_specs=HBM,
        out_shape=pltpu.HBM((2, 4, row_count, column_total), f32),
        scratch_shapes=[
            pltpu.VMEM((2, row_count, column_total), f32),
            pltpu.VMEM(messages[0].shape, f32),
            pltpu.SemaphoreType.DMA((2,)),
        ],
        input_output_aliases=aliases,
        compiler_params=params(10),
        cost_estimate=cost(10, 10),
    )(*operands)


SWAP = [(0, 1), (1, 0), (2, 3), (3, 2)]
CROSS = [(0, 2), (2, 0), (1, 3), (3, 1)]
CORNER = [(0, 3), (3, 0), (1, 2), (2, 1)]
MIDDLE = [(0, 0), (1, 2), (2, 1), (3, 3)]


def after(value, *earlier):
    return lax.optimization_barrier((value,) + earlier)[0]


def four_bands(swept, weights, exits, chain, gather, table, mix):
    owns, parts, nears, mets = [], [], [], []

    def filter_one(variable, *earlier):
        own, sent, part = longitude_pair(variable, after(swept, *earlier), weights, table)
        owns.append(own)
        parts.append(part)
        nears.append(lax.ppermute(sent, "band", SWAP))
        return part

    def cross_one(variable, *earlier):
        part = after(parts[variable], *earlier)
        total = add_near(variable, part, nears[variable], table)
        mets.append(lax.ppermute(total, "band", MIDDLE))
        return total

    exits = exchange(exits, "sub")
    mark = filter_one(0)
    mark = filter_one(1, mark)
    mark = cross_one(0, mark)
    mark = cross_one(1, mark)
    chained = chain([after(exits[0], mark)] + exits[1:])
    messages = exchange(chained, "sub")
    mark = filter_one(2, chained[0])
    mark = filter_one(3, mark)
    mark = cross_one(2, mark, mets[0])
    mark = cross_one(3, mark)
    messages = gather(messages, mark)
    across = lax.ppermute(messages, "band", CROSS)
    beside = lax.ppermute(messages, "band", SWAP)
    corner = lax.ppermute(across, "band", SWAP)
    messages = (messages, across, beside, corner)
    fars = [lax.ppermute(met, "band", SWAP) for met in mets]
    result = None
    for v in range(4):
        result = last_step(v, owns[v], nears[v], fars[v], mets[v], messages, mix, table, result)
    return result


def prefix(part, axis, combine, identity, reverse):
    count = lax.axis_size(axis)
    place = lax.axis_index(axis)
    ahead = count - 1 - place if reverse else place
    gathered = jax.tree.map(lambda a: lax.all_gather(a, axis), part)
    state = jax.tree.map(lambda a, e: jnp.zeros_like(a) + jnp.asarray(e, a.dtype), part, identity)

    def one(turn, state):
        source = count - 1 - turn if reverse else turn
        return combine(
            state, jax.tree.map(lambda a: lax.dynamic_index_in_dim(a, source, 0, False), gathered)
        )

    return lax.fori_loop(0, ahead, one, state)


def combine(earlier, later):
    return (earlier[0] * later[0], later[0] * earlier[1] + later[1])


def level_chain(values, decays, reverse):
    level_count = values.shape[0]
    visit_order = range(level_count - 1, -1, -1) if reverse else range(level_count)
    carry_state = jnp.zeros_like(values[0])
    level_gain = jnp.ones((values.shape[1],), f32)
    outputs = [None] * level_count
    carried = [None] * level_count
    for level_index in visit_order:
        factor = decays[level_index][:, None, None]
        carry_state = factor * carry_state + (1.0 - factor) * values[level_index]
        level_gain = level_gain * decays[level_index]
        outputs[level_index] = carry_state
        carried[level_index] = level_gain
    total_decay = level_gain[:, None, None]
    identity = (jnp.ones_like(total_decay), jnp.zeros_like(carry_state))
    incoming = prefix((total_decay, carry_state), "band", combine, identity, reverse)[1]
    return jnp.stack(
        [
            outputs[level_index] + carried[level_index][:, None, None] * incoming
            for level_index in range(level_count)
        ]
    )


def any_bands(swept, weights, exits, chain, gather, vert_length):
    column_count, group_count, row_count, _ = swept.shape
    messages = gather(exchange(chain(exchange(exits, "sub")), "sub"))
    (values,) = longitude(swept, weights, group_count, 0, 1)
    messages = messages.reshape(group_count, -1, LANES)
    states = messages[:, : 4 * column_count].reshape(group_count, 4, -1)
    inside = messages[:, 4 * column_count : 4 * column_count + 4, :row_count]
    values = values + jnp.einsum("gkr,gkc->grc", inside, states, precision=highest)
    decay = jnp.exp(-1.0 / vert_length)
    values = values.reshape(decay.shape + values.shape[1:])
    return level_chain(level_chain(values, decay, False), decay, True)


def per_device(background, obs_columns, obs_owner, obs_cell, lat_length, lon_length, vert_length):
    level_count, var_count, row_count, lon_count = background.shape
    sub_count = lax.axis_size("sub")
    group_count = level_count * var_count
    strip = row_count * lon_count
    column_count = lon_count // LANES
    capacity = 2 * obs_owner.shape[0] // sub_count
    chunk_count = capacity // LANES
    two_chips = lax.axis_size("band") == 4 and level_count == 2
    index = lax.axis_index("sub").astype(i32).reshape(1)
    band = lax.axis_index("band").astype(i32).reshape(1)

    if two_chips:
        vert_lengths = [vert_length] + [
            lax.ppermute(vert_length, "band", pairs) for pairs in (CROSS, SWAP, CORNER)
        ]
    packed = pack_observations(
        after(index, band),
        obs_columns, obs_owner[:, 0], obs_cell, sub_count, strip, capacity
    )
    got = exchange(packed, "sub")
    space = pltpu.VMEM if two_chips else pltpu.HBM
    weights = prepare(after(lon_length, packed[0]), lon_count, space)
    ready = list(weights)
    if two_chips:
        table, mix = tables(after(band, packed[0]), vert_lengths)
        ready.append(table)

    sizes = (sub_count, group_count, row_count, column_count, chunk_count, strip)
    swept, *exits = deposit_and_sweep(
        index,
        lat_length,
        [after(got[0], *ready)] + got[1:],
        background.reshape(group_count, row_count, lon_count),
        sizes,
    )

    def chain(arrived):
        inside, leaving = unit_responses(
            after(index, swept), lat_length, sub_count, row_count
        )
        return chain_states(index, lon_length, arrived, leaving, inside)

    def gather(parts, *earlier):
        return gather_messages(after(index, *earlier), parts)

    if two_chips:
        return four_bands(swept, weights, exits, chain, gather, table, mix)
    return any_bands(swept, weights, exits, chain, gather, vert_length)


def solution(mesh):
    placed = (
        P("band", None, "sub", None),
        P("band", None, "sub"),
        P("sub", None),
        P("sub"),
        P("band", None, None),
        P("band", None),
        P("band", None),
    )
    return jax.shard_map(
        per_device,
        mesh=mesh,
        in_specs=placed,
        out_specs=P("band", None, "sub", None),
        check_vma=False,
    )
```

time: 179 us -> 121 us (0.68)
  Pallas kernels: 97.2 us -> 42.4 us
  starting transfers between devices: 38.2 us -> 62.3 us
  waiting for transfers between devices: 26.1 us -> 12.9 us
  local copies, waits for them, and re-layouts: 13.2 us -> 2.09 us
  other arithmetic: 2.32 us -> 0 us
    pallas_call x16 -> x18, Pallas kernels: 87.6 us -> 38.3 us  [the longest x1 19.5 us: deposit_and_sweep(): pl.pallas_call(functools.partial(deposit_kernel, sizes), out_shape=[pltpu...]
    ppermute x12 -> x35, starting transfers between devices: 22.6 us -> 59.2 us  [the longest x21 32 us: exchange(): lax.ppermute(part, axis, [(at, at ^ k) for at in range(count)])]
    all_to_all x3 -> x0, starting transfers between devices: 14.6 us -> none  [the longest x1 6.37 us: per_device(): got = lax.all_to_all(packed, 'sub', split_axis=0, concat_axis=0, tiled=True)]
    ppermute x12 -> x35, waiting for transfers between devices: 24.5 us -> 12.9 us  [the longest x21 9.71 us: exchange(): lax.ppermute(part, axis, [(at, at ^ k) for at in range(count)])]
    unnamed x34 -> x8, local copies, waits for them, and re-layouts: 9.38 us -> 2.09 us
    pallas_call x1, Pallas kernels: 9.61 us -> 4.15 us  [pack_observations(): pl.pallas_call(functools.partial(pack_kernel, (sub_count, group_count, ch...]
    reshape x3 -> x0, local copies, waits for them, and re-layouts: 3.06 us -> none  [the longest x1 1.29 us: per_device(): lon_length.reshape(-1)]
    ppermute x4, starting transfers between devices: 1.03 us -> 3.14 us  [filter_one(): nears.append(lax.ppermute(sent, 'band', SWAP))]
  transfers between devices with their start and end apart: 19 -> 39, of which waited for: 3 -> 10; matrix products, arithmetic and copies ran while one was open for 3% -> 0% of each run, Pallas kernels for 20% -> 13%
where the time goes in v3:
time: 121 us; the launch traced here: 120 us
  starting transfers between devices  62.3 us (51%)
  Pallas kernels  42.4 us (35%)
  waiting for transfers between devices  12.9 us (11%)
  local copies, waits for them, and re-layouts  2.09 us (2%)
    ppermute x21, starting transfers between devices, exchange(): lax.ppermute(part, axis, [(at, at ^ k) for at in range(count)])  32 us
    pallas_call x1, Pallas kernels, deposit_and_sweep(): pl.pallas_call(functools.partial(deposit_kernel, sizes), out_shape=[pltpu...  19.5 us
    ppermute x4, starting transfers between devices, cross_one(): mets.append(lax.ppermute(total, 'band', MIDDLE))  14.7 us
    ppermute x21, waiting for transfers between devices, exchange(): lax.ppermute(part, axis, [(at, at ^ k) for at in range(count)])  9.71 us
    pallas_call x4, Pallas kernels, last_step(): pl.pallas_call(functools.partial(last_kernel, variable), in_specs=in_spec...  6.16 us
    pallas_call x4, Pallas kernels, longitude_pair(): pl.pallas_call(functools.partial(pair_kernel, variable), in_specs=[VMEM]...  5.75 us
    ppermute x4, starting transfers between devices, four_bands(): fars = [lax.ppermute(met, 'band', SWAP) for met in mets]  5.73 us
    pallas_call x1, Pallas kernels, pack_observations(): pl.pallas_call(functools.partial(pack_kernel, (sub_count, group_count, ch...  4.15 us
  transfers between devices with their start and end apart: 39, of which 10 were waited for; matrix products, arithmetic and copies ran while one was open for 0% of the time, Pallas kernels for 13%

profile of v3, /device:TPU:1, one launch (start us, length us, event | category | flops | bytes accessed | tf_op | source)
XLA Modules:
  0.0 120.2 jit_solution(16983867385701727686)
XLA Ops:
  0.0 4.2 %shard_map.73 = (f32[72,128]{1,0:T(8,128)S(1)}, f32[72,128]{1,0:T(8,128)S(1)}, f32[72,128]{1,0:T(8,128)S(1)}, f32[72,128]{1,0:T(8,128)S(1)}, f32[72,128]{1,0:T(8...) custom-call(s32[1]{0:T(128)} %bitcast.index, s32[32,128]{1,0:T(8,128)} %bitcast.6, ...), custom_call_target="tpu_custom_call" | custom-call | flops 10 | bytes 10 | tf_op jit(solution)/shard_map/pallas_call | solution.py:156
  4.2 2.1 %collective-permute-start.3 = (f32[72,128]{1,0:T(8,128)S(1)}, f32[72,128]{1,0:T(8,128)S(1)}, u32[]{:S(2)}, u32[]{:S(2)}) collective-permute-start(f32[72,128]{1,0:T(8,128)S(1)} %get-tuple-element.74), channel_id=1, source_target_pairs={{0,1},{1,0},{2,3},{3,2},{4,5},{5,4},{6,7},{7,6},{8,9},{9,8},{10,11... | collective-permute-start | bytes 110600 | tf_op jit(solution)/shard_map/ppermute | solution.py:40
  6.3 1.3 %collective-permute-start.4 = (f32[72,128]{1,0:T(8,128)S(1)}, f32[72,128]{1,0:T(8,128)S(1)}, u32[]{:S(2)}, u32[]{:S(2)}) collective-permute-start(f32[72,128]{1,0:T(8,128)S(1)} %get-tuple-element.75), channel_id=1, source_target_pairs={{0,2},{1,3},{2,0},{3,1},{4,6},{5,7},{6,4},{7,5},{8,10},{9,11},{10,... | collective-permute-start | bytes 110600 | tf_op jit(solution)/shard_map/ppermute | solution.py:40
  7.6 1.2 %collective-permute-start = (f32[2,4]{1,0:T(2,128)}, f32[2,4]{1,0:T(2,128)S(1)}, u32[]{:S(2)}, u32[]{:S(2)}) collective-permute-start(f32[2,4]{1,0:T(2,128)} %own.1), channel_id=1, source_target_pairs={{0,16},{16,0},{8,24},{24,8},{1,17},{17,1},{9,25},{25,9},{2,18},{18... | collective-permute-start | bytes 104 | tf_op jit(solution)/shard_map/ppermute | solution.py:948
  8.8 1.5 %collective-permute-start.1 = (f32[2,4]{1,0:T(2,128)}, f32[2,4]{1,0:T(2,128)S(1)}, u32[]{:S(2)}, u32[]{:S(2)}) collective-permute-start(f32[2,4]{1,0:T(2,128)} %own.1), channel_id=1, source_target_pairs={{0,8},{8,0},{16,24},{24,16},{1,9},{9,1},{17,25},{25,17},{2,10},{10... | collective-permute-start | bytes 104 | tf_op jit(solution)/shard_map/ppermute | solution.py:948
  10.5 0.9 collective-permute-done.1.beside_
  11.4 2.3 %collective-permute-start.6 = (f32[72,128]{1,0:T(8,128)S(1)}, f32[72,128]{1,0:T(8,128)S(1)}, u32[]{:S(2)}, u32[]{:S(2)}) collective-permute-start(f32[72,128]{1,0:T(8,128)S(1)} %get-tuple-element.77), channel_id=1, source_target_pairs={{0,4},{1,5},{2,6},{3,7},{4,0},{5,1},{6,2},{7,3},{8,12},{9,13},{10,... | collective-permute-start | bytes 110600 | tf_op jit(solution)/shard_map/ppermute | solution.py:40
  13.7 2.1 %collective-permute-start.7 = (f32[72,128]{1,0:T(8,128)S(1)}, f32[72,128]{1,0:T(8,128)S(1)}, u32[]{:S(2)}, u32[]{:S(2)}) collective-permute-start(f32[72,128]{1,0:T(8,128)S(1)} %get-tuple-element.78), channel_id=1, source_target_pairs={{0,5},{1,4},{2,7},{3,6},{4,1},{5,0},{6,3},{7,2},{8,13},{9,12},{10,... | collective-permute-start | bytes 110600 | tf_op jit(solution)/shard_map/ppermute | solution.py:40
  15.8 1.5 %collective-permute-start.8 = (f32[72,128]{1,0:T(8,128)S(1)}, f32[72,128]{1,0:T(8,128)S(1)}, u32[]{:S(2)}, u32[]{:S(2)}) collective-permute-start(f32[72,128]{1,0:T(8,128)S(1)} %get-tuple-element.79), channel_id=1, source_target_pairs={{0,6},{1,7},{2,4},{3,5},{4,2},{5,3},{6,0},{7,1},{8,14},{9,15},{10,... | collective-permute-start | bytes 110600 | tf_op jit(solution)/shard_map/ppermute | solution.py:40
  17.3 2.8 %collective-permute-start.9 = (f32[72,128]{1,0:T(8,128)S(1)}, f32[72,128]{1,0:T(8,128)S(1)}, u32[]{:S(2)}, u32[]{:S(2)}) collective-permute-start(f32[72,128]{1,0:T(8,128)S(1)} %get-tuple-element.80), channel_id=1, source_target_pairs={{0,7},{1,6},{2,5},{3,4},{4,3},{5,2},{6,1},{7,0},{8,15},{9,14},{10,... | collective-permute-start | bytes 110600 | tf_op jit(solution)/shard_map/ppermute | solution.py:40
  20.0 0.7 copy-done.1
  20.7 2.9 %shard_map.74 = (bf16[8,256,256]{2,1,0:T(8,128)(2,1)S(1)}, bf16[8,256,256]{2,1,0:T(8,128)(2,1)S(1)}, bf16[8,256,256]{2,1,0:T(8,128)(2,1)S(1)}, bf16[8,64,1536]{2,1,0:T(8,128)(2,1)S(1)}) custom-call(f32[2,4]{1,0:T(2,128)S(1)} %copy-done.1), custom_call_target="tpu_custom_call" | custom-call | flops 10 | bytes 10 | tf_op jit(solution)/shard_map/pallas_call | solution.py:436
  23.7 0.7 copy-done.3
  24.3 0.7 shard_map.75
  25.1 0.7 copy-done
  25.8 19.5 %shard_map.76 = (f32[12,8,96,128]{3,2,1,0:T(8,128)S(1)}, f32[48,128]{1,0:T(8,128)S(1)}, f32[48,128]{1,0:T(8,128)S(1)}, f32[48,128]{1,0:T(8,128)S(1)}, f32[48,128...) custom-call(s32[1]{0:T(128)} %bitcast.index, ...), custom_call_target="tpu_custom_call" | custom-call | flops 10 | bytes 10 | tf_op jit(solution)/shard_map/pallas_call | solution.py:309
  45.3 1.4 %shard_map.78 = (f32[2,96,1536]{2,1,0:T(8,128)S(1)}, f32[96,1536]{1,0:T(8,128)S(1)}, f32[96,1536]{1,0:T(8,128)S(1)}) custom-call(f32[12,8,96,128]{3,2,1,0:T(8,128)S(1)} %get-tuple-element.104.swept, bf16[8,256,256]{2,1,0:T(8,128)(2,1)S(1)} %get-tuple-element.67.near_high, bf16[8,256,256]{2,1,0:T(8,128)(2,1)S(1)} %get-tuple-element.68.near_low, ...), custom_call_target="tpu_custom_call" | custom-call | flops 10 | bytes 10 | tf_op jit(solution)/shard_map/pallas_call | solution.py:506
  46.8 2.1 %collective-permute-start.10 = (f32[96,1536]{1,0:T(8,128)S(1)}, f32[96,1536]{1,0:T(8,128)S(1)}, u32[]{:S(2)}, u32[]{:S(2)}) collective-permute-start(f32[96,1536]{1,0:T(8,128)S(1)} %get-tuple-element.90), channel_id=1, source_target_pairs={{0,8},{8,0},{16,24},{24,16},{1,9},{9,1},{17,25},{25,17},{2,10},{10... | collective-permute-start | bytes 1769480 | tf_op jit(solution)/shard_map/ppermute | solution.py:845
  48.9 1.4 %shard_map.79 = (f32[2,96,1536]{2,1,0:T(8,128)S(1)}, f32[96,1536]{1,0:T(8,128)S(1)}, f32[96,1536]{1,0:T(8,128)S(1)}) custom-call(f32[12,8,96,128]{3,2,1,0:T(8,128)S(1)} %get-tuple-element.104.swept, bf16[8,256,256]{2,1,0:T(8,128)(2,1)S(1)} %get-tuple-element.67.near_high, bf16[8,256,256]{2,1,0:T(8,128)(2,1)S(1)} %get-tuple-element.68.near_low, ...), custom_call_target="tpu_custom_call" | custom-call | flops 10 | bytes 10 | tf_op jit(solution)/shard_map/pallas_call | solution.py:506
  50.5 6.0 %collective-permute-start.13 = (f32[48,128]{1,0:T(8,128)S(1)}, f32[48,128]{1,0:T(8,128)S(1)}, u32[]{:S(2)}, u32[]{:S(2)}) collective-permute-start(f32[48,128]{1,0:T(8,128)S(1)} %get-tuple-element.95), channel_id=1, source_target_pairs={{0,2},{1,3},{2,0},{3,1},{4,6},{5,7},{6,4},{7,5},{8,10},{9,11},{10,... | collective-permute-start | bytes 73736 | tf_op jit(solution)/shard_map/ppermute | solution.py:40
  56.5 1.6 %collective-permute-start.15 = (f32[48,128]{1,0:T(8,128)S(1)}, f32[48,128]{1,0:T(8,128)S(1)}, u32[]{:S(2)}, u32[]{:S(2)}) collective-permute-start(f32[48,128]{1,0:T(8,128)S(1)} %get-tuple-element.97), channel_id=1, source_target_pairs={{0,4},{1,5},{2,6},{3,7},{4,0},{5,1},{6,2},{7,3},{8,12},{9,13},{10,... | collective-permute-start | bytes 73736 | tf_op jit(solution)/shard_map/ppermute | solution.py:40
  58.0 1.7 %collective-permute-start.16 = (f32[48,128]{1,0:T(8,128)S(1)}, f32[48,128]{1,0:T(8,128)S(1)}, u32[]{:S(2)}, u32[]{:S(2)}) collective-permute-start(f32[48,128]{1,0:T(8,128)S(1)} %get-tuple-element.98), channel_id=1, source_target_pairs={{0,5},{1,4},{2,7},{3,6},{4,1},{5,0},{6,3},{7,2},{8,13},{9,12},{10,... | collective-permute-start | bytes 73736 | tf_op jit(solution)/shard_map/ppermute | solution.py:40
  59.7 2.8 %collective-permute-start.17 = (f32[48,128]{1,0:T(8,128)S(1)}, f32[48,128]{1,0:T(8,128)S(1)}, u32[]{:S(2)}, u32[]{:S(2)}) collective-permute-start(f32[48,128]{1,0:T(8,128)S(1)} %get-tuple-element.99), channel_id=1, source_target_pairs={{0,6},{1,7},{2,4},{3,5},{4,2},{5,3},{6,0},{7,1},{8,14},{9,15},{10,... | collective-permute-start | bytes 73736 | tf_op jit(solution)/shard_map/ppermute | solution.py:40
  62.5 0.9 collective-permute-start.18
  63.4 1.5 %shard_map.77 = (f32[128,128]{1,0:T(8,128)S(1)}, f32[4,128]{1,0:T(4,128)S(1)}) custom-call(s32[1]{0:T(128)} %bitcast.index, f32[2,4,768]{2,1,0:T(4,128)S(1)} %copy-done), custom_call_target="tpu_custom_call" | custom-call | flops 10 | bytes 10 | tf_op jit(solution)/shard_map/pallas_call | solution.py:363
  65.1 5.5 %collective-permute-start.20 = (f32[96,1536]{1,0:T(8,128)S(1)}, f32[96,1536]{1,0:T(8,128)S(1)}, u32[]{:S(2)}, u32[]{:S(2)}) collective-permute-start(f32[96,1536]{1,0:T(8,128)S(1)} %shard_map.80), channel_id=1, source_target_pairs={{0,0},{8,16},{16,8},{24,24},{1,1},{9,17},{17,9},{25,25},{2,2},{10,... | collective-permute-start | bytes 1769480 | tf_op jit(solution)/shard_map/ppermute | solution.py:851
  70.6 1.4 %shard_map.82 = (f32[56,128]{1,0:T(8,128)S(1)}, f32[56,128]{1,0:T(8,128)S(1)}, f32[56,128]{1,0:T(8,128)S(1)}, f32[56,128]{1,0:T(8,128)S(1)}, f32[56,128]{1,0:T(8...) custom-call(s32[1]{0:T(128)} %bitcast.index, f32[2,4]{1,0:T(2,128)S(1)} %copy-done.2, ...), custom_call_target="tpu_custom_call" | custom-call | flops 10 | bytes 10 | tf_op jit(solution)/shard_map/pallas_call | solution.py:597
  72.0 1.4 %shard_map.83 = (f32[2,96,1536]{2,1,0:T(8,128)S(1)}, f32[96,1536]{1,0:T(8,128)S(1)}, f32[96,1536]{1,0:T(8,128)S(1)}) custom-call(f32[12,8,96,128]{3,2,1,0:T(8,128)S(1)} %get-tuple-element.104.swept, bf16[8,256,256]{2,1,0:T(8,128)(2,1)S(1)} %get-tuple-element.67.near_high, bf16[8,256,256]{2,1,0:T(8,128)(2,1)S(1)} %get-tuple-element.68.near_low, ...), custom_call_target="tpu_custom_call" | custom-call | flops 10 | bytes 10 | tf_op jit(solution)/shard_map/pallas_call | solution.py:506
  73.5 0.9 collective-permute-start.21
  74.3 1.4 %shard_map.84 = (f32[2,96,1536]{2,1,0:T(8,128)S(1)}, f32[96,1536]{1,0:T(8,128)S(1)}, f32[96,1536]{1,0:T(8,128)S(1)}) custom-call(f32[12,8,96,128]{3,2,1,0:T(8,128)S(1)} %get-tuple-element.104.swept, bf16[8,256,256]{2,1,0:T(8,128)(2,1)S(1)} %get-tuple-element.67.near_high, bf16[8,256,256]{2,1,0:T(8,128)(2,1)S(1)} %get-tuple-element.68.near_low, ...), custom_call_target="tpu_custom_call" | custom-call | flops 10 | bytes 10 | tf_op jit(solution)/shard_map/pallas_call | solution.py:506
  75.9 3.5 %collective-permute-start.36 = (f32[96,1536]{1,0:T(8,128)S(1)}, f32[96,1536]{1,0:T(8,128)S(1)}, u32[]{:S(2)}, u32[]{:S(2)}) collective-permute-start(f32[96,1536]{1,0:T(8,128)S(1)} %shard_map.81), channel_id=1, source_target_pairs={{0,0},{8,16},{16,8},{24,24},{1,1},{9,17},{17,9},{25,25},{2,2},{10,... | collective-permute-start | bytes 1769480 | tf_op jit(solution)/shard_map/ppermute | solution.py:851
  79.5 2.4 %collective-permute-start.34 = (f32[96,1536]{1,0:T(8,128)S(1)}, f32[96,1536]{1,0:T(8,128)S(1)}, u32[]{:S(2)}, u32[]{:S(2)}) collective-permute-start(f32[96,1536]{1,0:T(8,128)S(1)} %shard_map.85), channel_id=1, source_target_pairs={{0,0},{8,16},{16,8},{24,24},{1,1},{9,17},{17,9},{25,25},{2,2},{10,... | collective-permute-start | bytes 1769480 | tf_op jit(solution)/shard_map/ppermute | solution.py:851
  82.0 3.4 %collective-permute-start.22 = (f32[96,1536]{1,0:T(8,128)S(1)}, f32[96,1536]{1,0:T(8,128)S(1)}, u32[]{:S(2)}, u32[]{:S(2)}) collective-permute-start(f32[96,1536]{1,0:T(8,128)S(1)} %shard_map.86), channel_id=1, source_target_pairs={{0,0},{8,16},{16,8},{24,24},{1,1},{9,17},{17,9},{25,25},{2,2},{10,... | collective-permute-start | bytes 1769480 | tf_op jit(solution)/shard_map/ppermute | solution.py:851
  85.5 2.9 %collective-permute-done.24.rest_1_ = f32[56,128]{1,0:T(8,128)S(1)} collective-permute-done((f32[56,128]{1,0:T(8,128)S(1)}, f32[56,128]{1,0:T(8,128)S(1)}, u32[]{:S(2)}, u32[]{:S(2)}) %collective-permute-start.24) | collective-permute-done | bytes 28704 | tf_op jit(solution)/shard_map/ppermute | solution.py:40
  88.6 2.2 %collective-permute-start.27 = (f32[56,128]{1,0:T(8,128)S(1)}, f32[56,128]{1,0:T(8,128)S(1)}, u32[]{:S(2)}, u32[]{:S(2)}) collective-permute-start(f32[56,128]{1,0:T(8,128)S(1)} %get-tuple-element.116), channel_id=1, source_target_pairs={{0,4},{1,5},{2,6},{3,7},{4,0},{5,1},{6,2},{7,3},{8,12},{9,13},{10,... | collective-permute-start | bytes 86024 | tf_op jit(solution)/shard_map/ppermute | solution.py:40
  90.8 1.2 %collective-permute-done.26.rest_3_ = f32[56,128]{1,0:T(8,128)S(1)} collective-permute-done((f32[56,128]{1,0:T(8,128)S(1)}, f32[56,128]{1,0:T(8,128)S(1)}, u32[]{:S(2)}, u32[]{:S(2)}) %collective-permute-start.26) | collective-permute-done | bytes 28704 | tf_op jit(solution)/shard_map/ppermute | solution.py:40
  92.5 2.4 %collective-permute-start.29 = (f32[56,128]{1,0:T(8,128)S(1)}, f32[56,128]{1,0:T(8,128)S(1)}, u32[]{:S(2)}, u32[]{:S(2)}) collective-permute-start(f32[56,128]{1,0:T(8,128)S(1)} %get-tuple-element.118), channel_id=1, source_target_pairs={{0,6},{1,7},{2,4},{3,5},{4,2},{5,3},{6,0},{7,1},{8,14},{9,15},{10,... | collective-permute-start | bytes 86024 | tf_op jit(solution)/shard_map/ppermute | solution.py:40
  94.9 1.7 %collective-permute-done.28.rest_5_ = f32[56,128]{1,0:T(8,128)S(1)} collective-permute-done((f32[56,128]{1,0:T(8,128)S(1)}, f32[56,128]{1,0:T(8,128)S(1)}, u32[]{:S(2)}, u32[]{:S(2)}) %collective-permute-start.28) | collective-permute-done | bytes 28704 | tf_op jit(solution)/shard_map/ppermute | solution.py:40
  96.6 2.2 %collective-permute-start.30 = (f32[56,128]{1,0:T(8,128)S(1)}, f32[56,128]{1,0:T(8,128)S(1)}, u32[]{:S(2)}, u32[]{:S(2)}) collective-permute-start(f32[56,128]{1,0:T(8,128)S(1)} %get-tuple-element.119), channel_id=1, source_target_pairs={{0,7},{1,6},{2,5},{3,4},{4,3},{5,2},{6,1},{7,0},{8,15},{9,14},{10,... | collective-permute-start | bytes 86024 | tf_op jit(solution)/shard_map/ppermute | solution.py:40
  98.8 3.2 %collective-permute-done.30.rest_7_ = f32[56,128]{1,0:T(8,128)S(1)} collective-permute-done((f32[56,128]{1,0:T(8,128)S(1)}, f32[56,128]{1,0:T(8,128)S(1)}, u32[]{:S(2)}, u32[]{:S(2)}) %collective-permute-start.30) | collective-permute-done | bytes 28704 | tf_op jit(solution)/shard_map/ppermute | solution.py:40
  102.1 5.2 %collective-permute-start.38 = (f32[96,1536]{1,0:T(8,128)S(1)}, f32[96,1536]{1,0:T(8,128)S(1)}, u32[]{:S(2)}, u32[]{:S(2)}) collective-permute-start(f32[96,1536]{1,0:T(8,128)S(1)} %collective-permute-done.20.met), channel_id=1, source_target_pairs={{0,8},{8,0},{16,24},{24,16},{1,9},{9,1},{17,25},{25,17},{2,10},{10... | collective-permute-start | bytes 1769480 | tf_op jit(solution)/shard_map/ppermute | solution.py:870
  107.8 3.4 %collective-permute-start.32 = (f32[448,128]{1,0:T(8,128)S(1)}, f32[448,128]{1,0:T(8,128)S(1)}, u32[]{:S(2)}, u32[]{:S(2)}) collective-permute-start(f32[448,128]{1,0:T(8,128)S(1)} %shard_map.87.rest_0_), channel_id=1, source_target_pairs={{0,8},{8,0},{16,24},{24,16},{1,9},{9,1},{17,25},{25,17},{2,10},{10... | collective-permute-start | bytes 688136 | tf_op jit(solution)/shard_map/ppermute | solution.py:867
  111.2 1.1 collective-permute-done.32.rest_2_
  112.7 1.1 collective-permute-done.33.rest_3_
  113.8 1.5 %shard_map.88.rest_4_ = f32[2,4,96,1536]{3,2,1,0:T(8,128)} custom-call(f32[2,96,1536]{2,1,0:T(8,128)S(1)} %get-tuple-element.122.own, f32[96,1536]{1,0:T(8,128)S(1)} %collective-permute-done.10.near, f32[96,1536]{1,0:T(8,128)S(1)} %collective-permute-done.38.far, f32[96,1536]{1,0:T(8,128)S(1)} %collective-permute-done.20.met, ...), custom_call_target="tpu_custom_call" | custom-call | flops 10 | bytes 10 | tf_op jit(solution)/shard_map/pallas_call | solution.py:812
  115.4 1.5 %shard_map.89.rest_4_ = f32[2,4,96,1536]{3,2,1,0:T(8,128)} custom-call(f32[2,96,1536]{2,1,0:T(8,128)S(1)} %get-tuple-element.121.own, f32[96,1536]{1,0:T(8,128)S(1)} %collective-permute-done.11.near, f32[96,1536]{1,0:T(8,128)S(1)} %collective-permute-done.37.far, f32[96,1536]{1,0:T(8,128)S(1)} %collective-permute-done.36.met, ...), custom_call_target="tpu_custom_call", output_to_operand_aliasing={{}: (10, {})} | custom-call | flops 10 | bytes 10 | tf_op jit(solution)/shard_map/pallas_call | solution.py:812
  116.9 1.6 %shard_map.90.rest_4_ = f32[2,4,96,1536]{3,2,1,0:T(8,128)} custom-call(f32[2,96,1536]{2,1,0:T(8,128)S(1)} %get-tuple-element.120.own, f32[96,1536]{1,0:T(8,128)S(1)} %collective-permute-done.21.near, f32[96,1536]{1,0:T(8,128)S(1)} %collective-permute-done.35.far, f32[96,1536]{1,0:T(8,128)S(1)} %collective-permute-done.34.met, ...), custom_call_target="tpu_custom_call", output_to_operand_aliasing={{}: (10, {})} | custom-call | flops 10 | bytes 10 | tf_op jit(solution)/shard_map/pallas_call | solution.py:812
  118.5 1.5 %shard_map.91 = f32[2,4,96,1536]{3,2,1,0:T(8,128)} custom-call(f32[2,96,1536]{2,1,0:T(8,128)S(1)} %get-tuple-element.105.own, f32[96,1536]{1,0:T(8,128)S(1)} %collective-permute-done.19.near, f32[96,1536]{1,0:T(8,128)S(1)} %collective-permute-done.23.far, f32[96,1536]{1,0:T(8,128)S(1)} %collective-permute-done.22.met, ...), custom_call_target="tpu_custom_call", output_to_operand_aliasing={{}: (10, {})} | custom-call | flops 10 | bytes 10 | tf_op jit(solution)/shard_map/pallas_call | solution.py:812
  (57 shorter events, 2.7 us)
Async XLA Ops:
  4.2 11.6 %collective-permute-start.3 = (f32[72,128]{1,0:T(8,128)S(1)}, f32[72,128]{1,0:T(8,128)S(1)}, u32[]{:S(2)}, u32[]{:S(2)}) collective-permute-start(f32[72,128]{1,0:T(8,128)S(1)} %get-tuple-element.74), channel_id=1, source_target_pairs={{0,1},{1,0},{2,3},{3,2},{4,5},{5,4},{6,7},{7,6},{8,9},{9,8},{10,11... | collective-permute-start | bytes 110600 | tf_op jit(solution)/shard_map/ppermute | solution.py:40
  6.3 11.0 %collective-permute-start.4 = (f32[72,128]{1,0:T(8,128)S(1)}, f32[72,128]{1,0:T(8,128)S(1)}, u32[]{:S(2)}, u32[]{:S(2)}) collective-permute-start(f32[72,128]{1,0:T(8,128)S(1)} %get-tuple-element.75), channel_id=1, source_target_pairs={{0,2},{1,3},{2,0},{3,1},{4,6},{5,7},{6,4},{7,5},{8,10},{9,11},{10,... | collective-permute-start | bytes 110600 | tf_op jit(solution)/shard_map/ppermute | solution.py:40
  7.6 2.9 %collective-permute-start = (f32[2,4]{1,0:T(2,128)}, f32[2,4]{1,0:T(2,128)S(1)}, u32[]{:S(2)}, u32[]{:S(2)}) collective-permute-start(f32[2,4]{1,0:T(2,128)} %own.1), channel_id=1, source_target_pairs={{0,16},{16,0},{8,24},{24,8},{1,17},{17,1},{9,25},{25,9},{2,18},{18... | collective-permute-start | bytes 104 | tf_op jit(solution)/shard_map/ppermute | solution.py:948
  8.8 2.5 %collective-permute-start.1 = (f32[2,4]{1,0:T(2,128)}, f32[2,4]{1,0:T(2,128)S(1)}, u32[]{:S(2)}, u32[]{:S(2)}) collective-permute-start(f32[2,4]{1,0:T(2,128)} %own.1), channel_id=1, source_target_pairs={{0,8},{8,0},{16,24},{24,16},{1,9},{9,1},{17,25},{25,17},{2,10},{10... | collective-permute-start | bytes 104 | tf_op jit(solution)/shard_map/ppermute | solution.py:948
  10.3 3.3 %collective-permute-start.2 = (f32[2,4]{1,0:T(2,128)}, f32[2,4]{1,0:T(2,128)S(1)}, u32[]{:S(2)}, u32[]{:S(2)}) collective-permute-start(f32[2,4]{1,0:T(2,128)} %own.1), channel_id=1, source_target_pairs={{0,24},{24,0},{8,16},{16,8},{1,25},{25,1},{9,17},{17,9},{2,26},{26... | collective-permute-start | bytes 104 | tf_op jit(solution)/shard_map/ppermute | solution.py:948
  10.5 14.5 %collective-permute-start.5 = (f32[72,128]{1,0:T(8,128)S(1)}, f32[72,128]{1,0:T(8,128)S(1)}, u32[]{:S(2)}, u32[]{:S(2)}) collective-permute-start(f32[72,128]{1,0:T(8,128)S(1)} %get-tuple-element.76), channel_id=1, source_target_pairs={{0,3},{1,2},{2,1},{3,0},{4,7},{5,6},{6,5},{7,4},{8,11},{9,10},{10,... | collective-permute-start | bytes 110600 | tf_op jit(solution)/shard_map/ppermute | solution.py:40
  11.4 13.7 %collective-permute-start.6 = (f32[72,128]{1,0:T(8,128)S(1)}, f32[72,128]{1,0:T(8,128)S(1)}, u32[]{:S(2)}, u32[]{:S(2)}) collective-permute-start(f32[72,128]{1,0:T(8,128)S(1)} %get-tuple-element.77), channel_id=1, source_target_pairs={{0,4},{1,5},{2,6},{3,7},{4,0},{5,1},{6,2},{7,3},{8,12},{9,13},{10,... | collective-permute-start | bytes 110600 | tf_op jit(solution)/shard_map/ppermute | solution.py:40
  13.7 11.4 %collective-permute-start.7 = (f32[72,128]{1,0:T(8,128)S(1)}, f32[72,128]{1,0:T(8,128)S(1)}, u32[]{:S(2)}, u32[]{:S(2)}) collective-permute-start(f32[72,128]{1,0:T(8,128)S(1)} %get-tuple-element.78), channel_id=1, source_target_pairs={{0,5},{1,4},{2,7},{3,6},{4,1},{5,0},{6,3},{7,2},{8,13},{9,12},{10,... | collective-permute-start | bytes 110600 | tf_op jit(solution)/shard_map/ppermute | solution.py:40
  15.8 9.3 %collective-permute-start.8 = (f32[72,128]{1,0:T(8,128)S(1)}, f32[72,128]{1,0:T(8,128)S(1)}, u32[]{:S(2)}, u32[]{:S(2)}) collective-permute-start(f32[72,128]{1,0:T(8,128)S(1)} %get-tuple-element.79), channel_id=1, source_target_pairs={{0,6},{1,7},{2,4},{3,5},{4,2},{5,3},{6,0},{7,1},{8,14},{9,15},{10,... | collective-permute-start | bytes 110600 | tf_op jit(solution)/shard_map/ppermute | solution.py:40
  17.3 7.8 %collective-permute-start.9 = (f32[72,128]{1,0:T(8,128)S(1)}, f32[72,128]{1,0:T(8,128)S(1)}, u32[]{:S(2)}, u32[]{:S(2)}) collective-permute-start(f32[72,128]{1,0:T(8,128)S(1)} %get-tuple-element.80), channel_id=1, source_target_pairs={{0,7},{1,6},{2,5},{3,4},{4,3},{5,2},{6,1},{7,0},{8,15},{9,14},{10,... | collective-permute-start | bytes 110600 | tf_op jit(solution)/shard_map/ppermute | solution.py:40
  20.0 0.7 copy-start.1
  23.6 0.7 copy-start.3
  25.1 0.7 copy-start
  46.8 23.9 %copy-start.2 = (f32[2,4]{1,0:T(2,128)S(1)}, f32[2,4]{1,0:T(2,128)}, u32[]{:S(2)}) copy-start(f32[2,4]{1,0:T(2,128)} %lon_length.2) | copy-start | bytes 100
  46.8 13.0 %collective-permute-start.10 = (f32[96,1536]{1,0:T(8,128)S(1)}, f32[96,1536]{1,0:T(8,128)S(1)}, u32[]{:S(2)}, u32[]{:S(2)}) collective-permute-start(f32[96,1536]{1,0:T(8,128)S(1)} %get-tuple-element.90), channel_id=1, source_target_pairs={{0,8},{8,0},{16,24},{24,16},{1,9},{9,1},{17,25},{25,17},{2,10},{10... | collective-permute-start | bytes 1769480 | tf_op jit(solution)/shard_map/ppermute | solution.py:845
  50.3 12.2 %collective-permute-start.11 = (f32[96,1536]{1,0:T(8,128)S(1)}, f32[96,1536]{1,0:T(8,128)S(1)}, u32[]{:S(2)}, u32[]{:S(2)}) collective-permute-start(f32[96,1536]{1,0:T(8,128)S(1)} %get-tuple-element.92), channel_id=1, source_target_pairs={{0,8},{8,0},{16,24},{24,16},{1,9},{9,1},{17,25},{25,17},{2,10},{10... | collective-permute-start | bytes 1769480 | tf_op jit(solution)/shard_map/ppermute | solution.py:845
  50.4 6.1 %collective-permute-start.12 = (f32[48,128]{1,0:T(8,128)S(1)}, f32[48,128]{1,0:T(8,128)S(1)}, u32[]{:S(2)}, u32[]{:S(2)}) collective-permute-start(f32[48,128]{1,0:T(8,128)S(1)} %get-tuple-element.94), channel_id=1, source_target_pairs={{0,1},{1,0},{2,3},{3,2},{4,5},{5,4},{6,7},{7,6},{8,9},{9,8},{10,11... | collective-permute-start | bytes 73736 | tf_op jit(solution)/shard_map/ppermute | solution.py:40
  50.5 7.5 %collective-permute-start.13 = (f32[48,128]{1,0:T(8,128)S(1)}, f32[48,128]{1,0:T(8,128)S(1)}, u32[]{:S(2)}, u32[]{:S(2)}) collective-permute-start(f32[48,128]{1,0:T(8,128)S(1)} %get-tuple-element.95), channel_id=1, source_target_pairs={{0,2},{1,3},{2,0},{3,1},{4,6},{5,7},{6,4},{7,5},{8,10},{9,11},{10,... | collective-permute-start | bytes 73736 | tf_op jit(solution)/shard_map/ppermute | solution.py:40
  56.5 8.6 %collective-permute-start.14 = (f32[48,128]{1,0:T(8,128)S(1)}, f32[48,128]{1,0:T(8,128)S(1)}, u32[]{:S(2)}, u32[]{:S(2)}) collective-permute-start(f32[48,128]{1,0:T(8,128)S(1)} %get-tuple-element.96), channel_id=1, source_target_pairs={{0,3},{1,2},{2,1},{3,0},{4,7},{5,6},{6,5},{7,4},{8,11},{9,10},{10,... | collective-permute-start | bytes 73736 | tf_op jit(solution)/shard_map/ppermute | solution.py:40
  56.5 14.1 %collective-permute-start.15 = (f32[48,128]{1,0:T(8,128)S(1)}, f32[48,128]{1,0:T(8,128)S(1)}, u32[]{:S(2)}, u32[]{:S(2)}) collective-permute-start(f32[48,128]{1,0:T(8,128)S(1)} %get-tuple-element.97), channel_id=1, source_target_pairs={{0,4},{1,5},{2,6},{3,7},{4,0},{5,1},{6,2},{7,3},{8,12},{9,13},{10,... | collective-permute-start | bytes 73736 | tf_op jit(solution)/shard_map/ppermute | solution.py:40
  58.0 12.6 %collective-permute-start.16 = (f32[48,128]{1,0:T(8,128)S(1)}, f32[48,128]{1,0:T(8,128)S(1)}, u32[]{:S(2)}, u32[]{:S(2)}) collective-permute-start(f32[48,128]{1,0:T(8,128)S(1)} %get-tuple-element.98), channel_id=1, source_target_pairs={{0,5},{1,4},{2,7},{3,6},{4,1},{5,0},{6,3},{7,2},{8,13},{9,12},{10,... | collective-permute-start | bytes 73736 | tf_op jit(solution)/shard_map/ppermute | solution.py:40
  59.7 10.9 %collective-permute-start.17 = (f32[48,128]{1,0:T(8,128)S(1)}, f32[48,128]{1,0:T(8,128)S(1)}, u32[]{:S(2)}, u32[]{:S(2)}) collective-permute-start(f32[48,128]{1,0:T(8,128)S(1)} %get-tuple-element.99), channel_id=1, source_target_pairs={{0,6},{1,7},{2,4},{3,5},{4,2},{5,3},{6,0},{7,1},{8,14},{9,15},{10,... | collective-permute-start | bytes 73736 | tf_op jit(solution)/shard_map/ppermute | solution.py:40
  62.5 8.1 %collective-permute-start.18 = (f32[48,128]{1,0:T(8,128)S(1)}, f32[48,128]{1,0:T(8,128)S(1)}, u32[]{:S(2)}, u32[]{:S(2)}) collective-permute-start(f32[48,128]{1,0:T(8,128)S(1)} %get-tuple-element.100), channel_id=1, source_target_pairs={{0,7},{1,6},{2,5},{3,4},{4,3},{5,2},{6,1},{7,0},{8,15},{9,14},{10,... | collective-permute-start | bytes 73736 | tf_op jit(solution)/shard_map/ppermute | solution.py:40
  65.1 14.3 %collective-permute-start.20 = (f32[96,1536]{1,0:T(8,128)S(1)}, f32[96,1536]{1,0:T(8,128)S(1)}, u32[]{:S(2)}, u32[]{:S(2)}) collective-permute-start(f32[96,1536]{1,0:T(8,128)S(1)} %shard_map.80), channel_id=1, source_target_pairs={{0,0},{8,16},{16,8},{24,24},{1,1},{9,17},{17,9},{25,25},{2,2},{10,... | collective-permute-start | bytes 1769480 | tf_op jit(solution)/shard_map/ppermute | solution.py:851
  73.5 5.9 %collective-permute-start.21 = (f32[96,1536]{1,0:T(8,128)S(1)}, f32[96,1536]{1,0:T(8,128)S(1)}, u32[]{:S(2)}, u32[]{:S(2)}) collective-permute-start(f32[96,1536]{1,0:T(8,128)S(1)} %get-tuple-element.109), channel_id=1, source_target_pairs={{0,8},{8,0},{16,24},{24,16},{1,9},{9,1},{17,25},{25,17},{2,10},{10... | collective-permute-start | bytes 1769480 | tf_op jit(solution)/shard_map/ppermute | solution.py:845
  75.8 6.1 %collective-permute-start.19 = (f32[96,1536]{1,0:T(8,128)S(1)}, f32[96,1536]{1,0:T(8,128)S(1)}, u32[]{:S(2)}, u32[]{:S(2)}) collective-permute-start(f32[96,1536]{1,0:T(8,128)S(1)} %get-tuple-element.106), channel_id=1, source_target_pairs={{0,8},{8,0},{16,24},{24,16},{1,9},{9,1},{17,25},{25,17},{2,10},{10... | collective-permute-start | bytes 1769480 | tf_op jit(solution)/shard_map/ppermute | solution.py:845
  75.9 31.4 %collective-permute-start.36 = (f32[96,1536]{1,0:T(8,128)S(1)}, f32[96,1536]{1,0:T(8,128)S(1)}, u32[]{:S(2)}, u32[]{:S(2)}) collective-permute-start(f32[96,1536]{1,0:T(8,128)S(1)} %shard_map.81), channel_id=1, source_target_pairs={{0,0},{8,16},{16,8},{24,24},{1,1},{9,17},{17,9},{25,25},{2,2},{10,... | collective-permute-start | bytes 1769480 | tf_op jit(solution)/shard_map/ppermute | solution.py:851
  79.5 27.7 %collective-permute-start.34 = (f32[96,1536]{1,0:T(8,128)S(1)}, f32[96,1536]{1,0:T(8,128)S(1)}, u32[]{:S(2)}, u32[]{:S(2)}) collective-permute-start(f32[96,1536]{1,0:T(8,128)S(1)} %shard_map.85), channel_id=1, source_target_pairs={{0,0},{8,16},{16,8},{24,24},{1,1},{9,17},{17,9},{25,25},{2,2},{10,... | collective-permute-start | bytes 1769480 | tf_op jit(solution)/shard_map/ppermute | solution.py:851
  82.0 25.8 %collective-permute-start.22 = (f32[96,1536]{1,0:T(8,128)S(1)}, f32[96,1536]{1,0:T(8,128)S(1)}, u32[]{:S(2)}, u32[]{:S(2)}) collective-permute-start(f32[96,1536]{1,0:T(8,128)S(1)} %shard_map.86), channel_id=1, source_target_pairs={{0,0},{8,16},{16,8},{24,24},{1,1},{9,17},{17,9},{25,25},{2,2},{10,... | collective-permute-start | bytes 1769480 | tf_op jit(solution)/shard_map/ppermute | solution.py:851
  85.3 3.1 %collective-permute-start.24 = (f32[56,128]{1,0:T(8,128)S(1)}, f32[56,128]{1,0:T(8,128)S(1)}, u32[]{:S(2)}, u32[]{:S(2)}) collective-permute-start(f32[56,128]{1,0:T(8,128)S(1)} %get-tuple-element.113), channel_id=1, source_target_pairs={{0,1},{1,0},{2,3},{3,2},{4,5},{5,4},{6,7},{7,6},{8,9},{9,8},{10,11... | collective-permute-start | bytes 86024 | tf_op jit(solution)/shard_map/ppermute | solution.py:40
  85.4 3.2 %collective-permute-start.25 = (f32[56,128]{1,0:T(8,128)S(1)}, f32[56,128]{1,0:T(8,128)S(1)}, u32[]{:S(2)}, u32[]{:S(2)}) collective-permute-start(f32[56,128]{1,0:T(8,128)S(1)} %get-tuple-element.114), channel_id=1, source_target_pairs={{0,2},{1,3},{2,0},{3,1},{4,6},{5,7},{6,4},{7,5},{8,10},{9,11},{10,... | collective-permute-start | bytes 86024 | tf_op jit(solution)/shard_map/ppermute | solution.py:40
  88.4 3.6 %collective-permute-start.26 = (f32[56,128]{1,0:T(8,128)S(1)}, f32[56,128]{1,0:T(8,128)S(1)}, u32[]{:S(2)}, u32[]{:S(2)}) collective-permute-start(f32[56,128]{1,0:T(8,128)S(1)} %get-tuple-element.115), channel_id=1, source_target_pairs={{0,3},{1,2},{2,1},{3,0},{4,7},{5,6},{6,5},{7,4},{8,11},{9,10},{10,... | collective-permute-start | bytes 86024 | tf_op jit(solution)/shard_map/ppermute | solution.py:40
  88.6 3.9 %collective-permute-start.27 = (f32[56,128]{1,0:T(8,128)S(1)}, f32[56,128]{1,0:T(8,128)S(1)}, u32[]{:S(2)}, u32[]{:S(2)}) collective-permute-start(f32[56,128]{1,0:T(8,128)S(1)} %get-tuple-element.116), channel_id=1, source_target_pairs={{0,4},{1,5},{2,6},{3,7},{4,0},{5,1},{6,2},{7,3},{8,12},{9,13},{10,... | collective-permute-start | bytes 86024 | tf_op jit(solution)/shard_map/ppermute | solution.py:40
  92.0 4.5 %collective-permute-start.28 = (f32[56,128]{1,0:T(8,128)S(1)}, f32[56,128]{1,0:T(8,128)S(1)}, u32[]{:S(2)}, u32[]{:S(2)}) collective-permute-start(f32[56,128]{1,0:T(8,128)S(1)} %get-tuple-element.117), channel_id=1, source_target_pairs={{0,5},{1,4},{2,7},{3,6},{4,1},{5,0},{6,3},{7,2},{8,13},{9,12},{10,... | collective-permute-start | bytes 86024 | tf_op jit(solution)/shard_map/ppermute | solution.py:40
  92.5 6.2 %collective-permute-start.29 = (f32[56,128]{1,0:T(8,128)S(1)}, f32[56,128]{1,0:T(8,128)S(1)}, u32[]{:S(2)}, u32[]{:S(2)}) collective-permute-start(f32[56,128]{1,0:T(8,128)S(1)} %get-tuple-element.118), channel_id=1, source_target_pairs={{0,6},{1,7},{2,4},{3,5},{4,2},{5,3},{6,0},{7,1},{8,14},{9,15},{10,... | collective-permute-start | bytes 86024 | tf_op jit(solution)/shard_map/ppermute | solution.py:40
  96.6 5.4 %collective-permute-start.30 = (f32[56,128]{1,0:T(8,128)S(1)}, f32[56,128]{1,0:T(8,128)S(1)}, u32[]{:S(2)}, u32[]{:S(2)}) collective-permute-start(f32[56,128]{1,0:T(8,128)S(1)} %get-tuple-element.119), channel_id=1, source_target_pairs={{0,7},{1,6},{2,5},{3,4},{4,3},{5,2},{6,1},{7,0},{8,15},{9,14},{10,... | collective-permute-start | bytes 86024 | tf_op jit(solution)/shard_map/ppermute | solution.py:40
  102.0 5.8 %collective-permute-start.31 = (f32[448,128]{1,0:T(8,128)S(1)}, f32[448,128]{1,0:T(8,128)S(1)}, u32[]{:S(2)}, u32[]{:S(2)}) collective-permute-start(f32[448,128]{1,0:T(8,128)S(1)} %shard_map.87.rest_0_), channel_id=1, source_target_pairs={{0,16},{16,0},{8,24},{24,8},{1,17},{17,1},{9,25},{25,9},{2,18},{18... | collective-permute-start | bytes 688136 | tf_op jit(solution)/shard_map/ppermute | solution.py:866
  102.1 11.8 %collective-permute-start.38 = (f32[96,1536]{1,0:T(8,128)S(1)}, f32[96,1536]{1,0:T(8,128)S(1)}, u32[]{:S(2)}, u32[]{:S(2)}) collective-permute-start(f32[96,1536]{1,0:T(8,128)S(1)} %collective-permute-done.20.met), channel_id=1, source_target_pairs={{0,8},{8,0},{16,24},{24,16},{1,9},{9,1},{17,25},{25,17},{2,10},{10... | collective-permute-start | bytes 1769480 | tf_op jit(solution)/shard_map/ppermute | solution.py:870
  107.2 8.1 %collective-permute-start.37 = (f32[96,1536]{1,0:T(8,128)S(1)}, f32[96,1536]{1,0:T(8,128)S(1)}, u32[]{:S(2)}, u32[]{:S(2)}) collective-permute-start(f32[96,1536]{1,0:T(8,128)S(1)} %collective-permute-done.36.met), channel_id=1, source_target_pairs={{0,8},{8,0},{16,24},{24,16},{1,9},{9,1},{17,25},{25,17},{2,10},{10... | collective-permute-start | bytes 1769480 | tf_op jit(solution)/shard_map/ppermute | solution.py:870
  107.2 9.7 %collective-permute-start.35 = (f32[96,1536]{1,0:T(8,128)S(1)}, f32[96,1536]{1,0:T(8,128)S(1)}, u32[]{:S(2)}, u32[]{:S(2)}) collective-permute-start(f32[96,1536]{1,0:T(8,128)S(1)} %collective-permute-done.34.met), channel_id=1, source_target_pairs={{0,8},{8,0},{16,24},{24,16},{1,9},{9,1},{17,25},{25,17},{2,10},{10... | collective-permute-start | bytes 1769480 | tf_op jit(solution)/shard_map/ppermute | solution.py:870
  107.8 10.8 %collective-permute-start.23 = (f32[96,1536]{1,0:T(8,128)S(1)}, f32[96,1536]{1,0:T(8,128)S(1)}, u32[]{:S(2)}, u32[]{:S(2)}) collective-permute-start(f32[96,1536]{1,0:T(8,128)S(1)} %collective-permute-done.22.met), channel_id=1, source_target_pairs={{0,8},{8,0},{16,24},{24,16},{1,9},{9,1},{17,25},{25,17},{2,10},{10... | collective-permute-start | bytes 1769480 | tf_op jit(solution)/shard_map/ppermute | solution.py:870
  107.8 4.5 %collective-permute-start.32 = (f32[448,128]{1,0:T(8,128)S(1)}, f32[448,128]{1,0:T(8,128)S(1)}, u32[]{:S(2)}, u32[]{:S(2)}) collective-permute-start(f32[448,128]{1,0:T(8,128)S(1)} %shard_map.87.rest_0_), channel_id=1, source_target_pairs={{0,8},{8,0},{16,24},{24,16},{1,9},{9,1},{17,25},{25,17},{2,10},{10... | collective-permute-start | bytes 688136 | tf_op jit(solution)/shard_map/ppermute | solution.py:867
  112.4 1.5 %collective-permute-start.33 = (f32[448,128]{1,0:T(8,128)S(1)}, f32[448,128]{1,0:T(8,128)S(1)}, u32[]{:S(2)}, u32[]{:S(2)}) collective-permute-start(f32[448,128]{1,0:T(8,128)S(1)} %collective-permute-done.31.rest_1_), channel_id=1, source_target_pairs={{0,8},{8,0},{16,24},{24,16},{1,9},{9,1},{17,25},{25,17},{2,10},{10... | collective-permute-start | bytes 688136 | tf_op jit(solution)/shard_map/ppermute | solution.py:868

commit v4 on v3

--- a/solution.py
+++ b/solution.py
@@ -175,7 +175,7 @@
 def deposit_kernel(sizes, index, lat_length, field, *rest):
     sub_count, group_count, row_count, column_count, chunk_count, strip = sizes
     arrived, swept, leaving = rest[:sub_count], rest[sub_count], rest[sub_count + 1 :][:sub_count]
-    got, exits, loaded, *rest = rest[2 * sub_count + 1 :]
+    got, exits, loaded, all_lengths, length_sem, *rest = rest[2 * sub_count + 1 :]
     totals, (decay, integers, words, word_sem, sems) = rest[:CHAINS], rest[CHAINS:]
     tiles = group_count // SUBLANES
     word_row = chunk_count * group_count
@@ -187,6 +187,8 @@
 
     for group in range(group_count):
         load(group).start()
+    fetch = pltpu.make_async_copy(lat_length, all_lengths, length_sem)
+    fetch.start()
     for source in range(sub_count):
         got[source] = arrived[source][...]
         integers[source * word_rows : (source + 1) * word_rows, :] = arrived[source][
@@ -194,16 +196,6 @@
         ].astype(i32)
     hand_over = pltpu.make_async_copy(integers, words, word_sem)
     hand_over.start()
-    here = index[0] * row_count
-    for tile in range(tiles):
-        lengths = jnp.concatenate(
-            [lat_length[2 * tile + k].astype(f32) for k in range(SUBLANES // 4)], axis=0
-        )
-        lengths = pltpu.roll(lengths, jnp.where(here > 0, lengths.shape[1] - here, 0), 1)
-        keep = jnp.exp(-1.0 / lengths[:, :LANES])
-        for row in range(row_count):
-            decay[row, tile] = jnp.broadcast_to(keep[:, row : row + 1], (SUBLANES, LANES))
-
     def clear(row, carry):
         for total in totals:
             for tile in range(tiles):
@@ -246,8 +238,20 @@
 
     flat = [total.reshape(tiles, -1, SUBLANES, LANES) for total in totals]
     lax.fori_loop(0, sub_count, one_source, 0)
+    fetch.wait()
+    here = index[0] * row_count
+    for tile in range(tiles):
+        lengths = jnp.concatenate(
+            [all_lengths[2 * tile + k] for k in range(SUBLANES // 4)], axis=0
+        )
+        lengths = pltpu.roll(lengths, jnp.where(here > 0, lengths.shape[1] - here, 0), 1)
+        keep = jnp.exp(-1.0 / lengths[:, :LANES])
+        for row in range(row_count):
+            decay[row, tile] = jnp.broadcast_to(keep[:, row : row + 1], (SUBLANES, LANES))
+
     for group in range(group_count):
         load(group).wait()
+
 
     for tile in range(tiles):
         groups = slice(tile * SUBLANES, (tile + 1) * SUBLANES)
@@ -312,12 +316,14 @@
             pltpu.VMEM((column_count, group_count, row_count, LANES), f32),
         ]
         + [pltpu.VMEM((exit_rows, LANES), f32)] * sub_count,
-        in_specs=[SMEM, VMEM, HBM] + [VMEM] * sub_count,
+        in_specs=[SMEM, HBM, HBM] + [VMEM] * sub_count,
         out_specs=[VMEM] * (sub_count + 1),
         scratch_shapes=[
             pltpu.VMEM((sub_count, rows, LANES), f32),
             pltpu.VMEM((group_count * exit_rows, LANES), f32),
             pltpu.VMEM(plain, f32),
+            pltpu.VMEM(lat_length.shape, f32),
+            pltpu.SemaphoreType.DMA,
         ]
         + [pltpu.VMEM(dump, f32)] * CHAINS
         + [
@@ -329,7 +335,7 @@
         ],
         compiler_params=params(26),
         cost_estimate=cost(10, 10),
-    )(index, lat_length, *in_hbm(field), *pinned(*got))
+    )(index, *in_hbm(lat_length, field), *pinned(*got))
 
 
 def unit_kernel(sizes, index, lat_length, inside, leaving, decay, held):
@@ -478,36 +484,42 @@
         out[0, :, at * BLOCK : (at + 1) * BLOCK] = piece
 
 
-def pair_kernel(variable, swept, near_high, near_low, moment, spread, table, own, sent, part):
+def pair_kernel(variables, swept, near_high, near_low, moment, spread, table, own, sent, part):
     column_count = swept.shape[0]
-    for level in range(2):
-        group = level * 4 + variable
-        pieces = [
-            jnp.concatenate([swept[2 * at, group], swept[2 * at + 1, group]], axis=1)
-            for at in range(column_count // 2)
-        ]
-        pieces = circle(
-            pieces, near_high[group], near_low[group], moment[group], spread[group]
-        )
-        for target, first in ((sent, 0), (part, 2)):
-            weight = table[variable, first + level : first + level + 1, :]
-            weight = jnp.concatenate([weight, weight], axis=1)
+    for place, variable in enumerate(variables):
+        for level in range(2):
+            group = level * 4 + variable
+            pieces = [
+                jnp.concatenate([swept[2 * at, group], swept[2 * at + 1, group]], axis=1)
+                for at in range(column_count // 2)
+            ]
+            pieces = circle(
+                pieces, near_high[group], near_low[group], moment[group], spread[group]
+            )
+            for target, first in ((sent, 0), (part, 2)):
+                weight = table[variable, first + level : first + level + 1, :]
+                weight = jnp.concatenate([weight, weight], axis=1)
+                for at, piece in enumerate(pieces):
+                    spot = slice(at * BLOCK, (at + 1) * BLOCK)
+                    value = weight * piece
+                    target[place, :, spot] = target[place, :, spot] + value if level else value
             for at, piece in enumerate(pieces):
-                spot = slice(at * BLOCK, (at + 1) * BLOCK)
-                value = weight * piece
-                target[:, spot] = target[:, spot] + value if level else value
-        for at, piece in enumerate(pieces):
-            own[level, :, at * BLOCK : (at + 1) * BLOCK] = piece
-
-
-def longitude_pair(variable, swept, weights, table):
+                own[place, level, :, at * BLOCK : (at + 1) * BLOCK] = piece
+
+
+def longitude_pair(variables, swept, weights, table):
     column_count, _, row_count, _ = swept.shape
     shape = (row_count, column_count * LANES)
-    return pl.pallas_call(
-        functools.partial(pair_kernel, variable),
+    count = len(variables)
+    return pl.pallas_call(
+        functools.partial(pair_kernel, variables),
         in_specs=[VMEM] * 6,
         out_specs=[VMEM] * 3,
-        out_shape=[pltpu.VMEM((2,) + shape, f32), pltpu.VMEM(shape, f32), pltpu.VMEM(shape, f32)],
+        out_shape=[
+            pltpu.VMEM((count, 2) + shape, f32),
+            pltpu.VMEM((count,) + shape, f32),
+            pltpu.VMEM((count,) + shape, f32),
+        ],
         compiler_params=params(10),
         cost_estimate=cost(10, 10),
     )(*pinned(swept, *weights, table))
@@ -541,9 +553,9 @@
     )(*operands)
 
 
-def chain_kernel(sub_count, index, lon_length, leaving, inside, *rest):
-    arrived, outs = rest[:sub_count], rest[sub_count : 2 * sub_count]
-    exits, out, held, *weights = rest[2 * sub_count :]
+def chain_kernel(sub_count, layout, index, lon_length, leaving, inside, *rest):
+    arrived, outs = rest[:sub_count], rest[sub_count:][: len(layout)]
+    exits, out, held, *weights = rest[sub_count + len(layout) :]
     for k, part in enumerate(arrived):
         exits[index[0] ^ k] = part[...]
     column_count = exits.shape[1] // 4
@@ -584,46 +596,70 @@
         out[at + 4 : (block + 1) * message_rows, :] = jnp.zeros(
             (message_rows - 4 * column_count - 4, LANES), f32
         )
-    for k, target in enumerate(outs):
-        at = pl.multiple_of((index[0] ^ k) * message_rows, SUBLANES)
-        target[...] = out[pl.ds(at, message_rows), :]
-
-
-def chain_states(index, lon_length, exits, leaving, inside):
+    for target, members in zip(outs, layout):
+        for place, k in enumerate(members):
+            at = pl.multiple_of((index[0] ^ k) * message_rows, SUBLANES)
+            to = place * message_rows
+            target[to : to + message_rows, :] = out[pl.ds(at, message_rows), :]
+
+
+def chain_states(layout, index, lon_length, exits, leaving, inside):
     sub_count = len(exits)
     rows = exits[0].shape[0]
     column_total = rows // 4 * LANES
     message_rows = rows + 8
     return pl.pallas_call(
-        functools.partial(chain_kernel, sub_count),
+        functools.partial(chain_kernel, sub_count, layout),
         in_specs=[SMEM, SMEM, SMEM, VMEM] + [VMEM] * sub_count,
-        out_specs=[VMEM] * sub_count,
+        out_specs=[VMEM] * len(layout),
         scratch_shapes=[
             pltpu.VMEM((sub_count, rows, LANES), f32),
             pltpu.VMEM((sub_count * message_rows, LANES), f32),
             pltpu.VMEM((sub_count * rows, LANES), f32),
         ]
         + [pltpu.VMEM((1,) + shape, bf16) for shape in weight_shapes(column_total)],
-        out_shape=[pltpu.VMEM((message_rows, LANES), f32)] * sub_count,
+        out_shape=[
+            pltpu.VMEM((len(members) * message_rows, LANES), f32) for members in layout
+        ],
         compiler_params=params(16),
         cost_estimate=cost(10, 10),
     )(index, lon_length, leaving, *pinned(inside, *exits))
 
 
-def gather_kernel(index, *rest):
+def join_kernel(kept, came, *outs):
+    rows = kept.shape[0] // len(outs)
+    for at, out in enumerate(outs):
+        out[:rows, :] = kept[at * rows : (at + 1) * rows, :]
+        out[rows:, :] = came[at * rows : (at + 1) * rows, :]
+
+
+def join_pairs(kept, came, count):
+    rows = 2 * kept.shape[0] // count
+    return pl.pallas_call(
+        join_kernel,
+        in_specs=[VMEM] * 2,
+        out_specs=[VMEM] * count,
+        out_shape=[pltpu.VMEM((rows, LANES), f32)] * count,
+        compiler_params=params(4),
+        cost_estimate=cost(10, 10),
+    )(*pinned(kept, came))
+
+
+def gather_kernel(layout, index, *rest):
     *parts, out = rest
-    rows = parts[0].shape[0]
-    for k, part in enumerate(parts):
-        out[pl.ds(pl.multiple_of((index[0] ^ k) * rows, SUBLANES), rows), :] = part[...]
-
-
-def gather_messages(index, parts):
-    rows = parts[0].shape[0]
-    return pl.pallas_call(
-        gather_kernel,
+    rows = out.shape[0] // sum(len(members) for members in layout)
+    for part, members in zip(parts, layout):
+        for place, k in enumerate(members):
+            at = pl.multiple_of((index[0] ^ k) * rows, SUBLANES)
+            out[pl.ds(at, rows), :] = part[place * rows : (place + 1) * rows, :]
+
+
+def gather_messages(layout, index, parts):
+    return pl.pallas_call(
+        functools.partial(gather_kernel, layout),
         in_specs=[SMEM] + [VMEM] * len(parts),
         out_specs=VMEM,
-        out_shape=pltpu.VMEM((len(parts) * rows, LANES), f32),
+        out_shape=pltpu.VMEM((sum(part.shape[0] for part in parts), LANES), f32),
         compiler_params=params(4),
         cost_estimate=cost(10, 10),
     )(index, *pinned(*parts))
@@ -733,30 +769,28 @@
     )(index, *lengths)
 
 
-ADD_FLOPS = 10
-
-
-def add_kernel(variable, part, near, table, total):
-    weight = table[variable, 4:5, :]
-    for column in range(part.shape[1] // LANES):
-        at = slice(column * LANES, (column + 1) * LANES)
-        total[:, at] = part[:, at] + weight * near[:, at]
-
-
-def add_near(variable, part, near, table):
-    return pl.pallas_call(
-        functools.partial(add_kernel, variable),
+def add_kernel(variables, part, near, table, total):
+    for place, variable in enumerate(variables):
+        weight = table[variable, 4:5, :]
+        for column in range(part.shape[2] // LANES):
+            at = slice(column * LANES, (column + 1) * LANES)
+            total[place, :, at] = part[place, :, at] + weight * near[place, :, at]
+
+
+def add_near(variables, part, near, table):
+    return pl.pallas_call(
+        functools.partial(add_kernel, variables),
         in_specs=[VMEM] * 3,
         out_specs=VMEM,
         out_shape=pltpu.VMEM(part.shape, f32),
         compiler_params=params(4),
-        cost_estimate=cost(ADD_FLOPS, 10),
+        cost_estimate=cost(10, 10),
     )(*pinned(part, near, table))
 
 
-def last_kernel(variable, own, near, far, met, mix, table, *rest):
+def last_kernel(variable, place, own, near, far, met, mix, table, *rest):
     out, added, message, sems = rest[-4:]
-    row_count, column_total = near.shape
+    _, row_count, column_total = near.shape
     column_count = column_total // LANES
     stride = message.shape[0] // SUBLANES
     first = 0
@@ -790,9 +824,10 @@
         weights = [table[variable, 5 + level * 5 + k : 6 + level * 5 + k, :] for k in range(5)]
         for column in range(column_count):
             at = slice(column * LANES, (column + 1) * LANES)
-            value = total[:, at] + weights[0] * own[0, :, at] + weights[1] * own[1, :, at]
-            value = value + weights[2] * near[:, at] + weights[3] * far[:, at]
-            added[level, :, at] = value + weights[4] * met[:, at]
+            value = total[:, at] + weights[0] * own[place, 0, :, at]
+            value = value + weights[1] * own[place, 1, :, at]
+            value = value + weights[2] * near[place, :, at] + weights[3] * far[place, :, at]
+            added[level, :, at] = value + weights[4] * met[place, :, at]
         copy = pltpu.make_async_copy(added.at[level], out.at[level, variable], sems.at[level])
         copy.start()
         copies.append(copy)
@@ -800,8 +835,8 @@
         copy.wait()
 
 
-def last_step(variable, own, near, far, met, messages, mix, table, so_far):
-    _, row_count, column_total = own.shape
+def last_step(variable, place, own, near, far, met, messages, mix, table, so_far):
+    _, _, row_count, column_total = own.shape
     operands = pinned(own, near, far, met, mix, table, *messages)
     in_specs = [VMEM] * 10
     aliases = {}
@@ -810,7 +845,7 @@
         in_specs.append(HBM)
         aliases = {10: 0}
     return pl.pallas_call(
-        functools.partial(last_kernel, variable),
+        functools.partial(last_kernel, variable, place),
         in_specs=in_specs,
         out_specs=HBM,
         out_shape=pltpu.HBM((2, 4, row_count, column_total), f32),
@@ -825,6 +860,7 @@
     )(*operands)
 
 
+CHUNKS = ((0, 1), (2, 3))
 SWAP = [(0, 1), (1, 0), (2, 3), (3, 2)]
 CROSS = [(0, 2), (2, 0), (1, 3), (3, 1)]
 CORNER = [(0, 3), (3, 0), (1, 2), (2, 1)]
@@ -835,42 +871,63 @@
     return lax.optimization_barrier((value,) + earlier)[0]
 
 
-def four_bands(swept, weights, exits, chain, gather, table, mix):
+def four_bands(swept, weights, exits, units, chain, gather, table, mix):
     owns, parts, nears, mets = [], [], [], []
 
-    def filter_one(variable, *earlier):
-        own, sent, part = longitude_pair(variable, after(swept, *earlier), weights, table)
+    def filter_some(at, *earlier):
+        own, sent, part = longitude_pair(CHUNKS[at], after(swept, *earlier), weights, table)
         owns.append(own)
         parts.append(part)
         nears.append(lax.ppermute(sent, "band", SWAP))
         return part
 
-    def cross_one(variable, *earlier):
-        part = after(parts[variable], *earlier)
-        total = add_near(variable, part, nears[variable], table)
+    def cross_some(at, *earlier):
+        part = after(parts[at], *earlier)
+        total = add_near(CHUNKS[at], part, nears[at], table)
         mets.append(lax.ppermute(total, "band", MIDDLE))
         return total
 
-    exits = exchange(exits, "sub")
-    mark = filter_one(0)
-    mark = filter_one(1, mark)
-    mark = cross_one(0, mark)
-    mark = cross_one(1, mark)
-    chained = chain([after(exits[0], mark)] + exits[1:])
-    messages = exchange(chained, "sub")
-    mark = filter_one(2, chained[0])
-    mark = filter_one(3, mark)
-    mark = cross_one(2, mark, mets[0])
-    mark = cross_one(3, mark)
-    messages = gather(messages, mark)
+    last = len(CHUNKS) - 1
+    mark = filter_some(0)
+    mark = filter_some(1, mark)
+    mark = cross_some(0, mark)
+    exits = exchange([after(part, mark) for part in exits], "sub")
+    response = units(mark)
+    if last > 1:
+        mark = filter_some(2, mark)
+    mark = cross_some(1, mark, *response)
+    if last > 1:
+        mark = cross_some(2, mark)
+    kept, sent = chain(
+        [[0, 2, 4, 6], [1, 3, 5, 7]], [after(exits[0], mark)] + exits[1:], response
+    )
+    came = lax.ppermute(sent, "sub", [(at, at ^ 1) for at in range(8)])
+    pairs = join_pairs(kept, came, 4)
+    pairs = [pairs[0]] + [
+        lax.ppermute(pairs[k], "sub", [(at, at ^ (2 * k)) for at in range(8)]) for k in (1, 2, 3)
+    ]
+    messages = gather([[0, 1], [2, 3], [4, 5], [6, 7]], pairs)
+    mets = [after(met, messages) for met in mets]
     across = lax.ppermute(messages, "band", CROSS)
     beside = lax.ppermute(messages, "band", SWAP)
     corner = lax.ppermute(across, "band", SWAP)
     messages = (messages, across, beside, corner)
     fars = [lax.ppermute(met, "band", SWAP) for met in mets]
     result = None
-    for v in range(4):
-        result = last_step(v, owns[v], nears[v], fars[v], mets[v], messages, mix, table, result)
+    for at, variables in enumerate(CHUNKS):
+        for place, variable in enumerate(variables):
+            result = last_step(
+                variable,
+                place,
+                owns[at],
+                nears[at],
+                fars[at],
+                mets[at],
+                messages,
+                mix,
+                table,
+                result,
+            )
     return result
 
 
@@ -918,9 +975,11 @@
     )
 
 
-def any_bands(swept, weights, exits, chain, gather, vert_length):
+def any_bands(swept, weights, exits, units, chain, gather, vert_length):
     column_count, group_count, row_count, _ = swept.shape
-    messages = gather(exchange(chain(exchange(exits, "sub")), "sub"))
+    layout = [[k] for k in range(len(exits))]
+    chained = chain(layout, exchange(exits, "sub"), units())
+    messages = gather(layout, exchange(chained, "sub"))
     (values,) = longitude(swept, weights, group_count, 0, 1)
     messages = messages.reshape(group_count, -1, LANES)
     states = messages[:, : 4 * column_count].reshape(group_count, 4, -1)
@@ -939,14 +998,10 @@
     column_count = lon_count // LANES
     capacity = 2 * obs_owner.shape[0] // sub_count
     chunk_count = capacity // LANES
-    two_chips = lax.axis_size("band") == 4 and level_count == 2
+    two_chips = lax.axis_size("band") == 4 and level_count == 2 and sub_count == 8
     index = lax.axis_index("sub").astype(i32).reshape(1)
     band = lax.axis_index("band").astype(i32).reshape(1)
 
-    if two_chips:
-        vert_lengths = [vert_length] + [
-            lax.ppermute(vert_length, "band", pairs) for pairs in (CROSS, SWAP, CORNER)
-        ]
     packed = pack_observations(
         after(index, band),
         obs_columns, obs_owner[:, 0], obs_cell, sub_count, strip, capacity
@@ -956,6 +1011,10 @@
     weights = prepare(after(lon_length, packed[0]), lon_count, space)
     ready = list(weights)
     if two_chips:
+        vert_length = after(vert_length, *packed)
+        vert_lengths = [vert_length] + [
+            lax.ppermute(vert_length, "band", pairs) for pairs in (CROSS, SWAP, CORNER)
+        ]
         table, mix = tables(after(band, packed[0]), vert_lengths)
         ready.append(table)
 
@@ -968,18 +1027,20 @@
         sizes,
     )
 
-    def chain(arrived):
-        inside, leaving = unit_responses(
-            after(index, swept), lat_length, sub_count, row_count
-        )
-        return chain_states(index, lon_length, arrived, leaving, inside)
-
-    def gather(parts, *earlier):
-        return gather_messages(after(index, *earlier), parts)
+    def units(*earlier):
+        start = after(index, swept, *earlier)
+        return unit_responses(start, lat_length, sub_count, row_count)
+
+    def chain(layout, arrived, response):
+        inside, leaving = response
+        return chain_states(layout, index, lon_length, arrived, leaving, inside)
+
+    def gather(layout, parts, *earlier):
+        return gather_messages(layout, after(index, *earlier), parts)
 
     if two_chips:
-        return four_bands(swept, weights, exits, chain, gather, table, mix)
-    return any_bands(swept, weights, exits, chain, gather, vert_length)
+        return four_bands(swept, weights, exits, units, chain, gather, table, mix)
+    return any_bands(swept, weights, exits, units, chain, gather, vert_length)
 
 
 def solution(mesh):

time: 121 us -> 108 us (0.89)
  starting transfers between devices: 62.3 us -> 51 us
  Pallas kernels: 42.4 us -> 36.8 us
  waiting for transfers between devices: 12.9 us -> 17.8 us
    ppermute x8, waiting for transfers between devices: 0.02 us -> 7.86 us  [the longest x1 4.25 us: four_bands(): came = lax.ppermute(sent, 'sub', [(at, at ^ 1) for at in range(8)])]
    ppermute x21 -> x14, waiting for transfers between devices: 9.71 us -> 2.95 us  [exchange(): lax.ppermute(part, axis, [(at, at ^ k) for at in range(count)])]
    ppermute x8, starting transfers between devices: 17.9 us -> 12.2 us  [the longest x2 5.74 us: cross_some(): mets.append(lax.ppermute(total, 'band', MIDDLE))]
    ppermute x1, waiting for transfers between devices: 0.01 us -> 4.91 us  [four_bands(): across = lax.ppermute(messages, 'band', CROSS)]
    pallas_call x1, Pallas kernels: 19.5 us -> 14.8 us  [deposit_and_sweep(): pl.pallas_call(functools.partial(deposit_kernel, sizes), out_shape=[pltpu...]
    ppermute x1, starting transfers between devices: 0.07 us -> 4.33 us  [four_bands(): across = lax.ppermute(messages, 'band', CROSS)]
    ppermute x4 -> x2, starting transfers between devices: 5.73 us -> 1.58 us  [four_bands(): fars = [lax.ppermute(met, 'band', SWAP) for met in mets]]
    ppermute x21 -> x14, starting transfers between devices: 32 us -> 28.4 us  [exchange(): lax.ppermute(part, axis, [(at, at ^ k) for at in range(count)])]
  transfers between devices with their start and end apart: 39 -> 30, of which waited for: 10 -> 10; matrix products, arithmetic and copies ran while one was open for 0% -> 0% of each run, Pallas kernels for 13% -> 12%
where the time goes in v4:
time: 108 us; the launch traced here: 107 us
  starting transfers between devices  51 us (47%)
  Pallas kernels  36.8 us (34%)
  waiting for transfers between devices  17.8 us (16%)
  local copies, waits for them, and re-layouts  1.36 us (1%)
    ppermute x14, starting transfers between devices, exchange(): lax.ppermute(part, axis, [(at, at ^ k) for at in range(count)])  28.4 us
    pallas_call x1, Pallas kernels, deposit_and_sweep(): pl.pallas_call(functools.partial(deposit_kernel, sizes), out_shape=[pltpu...  14.8 us
    pallas_call x4, Pallas kernels, last_step(): pl.pallas_call(functools.partial(last_kernel, variable, place), in_specs=...  6.08 us
    ppermute x2, starting transfers between devices, cross_some(): mets.append(lax.ppermute(total, 'band', MIDDLE))  5.74 us
    pallas_call x2, Pallas kernels, longitude_pair(): pl.pallas_call(functools.partial(pair_kernel, variables), in_specs=[VMEM]...  4.97 us
    ppermute x1, waiting for transfers between devices, four_bands(): across = lax.ppermute(messages, 'band', CROSS)  4.91 us
    ppermute x1, starting transfers between devices, four_bands(): across = lax.ppermute(messages, 'band', CROSS)  4.33 us
    ppermute x1, waiting for transfers between devices, four_bands(): came = lax.ppermute(sent, 'sub', [(at, at ^ 1) for at in range(8)])  4.25 us
  transfers between devices with their start and end apart: 30, of which 10 were waited for; matrix products, arithmetic and copies ran while one was open for 0% of the time, Pallas kernels for 12%

profile of v4, /device:TPU:1, one launch (start us, length us, event | category | flops | bytes accessed | tf_op | source)
XLA Modules:
  0.0 107.4 jit_solution(15869661058774766032)
XLA Ops:
  0.0 4.2 %shard_map.73 = (f32[72,128]{1,0:T(8,128)S(1)}, f32[72,128]{1,0:T(8,128)S(1)}, f32[72,128]{1,0:T(8,128)S(1)}, f32[72,128]{1,0:T(8,128)S(1)}, f32[72,128]{1,0:T(8...) custom-call(s32[1]{0:T(128)} %bitcast.index, s32[32,128]{1,0:T(8,128)} %bitcast.6, ...), custom_call_target="tpu_custom_call" | custom-call | flops 10 | bytes 10 | tf_op jit(solution)/shard_map/pallas_call | solution.py:156
  4.2 2.1 %collective-permute-start.3 = (f32[72,128]{1,0:T(8,128)S(1)}, f32[72,128]{1,0:T(8,128)S(1)}, u32[]{:S(2)}, u32[]{:S(2)}) collective-permute-start(f32[72,128]{1,0:T(8,128)S(1)} %get-tuple-element.70), channel_id=1, source_target_pairs={{0,1},{1,0},{2,3},{3,2},{4,5},{5,4},{6,7},{7,6},{8,9},{9,8},{10,11... | collective-permute-start | bytes 110600 | tf_op jit(solution)/shard_map/ppermute | solution.py:40
  6.3 1.3 %collective-permute-start.4 = (f32[72,128]{1,0:T(8,128)S(1)}, f32[72,128]{1,0:T(8,128)S(1)}, u32[]{:S(2)}, u32[]{:S(2)}) collective-permute-start(f32[72,128]{1,0:T(8,128)S(1)} %get-tuple-element.71), channel_id=1, source_target_pairs={{0,2},{1,3},{2,0},{3,1},{4,6},{5,7},{6,4},{7,5},{8,10},{9,11},{10,... | collective-permute-start | bytes 110600 | tf_op jit(solution)/shard_map/ppermute | solution.py:40
  7.6 1.2 %collective-permute-start = (f32[2,4]{1,0:T(2,128)}, f32[2,4]{1,0:T(2,128)S(1)}, u32[]{:S(2)}, u32[]{:S(2)}) collective-permute-start(f32[2,4]{1,0:T(2,128)} %own), channel_id=1, source_target_pairs={{0,16},{16,0},{8,24},{24,8},{1,17},{17,1},{9,25},{25,9},{2,18},{18... | collective-permute-start | bytes 104 | tf_op jit(solution)/shard_map/ppermute | solution.py:1016
  8.8 1.5 %collective-permute-start.1 = (f32[2,4]{1,0:T(2,128)}, f32[2,4]{1,0:T(2,128)S(1)}, u32[]{:S(2)}, u32[]{:S(2)}) collective-permute-start(f32[2,4]{1,0:T(2,128)} %own), channel_id=1, source_target_pairs={{0,8},{8,0},{16,24},{24,16},{1,9},{9,1},{17,25},{25,17},{2,10},{10... | collective-permute-start | bytes 104 | tf_op jit(solution)/shard_map/ppermute | solution.py:1016
  10.5 0.9 collective-permute-done.1.beside_
  11.4 2.3 %collective-permute-start.6 = (f32[72,128]{1,0:T(8,128)S(1)}, f32[72,128]{1,0:T(8,128)S(1)}, u32[]{:S(2)}, u32[]{:S(2)}) collective-permute-start(f32[72,128]{1,0:T(8,128)S(1)} %get-tuple-element.73), channel_id=1, source_target_pairs={{0,4},{1,5},{2,6},{3,7},{4,0},{5,1},{6,2},{7,3},{8,12},{9,13},{10,... | collective-permute-start | bytes 110600 | tf_op jit(solution)/shard_map/ppermute | solution.py:40
  13.7 2.1 %collective-permute-start.7 = (f32[72,128]{1,0:T(8,128)S(1)}, f32[72,128]{1,0:T(8,128)S(1)}, u32[]{:S(2)}, u32[]{:S(2)}) collective-permute-start(f32[72,128]{1,0:T(8,128)S(1)} %get-tuple-element.74), channel_id=1, source_target_pairs={{0,5},{1,4},{2,7},{3,6},{4,1},{5,0},{6,3},{7,2},{8,13},{9,12},{10,... | collective-permute-start | bytes 110600 | tf_op jit(solution)/shard_map/ppermute | solution.py:40
  15.8 1.5 %collective-permute-start.8 = (f32[72,128]{1,0:T(8,128)S(1)}, f32[72,128]{1,0:T(8,128)S(1)}, u32[]{:S(2)}, u32[]{:S(2)}) collective-permute-start(f32[72,128]{1,0:T(8,128)S(1)} %get-tuple-element.75), channel_id=1, source_target_pairs={{0,6},{1,7},{2,4},{3,5},{4,2},{5,3},{6,0},{7,1},{8,14},{9,15},{10,... | collective-permute-start | bytes 110600 | tf_op jit(solution)/shard_map/ppermute | solution.py:40
  17.3 2.8 %collective-permute-start.9 = (f32[72,128]{1,0:T(8,128)S(1)}, f32[72,128]{1,0:T(8,128)S(1)}, u32[]{:S(2)}, u32[]{:S(2)}) collective-permute-start(f32[72,128]{1,0:T(8,128)S(1)} %get-tuple-element.76), channel_id=1, source_target_pairs={{0,7},{1,6},{2,5},{3,4},{4,3},{5,2},{6,1},{7,0},{8,15},{9,14},{10,... | collective-permute-start | bytes 110600 | tf_op jit(solution)/shard_map/ppermute | solution.py:40
  20.0 0.7 copy-done.1
  20.7 2.9 %shard_map.74 = (bf16[8,256,256]{2,1,0:T(8,128)(2,1)S(1)}, bf16[8,256,256]{2,1,0:T(8,128)(2,1)S(1)}, bf16[8,256,256]{2,1,0:T(8,128)(2,1)S(1)}, bf16[8,64,1536]{2,1,0:T(8,128)(2,1)S(1)}) custom-call(f32[2,4]{1,0:T(2,128)S(1)} %copy-done.1), custom_call_target="tpu_custom_call" | custom-call | flops 10 | bytes 10 | tf_op jit(solution)/shard_map/pallas_call | solution.py:442
  23.7 0.7 copy-done.3
  24.3 0.7 shard_map.75
  25.1 14.8 %shard_map.76 = (f32[12,8,96,128]{3,2,1,0:T(8,128)S(1)}, f32[48,128]{1,0:T(8,128)S(1)}, f32[48,128]{1,0:T(8,128)S(1)}, f32[48,128]{1,0:T(8,128)S(1)}, f32[48,128...) custom-call(s32[1]{0:T(128)} %bitcast.index, ...), custom_call_target="tpu_custom_call" | custom-call | flops 10 | bytes 10 | tf_op jit(solution)/shard_map/pallas_call | solution.py:313
  39.9 2.5 %shard_map.77 = (f32[2,2,96,1536]{3,2,1,0:T(8,128)S(1)}, f32[2,96,1536]{2,1,0:T(8,128)S(1)}, f32[2,96,1536]{2,1,0:T(8,128)S(1)}) custom-call(f32[12,8,96,128]{3,2,1,0:T(8,128)S(1)} %get-tuple-element.82.swept, bf16[8,256,256]{2,1,0:T(8,128)(2,1)S(1)} %get-tuple-element.65.near_high, bf16[8,256,256]{2,1,0:T(8,128)(2,1)S(1)} %get-tuple-element.66.near_low, ...), custom_call_target="tpu_custom_call" | custom-call | flops 10 | bytes 10 | tf_op jit(solution)/shard_map/pallas_call | solution.py:514
  42.4 2.1 %collective-permute-start.11 = (f32[2,96,1536]{2,1,0:T(8,128)S(1)}, f32[2,96,1536]{2,1,0:T(8,128)S(1)}, u32[]{:S(2)}, u32[]{:S(2)}) collective-permute-start(f32[2,96,1536]{2,1,0:T(8,128)S(1)} %get-tuple-element.87), channel_id=1, source_target_pairs={{0,8},{8,0},{16,24},{24,16},{1,9},{9,1},{17,25},{25,17},{2,10},{10... | collective-permute-start | bytes 3538952 | tf_op jit(solution)/shard_map/ppermute | solution.py:881
  44.5 2.5 %shard_map.78 = (f32[2,2,96,1536]{3,2,1,0:T(8,128)S(1)}, f32[2,96,1536]{2,1,0:T(8,128)S(1)}, f32[2,96,1536]{2,1,0:T(8,128)S(1)}) custom-call(f32[12,8,96,128]{3,2,1,0:T(8,128)S(1)} %get-tuple-element.82.swept, bf16[8,256,256]{2,1,0:T(8,128)(2,1)S(1)} %get-tuple-element.65.near_high, bf16[8,256,256]{2,1,0:T(8,128)(2,1)S(1)} %get-tuple-element.66.near_low, ...), custom_call_target="tpu_custom_call" | custom-call | flops 10 | bytes 10 | tf_op jit(solution)/shard_map/pallas_call | solution.py:514
  47.1 0.1 shard_map.79
  47.2 3.5 %collective-permute-start.28 = (f32[2,96,1536]{2,1,0:T(8,128)S(1)}, f32[2,96,1536]{2,1,0:T(8,128)S(1)}, u32[]{:S(2)}, u32[]{:S(2)}) collective-permute-start(f32[2,96,1536]{2,1,0:T(8,128)S(1)} %shard_map.79), channel_id=1, source_target_pairs={{0,0},{8,16},{16,8},{24,24},{1,1},{9,17},{17,9},{25,25},{2,2},{10,... | collective-permute-start | bytes 3538952 | tf_op jit(solution)/shard_map/ppermute | solution.py:887
  50.8 1.5 %shard_map.80 = (f32[128,128]{1,0:T(8,128)S(1)}, f32[4,128]{1,0:T(4,128)S(1)}) custom-call(s32[1]{0:T(128)} %bitcast.index, f32[2,4,768]{2,1,0:T(4,128)S(1)} %copy-done), custom_call_target="tpu_custom_call" | custom-call | flops 10 | bytes 10 | tf_op jit(solution)/shard_map/pallas_call | solution.py:369
  52.3 0.1 shard_map.81
  52.5 2.2 %collective-permute-start.12 = (f32[2,96,1536]{2,1,0:T(8,128)S(1)}, f32[2,96,1536]{2,1,0:T(8,128)S(1)}, u32[]{:S(2)}, u32[]{:S(2)}) collective-permute-start(f32[2,96,1536]{2,1,0:T(8,128)S(1)} %shard_map.81), channel_id=1, source_target_pairs={{0,0},{8,16},{16,8},{24,24},{1,1},{9,17},{17,9},{25,25},{2,2},{10,... | collective-permute-start | bytes 3538952 | tf_op jit(solution)/shard_map/ppermute | solution.py:887
  54.7 2.7 %collective-permute-start.19 = (f32[48,128]{1,0:T(8,128)S(1)}, f32[48,128]{1,0:T(8,128)S(1)}, u32[]{:S(2)}, u32[]{:S(2)}) collective-permute-start(f32[48,128]{1,0:T(8,128)S(1)} %get-tuple-element.108), channel_id=1, source_target_pairs={{0,7},{1,6},{2,5},{3,4},{4,3},{5,2},{6,1},{7,0},{8,15},{9,14},{10,... | collective-permute-start | bytes 73736 | tf_op jit(solution)/shard_map/ppermute | solution.py:40
  57.4 10.3 %collective-permute-start.17 = (f32[48,128]{1,0:T(8,128)S(1)}, f32[48,128]{1,0:T(8,128)S(1)}, u32[]{:S(2)}, u32[]{:S(2)}) collective-permute-start(f32[48,128]{1,0:T(8,128)S(1)} %get-tuple-element.104), channel_id=1, source_target_pairs={{0,5},{1,4},{2,7},{3,6},{4,1},{5,0},{6,3},{7,2},{8,13},{9,12},{10,... | collective-permute-start | bytes 73736 | tf_op jit(solution)/shard_map/ppermute | solution.py:40
  67.7 1.5 %collective-permute-start.16 = (f32[48,128]{1,0:T(8,128)S(1)}, f32[48,128]{1,0:T(8,128)S(1)}, u32[]{:S(2)}, u32[]{:S(2)}) collective-permute-start(f32[48,128]{1,0:T(8,128)S(1)} %get-tuple-element.102), channel_id=1, source_target_pairs={{0,4},{1,5},{2,6},{3,7},{4,0},{5,1},{6,2},{7,3},{8,12},{9,13},{10,... | collective-permute-start | bytes 73736 | tf_op jit(solution)/shard_map/ppermute | solution.py:40
  69.3 1.0 collective-permute-start.14
  70.4 0.9 collective-permute-done.16.rest_4_
  71.3 0.6 collective-permute-start.13
  71.9 1.0 collective-permute-done.15.rest_3_
  72.9 1.0 collective-permute-done.13.rest_1_
  73.9 1.3 %shard_map.82 = (f32[224,128]{1,0:T(8,128)S(1)}, f32[224,128]{1,0:T(8,128)S(1)}) custom-call(s32[1]{0:T(128)} %bitcast.index, f32[2,4]{1,0:T(2,128)S(1)} %copy-done.2, f32[4,128]{1,0:T(4,128)S(1)} %get-tuple-element.90.leaving, f32[128,128]{1,0:T(8,128)S(1)} %get-tuple-element.89.inside, f32[48,128]{1,0:T(8,128)S(1)} %get-tuple-element.94.rest_0_, ...), custom_call_target="tpu_custom_call" | custom-call | flops 10 | bytes 10 | tf_op jit(solution)/shard_map/pallas_call | solution.py:611
  75.3 0.7 collective-permute-start.20
  76.0 4.3 %collective-permute-done.20.came = f32[224,128]{1,0:T(8,128)S(1)} collective-permute-done((f32[224,128]{1,0:T(8,128)S(1)}, f32[224,128]{1,0:T(8,128)S(1)}, u32[]{:S(2)}, u32[]{:S(2)}) %collective-permute-start.20) | collective-permute-done | bytes 114720 | tf_op jit(solution)/shard_map/ppermute | solution.py:904
  80.3 1.9 %collective-permute-start.22 = (f32[112,128]{1,0:T(8,128)S(1)}, f32[112,128]{1,0:T(8,128)S(1)}, u32[]{:S(2)}, u32[]{:S(2)}) collective-permute-start(f32[112,128]{1,0:T(8,128)S(1)} %get-tuple-element.113), channel_id=1, source_target_pairs={{0,4},{1,5},{2,6},{3,7},{4,0},{5,1},{6,2},{7,3},{8,12},{9,13},{10,... | collective-permute-start | bytes 172040 | tf_op jit(solution)/shard_map/ppermute | solution.py:907
  82.2 1.7 %collective-permute-start.23 = (f32[112,128]{1,0:T(8,128)S(1)}, f32[112,128]{1,0:T(8,128)S(1)}, u32[]{:S(2)}, u32[]{:S(2)}) collective-permute-start(f32[112,128]{1,0:T(8,128)S(1)} %get-tuple-element.114), channel_id=1, source_target_pairs={{0,6},{1,7},{2,4},{3,5},{4,2},{5,3},{6,0},{7,1},{8,14},{9,15},{10,... | collective-permute-start | bytes 172040 | tf_op jit(solution)/shard_map/ppermute | solution.py:907
  83.9 0.5 collective-permute-done.22.rest_2_
  84.4 3.1 %collective-permute-done.23.rest_3_ = f32[112,128]{1,0:T(8,128)S(1)} collective-permute-done((f32[112,128]{1,0:T(8,128)S(1)}, f32[112,128]{1,0:T(8,128)S(1)}, u32[]{:S(2)}, u32[]{:S(2)}) %collective-permute-start.23) | collective-permute-done | bytes 57376 | tf_op jit(solution)/shard_map/ppermute | solution.py:907
  87.5 1.5 %collective-permute-start.29 = (f32[2,96,1536]{2,1,0:T(8,128)S(1)}, f32[2,96,1536]{2,1,0:T(8,128)S(1)}, u32[]{:S(2)}, u32[]{:S(2)}) collective-permute-start(f32[2,96,1536]{2,1,0:T(8,128)S(1)} %collective-permute-done.28.met), channel_id=1, source_target_pairs={{0,8},{8,0},{16,24},{24,16},{1,9},{9,1},{17,25},{25,17},{2,10},{10... | collective-permute-start | bytes 3538952 | tf_op jit(solution)/shard_map/ppermute | solution.py:915
  89.1 4.3 %collective-permute-start.25 = (f32[448,128]{1,0:T(8,128)S(1)}, f32[448,128]{1,0:T(8,128)S(1)}, u32[]{:S(2)}, u32[]{:S(2)}) collective-permute-start(f32[448,128]{1,0:T(8,128)S(1)} %shard_map.84.rest_0_), channel_id=1, source_target_pairs={{0,16},{16,0},{8,24},{24,8},{1,17},{17,1},{9,25},{25,9},{2,18},{18... | collective-permute-start | bytes 688136 | tf_op jit(solution)/shard_map/ppermute | solution.py:911
  93.4 0.7 collective-permute-start.26
  94.1 4.9 %collective-permute-done.25.rest_1_ = f32[448,128]{1,0:T(8,128)S(1)} collective-permute-done((f32[448,128]{1,0:T(8,128)S(1)}, f32[448,128]{1,0:T(8,128)S(1)}, u32[]{:S(2)}, u32[]{:S(2)}) %collective-permute-start.25) | collective-permute-done | bytes 229408 | tf_op jit(solution)/shard_map/ppermute | solution.py:911
  99.0 0.9 collective-permute-start.27
  100.0 1.1 %collective-permute-done.27.rest_3_ = f32[448,128]{1,0:T(8,128)S(1)} collective-permute-done((f32[448,128]{1,0:T(8,128)S(1)}, f32[448,128]{1,0:T(8,128)S(1)}, u32[]{:S(2)}, u32[]{:S(2)}) %collective-permute-start.27) | collective-permute-done | bytes 229408 | tf_op jit(solution)/shard_map/ppermute | solution.py:913
  101.1 1.6 %shard_map.85.rest_4_ = f32[2,4,96,1536]{3,2,1,0:T(8,128)} custom-call(f32[2,2,96,1536]{3,2,1,0:T(8,128)S(1)} %get-tuple-element.117.own, f32[2,96,1536]{2,1,0:T(8,128)S(1)} %collective-permute-done.11.near, f32[2,96,1536]{2,1,0:T(8,128)S(1)} %collective-permute-done.29.far, f32[2,96,1536]{2,1,0:T(8,128)S(1)} %collective-permute-done.28.met, ...), custom_call_target="tpu_custom_call" | custom-call | flops 10 | bytes 10 | tf_op jit(solution)/shard_map/pallas_call | solution.py:847
  102.7 1.6 %shard_map.86.rest_4_ = f32[2,4,96,1536]{3,2,1,0:T(8,128)} custom-call(f32[2,2,96,1536]{3,2,1,0:T(8,128)S(1)} %get-tuple-element.117.own, f32[2,96,1536]{2,1,0:T(8,128)S(1)} %collective-permute-done.11.near, f32[2,96,1536]{2,1,0:T(8,128)S(1)} %collective-permute-done.29.far, ...), custom_call_target="tpu_custom_call", output_to_operand_aliasing={{}: (10, {})} | custom-call | flops 10 | bytes 10 | tf_op jit(solution)/shard_map/pallas_call | solution.py:847
  104.3 1.5 %shard_map.87.rest_4_ = f32[2,4,96,1536]{3,2,1,0:T(8,128)} custom-call(f32[2,2,96,1536]{3,2,1,0:T(8,128)S(1)} %get-tuple-element.83.own, f32[2,96,1536]{2,1,0:T(8,128)S(1)} %collective-permute-done.10.near, f32[2,96,1536]{2,1,0:T(8,128)S(1)} %collective-permute-done.24.far, ...), custom_call_target="tpu_custom_call", output_to_operand_aliasing={{}: (10, {})} | custom-call | flops 10 | bytes 10 | tf_op jit(solution)/shard_map/pallas_call | solution.py:847
  105.7 1.5 %shard_map.88 = f32[2,4,96,1536]{3,2,1,0:T(8,128)} custom-call(f32[2,2,96,1536]{3,2,1,0:T(8,128)S(1)} %get-tuple-element.83.own, f32[2,96,1536]{2,1,0:T(8,128)S(1)} %collective-permute-done.10.near, f32[2,96,1536]{2,1,0:T(8,128)S(1)} %collective-permute-done.24.far, f32[2,96,1536]{2,1,0:T(8,128)S(1)} %collective-permute-done.12.met, ...), custom_call_target="tpu_custom_call", output_to_operand_aliasing={{}: (10, {})} | custom-call | flops 10 | bytes 10 | tf_op jit(solution)/shard_map/pallas_call | solution.py:847
  (36 shorter events, 0.7 us)
Async XLA Ops:
  4.2 11.6 %collective-permute-start.3 = (f32[72,128]{1,0:T(8,128)S(1)}, f32[72,128]{1,0:T(8,128)S(1)}, u32[]{:S(2)}, u32[]{:S(2)}) collective-permute-start(f32[72,128]{1,0:T(8,128)S(1)} %get-tuple-element.70), channel_id=1, source_target_pairs={{0,1},{1,0},{2,3},{3,2},{4,5},{5,4},{6,7},{7,6},{8,9},{9,8},{10,11... | collective-permute-start | bytes 110600 | tf_op jit(solution)/shard_map/ppermute | solution.py:40
  6.3 11.0 %collective-permute-start.4 = (f32[72,128]{1,0:T(8,128)S(1)}, f32[72,128]{1,0:T(8,128)S(1)}, u32[]{:S(2)}, u32[]{:S(2)}) collective-permute-start(f32[72,128]{1,0:T(8,128)S(1)} %get-tuple-element.71), channel_id=1, source_target_pairs={{0,2},{1,3},{2,0},{3,1},{4,6},{5,7},{6,4},{7,5},{8,10},{9,11},{10,... | collective-permute-start | bytes 110600 | tf_op jit(solution)/shard_map/ppermute | solution.py:40
  7.6 2.9 %collective-permute-start = (f32[2,4]{1,0:T(2,128)}, f32[2,4]{1,0:T(2,128)S(1)}, u32[]{:S(2)}, u32[]{:S(2)}) collective-permute-start(f32[2,4]{1,0:T(2,128)} %own), channel_id=1, source_target_pairs={{0,16},{16,0},{8,24},{24,8},{1,17},{17,1},{9,25},{25,9},{2,18},{18... | collective-permute-start | bytes 104 | tf_op jit(solution)/shard_map/ppermute | solution.py:1016
  8.8 2.5 %collective-permute-start.1 = (f32[2,4]{1,0:T(2,128)}, f32[2,4]{1,0:T(2,128)S(1)}, u32[]{:S(2)}, u32[]{:S(2)}) collective-permute-start(f32[2,4]{1,0:T(2,128)} %own), channel_id=1, source_target_pairs={{0,8},{8,0},{16,24},{24,16},{1,9},{9,1},{17,25},{25,17},{2,10},{10... | collective-permute-start | bytes 104 | tf_op jit(solution)/shard_map/ppermute | solution.py:1016
  10.3 3.3 %collective-permute-start.2 = (f32[2,4]{1,0:T(2,128)}, f32[2,4]{1,0:T(2,128)S(1)}, u32[]{:S(2)}, u32[]{:S(2)}) collective-permute-start(f32[2,4]{1,0:T(2,128)} %own), channel_id=1, source_target_pairs={{0,24},{24,0},{8,16},{16,8},{1,25},{25,1},{9,17},{17,9},{2,26},{26... | collective-permute-start | bytes 104 | tf_op jit(solution)/shard_map/ppermute | solution.py:1016
  10.5 14.5 %collective-permute-start.5 = (f32[72,128]{1,0:T(8,128)S(1)}, f32[72,128]{1,0:T(8,128)S(1)}, u32[]{:S(2)}, u32[]{:S(2)}) collective-permute-start(f32[72,128]{1,0:T(8,128)S(1)} %get-tuple-element.72), channel_id=1, source_target_pairs={{0,3},{1,2},{2,1},{3,0},{4,7},{5,6},{6,5},{7,4},{8,11},{9,10},{10,... | collective-permute-start | bytes 110600 | tf_op jit(solution)/shard_map/ppermute | solution.py:40
  11.4 13.7 %collective-permute-start.6 = (f32[72,128]{1,0:T(8,128)S(1)}, f32[72,128]{1,0:T(8,128)S(1)}, u32[]{:S(2)}, u32[]{:S(2)}) collective-permute-start(f32[72,128]{1,0:T(8,128)S(1)} %get-tuple-element.73), channel_id=1, source_target_pairs={{0,4},{1,5},{2,6},{3,7},{4,0},{5,1},{6,2},{7,3},{8,12},{9,13},{10,... | collective-permute-start | bytes 110600 | tf_op jit(solution)/shard_map/ppermute | solution.py:40
  13.7 11.4 %collective-permute-start.7 = (f32[72,128]{1,0:T(8,128)S(1)}, f32[72,128]{1,0:T(8,128)S(1)}, u32[]{:S(2)}, u32[]{:S(2)}) collective-permute-start(f32[72,128]{1,0:T(8,128)S(1)} %get-tuple-element.74), channel_id=1, source_target_pairs={{0,5},{1,4},{2,7},{3,6},{4,1},{5,0},{6,3},{7,2},{8,13},{9,12},{10,... | collective-permute-start | bytes 110600 | tf_op jit(solution)/shard_map/ppermute | solution.py:40
  15.8 9.3 %collective-permute-start.8 = (f32[72,128]{1,0:T(8,128)S(1)}, f32[72,128]{1,0:T(8,128)S(1)}, u32[]{:S(2)}, u32[]{:S(2)}) collective-permute-start(f32[72,128]{1,0:T(8,128)S(1)} %get-tuple-element.75), channel_id=1, source_target_pairs={{0,6},{1,7},{2,4},{3,5},{4,2},{5,3},{6,0},{7,1},{8,14},{9,15},{10,... | collective-permute-start | bytes 110600 | tf_op jit(solution)/shard_map/ppermute | solution.py:40
  17.3 7.8 %collective-permute-start.9 = (f32[72,128]{1,0:T(8,128)S(1)}, f32[72,128]{1,0:T(8,128)S(1)}, u32[]{:S(2)}, u32[]{:S(2)}) collective-permute-start(f32[72,128]{1,0:T(8,128)S(1)} %get-tuple-element.76), channel_id=1, source_target_pairs={{0,7},{1,6},{2,5},{3,4},{4,3},{5,2},{6,1},{7,0},{8,15},{9,14},{10,... | collective-permute-start | bytes 110600 | tf_op jit(solution)/shard_map/ppermute | solution.py:40
  20.0 0.7 copy-start.1
  23.6 0.7 copy-start.3
  42.4 4.7 %collective-permute-start.11 = (f32[2,96,1536]{2,1,0:T(8,128)S(1)}, f32[2,96,1536]{2,1,0:T(8,128)S(1)}, u32[]{:S(2)}, u32[]{:S(2)}) collective-permute-start(f32[2,96,1536]{2,1,0:T(8,128)S(1)} %get-tuple-element.87), channel_id=1, source_target_pairs={{0,8},{8,0},{16,24},{24,16},{1,9},{9,1},{17,25},{25,17},{2,10},{10... | collective-permute-start | bytes 3538952 | tf_op jit(solution)/shard_map/ppermute | solution.py:881
  47.0 5.3 %collective-permute-start.10 = (f32[2,96,1536]{2,1,0:T(8,128)S(1)}, f32[2,96,1536]{2,1,0:T(8,128)S(1)}, u32[]{:S(2)}, u32[]{:S(2)}) collective-permute-start(f32[2,96,1536]{2,1,0:T(8,128)S(1)} %get-tuple-element.84), channel_id=1, source_target_pairs={{0,8},{8,0},{16,24},{24,16},{1,9},{9,1},{17,25},{25,17},{2,10},{10... | collective-permute-start | bytes 3538952 | tf_op jit(solution)/shard_map/ppermute | solution.py:881
  47.1 3.7 %copy-start = (f32[2,4,768]{2,1,0:T(4,128)S(1)}, f32[2,4,768]{2,1,0:T(4,128)}, u32[]{:S(2)}) copy-start(f32[2,4,768]{2,1,0:T(4,128)} %lat_length.3) | copy-start | bytes 73732
  47.2 40.3 %collective-permute-start.28 = (f32[2,96,1536]{2,1,0:T(8,128)S(1)}, f32[2,96,1536]{2,1,0:T(8,128)S(1)}, u32[]{:S(2)}, u32[]{:S(2)}) collective-permute-start(f32[2,96,1536]{2,1,0:T(8,128)S(1)} %shard_map.79), channel_id=1, source_target_pairs={{0,0},{8,16},{16,8},{24,24},{1,1},{9,17},{17,9},{25,25},{2,2},{10,... | collective-permute-start | bytes 3538952 | tf_op jit(solution)/shard_map/ppermute | solution.py:887
  52.3 21.6 %copy-start.2 = (f32[2,4]{1,0:T(2,128)S(1)}, f32[2,4]{1,0:T(2,128)}, u32[]{:S(2)}) copy-start(f32[2,4]{1,0:T(2,128)} %lon_length.2) | copy-start | bytes 100
  52.5 36.5 %collective-permute-start.12 = (f32[2,96,1536]{2,1,0:T(8,128)S(1)}, f32[2,96,1536]{2,1,0:T(8,128)S(1)}, u32[]{:S(2)}, u32[]{:S(2)}) collective-permute-start(f32[2,96,1536]{2,1,0:T(8,128)S(1)} %shard_map.81), channel_id=1, source_target_pairs={{0,0},{8,16},{16,8},{24,24},{1,1},{9,17},{17,9},{25,25},{2,2},{10,... | collective-permute-start | bytes 3538952 | tf_op jit(solution)/shard_map/ppermute | solution.py:887
  54.7 13.0 %collective-permute-start.19 = (f32[48,128]{1,0:T(8,128)S(1)}, f32[48,128]{1,0:T(8,128)S(1)}, u32[]{:S(2)}, u32[]{:S(2)}) collective-permute-start(f32[48,128]{1,0:T(8,128)S(1)} %get-tuple-element.108), channel_id=1, source_target_pairs={{0,7},{1,6},{2,5},{3,4},{4,3},{5,2},{6,1},{7,0},{8,15},{9,14},{10,... | collective-permute-start | bytes 73736 | tf_op jit(solution)/shard_map/ppermute | solution.py:40
  57.4 11.9 %collective-permute-start.18 = (f32[48,128]{1,0:T(8,128)S(1)}, f32[48,128]{1,0:T(8,128)S(1)}, u32[]{:S(2)}, u32[]{:S(2)}) collective-permute-start(f32[48,128]{1,0:T(8,128)S(1)} %get-tuple-element.106), channel_id=1, source_target_pairs={{0,6},{1,7},{2,4},{3,5},{4,2},{5,3},{6,0},{7,1},{8,14},{9,15},{10,... | collective-permute-start | bytes 73736 | tf_op jit(solution)/shard_map/ppermute | solution.py:40
  57.4 11.9 %collective-permute-start.17 = (f32[48,128]{1,0:T(8,128)S(1)}, f32[48,128]{1,0:T(8,128)S(1)}, u32[]{:S(2)}, u32[]{:S(2)}) collective-permute-start(f32[48,128]{1,0:T(8,128)S(1)} %get-tuple-element.104), channel_id=1, source_target_pairs={{0,5},{1,4},{2,7},{3,6},{4,1},{5,0},{6,3},{7,2},{8,13},{9,12},{10,... | collective-permute-start | bytes 73736 | tf_op jit(solution)/shard_map/ppermute | solution.py:40
  67.7 3.6 %collective-permute-start.16 = (f32[48,128]{1,0:T(8,128)S(1)}, f32[48,128]{1,0:T(8,128)S(1)}, u32[]{:S(2)}, u32[]{:S(2)}) collective-permute-start(f32[48,128]{1,0:T(8,128)S(1)} %get-tuple-element.102), channel_id=1, source_target_pairs={{0,4},{1,5},{2,6},{3,7},{4,0},{5,1},{6,2},{7,3},{8,12},{9,13},{10,... | collective-permute-start | bytes 73736 | tf_op jit(solution)/shard_map/ppermute | solution.py:40
  69.2 3.7 %collective-permute-start.15 = (f32[48,128]{1,0:T(8,128)S(1)}, f32[48,128]{1,0:T(8,128)S(1)}, u32[]{:S(2)}, u32[]{:S(2)}) collective-permute-start(f32[48,128]{1,0:T(8,128)S(1)} %get-tuple-element.100), channel_id=1, source_target_pairs={{0,3},{1,2},{2,1},{3,0},{4,7},{5,6},{6,5},{7,4},{8,11},{9,10},{10,... | collective-permute-start | bytes 73736 | tf_op jit(solution)/shard_map/ppermute | solution.py:40
  69.3 3.6 %collective-permute-start.14 = (f32[48,128]{1,0:T(8,128)S(1)}, f32[48,128]{1,0:T(8,128)S(1)}, u32[]{:S(2)}, u32[]{:S(2)}) collective-permute-start(f32[48,128]{1,0:T(8,128)S(1)} %get-tuple-element.98), channel_id=1, source_target_pairs={{0,2},{1,3},{2,0},{3,1},{4,6},{5,7},{6,4},{7,5},{8,10},{9,11},{10,... | collective-permute-start | bytes 73736 | tf_op jit(solution)/shard_map/ppermute | solution.py:40
  71.3 2.7 %collective-permute-start.13 = (f32[48,128]{1,0:T(8,128)S(1)}, f32[48,128]{1,0:T(8,128)S(1)}, u32[]{:S(2)}, u32[]{:S(2)}) collective-permute-start(f32[48,128]{1,0:T(8,128)S(1)} %get-tuple-element.96), channel_id=1, source_target_pairs={{0,1},{1,0},{2,3},{3,2},{4,5},{5,4},{6,7},{7,6},{8,9},{9,8},{10,11... | collective-permute-start | bytes 73736 | tf_op jit(solution)/shard_map/ppermute | solution.py:40
  75.3 4.9 %collective-permute-start.20 = (f32[224,128]{1,0:T(8,128)S(1)}, f32[224,128]{1,0:T(8,128)S(1)}, u32[]{:S(2)}, u32[]{:S(2)}) collective-permute-start(f32[224,128]{1,0:T(8,128)S(1)} %get-tuple-element.110), channel_id=1, source_target_pairs={{0,1},{1,0},{2,3},{3,2},{4,5},{5,4},{6,7},{7,6},{8,9},{9,8},{10,11... | collective-permute-start | bytes 344072 | tf_op jit(solution)/shard_map/ppermute | solution.py:904
  80.3 3.6 %collective-permute-start.21 = (f32[112,128]{1,0:T(8,128)S(1)}, f32[112,128]{1,0:T(8,128)S(1)}, u32[]{:S(2)}, u32[]{:S(2)}) collective-permute-start(f32[112,128]{1,0:T(8,128)S(1)} %get-tuple-element.112), channel_id=1, source_target_pairs={{0,2},{1,3},{2,0},{3,1},{4,6},{5,7},{6,4},{7,5},{8,10},{9,11},{10,... | collective-permute-start | bytes 172040 | tf_op jit(solution)/shard_map/ppermute | solution.py:907
  80.3 4.0 %collective-permute-start.22 = (f32[112,128]{1,0:T(8,128)S(1)}, f32[112,128]{1,0:T(8,128)S(1)}, u32[]{:S(2)}, u32[]{:S(2)}) collective-permute-start(f32[112,128]{1,0:T(8,128)S(1)} %get-tuple-element.113), channel_id=1, source_target_pairs={{0,4},{1,5},{2,6},{3,7},{4,0},{5,1},{6,2},{7,3},{8,12},{9,13},{10,... | collective-permute-start | bytes 172040 | tf_op jit(solution)/shard_map/ppermute | solution.py:907
  82.2 5.3 %collective-permute-start.23 = (f32[112,128]{1,0:T(8,128)S(1)}, f32[112,128]{1,0:T(8,128)S(1)}, u32[]{:S(2)}, u32[]{:S(2)}) collective-permute-start(f32[112,128]{1,0:T(8,128)S(1)} %get-tuple-element.114), channel_id=1, source_target_pairs={{0,6},{1,7},{2,4},{3,5},{4,2},{5,3},{6,0},{7,1},{8,14},{9,15},{10,... | collective-permute-start | bytes 172040 | tf_op jit(solution)/shard_map/ppermute | solution.py:907
  87.5 13.6 %collective-permute-start.29 = (f32[2,96,1536]{2,1,0:T(8,128)S(1)}, f32[2,96,1536]{2,1,0:T(8,128)S(1)}, u32[]{:S(2)}, u32[]{:S(2)}) collective-permute-start(f32[2,96,1536]{2,1,0:T(8,128)S(1)} %collective-permute-done.28.met), channel_id=1, source_target_pairs={{0,8},{8,0},{16,24},{24,16},{1,9},{9,1},{17,25},{25,17},{2,10},{10... | collective-permute-start | bytes 3538952 | tf_op jit(solution)/shard_map/ppermute | solution.py:915
  89.0 15.3 %collective-permute-start.24 = (f32[2,96,1536]{2,1,0:T(8,128)S(1)}, f32[2,96,1536]{2,1,0:T(8,128)S(1)}, u32[]{:S(2)}, u32[]{:S(2)}) collective-permute-start(f32[2,96,1536]{2,1,0:T(8,128)S(1)} %collective-permute-done.12.met), channel_id=1, source_target_pairs={{0,8},{8,0},{16,24},{24,16},{1,9},{9,1},{17,25},{25,17},{2,10},{10... | collective-permute-start | bytes 3538952 | tf_op jit(solution)/shard_map/ppermute | solution.py:915
  89.1 9.9 %collective-permute-start.25 = (f32[448,128]{1,0:T(8,128)S(1)}, f32[448,128]{1,0:T(8,128)S(1)}, u32[]{:S(2)}, u32[]{:S(2)}) collective-permute-start(f32[448,128]{1,0:T(8,128)S(1)} %shard_map.84.rest_0_), channel_id=1, source_target_pairs={{0,16},{16,0},{8,24},{24,8},{1,17},{17,1},{9,25},{25,9},{2,18},{18... | collective-permute-start | bytes 688136 | tf_op jit(solution)/shard_map/ppermute | solution.py:911
  93.4 6.6 %collective-permute-start.26 = (f32[448,128]{1,0:T(8,128)S(1)}, f32[448,128]{1,0:T(8,128)S(1)}, u32[]{:S(2)}, u32[]{:S(2)}) collective-permute-start(f32[448,128]{1,0:T(8,128)S(1)} %shard_map.84.rest_0_), channel_id=1, source_target_pairs={{0,8},{8,0},{16,24},{24,16},{1,9},{9,1},{17,25},{25,17},{2,10},{10... | collective-permute-start | bytes 688136 | tf_op jit(solution)/shard_map/ppermute | solution.py:912
  99.0 2.1 %collective-permute-start.27 = (f32[448,128]{1,0:T(8,128)S(1)}, f32[448,128]{1,0:T(8,128)S(1)}, u32[]{:S(2)}, u32[]{:S(2)}) collective-permute-start(f32[448,128]{1,0:T(8,128)S(1)} %collective-permute-done.25.rest_1_), channel_id=1, source_target_pairs={{0,8},{8,0},{16,24},{24,16},{1,9},{9,1},{17,25},{25,17},{2,10},{10... | collective-permute-start | bytes 688136 | tf_op jit(solution)/shard_map/ppermute | solution.py:913

commit v5 on v4

--- a/solution.py
+++ b/solution.py
@@ -34,14 +34,53 @@
     return [pltpu.with_memory_space_constraint(array, pltpu.HBM) for array in arrays]
 
 
-def exchange(parts, axis):
-    count = len(parts)
-    moved = [
-        lax.ppermute(part, axis, [(at, at ^ k) for at in range(count)])
-        for k, part in enumerate(parts)
-        if k
-    ]
-    return list(parts[:1]) + moved
+EVEN_ODD = ((0, 2, 4, 6), (1, 3, 5, 7))
+BY_PAIRS = ((0, 1), (2, 3), (4, 5), (6, 7))
+
+
+def leaving_layout(sub_count):
+    return EVEN_ODD if sub_count == 8 else tuple((k,) for k in range(sub_count))
+
+
+def arriving_layout(sub_count):
+    return BY_PAIRS if sub_count == 8 else tuple((k,) for k in range(sub_count))
+
+
+def join_kernel(kept, came, *outs):
+    rows = kept.shape[0] // len(outs)
+    for at, out in enumerate(outs):
+        out[:rows, :] = kept[at * rows : (at + 1) * rows, :]
+        out[rows:, :] = came[at * rows : (at + 1) * rows, :]
+
+
+def join_pairs(kept, came, count):
+    rows = 2 * kept.shape[0] // count
+    return pl.pallas_call(
+        join_kernel,
+        in_specs=[VMEM] * 2,
+        out_specs=[VMEM] * count,
+        out_shape=[pltpu.VMEM((rows, LANES), f32)] * count,
+        compiler_params=params(4),
+        cost_estimate=cost(10, 10),
+    )(*pinned(kept, came))
+
+
+def after(value, *earlier):
+    return lax.optimization_barrier((value,) + earlier)[0]
+
+
+def exchange(parts, sub_count, meanwhile=None):
+    def move(part, k):
+        return lax.ppermute(part, "sub", [(at, at ^ k) for at in range(sub_count)])
+
+    if sub_count != 8:
+        return [parts[0]] + [move(parts[k], k) for k in range(1, sub_count)]
+    kept, sent = parts
+    came = move(sent, 1)
+    if meanwhile is not None:
+        kept = after(kept, *meanwhile(came))
+    pairs = join_pairs(kept, came, 4)
+    return [pairs[0]] + [move(pairs[k], 2 * k) for k in (1, 2, 3)]
 
 
 def cost(flops, read):
@@ -57,7 +96,7 @@
     return high, (x - high.astype(f32)).astype(bf16)
 
 
-def pack_kernel(sizes, index, owners, cells, values, *rest):
+def pack_kernel(sizes, layout, index, owners, cells, values, *rest):
     outs, (packed, places, tally, sorted_, joined, counts, sem) = rest[:-7], rest[-7:]
     sub_count, group_count, chunk_count, strip = sizes
     block_count = owners.shape[0]
@@ -142,8 +181,10 @@
             word = (cell - (cell & 127)) + ((cell - lane) & 127)
             word = jnp.where(filled, word, strip).astype(f32)
             packed[sub, word_row + chunk : word_row + chunk + 1, :] = word[:1]
-    for k, out in enumerate(outs):
-        out[...] = packed[index[0] ^ k]
+    rows = packed.shape[1]
+    for out, members in zip(outs, layout):
+        for at, k in enumerate(members):
+            out[at * rows : (at + 1) * rows, :] = packed[index[0] ^ k]
 
 
 def pack_observations(index, obs_values, owners, cells, sub_count, strip, capacity):
@@ -153,11 +194,12 @@
     block_count = obs_count // LANES
     rows = chunk_count * group_count + SUBLANES * (-(-chunk_count // SUBLANES))
     tiles = group_count // SUBLANES
-    return pl.pallas_call(
-        functools.partial(pack_kernel, (sub_count, group_count, chunk_count, strip)),
-        out_shape=[pltpu.VMEM((rows, LANES), f32)] * sub_count,
+    layout = leaving_layout(sub_count)
+    return pl.pallas_call(
+        functools.partial(pack_kernel, (sub_count, group_count, chunk_count, strip), layout),
+        out_shape=[pltpu.VMEM((len(members) * rows, LANES), f32) for members in layout],
         in_specs=[SMEM, VMEM, VMEM, VMEM],
-        out_specs=[VMEM] * sub_count,
+        out_specs=[VMEM] * len(layout),
         scratch_shapes=[
             pltpu.VMEM((sub_count, rows, LANES), f32),
             pltpu.VMEM((block_count, LANES), i32),
@@ -172,43 +214,106 @@
     )(index, *in_hbm(owners.reshape(block_count, LANES), cells.reshape(block_count, LANES), obs_values))
 
 
-def deposit_kernel(sizes, index, lat_length, field, *rest):
+def ready_kernel(sizes, index, lat_length, field, decay, *rest):
     sub_count, group_count, row_count, column_count, chunk_count, strip = sizes
-    arrived, swept, leaving = rest[:sub_count], rest[sub_count], rest[sub_count + 1 :][:sub_count]
-    got, exits, loaded, all_lengths, length_sem, *rest = rest[2 * sub_count + 1 :]
-    totals, (decay, integers, words, word_sem, sems) = rest[:CHAINS], rest[CHAINS:]
+    totals, (loaded, all_lengths, sem, sems) = rest[:CHAINS], rest[CHAINS:]
     tiles = group_count // SUBLANES
-    word_row = chunk_count * group_count
-    word_rows = got.shape[1] - word_row
-    span = row_count * column_count
 
     def load(group):
         return pltpu.make_async_copy(field.at[group], loaded.at[group], sems.at[group])
 
+    fetch = pltpu.make_async_copy(lat_length, all_lengths, sem)
+    fetch.start()
     for group in range(group_count):
         load(group).start()
-    fetch = pltpu.make_async_copy(lat_length, all_lengths, length_sem)
-    fetch.start()
-    for source in range(sub_count):
-        got[source] = arrived[source][...]
-        integers[source * word_rows : (source + 1) * word_rows, :] = arrived[source][
-            word_row:, :
-        ].astype(i32)
-    hand_over = pltpu.make_async_copy(integers, words, word_sem)
-    hand_over.start()
+
     def clear(row, carry):
-        for total in totals:
+        for total in totals[1:]:
             for tile in range(tiles):
                 for column in range(column_count):
                     total[tile, row, column] = jnp.zeros((SUBLANES, LANES), f32)
         return carry
 
     lax.fori_loop(0, row_count, clear, 0)
+    fetch.wait()
+    shift = index[0] * row_count
+    for tile in range(tiles):
+        lengths = jnp.concatenate(
+            [all_lengths[2 * tile + k] for k in range(SUBLANES // 4)], axis=0
+        )
+        lengths = pltpu.roll(lengths, jnp.where(shift > 0, lengths.shape[1] - shift, 0), 1)
+        keep = jnp.exp(-1.0 / lengths[:, :LANES])
+        for row in range(row_count):
+            decay[row, tile] = jnp.broadcast_to(keep[:, row : row + 1], (SUBLANES, LANES))
+    for group in range(group_count):
+        load(group).wait()
+    for tile in range(tiles):
+        groups = slice(tile * SUBLANES, (tile + 1) * SUBLANES)
+
+        def turn_rows(at, carry):
+            rows = pl.ds(pl.multiple_of(at * SUBLANES, SUBLANES), SUBLANES)
+            for column in range(column_count):
+                lanes = slice(column * LANES, (column + 1) * LANES)
+                totals[0][tile, rows, column] = jnp.swapaxes(loaded[groups, rows, lanes], 0, 1)
+            return carry
+
+        lax.fori_loop(0, row_count // SUBLANES, turn_rows, 0)
+
+
+def dump_shape(sizes):
+    _, group_count, row_count, column_count, _, _ = sizes
+    return (group_count // SUBLANES, row_count + 1, column_count, SUBLANES, LANES)
+
+
+def make_ready(index, lat_length, field, sizes):
+    sub_count, group_count, row_count, column_count, chunk_count, strip = sizes
+    tiles = group_count // SUBLANES
+    return pl.pallas_call(
+        functools.partial(ready_kernel, sizes),
+        in_specs=[SMEM, HBM, HBM],
+        out_specs=[VMEM] * (1 + CHAINS),
+        out_shape=[pltpu.VMEM((row_count, tiles, SUBLANES, LANES), f32)]
+        + [pltpu.VMEM(dump_shape(sizes), f32)] * CHAINS,
+        scratch_shapes=[
+            pltpu.VMEM((group_count, row_count, column_count * LANES), f32),
+            pltpu.VMEM(lat_length.shape, f32),
+            pltpu.SemaphoreType.DMA,
+            pltpu.SemaphoreType.DMA((group_count,)),
+        ],
+        compiler_params=params(6),
+        cost_estimate=cost(10, 10),
+    )(index, *in_hbm(lat_length, field))
+
+
+def deposit_kernel(sizes, index, decay, *rest):
+    sub_count, group_count, row_count, column_count, chunk_count, strip = sizes
+    here, away = arriving_layout(sub_count), leaving_layout(sub_count)
+    arrived, swept = rest[: len(here)], rest[len(here) + CHAINS]
+    rest = rest[len(here) + CHAINS + 1 :]
+    leaving, totals = rest[: len(away)], rest[len(away) :][:CHAINS]
+    got, exits, integers, words, word_sems = rest[len(away) + CHAINS :]
+    tiles = group_count // SUBLANES
+    word_row = chunk_count * group_count
+    block_rows = got.shape[1]
+    word_rows = block_rows - word_row
+    sources = [(part, at) for part, members in zip(arrived, here) for at in range(len(members))]
+    for source, (part, at) in enumerate(sources):
+        block = part[at * block_rows : (at + 1) * block_rows, :]
+        integers[source * word_rows : (source + 1) * word_rows, :] = block[word_row:].astype(i32)
+
+    def hand_over(source):
+        span = pl.ds(source * word_rows, word_rows)
+        return pltpu.make_async_copy(integers.at[span], words.at[span], word_sems.at[source])
+
+    for source in range(sub_count):
+        hand_over(source).start()
+    for source, (part, at) in enumerate(sources):
+        got[source] = part[at * block_rows : (at + 1) * block_rows, :]
     lane = lax.broadcasted_iota(i32, (SUBLANES, LANES), 1)
-    hand_over.wait()
 
     def one_source(source, carry):
         first = source * word_rows
+        hand_over(source).wait()
 
         def more(chunk):
             last = jnp.minimum(chunk, chunk_count - 1)
@@ -238,30 +343,14 @@
 
     flat = [total.reshape(tiles, -1, SUBLANES, LANES) for total in totals]
     lax.fori_loop(0, sub_count, one_source, 0)
-    fetch.wait()
-    here = index[0] * row_count
-    for tile in range(tiles):
-        lengths = jnp.concatenate(
-            [all_lengths[2 * tile + k] for k in range(SUBLANES // 4)], axis=0
-        )
-        lengths = pltpu.roll(lengths, jnp.where(here > 0, lengths.shape[1] - here, 0), 1)
-        keep = jnp.exp(-1.0 / lengths[:, :LANES])
-        for row in range(row_count):
-            decay[row, tile] = jnp.broadcast_to(keep[:, row : row + 1], (SUBLANES, LANES))
-
-    for group in range(group_count):
-        load(group).wait()
-
-
     for tile in range(tiles):
         groups = slice(tile * SUBLANES, (tile + 1) * SUBLANES)
 
         def add_rows(at, carry):
             rows = pl.ds(pl.multiple_of(at * SUBLANES, SUBLANES), SUBLANES)
             for column in range(column_count):
-                lanes = slice(column * LANES, (column + 1) * LANES)
-                value = jnp.swapaxes(loaded[groups, rows, lanes], 0, 1)
-                for total in totals:
+                value = totals[0][tile, rows, column]
+                for total in totals[1:]:
                     value = value + total[tile, rows, column]
                 totals[0][tile, rows, column] = value
             return carry
@@ -298,44 +387,39 @@
 
         lax.fori_loop(0, row_count // SUBLANES, turn_rows, 0)
     rows = 4 * column_count
-    for k, out in enumerate(leaving):
-        out[...] = exits[pl.ds(pl.multiple_of((index[0] ^ k) * rows, SUBLANES), rows), :]
-
-
-def deposit_and_sweep(index, lat_length, got, field, sizes):
+    for out, members in zip(leaving, away):
+        for at, k in enumerate(members):
+            first = pl.multiple_of((index[0] ^ k) * rows, SUBLANES)
+            out[at * rows : (at + 1) * rows, :] = exits[pl.ds(first, rows), :]
+
+
+def deposit_and_sweep(index, decay, totals, got, sizes):
     sub_count, group_count, row_count, column_count, chunk_count, strip = sizes
-    tiles = group_count // SUBLANES
-    rows = got[0].shape[0]
+    here, away = arriving_layout(sub_count), leaving_layout(sub_count)
+    rows = got[0].shape[0] // len(here[0])
     word_rows = rows - chunk_count * group_count
     exit_rows = 4 * column_count
-    plain = (group_count, row_count, column_count * LANES)
-    dump = (tiles, row_count + 1, column_count, SUBLANES, LANES)
-    return pl.pallas_call(
+    results = pl.pallas_call(
         functools.partial(deposit_kernel, sizes),
-        out_shape=[
-            pltpu.VMEM((column_count, group_count, row_count, LANES), f32),
-        ]
-        + [pltpu.VMEM((exit_rows, LANES), f32)] * sub_count,
-        in_specs=[SMEM, HBM, HBM] + [VMEM] * sub_count,
-        out_specs=[VMEM] * (sub_count + 1),
+        out_shape=[pltpu.VMEM((column_count, group_count, row_count, LANES), f32)]
+        + [pltpu.VMEM((len(members) * exit_rows, LANES), f32) for members in away]
+        + [pltpu.VMEM(dump_shape(sizes), f32)] * CHAINS,
+        in_specs=[SMEM] + [VMEM] * (1 + len(here) + CHAINS),
+        out_specs=[VMEM] * (1 + len(away) + CHAINS),
         scratch_shapes=[
             pltpu.VMEM((sub_count, rows, LANES), f32),
             pltpu.VMEM((group_count * exit_rows, LANES), f32),
-            pltpu.VMEM(plain, f32),
-            pltpu.VMEM(lat_length.shape, f32),
-            pltpu.SemaphoreType.DMA,
-        ]
-        + [pltpu.VMEM(dump, f32)] * CHAINS
-        + [
-            pltpu.VMEM((row_count, tiles, SUBLANES, LANES), f32),
             pltpu.VMEM((sub_count * word_rows, LANES), i32),
             pltpu.SMEM((sub_count * word_rows, LANES), i32),
-            pltpu.SemaphoreType.DMA,
-            pltpu.SemaphoreType.DMA((group_count,)),
+            pltpu.SemaphoreType.DMA((sub_count,)),
         ],
-        compiler_params=params(26),
-        cost_estimate=cost(10, 10),
-    )(index, *in_hbm(lat_length, field), *pinned(*got))
+        input_output_aliases={
+            2 + len(here) + k: 1 + len(away) + k for k in range(CHAINS)
+        },
+        compiler_params=params(6),
+        cost_estimate=cost(10, 10),
+    )(index, *pinned(decay, *got, *totals))
+    return results[: 1 + len(away)]
 
 
 def unit_kernel(sizes, index, lat_length, inside, leaving, decay, held):
@@ -553,11 +637,14 @@
     )(*operands)
 
 
-def chain_kernel(sub_count, layout, index, lon_length, leaving, inside, *rest):
-    arrived, outs = rest[:sub_count], rest[sub_count:][: len(layout)]
-    exits, out, held, *weights = rest[sub_count + len(layout) :]
-    for k, part in enumerate(arrived):
-        exits[index[0] ^ k] = part[...]
+def chain_kernel(sub_count, index, lon_length, leaving, inside, *rest):
+    here, away = arriving_layout(sub_count), leaving_layout(sub_count)
+    arrived, outs = rest[: len(here)], rest[len(here) :][: len(away)]
+    exits, out, held, *weights = rest[len(here) + len(away) :]
+    rows = exits.shape[1]
+    for part, members in zip(arrived, here):
+        for at, k in enumerate(members):
+            exits[index[0] ^ k] = part[at * rows : (at + 1) * rows, :]
     column_count = exits.shape[1] // 4
     shape = (column_count, LANES)
     group = index[0]
@@ -596,22 +683,22 @@
         out[at + 4 : (block + 1) * message_rows, :] = jnp.zeros(
             (message_rows - 4 * column_count - 4, LANES), f32
         )
-    for target, members in zip(outs, layout):
+    for target, members in zip(outs, away):
         for place, k in enumerate(members):
             at = pl.multiple_of((index[0] ^ k) * message_rows, SUBLANES)
             to = place * message_rows
             target[to : to + message_rows, :] = out[pl.ds(at, message_rows), :]
 
 
-def chain_states(layout, index, lon_length, exits, leaving, inside):
-    sub_count = len(exits)
-    rows = exits[0].shape[0]
+def chain_states(sub_count, index, lon_length, exits, leaving, inside):
+    here, away = arriving_layout(sub_count), leaving_layout(sub_count)
+    rows = exits[0].shape[0] // len(here[0])
     column_total = rows // 4 * LANES
     message_rows = rows + 8
     return pl.pallas_call(
-        functools.partial(chain_kernel, sub_count, layout),
-        in_specs=[SMEM, SMEM, SMEM, VMEM] + [VMEM] * sub_count,
-        out_specs=[VMEM] * len(layout),
+        functools.partial(chain_kernel, sub_count),
+        in_specs=[SMEM, SMEM, SMEM, VMEM] + [VMEM] * len(here),
+        out_specs=[VMEM] * len(away),
         scratch_shapes=[
             pltpu.VMEM((sub_count, rows, LANES), f32),
             pltpu.VMEM((sub_count * message_rows, LANES), f32),
@@ -619,30 +706,11 @@
         ]
         + [pltpu.VMEM((1,) + shape, bf16) for shape in weight_shapes(column_total)],
         out_shape=[
-            pltpu.VMEM((len(members) * message_rows, LANES), f32) for members in layout
+            pltpu.VMEM((len(members) * message_rows, LANES), f32) for members in away
         ],
         compiler_params=params(16),
         cost_estimate=cost(10, 10),
     )(index, lon_length, leaving, *pinned(inside, *exits))
-
-
-def join_kernel(kept, came, *outs):
-    rows = kept.shape[0] // len(outs)
-    for at, out in enumerate(outs):
-        out[:rows, :] = kept[at * rows : (at + 1) * rows, :]
-        out[rows:, :] = came[at * rows : (at + 1) * rows, :]
-
-
-def join_pairs(kept, came, count):
-    rows = 2 * kept.shape[0] // count
-    return pl.pallas_call(
-        join_kernel,
-        in_specs=[VMEM] * 2,
-        out_specs=[VMEM] * count,
-        out_shape=[pltpu.VMEM((rows, LANES), f32)] * count,
-        compiler_params=params(4),
-        cost_estimate=cost(10, 10),
-    )(*pinned(kept, came))
 
 
 def gather_kernel(layout, index, *rest):
@@ -788,76 +856,91 @@
     )(*pinned(part, near, table))
 
 
-def last_kernel(variable, place, own, near, far, met, mix, table, *rest):
-    out, added, message, sems = rest[-4:]
-    _, row_count, column_total = near.shape
+def dense_kernel(variables, own, near, far, met, table, out):
+    for place, variable in enumerate(variables):
+        for level in range(2):
+            weights = [table[variable, 5 + level * 5 + k : 6 + level * 5 + k, :] for k in range(5)]
+            for column in range(near.shape[2] // LANES):
+                at = slice(column * LANES, (column + 1) * LANES)
+                value = weights[0] * own[place, 0, :, at] + weights[1] * own[place, 1, :, at]
+                value = value + weights[2] * near[place, :, at] + weights[3] * far[place, :, at]
+                out[place, level, :, at] = value + weights[4] * met[place, :, at]
+
+
+def dense_part(variables, own, near, far, met, table):
+    return pl.pallas_call(
+        functools.partial(dense_kernel, variables),
+        in_specs=[VMEM] * 5,
+        out_specs=VMEM,
+        out_shape=pltpu.VMEM(own.shape, f32),
+        compiler_params=params(4),
+        cost_estimate=cost(10, 10),
+    )(*pinned(own, near, far, met, table))
+
+
+def finish_kernel(mix, *rest):
+    *dense, out, added, message, sems = rest
+    messages, dense = dense[:4], dense[4:]
+    _, _, row_count, column_total = dense[0].shape
     column_count = column_total // LANES
     stride = message.shape[0] // SUBLANES
-    first = 0
-    for at, part in enumerate(rest[:4]):
-        for level in range(2):
-            source = (level * 4 + variable) * stride
-            target = (2 * at + level) * stride
-            message[target : target + stride, :] = part[source : source + stride, :]
-    lanes = []
-    for column in range(column_count):
-        lanes.append(
-            jnp.concatenate(
-                [
-                    message[pl.ds(first + k * column_count + column, SUBLANES, stride=stride), :]
-                    for k in range(4)
-                ],
-                axis=0,
-            )
-        )
-    high, low = split(jnp.concatenate(lanes, axis=1))
-    states = jnp.concatenate([high, high, low, low], axis=0)
-    inside = [
-        message[pl.ds(first + 4 * column_count + k, SUBLANES, stride=stride), :] for k in range(4)
-    ]
     copies = []
-    for level in range(2):
-        mixed = jnp.concatenate([part * mix[level, variable] for part in inside], axis=0)
-        high, low = split(mixed)
-        mixed = jnp.concatenate([high, low, high, low], axis=0)
-        total = dot(mixed, states, (((0,), (0,)), ((), ())))[:row_count]
-        weights = [table[variable, 5 + level * 5 + k : 6 + level * 5 + k, :] for k in range(5)]
-        for column in range(column_count):
-            at = slice(column * LANES, (column + 1) * LANES)
-            value = total[:, at] + weights[0] * own[place, 0, :, at]
-            value = value + weights[1] * own[place, 1, :, at]
-            value = value + weights[2] * near[place, :, at] + weights[3] * far[place, :, at]
-            added[level, :, at] = value + weights[4] * met[place, :, at]
-        copy = pltpu.make_async_copy(added.at[level], out.at[level, variable], sems.at[level])
-        copy.start()
-        copies.append(copy)
+    for chunk, variables in enumerate(CHUNKS):
+        for place, variable in enumerate(variables):
+            for at, part in enumerate(messages):
+                for level in range(2):
+                    source = (level * 4 + variable) * stride
+                    target = (2 * at + level) * stride
+                    message[target : target + stride, :] = part[source : source + stride, :]
+            lanes = []
+            for column in range(column_count):
+                lanes.append(
+                    jnp.concatenate(
+                        [
+                            message[pl.ds(k * column_count + column, SUBLANES, stride=stride), :]
+                            for k in range(4)
+                        ],
+                        axis=0,
+                    )
+                )
+            high, low = split(jnp.concatenate(lanes, axis=1))
+            states = jnp.concatenate([high, high, low, low], axis=0)
+            inside = [
+                message[pl.ds(4 * column_count + k, SUBLANES, stride=stride), :] for k in range(4)
+            ]
+            for level in range(2):
+                mixed = jnp.concatenate([part * mix[level, variable] for part in inside], axis=0)
+                high, low = split(mixed)
+                mixed = jnp.concatenate([high, low, high, low], axis=0)
+                total = dot(mixed, states, (((0,), (0,)), ((), ())))[:row_count]
+                added[variable, level] = total + dense[chunk][place, level]
+                copies.append(
+                    pltpu.make_async_copy(
+                        added.at[variable, level],
+                        out.at[level, variable],
+                        sems.at[2 * variable + level],
+                    )
+                )
+                copies[-1].start()
     for copy in copies:
         copy.wait()
 
 
-def last_step(variable, place, own, near, far, met, messages, mix, table, so_far):
-    _, _, row_count, column_total = own.shape
-    operands = pinned(own, near, far, met, mix, table, *messages)
-    in_specs = [VMEM] * 10
-    aliases = {}
-    if so_far is not None:
-        operands.append(so_far)
-        in_specs.append(HBM)
-        aliases = {10: 0}
-    return pl.pallas_call(
-        functools.partial(last_kernel, variable, place),
-        in_specs=in_specs,
+def finish(mix, messages, dense):
+    _, _, row_count, column_total = dense[0].shape
+    return pl.pallas_call(
+        finish_kernel,
+        in_specs=[VMEM] * (1 + len(messages) + len(dense)),
         out_specs=HBM,
         out_shape=pltpu.HBM((2, 4, row_count, column_total), f32),
         scratch_shapes=[
-            pltpu.VMEM((2, row_count, column_total), f32),
+            pltpu.VMEM((4, 2, row_count, column_total), f32),
             pltpu.VMEM(messages[0].shape, f32),
-            pltpu.SemaphoreType.DMA((2,)),
+            pltpu.SemaphoreType.DMA((8,)),
         ],
-        input_output_aliases=aliases,
-        compiler_params=params(10),
-        cost_estimate=cost(10, 10),
-    )(*operands)
+        compiler_params=params(12),
+        cost_estimate=cost(10, 10),
+    )(*pinned(mix, *messages, *dense))
 
 
 CHUNKS = ((0, 1), (2, 3))
@@ -865,10 +948,6 @@
 CROSS = [(0, 2), (2, 0), (1, 3), (3, 1)]
 CORNER = [(0, 3), (3, 0), (1, 2), (2, 1)]
 MIDDLE = [(0, 0), (1, 2), (2, 1), (3, 3)]
-
-
-def after(value, *earlier):
-    return lax.optimization_barrier((value,) + earlier)[0]
 
 
 def four_bands(swept, weights, exits, units, chain, gather, table, mix):
@@ -887,48 +966,25 @@
         mets.append(lax.ppermute(total, "band", MIDDLE))
         return total
 
-    last = len(CHUNKS) - 1
-    mark = filter_some(0)
-    mark = filter_some(1, mark)
-    mark = cross_some(0, mark)
-    exits = exchange([after(part, mark) for part in exits], "sub")
-    response = units(mark)
-    if last > 1:
-        mark = filter_some(2, mark)
-    mark = cross_some(1, mark, *response)
-    if last > 1:
-        mark = cross_some(2, mark)
-    kept, sent = chain(
-        [[0, 2, 4, 6], [1, 3, 5, 7]], [after(exits[0], mark)] + exits[1:], response
-    )
-    came = lax.ppermute(sent, "sub", [(at, at ^ 1) for at in range(8)])
-    pairs = join_pairs(kept, came, 4)
-    pairs = [pairs[0]] + [
-        lax.ppermute(pairs[k], "sub", [(at, at ^ (2 * k)) for at in range(8)]) for k in (1, 2, 3)
-    ]
-    messages = gather([[0, 1], [2, 3], [4, 5], [6, 7]], pairs)
-    mets = [after(met, messages) for met in mets]
+    first = filter_some(0)
+    response = units(first)
+
+    def before_second_stage(came):
+        return (cross_some(0, filter_some(1, came, *response)),)
+
+    exits = exchange(exits, 8, before_second_stage)
+    mark = cross_some(1, exits[0])
+    messages = exchange(chain([after(exits[0], mark)] + exits[1:], response), 8)
+    messages = gather(messages)
     across = lax.ppermute(messages, "band", CROSS)
     beside = lax.ppermute(messages, "band", SWAP)
-    corner = lax.ppermute(across, "band", SWAP)
-    messages = (messages, across, beside, corner)
-    fars = [lax.ppermute(met, "band", SWAP) for met in mets]
-    result = None
+    dense = []
     for at, variables in enumerate(CHUNKS):
-        for place, variable in enumerate(variables):
-            result = last_step(
-                variable,
-                place,
-                owns[at],
-                nears[at],
-                fars[at],
-                mets[at],
-                messages,
-                mix,
-                table,
-                result,
-            )
-    return result
+        met = after(mets[at], messages)
+        far = lax.ppermute(met, "band", SWAP)
+        dense.append(dense_part(variables, owns[at], nears[at], far, met, table))
+    corner = lax.ppermute(after(across, *dense), "band", SWAP)
+    return finish(mix, (messages, across, beside, corner), dense)
 
 
 def prefix(part, axis, combine, identity, reverse):
@@ -977,9 +1033,9 @@
 
 def any_bands(swept, weights, exits, units, chain, gather, vert_length):
     column_count, group_count, row_count, _ = swept.shape
-    layout = [[k] for k in range(len(exits))]
-    chained = chain(layout, exchange(exits, "sub"), units())
-    messages = gather(layout, exchange(chained, "sub"))
+    sub_count = lax.axis_size("sub")
+    chained = chain(exchange(exits, sub_count), units())
+    messages = gather(exchange(chained, sub_count))
     (values,) = longitude(swept, weights, group_count, 0, 1)
     messages = messages.reshape(group_count, -1, LANES)
     states = messages[:, : 4 * column_count].reshape(group_count, 4, -1)
@@ -1006,37 +1062,41 @@
         after(index, band),
         obs_columns, obs_owner[:, 0], obs_cell, sub_count, strip, capacity
     )
-    got = exchange(packed, "sub")
-    space = pltpu.VMEM if two_chips else pltpu.HBM
-    weights = prepare(after(lon_length, packed[0]), lon_count, space)
-    ready = list(weights)
+    vert_lengths = []
     if two_chips:
         vert_length = after(vert_length, *packed)
         vert_lengths = [vert_length] + [
             lax.ppermute(vert_length, "band", pairs) for pairs in (CROSS, SWAP, CORNER)
         ]
-        table, mix = tables(after(band, packed[0]), vert_lengths)
+    space = pltpu.VMEM if two_chips else pltpu.HBM
+    weights = prepare(after(lon_length, *packed), lon_count, space)
+    got = exchange(packed, sub_count, lambda came: (*vert_lengths, weights[0]))
+    ready = list(weights)
+    if two_chips:
+        table, mix = tables(after(band, got[0]), vert_lengths)
         ready.append(table)
 
     sizes = (sub_count, group_count, row_count, column_count, chunk_count, strip)
-    swept, *exits = deposit_and_sweep(
-        index,
+    decay, *totals = make_ready(
+        after(index, got[0]),
         lat_length,
-        [after(got[0], *ready)] + got[1:],
         background.reshape(group_count, row_count, lon_count),
         sizes,
     )
+    swept, *exits = deposit_and_sweep(
+        index, decay, totals, [after(got[0], *ready)] + got[1:], sizes
+    )
 
     def units(*earlier):
         start = after(index, swept, *earlier)
         return unit_responses(start, lat_length, sub_count, row_count)
 
-    def chain(layout, arrived, response):
+    def chain(arrived, response):
         inside, leaving = response
-        return chain_states(layout, index, lon_length, arrived, leaving, inside)
-
-    def gather(layout, parts, *earlier):
-        return gather_messages(layout, after(index, *earlier), parts)
+        return chain_states(sub_count, index, lon_length, arrived, leaving, inside)
+
+    def gather(parts):
+        return gather_messages(arriving_layout(sub_count), index, parts)
 
     if two_chips:
         return four_bands(swept, weights, exits, units, chain, gather, table, mix)

time: 108 us -> 97.6 us (0.904)
  starting transfers between devices: 51 us -> 44.1 us
  waiting for transfers between devices: 17.8 us -> 15.6 us
    ppermute x21 -> x15, starting transfers between devices: 35.2 us -> 30.8 us  [the longest x12 27 us: move(): return lax.ppermute(part, 'sub', [(at, at ^ k) for at in range(sub_count)])]
    ppermute x1, starting transfers between devices: 4.33 us -> 1.72 us  [four_bands(): across = lax.ppermute(messages, 'band', CROSS)]
    pallas_call x1, Pallas kernels: 14.8 us -> 12.2 us  [deposit_and_sweep(): pl.pallas_call(functools.partial(deposit_kernel, sizes), out_shape=[pltpu...]
    ppermute x1, waiting for transfers between devices: 4.91 us -> 2.61 us  [four_bands(): across = lax.ppermute(messages, 'band', CROSS)]
    pallas_call x5, Pallas kernels: 7.43 us -> 9.27 us  [the longest x1 3.33 us: make_ready(): pl.pallas_call(functools.partial(ready_kernel, sizes), in_specs=[SMEM, HB...]
    ppermute x21 -> x15, waiting for transfers between devices: 11.9 us -> 12.4 us  [the longest x12 10.8 us: move(): return lax.ppermute(part, 'sub', [(at, at ^ k) for at in range(sub_count)])]
  transfers between devices with their start and end apart: 30 -> 24, of which waited for: 10 -> 10; matrix products, arithmetic and copies ran while one was open for 0% -> 0% of each run, Pallas kernels for 12% -> 18%
where the time goes in v5:
time: 97.6 us; the launch traced here: 96.9 us
  starting transfers between devices  44.1 us (45%)
  Pallas kernels  36.1 us (37%)
  waiting for transfers between devices  15.6 us (16%)
    ppermute x12, starting transfers between devices, move(): return lax.ppermute(part, 'sub', [(at, at ^ k) for at in range(sub_count)])  27 us
    pallas_call x1, Pallas kernels, deposit_and_sweep(): pl.pallas_call(functools.partial(deposit_kernel, sizes), out_shape=[pltpu...  12.2 us
    ppermute x12, waiting for transfers between devices, move(): return lax.ppermute(part, 'sub', [(at, at ^ k) for at in range(sub_count)])  10.8 us
    ppermute x2, starting transfers between devices, cross_some(): mets.append(lax.ppermute(total, 'band', MIDDLE))  5.98 us
    pallas_call x2, Pallas kernels, longitude_pair(): pl.pallas_call(functools.partial(pair_kernel, variables), in_specs=[VMEM]...  4.98 us
    pallas_call x1, Pallas kernels, pack_observations(): pl.pallas_call(functools.partial(pack_kernel, (sub_count, group_count, ch...  4.15 us
    pallas_call x1, Pallas kernels, make_ready(): pl.pallas_call(functools.partial(ready_kernel, sizes), in_specs=[SMEM, HB...  3.33 us
    ppermute x2, starting transfers between devices, filter_some(): nears.append(lax.ppermute(sent, 'band', SWAP))  3.03 us
  transfers between devices with their start and end apart: 24, of which 10 were waited for; matrix products, arithmetic and copies ran while one was open for 0% of the time, Pallas kernels for 18%

profile of v5, /device:TPU:1, one launch (start us, length us, event | category | flops | bytes accessed | tf_op | source)
XLA Modules:
  0.0 96.9 jit_solution(6760223934265226092)
XLA Ops:
  0.0 4.2 %shard_map.73 = (f32[288,128]{1,0:T(8,128)S(1)}, f32[288,128]{1,0:T(8,128)S(1)}) custom-call(s32[1]{0:T(128)} %bitcast.1.index, s32[32,128]{1,0:T(8,128)} %bitcast.6, s32[32,128]{1,0:T(8,128)} %bitcast.7, f32[2,4,4096]{2,1,0:T(4,128)} %values.1), custom_call_target="tpu_custom_call" | custom-call | flops 10 | bytes 10 | tf_op jit(solution)/shard_map/pallas_call | solution.py:198
  4.2 2.1 %collective-permute-start.3 = (f32[288,128]{1,0:T(8,128)S(1)}, f32[288,128]{1,0:T(8,128)S(1)}, u32[]{:S(2)}, u32[]{:S(2)}) collective-permute-start(f32[288,128]{1,0:T(8,128)S(1)} %get-tuple-element.61), channel_id=1, source_target_pairs={{0,1},{1,0},{2,3},{3,2},{4,5},{5,4},{6,7},{7,6},{8,9},{9,8},{10,11... | collective-permute-start | bytes 442376 | tf_op jit(solution)/shard_map/ppermute | solution.py:74
  6.3 2.1 %collective-permute-start.2 = (f32[2,4]{1,0:T(2,128)}, f32[2,4]{1,0:T(2,128)S(1)}, u32[]{:S(2)}, u32[]{:S(2)}) collective-permute-start(f32[2,4]{1,0:T(2,128)} %own), channel_id=1, source_target_pairs={{0,24},{24,0},{8,16},{16,8},{1,25},{25,1},{9,17},{17,9},{2,26},{26... | collective-permute-start | bytes 104 | tf_op jit(solution)/shard_map/ppermute | solution.py:1069
  8.3 0.0 collective-permute-start.1
  8.3 0.2 collective-permute-start
  8.6 0.7 copy-done.1
  9.3 2.9 %shard_map.74 = (bf16[8,256,256]{2,1,0:T(8,128)(2,1)S(1)}, bf16[8,256,256]{2,1,0:T(8,128)(2,1)S(1)}, bf16[8,256,256]{2,1,0:T(8,128)(2,1)S(1)}, bf16[8,64,1536]{2,1,0:T(8,128)(2,1)S(1)}) custom-call(f32[2,4]{1,0:T(2,128)S(1)} %copy-done.1), custom_call_target="tpu_custom_call" | custom-call | flops 10 | bytes 10 | tf_op jit(solution)/shard_map/pallas_call | solution.py:526
  12.3 1.4 %collective-permute-start.4 = (f32[144,128]{1,0:T(8,128)S(1)}, f32[144,128]{1,0:T(8,128)S(1)}, u32[]{:S(2)}, u32[]{:S(2)}) collective-permute-start(f32[144,128]{1,0:T(8,128)S(1)} %get-tuple-element.76), channel_id=1, source_target_pairs={{0,2},{1,3},{2,0},{3,1},{4,6},{5,7},{6,4},{7,5},{8,10},{9,11},{10,... | collective-permute-start | bytes 221192 | tf_op jit(solution)/shard_map/ppermute | solution.py:74
  13.6 2.3 %collective-permute-start.5 = (f32[144,128]{1,0:T(8,128)S(1)}, f32[144,128]{1,0:T(8,128)S(1)}, u32[]{:S(2)}, u32[]{:S(2)}) collective-permute-start(f32[144,128]{1,0:T(8,128)S(1)} %get-tuple-element.77), channel_id=1, source_target_pairs={{0,4},{1,5},{2,6},{3,7},{4,0},{5,1},{6,2},{7,3},{8,12},{9,13},{10,... | collective-permute-start | bytes 221192 | tf_op jit(solution)/shard_map/ppermute | solution.py:74
  16.0 3.3 %shard_map.77 = (f32[96,1,8,128]{3,2,1,0:T(8,128)S(1)}, f32[1,97,12,8,128]{4,3,2,1,0:T(8,128)S(1)}, f32[1,97,12,8,128]{4,3,2,1,0:T(8,128)S(1)}, f32[1,97,12,8,12...) custom-call(s32[1]{0:T(128)} %bitcast.1.index, f32[2,4,768]{2,1,0:T(4,128)} %lat_length.3, f32[8,96,1536]{2,1,0:T(8,128)} %bitcast.5), custom_call_target="tpu_custom_call" | custom-call | flops 10 | bytes 10 | tf_op jit(solution)/shard_map/pallas_call | solution.py:271
  19.3 0.7 shard_map.76
  20.0 0.9 collective-permute-done.6.rest_3_
  21.0 12.2 %shard_map.78 = (f32[12,8,96,128]{3,2,1,0:T(8,128)S(1)}, f32[192,128]{1,0:T(8,128)S(1)}, f32[192,128]{1,0:T(8,128)S(1)}, f32[1,97,12,8,128]{4,3,2,1,0:T(8,128)S(...) custom-call(s32[1]{0:T(128)} %bitcast.1.index, ...), custom_call_target="tpu_custom_call", output_to_operand_aliasing={{3}: (6, {}), {4}: (7, {}), {5}: (8, {}), {6}: (9, {})} | custom-call | flops 10 | bytes 10 | tf_op jit(solution)/shard_map/pallas_call | solution.py:402
  33.2 11.7 %collective-permute-start.7 = (f32[192,128]{1,0:T(8,128)S(1)}, f32[192,128]{1,0:T(8,128)S(1)}, u32[]{:S(2)}, u32[]{:S(2)}) collective-permute-start(f32[192,128]{1,0:T(8,128)S(1)} %get-tuple-element.89), channel_id=1, source_target_pairs={{0,1},{1,0},{2,3},{3,2},{4,5},{5,4},{6,7},{7,6},{8,9},{9,8},{10,11... | collective-permute-start | bytes 294920 | tf_op jit(solution)/shard_map/ppermute | solution.py:74
  44.9 2.5 %shard_map.79 = (f32[2,2,96,1536]{3,2,1,0:T(8,128)S(1)}, f32[2,96,1536]{2,1,0:T(8,128)S(1)}, f32[2,96,1536]{2,1,0:T(8,128)S(1)}) custom-call(f32[12,8,96,128]{3,2,1,0:T(8,128)S(1)} %get-tuple-element.90.swept, bf16[8,256,256]{2,1,0:T(8,128)(2,1)S(1)} %get-tuple-element.64.near_high, bf16[8,256,256]{2,1,0:T(8,128)(2,1)S(1)} %get-tuple-element.71.near_low, ...), custom_call_target="tpu_custom_call" | custom-call | flops 10 | bytes 10 | tf_op jit(solution)/shard_map/pallas_call | solution.py:598
  47.4 2.9 %collective-permute-start.8 = (f32[2,96,1536]{2,1,0:T(8,128)S(1)}, f32[2,96,1536]{2,1,0:T(8,128)S(1)}, u32[]{:S(2)}, u32[]{:S(2)}) collective-permute-start(f32[2,96,1536]{2,1,0:T(8,128)S(1)} %get-tuple-element.93), channel_id=1, source_target_pairs={{0,8},{8,0},{16,24},{24,16},{1,9},{9,1},{17,25},{25,17},{2,10},{10... | collective-permute-start | bytes 3538952 | tf_op jit(solution)/shard_map/ppermute | solution.py:960
  50.4 1.5 %shard_map.80 = (f32[128,128]{1,0:T(8,128)S(1)}, f32[4,128]{1,0:T(4,128)S(1)}) custom-call(s32[1]{0:T(128)} %bitcast.1.index, f32[2,4,768]{2,1,0:T(4,128)S(1)} %copy-done), custom_call_target="tpu_custom_call" | custom-call | flops 10 | bytes 10 | tf_op jit(solution)/shard_map/pallas_call | solution.py:453
  51.9 2.5 %shard_map.81 = (f32[2,2,96,1536]{3,2,1,0:T(8,128)S(1)}, f32[2,96,1536]{2,1,0:T(8,128)S(1)}, f32[2,96,1536]{2,1,0:T(8,128)S(1)}) custom-call(f32[12,8,96,128]{3,2,1,0:T(8,128)S(1)} %get-tuple-element.90.swept, bf16[8,256,256]{2,1,0:T(8,128)(2,1)S(1)} %get-tuple-element.64.near_high, bf16[8,256,256]{2,1,0:T(8,128)(2,1)S(1)} %get-tuple-element.71.near_low, ...), custom_call_target="tpu_custom_call" | custom-call | flops 10 | bytes 10 | tf_op jit(solution)/shard_map/pallas_call | solution.py:598
  54.4 0.1 collective-permute-start.9
  54.5 0.1 shard_map.82
  54.6 0.0 copy-start.2
  54.6 3.5 %collective-permute-start.19 = (f32[2,96,1536]{2,1,0:T(8,128)S(1)}, f32[2,96,1536]{2,1,0:T(8,128)S(1)}, u32[]{:S(2)}, u32[]{:S(2)}) collective-permute-start(f32[2,96,1536]{2,1,0:T(8,128)S(1)} %shard_map.82), channel_id=1, source_target_pairs={{0,0},{8,16},{16,8},{24,24},{1,1},{9,17},{17,9},{25,25},{2,2},{10,... | collective-permute-start | bytes 3538952 | tf_op jit(solution)/shard_map/ppermute | solution.py:966
  58.2 0.1 shard_map.84
  58.3 2.5 %collective-permute-start.21 = (f32[2,96,1536]{2,1,0:T(8,128)S(1)}, f32[2,96,1536]{2,1,0:T(8,128)S(1)}, u32[]{:S(2)}, u32[]{:S(2)}) collective-permute-start(f32[2,96,1536]{2,1,0:T(8,128)S(1)} %shard_map.84), channel_id=1, source_target_pairs={{0,0},{8,16},{16,8},{24,24},{1,1},{9,17},{17,9},{25,25},{2,2},{10,... | collective-permute-start | bytes 3538952 | tf_op jit(solution)/shard_map/ppermute | solution.py:966
  60.8 0.1 collective-permute-start.10
  60.9 3.3 %collective-permute-start.11 = (f32[96,128]{1,0:T(8,128)S(1)}, f32[96,128]{1,0:T(8,128)S(1)}, u32[]{:S(2)}, u32[]{:S(2)}) collective-permute-start(f32[96,128]{1,0:T(8,128)S(1)} %get-tuple-element.100), channel_id=1, source_target_pairs={{0,4},{1,5},{2,6},{3,7},{4,0},{5,1},{6,2},{7,3},{8,12},{9,13},{10,... | collective-permute-start | bytes 147464 | tf_op jit(solution)/shard_map/ppermute | solution.py:74
  64.2 1.1 %collective-permute-start.12 = (f32[96,128]{1,0:T(8,128)S(1)}, f32[96,128]{1,0:T(8,128)S(1)}, u32[]{:S(2)}, u32[]{:S(2)}) collective-permute-start(f32[96,128]{1,0:T(8,128)S(1)} %get-tuple-element.101), channel_id=1, source_target_pairs={{0,6},{1,7},{2,4},{3,5},{4,2},{5,3},{6,0},{7,1},{8,14},{9,15},{10,... | collective-permute-start | bytes 147464 | tf_op jit(solution)/shard_map/ppermute | solution.py:74
  65.3 0.7 collective-permute-done.11.rest_2_
  66.0 3.1 %collective-permute-done.12.rest_3_ = f32[96,128]{1,0:T(8,128)S(1)} collective-permute-done((f32[96,128]{1,0:T(8,128)S(1)}, f32[96,128]{1,0:T(8,128)S(1)}, u32[]{:S(2)}, u32[]{:S(2)}) %collective-permute-start.12) | collective-permute-done | bytes 49184 | tf_op jit(solution)/shard_map/ppermute | solution.py:74
  69.0 1.4 %shard_map.85 = (f32[224,128]{1,0:T(8,128)S(1)}, f32[224,128]{1,0:T(8,128)S(1)}) custom-call(s32[1]{0:T(128)} %bitcast.1.index, f32[2,4]{1,0:T(2,128)S(1)} %copy-done.2, f32[4,128]{1,0:T(4,128)S(1)} %get-tuple-element.86.leaving, f32[128,128]{1,0:T(8,128)S(1)} %get-tuple-element.87.inside, f32[96,128]{1,0:T(8,128)S(1)} %get-tuple-element.98.rest_0_, ...), custom_call_target="tpu_custom_call" | custom-call | flops 10 | bytes 10 | tf_op jit(solution)/shard_map/pallas_call | solution.py:698
  70.4 1.4 %collective-permute-start.13 = (f32[224,128]{1,0:T(8,128)S(1)}, f32[224,128]{1,0:T(8,128)S(1)}, u32[]{:S(2)}, u32[]{:S(2)}) collective-permute-start(f32[224,128]{1,0:T(8,128)S(1)} %get-tuple-element.103), channel_id=1, source_target_pairs={{0,1},{1,0},{2,3},{3,2},{4,5},{5,4},{6,7},{7,6},{8,9},{9,8},{10,11... | collective-permute-start | bytes 344072 | tf_op jit(solution)/shard_map/ppermute | solution.py:74
  71.8 3.8 %collective-permute-done.13.came = f32[224,128]{1,0:T(8,128)S(1)} collective-permute-done((f32[224,128]{1,0:T(8,128)S(1)}, f32[224,128]{1,0:T(8,128)S(1)}, u32[]{:S(2)}, u32[]{:S(2)}) %collective-permute-start.13) | collective-permute-done | bytes 114720 | tf_op jit(solution)/shard_map/ppermute | solution.py:74
  75.6 0.3 collective-permute-start.14
  75.9 0.7 collective-permute-start.15
  76.6 2.7 %collective-permute-start.16 = (f32[112,128]{1,0:T(8,128)S(1)}, f32[112,128]{1,0:T(8,128)S(1)}, u32[]{:S(2)}, u32[]{:S(2)}) collective-permute-start(f32[112,128]{1,0:T(8,128)S(1)} %get-tuple-element.107), channel_id=1, source_target_pairs={{0,6},{1,7},{2,4},{3,5},{4,2},{5,3},{6,0},{7,1},{8,14},{9,15},{10,... | collective-permute-start | bytes 172040 | tf_op jit(solution)/shard_map/ppermute | solution.py:74
  79.2 0.7 collective-permute-done.15.rest_2_
  79.9 1.7 %collective-permute-done.16.rest_3_ = f32[112,128]{1,0:T(8,128)S(1)} collective-permute-done((f32[112,128]{1,0:T(8,128)S(1)}, f32[112,128]{1,0:T(8,128)S(1)}, u32[]{:S(2)}, u32[]{:S(2)}) %collective-permute-start.16) | collective-permute-done | bytes 57376 | tf_op jit(solution)/shard_map/ppermute | solution.py:74
  81.6 2.7 %collective-permute-start.20 = (f32[2,96,1536]{2,1,0:T(8,128)S(1)}, f32[2,96,1536]{2,1,0:T(8,128)S(1)}, u32[]{:S(2)}, u32[]{:S(2)}) collective-permute-start(f32[2,96,1536]{2,1,0:T(8,128)S(1)} %collective-permute-done.19.met), channel_id=1, source_target_pairs={{0,8},{8,0},{16,24},{24,16},{1,9},{9,1},{17,25},{25,17},{2,10},{10... | collective-permute-start | bytes 3538952 | tf_op jit(solution)/shard_map/ppermute | solution.py:984
  84.3 0.5 collective-permute-done.21.met
  84.8 1.7 %collective-permute-start.17 = (f32[448,128]{1,0:T(8,128)S(1)}, f32[448,128]{1,0:T(8,128)S(1)}, u32[]{:S(2)}, u32[]{:S(2)}) collective-permute-start(f32[448,128]{1,0:T(8,128)S(1)} %shard_map.87.rest_0_), channel_id=1, source_target_pairs={{0,16},{16,0},{8,24},{24,8},{1,17},{17,1},{9,25},{25,9},{2,18},{18... | collective-permute-start | bytes 688136 | tf_op jit(solution)/shard_map/ppermute | solution.py:979
  86.5 0.3 collective-permute-start.18
  86.8 1.1 %shard_map.88.rest_4_ = f32[2,2,96,1536]{3,2,1,0:T(8,128)S(1)} custom-call(f32[2,2,96,1536]{3,2,1,0:T(8,128)S(1)} %get-tuple-element.108.own, f32[2,96,1536]{2,1,0:T(8,128)S(1)} %collective-permute-done.8.near, f32[2,96,1536]{2,1,0:T(8,128)S(1)} %collective-permute-done.20.far, f32[2,96,1536]{2,1,0:T(8,128)S(1)} %collective-permute-done.19.met, ...), custom_call_target="tpu_custom_call" | custom-call | flops 10 | bytes 10 | tf_op jit(solution)/shard_map/pallas_call | solution.py:871
  87.9 0.5 collective-permute-done.22.far
  88.4 1.0 shard_map.89.rest_5_
  89.4 2.6 %collective-permute-done.17.rest_1_ = f32[448,128]{1,0:T(8,128)S(1)} collective-permute-done((f32[448,128]{1,0:T(8,128)S(1)}, f32[448,128]{1,0:T(8,128)S(1)}, u32[]{:S(2)}, u32[]{:S(2)}) %collective-permute-start.17) | collective-permute-done | bytes 229408 | tf_op jit(solution)/shard_map/ppermute | solution.py:979
  92.0 1.1 %collective-permute-start.23 = (f32[448,128]{1,0:T(8,128)S(1)}, f32[448,128]{1,0:T(8,128)S(1)}, u32[]{:S(2)}, u32[]{:S(2)}) collective-permute-start(f32[448,128]{1,0:T(8,128)S(1)} %collective-permute-done.17.rest_1_), channel_id=1, source_target_pairs={{0,8},{8,0},{16,24},{24,16},{1,9},{9,1},{17,25},{25,17},{2,10},{10... | collective-permute-start | bytes 688136 | tf_op jit(solution)/shard_map/ppermute | solution.py:986
  93.1 1.1 %collective-permute-done.23.rest_3_ = f32[448,128]{1,0:T(8,128)S(1)} collective-permute-done((f32[448,128]{1,0:T(8,128)S(1)}, f32[448,128]{1,0:T(8,128)S(1)}, u32[]{:S(2)}, u32[]{:S(2)}) %collective-permute-start.23) | collective-permute-done | bytes 229408 | tf_op jit(solution)/shard_map/ppermute | solution.py:986
  94.2 2.5 %shard_map.90 = f32[2,4,96,1536]{3,2,1,0:T(8,128)} custom-call(f32[2,4,8,128]{3,2,1,0:T(8,128)S(1)} %get-tuple-element.68.mix, f32[448,128]{1,0:T(8,128)S(1)} %shard_map.87.rest_0_, f32[448,128]{1,0:T(8,128)S(1)} %collective-permute-done.17.rest_1_, f32[448,128]{1,0:T(8,128)S(1)} %collective-permute-done.18.rest_2_, ...), custom_call_target="tpu_custom_call" | custom-call | flops 10 | bytes 10 | tf_op jit(solution)/shard_map/pallas_call | solution.py:931
  (26 shorter events, 0.1 us)
Async XLA Ops:
  4.2 8.1 %collective-permute-start.3 = (f32[288,128]{1,0:T(8,128)S(1)}, f32[288,128]{1,0:T(8,128)S(1)}, u32[]{:S(2)}, u32[]{:S(2)}) collective-permute-start(f32[288,128]{1,0:T(8,128)S(1)} %get-tuple-element.61), channel_id=1, source_target_pairs={{0,1},{1,0},{2,3},{3,2},{4,5},{5,4},{6,7},{7,6},{8,9},{9,8},{10,11... | collective-permute-start | bytes 442376 | tf_op jit(solution)/shard_map/ppermute | solution.py:74
  6.3 5.9 %collective-permute-start.2 = (f32[2,4]{1,0:T(2,128)}, f32[2,4]{1,0:T(2,128)S(1)}, u32[]{:S(2)}, u32[]{:S(2)}) collective-permute-start(f32[2,4]{1,0:T(2,128)} %own), channel_id=1, source_target_pairs={{0,24},{24,0},{8,16},{16,8},{1,25},{25,1},{9,17},{17,9},{2,26},{26... | collective-permute-start | bytes 104 | tf_op jit(solution)/shard_map/ppermute | solution.py:1069
  8.3 3.9 %collective-permute-start.1 = (f32[2,4]{1,0:T(2,128)}, f32[2,4]{1,0:T(2,128)S(1)}, u32[]{:S(2)}, u32[]{:S(2)}) collective-permute-start(f32[2,4]{1,0:T(2,128)} %own), channel_id=1, source_target_pairs={{0,8},{8,0},{16,24},{24,16},{1,9},{9,1},{17,25},{25,17},{2,10},{10... | collective-permute-start | bytes 104 | tf_op jit(solution)/shard_map/ppermute | solution.py:1069
  8.3 3.9 %collective-permute-start = (f32[2,4]{1,0:T(2,128)}, f32[2,4]{1,0:T(2,128)S(1)}, u32[]{:S(2)}, u32[]{:S(2)}) collective-permute-start(f32[2,4]{1,0:T(2,128)} %own), channel_id=1, source_target_pairs={{0,16},{16,0},{8,24},{24,8},{1,17},{17,1},{9,25},{25,9},{2,18},{18... | collective-permute-start | bytes 104 | tf_op jit(solution)/shard_map/ppermute | solution.py:1069
  8.6 0.7 copy-start.1
  12.3 7.7 %collective-permute-start.4 = (f32[144,128]{1,0:T(8,128)S(1)}, f32[144,128]{1,0:T(8,128)S(1)}, u32[]{:S(2)}, u32[]{:S(2)}) collective-permute-start(f32[144,128]{1,0:T(8,128)S(1)} %get-tuple-element.76), channel_id=1, source_target_pairs={{0,2},{1,3},{2,0},{3,1},{4,6},{5,7},{6,4},{7,5},{8,10},{9,11},{10,... | collective-permute-start | bytes 221192 | tf_op jit(solution)/shard_map/ppermute | solution.py:74
  13.6 6.4 %collective-permute-start.5 = (f32[144,128]{1,0:T(8,128)S(1)}, f32[144,128]{1,0:T(8,128)S(1)}, u32[]{:S(2)}, u32[]{:S(2)}) collective-permute-start(f32[144,128]{1,0:T(8,128)S(1)} %get-tuple-element.77), channel_id=1, source_target_pairs={{0,4},{1,5},{2,6},{3,7},{4,0},{5,1},{6,2},{7,3},{8,12},{9,13},{10,... | collective-permute-start | bytes 221192 | tf_op jit(solution)/shard_map/ppermute | solution.py:74
  15.9 5.0 %collective-permute-start.6 = (f32[144,128]{1,0:T(8,128)S(1)}, f32[144,128]{1,0:T(8,128)S(1)}, u32[]{:S(2)}, u32[]{:S(2)}) collective-permute-start(f32[144,128]{1,0:T(8,128)S(1)} %get-tuple-element.78), channel_id=1, source_target_pairs={{0,6},{1,7},{2,4},{3,5},{4,2},{5,3},{6,0},{7,1},{8,14},{9,15},{10,... | collective-permute-start | bytes 221192 | tf_op jit(solution)/shard_map/ppermute | solution.py:74
  15.9 3.3 %copy-start.3 = (f32[2,4]{1,0:T(2,128)S(1)}, f32[2,4]{1,0:T(2,128)}, u32[]{:S(2)}) copy-start(f32[2,4]{1,0:T(2,128)} %own) | copy-start | bytes 100
  33.2 18.7 %collective-permute-start.7 = (f32[192,128]{1,0:T(8,128)S(1)}, f32[192,128]{1,0:T(8,128)S(1)}, u32[]{:S(2)}, u32[]{:S(2)}) collective-permute-start(f32[192,128]{1,0:T(8,128)S(1)} %get-tuple-element.89), channel_id=1, source_target_pairs={{0,1},{1,0},{2,3},{3,2},{4,5},{5,4},{6,7},{7,6},{8,9},{9,8},{10,11... | collective-permute-start | bytes 294920 | tf_op jit(solution)/shard_map/ppermute | solution.py:74
  44.9 5.4 %copy-start = (f32[2,4,768]{2,1,0:T(4,128)S(1)}, f32[2,4,768]{2,1,0:T(4,128)}, u32[]{:S(2)}) copy-start(f32[2,4,768]{2,1,0:T(4,128)} %lat_length.3) | copy-start | bytes 73732
  47.4 7.1 %collective-permute-start.8 = (f32[2,96,1536]{2,1,0:T(8,128)S(1)}, f32[2,96,1536]{2,1,0:T(8,128)S(1)}, u32[]{:S(2)}, u32[]{:S(2)}) collective-permute-start(f32[2,96,1536]{2,1,0:T(8,128)S(1)} %get-tuple-element.93), channel_id=1, source_target_pairs={{0,8},{8,0},{16,24},{24,16},{1,9},{9,1},{17,25},{25,17},{2,10},{10... | collective-permute-start | bytes 3538952 | tf_op jit(solution)/shard_map/ppermute | solution.py:960
  54.4 3.8 %collective-permute-start.9 = (f32[2,96,1536]{2,1,0:T(8,128)S(1)}, f32[2,96,1536]{2,1,0:T(8,128)S(1)}, u32[]{:S(2)}, u32[]{:S(2)}) collective-permute-start(f32[2,96,1536]{2,1,0:T(8,128)S(1)} %get-tuple-element.97), channel_id=1, source_target_pairs={{0,8},{8,0},{16,24},{24,16},{1,9},{9,1},{17,25},{25,17},{2,10},{10... | collective-permute-start | bytes 3538952 | tf_op jit(solution)/shard_map/ppermute | solution.py:960
  54.6 14.4 %copy-start.2 = (f32[2,4]{1,0:T(2,128)S(1)}, f32[2,4]{1,0:T(2,128)}, u32[]{:S(2)}) copy-start(f32[2,4]{1,0:T(2,128)} %lon_length.2) | copy-start | bytes 100
  54.6 27.0 %collective-permute-start.19 = (f32[2,96,1536]{2,1,0:T(8,128)S(1)}, f32[2,96,1536]{2,1,0:T(8,128)S(1)}, u32[]{:S(2)}, u32[]{:S(2)}) collective-permute-start(f32[2,96,1536]{2,1,0:T(8,128)S(1)} %shard_map.82), channel_id=1, source_target_pairs={{0,0},{8,16},{16,8},{24,24},{1,1},{9,17},{17,9},{25,25},{2,2},{10,... | collective-permute-start | bytes 3538952 | tf_op jit(solution)/shard_map/ppermute | solution.py:966
  58.3 26.5 %collective-permute-start.21 = (f32[2,96,1536]{2,1,0:T(8,128)S(1)}, f32[2,96,1536]{2,1,0:T(8,128)S(1)}, u32[]{:S(2)}, u32[]{:S(2)}) collective-permute-start(f32[2,96,1536]{2,1,0:T(8,128)S(1)} %shard_map.84), channel_id=1, source_target_pairs={{0,0},{8,16},{16,8},{24,24},{1,1},{9,17},{17,9},{25,25},{2,2},{10,... | collective-permute-start | bytes 3538952 | tf_op jit(solution)/shard_map/ppermute | solution.py:966
  60.8 4.5 %collective-permute-start.10 = (f32[96,128]{1,0:T(8,128)S(1)}, f32[96,128]{1,0:T(8,128)S(1)}, u32[]{:S(2)}, u32[]{:S(2)}) collective-permute-start(f32[96,128]{1,0:T(8,128)S(1)} %get-tuple-element.99), channel_id=1, source_target_pairs={{0,2},{1,3},{2,0},{3,1},{4,6},{5,7},{6,4},{7,5},{8,10},{9,11},{10,... | collective-permute-start | bytes 147464 | tf_op jit(solution)/shard_map/ppermute | solution.py:74
  60.9 5.1 %collective-permute-start.11 = (f32[96,128]{1,0:T(8,128)S(1)}, f32[96,128]{1,0:T(8,128)S(1)}, u32[]{:S(2)}, u32[]{:S(2)}) collective-permute-start(f32[96,128]{1,0:T(8,128)S(1)} %get-tuple-element.100), channel_id=1, source_target_pairs={{0,4},{1,5},{2,6},{3,7},{4,0},{5,1},{6,2},{7,3},{8,12},{9,13},{10,... | collective-permute-start | bytes 147464 | tf_op jit(solution)/shard_map/ppermute | solution.py:74
  64.2 4.8 %collective-permute-start.12 = (f32[96,128]{1,0:T(8,128)S(1)}, f32[96,128]{1,0:T(8,128)S(1)}, u32[]{:S(2)}, u32[]{:S(2)}) collective-permute-start(f32[96,128]{1,0:T(8,128)S(1)} %get-tuple-element.101), channel_id=1, source_target_pairs={{0,6},{1,7},{2,4},{3,5},{4,2},{5,3},{6,0},{7,1},{8,14},{9,15},{10,... | collective-permute-start | bytes 147464 | tf_op jit(solution)/shard_map/ppermute | solution.py:74
  70.4 5.2 %collective-permute-start.13 = (f32[224,128]{1,0:T(8,128)S(1)}, f32[224,128]{1,0:T(8,128)S(1)}, u32[]{:S(2)}, u32[]{:S(2)}) collective-permute-start(f32[224,128]{1,0:T(8,128)S(1)} %get-tuple-element.103), channel_id=1, source_target_pairs={{0,1},{1,0},{2,3},{3,2},{4,5},{5,4},{6,7},{7,6},{8,9},{9,8},{10,11... | collective-permute-start | bytes 344072 | tf_op jit(solution)/shard_map/ppermute | solution.py:74
  75.6 3.6 %collective-permute-start.14 = (f32[112,128]{1,0:T(8,128)S(1)}, f32[112,128]{1,0:T(8,128)S(1)}, u32[]{:S(2)}, u32[]{:S(2)}) collective-permute-start(f32[112,128]{1,0:T(8,128)S(1)} %get-tuple-element.105), channel_id=1, source_target_pairs={{0,2},{1,3},{2,0},{3,1},{4,6},{5,7},{6,4},{7,5},{8,10},{9,11},{10,... | collective-permute-start | bytes 172040 | tf_op jit(solution)/shard_map/ppermute | solution.py:74
  75.9 4.0 %collective-permute-start.15 = (f32[112,128]{1,0:T(8,128)S(1)}, f32[112,128]{1,0:T(8,128)S(1)}, u32[]{:S(2)}, u32[]{:S(2)}) collective-permute-start(f32[112,128]{1,0:T(8,128)S(1)} %get-tuple-element.106), channel_id=1, source_target_pairs={{0,4},{1,5},{2,6},{3,7},{4,0},{5,1},{6,2},{7,3},{8,12},{9,13},{10,... | collective-permute-start | bytes 172040 | tf_op jit(solution)/shard_map/ppermute | solution.py:74
  76.6 5.0 %collective-permute-start.16 = (f32[112,128]{1,0:T(8,128)S(1)}, f32[112,128]{1,0:T(8,128)S(1)}, u32[]{:S(2)}, u32[]{:S(2)}) collective-permute-start(f32[112,128]{1,0:T(8,128)S(1)} %get-tuple-element.107), channel_id=1, source_target_pairs={{0,6},{1,7},{2,4},{3,5},{4,2},{5,3},{6,0},{7,1},{8,14},{9,15},{10,... | collective-permute-start | bytes 172040 | tf_op jit(solution)/shard_map/ppermute | solution.py:74
  81.6 5.2 %collective-permute-start.20 = (f32[2,96,1536]{2,1,0:T(8,128)S(1)}, f32[2,96,1536]{2,1,0:T(8,128)S(1)}, u32[]{:S(2)}, u32[]{:S(2)}) collective-permute-start(f32[2,96,1536]{2,1,0:T(8,128)S(1)} %collective-permute-done.19.met), channel_id=1, source_target_pairs={{0,8},{8,0},{16,24},{24,16},{1,9},{9,1},{17,25},{25,17},{2,10},{10... | collective-permute-start | bytes 3538952 | tf_op jit(solution)/shard_map/ppermute | solution.py:984
  84.8 3.6 %collective-permute-start.22 = (f32[2,96,1536]{2,1,0:T(8,128)S(1)}, f32[2,96,1536]{2,1,0:T(8,128)S(1)}, u32[]{:S(2)}, u32[]{:S(2)}) collective-permute-start(f32[2,96,1536]{2,1,0:T(8,128)S(1)} %collective-permute-done.21.met), channel_id=1, source_target_pairs={{0,8},{8,0},{16,24},{24,16},{1,9},{9,1},{17,25},{25,17},{2,10},{10... | collective-permute-start | bytes 3538952 | tf_op jit(solution)/shard_map/ppermute | solution.py:984
  84.8 7.2 %collective-permute-start.17 = (f32[448,128]{1,0:T(8,128)S(1)}, f32[448,128]{1,0:T(8,128)S(1)}, u32[]{:S(2)}, u32[]{:S(2)}) collective-permute-start(f32[448,128]{1,0:T(8,128)S(1)} %shard_map.87.rest_0_), channel_id=1, source_target_pairs={{0,16},{16,0},{8,24},{24,8},{1,17},{17,1},{9,25},{25,9},{2,18},{18... | collective-permute-start | bytes 688136 | tf_op jit(solution)/shard_map/ppermute | solution.py:979
  86.5 6.6 %collective-permute-start.18 = (f32[448,128]{1,0:T(8,128)S(1)}, f32[448,128]{1,0:T(8,128)S(1)}, u32[]{:S(2)}, u32[]{:S(2)}) collective-permute-start(f32[448,128]{1,0:T(8,128)S(1)} %shard_map.87.rest_0_), channel_id=1, source_target_pairs={{0,8},{8,0},{16,24},{24,16},{1,9},{9,1},{17,25},{25,17},{2,10},{10... | collective-permute-start | bytes 688136 | tf_op jit(solution)/shard_map/ppermute | solution.py:980
  92.0 2.2 %collective-permute-start.23 = (f32[448,128]{1,0:T(8,128)S(1)}, f32[448,128]{1,0:T(8,128)S(1)}, u32[]{:S(2)}, u32[]{:S(2)}) collective-permute-start(f32[448,128]{1,0:T(8,128)S(1)} %collective-permute-done.17.rest_1_), channel_id=1, source_target_pairs={{0,8},{8,0},{16,24},{24,16},{1,9},{9,1},{17,25},{25,17},{2,10},{10... | collective-permute-start | bytes 688136 | tf_op jit(solution)/shard_map/ppermute | solution.py:986

commit v6 on v5

--- a/solution.py
+++ b/solution.py
@@ -171,15 +171,15 @@
     word_row = chunk_count * group_count
     word_rows = packed.shape[1] - word_row
     for sub in range(sub_count):
-        packed[sub, word_row:, :] = jnp.full((word_rows, LANES), float(strip), f32)
+        packed[sub, word_row:, :] = jnp.full((word_rows, LANES), 8.0 * strip, f32)
         for chunk in range(chunk_count):
             for tile in range(tiles):
                 at = chunk * group_count + tile * SUBLANES
                 packed[sub, at : at + SUBLANES, :] = joined[sub, chunk, tile]
             filled = lane + chunk * LANES < ends[sub]
             cell = jnp.where(filled, joined[sub, chunk, tiles], 0.0).astype(i32)
-            word = (cell - (cell & 127)) + ((cell - lane) & 127)
-            word = jnp.where(filled, word, strip).astype(f32)
+            word = 8 * (cell - (cell & 127)) + ((cell - lane) & 127)
+            word = jnp.where(filled, word, 8 * strip).astype(f32)
             packed[sub, word_row + chunk : word_row + chunk + 1, :] = word[:1]
     rows = packed.shape[1]
     for out, members in zip(outs, layout):
@@ -317,7 +317,7 @@
 
         def more(chunk):
             last = jnp.minimum(chunk, chunk_count - 1)
-            return (chunk < chunk_count) & (words[first + last, 0] < strip)
+            return (chunk < chunk_count) & (words[first + last, 0] < 8 * strip)
 
         def one_chunk(chunk):
             blocks = [
@@ -330,41 +330,34 @@
             ]
             for slot in range(LANES):
                 word = words[first + chunk, slot]
-                target = lax.shift_right_logical(word, 7)
+                target = pl.multiple_of(lax.shift_right_logical(word, 7), SUBLANES)
                 turn = word & 127
                 for tile in range(tiles):
                     value = pltpu.roll(jnp.where(lane == slot, blocks[tile], 0.0), turn, 1)
                     total = flat[slot % CHAINS]
-                    total[tile, target] = total[tile, target] + value
+                    at = pl.ds(target, SUBLANES)
+                    total[tile, at, :] = total[tile, at, :] + value
             return chunk + 1
 
         lax.while_loop(more, one_chunk, jnp.int32(0))
         return carry
 
-    flat = [total.reshape(tiles, -1, SUBLANES, LANES) for total in totals]
+    flat = [total.reshape(tiles, -1, LANES) for total in totals]
     lax.fori_loop(0, sub_count, one_source, 0)
     for tile in range(tiles):
         groups = slice(tile * SUBLANES, (tile + 1) * SUBLANES)
 
-        def add_rows(at, carry):
-            rows = pl.ds(pl.multiple_of(at * SUBLANES, SUBLANES), SUBLANES)
-            for column in range(column_count):
-                value = totals[0][tile, rows, column]
-                for total in totals[1:]:
-                    value = value + total[tile, rows, column]
-                totals[0][tile, rows, column] = value
-            return carry
-
-        lax.fori_loop(0, row_count // SUBLANES, add_rows, 0)
-
-        def sweep(source, target, turn):
+        def sweep(sources, target, turn):
             def one_row(step, state):
                 row = row_count - 1 - step if turn % 2 else step
                 keep = decay[row, tile]
                 take = 1.0 - keep
                 following = []
                 for column in range(column_count):
-                    value = keep * state[column] + take * source[tile, row, column]
+                    value = sources[0][tile, row, column]
+                    for source in sources[1:]:
+                        value = value + source[tile, row, column]
+                    value = keep * state[column] + take * value
                     target[tile, row, column] = value
                     following.append(value)
                 return tuple(following)
@@ -377,7 +370,8 @@
                 exits[pl.ds(at, SUBLANES, stride=message_rows), :] = state[column]
 
         for turn in range(4):
-            sweep(totals[turn % 2], totals[1 - turn % 2], turn)
+            sources = totals if turn == 0 else totals[turn % 2 : turn % 2 + 1]
+            sweep(sources, totals[1 - turn % 2], turn)
 
         def turn_rows(at, carry):
             rows = pl.ds(pl.multiple_of(at * SUBLANES, SUBLANES), SUBLANES)

time: 97.6 us -> 95 us (0.973)
  starting transfers between devices: 44.1 us -> 40.9 us
  waiting for transfers between devices: 15.6 us -> 16.7 us
    ppermute x12, starting transfers between devices: 27 us -> 24.4 us  [move(): return lax.ppermute(part, 'sub', [(at, at ^ k) for at in range(sub_count)])]
  transfers between devices with their start and end apart: 24 -> 24, of which waited for: 10 -> 8; matrix products, arithmetic and copies ran while one was open for 0% -> 0% of each run, Pallas kernels for 18% -> 18%
where the time goes in v6:
time: 95 us; the launch traced here: 94.6 us
  starting transfers between devices  40.9 us (43%)
  Pallas kernels  36 us (38%)
  waiting for transfers between devices  16.7 us (18%)
    ppermute x12, starting transfers between devices, move(): return lax.ppermute(part, 'sub', [(at, at ^ k) for at in range(sub_count)])  24.4 us
    pallas_call x1, Pallas kernels, deposit_and_sweep(): pl.pallas_call(functools.partial(deposit_kernel, sizes), out_shape=[pltpu...  12.1 us
    ppermute x12, waiting for transfers between devices, move(): return lax.ppermute(part, 'sub', [(at, at ^ k) for at in range(sub_count)])  11.2 us
    ppermute x2, starting transfers between devices, cross_some(): mets.append(lax.ppermute(total, 'band', MIDDLE))  5.98 us
    pallas_call x2, Pallas kernels, longitude_pair(): pl.pallas_call(functools.partial(pair_kernel, variables), in_specs=[VMEM]...  4.97 us
    pallas_call x1, Pallas kernels, pack_observations(): pl.pallas_call(functools.partial(pack_kernel, (sub_count, group_count, ch...  4.16 us
    pallas_call x1, Pallas kernels, make_ready(): pl.pallas_call(functools.partial(ready_kernel, sizes), in_specs=[SMEM, HB...  3.33 us
    ppermute x1, waiting for transfers between devices, four_bands(): across = lax.ppermute(messages, 'band', CROSS)  3.15 us
  transfers between devices with their start and end apart: 24, of which 8 were waited for; matrix products, arithmetic and copies ran while one was open for 0% of the time, Pallas kernels for 18%

profile of v6, /device:TPU:1, one launch (start us, length us, event | category | flops | bytes accessed | tf_op | source)
XLA Modules:
  0.0 94.6 jit_solution(14179812119926671442)
XLA Ops:
  0.0 4.2 %shard_map.73 = (f32[288,128]{1,0:T(8,128)S(1)}, f32[288,128]{1,0:T(8,128)S(1)}) custom-call(s32[1]{0:T(128)} %bitcast.1.index, s32[32,128]{1,0:T(8,128)} %bitcast.6, s32[32,128]{1,0:T(8,128)} %bitcast.7, f32[2,4,4096]{2,1,0:T(4,128)} %values.1), custom_call_target="tpu_custom_call" | custom-call | flops 10 | bytes 10 | tf_op jit(solution)/shard_map/pallas_call | solution.py:198
  4.2 2.1 %collective-permute-start.3 = (f32[288,128]{1,0:T(8,128)S(1)}, f32[288,128]{1,0:T(8,128)S(1)}, u32[]{:S(2)}, u32[]{:S(2)}) collective-permute-start(f32[288,128]{1,0:T(8,128)S(1)} %get-tuple-element.61), channel_id=1, source_target_pairs={{0,1},{1,0},{2,3},{3,2},{4,5},{5,4},{6,7},{7,6},{8,9},{9,8},{10,11... | collective-permute-start | bytes 442376 | tf_op jit(solution)/shard_map/ppermute | solution.py:74
  6.3 2.1 %collective-permute-start.2 = (f32[2,4]{1,0:T(2,128)}, f32[2,4]{1,0:T(2,128)S(1)}, u32[]{:S(2)}, u32[]{:S(2)}) collective-permute-start(f32[2,4]{1,0:T(2,128)} %own), channel_id=1, source_target_pairs={{0,24},{24,0},{8,16},{16,8},{1,25},{25,1},{9,17},{17,9},{2,26},{26... | collective-permute-start | bytes 104 | tf_op jit(solution)/shard_map/ppermute | solution.py:1063
  8.4 0.0 collective-permute-start.1
  8.4 0.2 collective-permute-start
  8.6 0.7 copy-done.1
  9.3 2.9 %shard_map.74 = (bf16[8,256,256]{2,1,0:T(8,128)(2,1)S(1)}, bf16[8,256,256]{2,1,0:T(8,128)(2,1)S(1)}, bf16[8,256,256]{2,1,0:T(8,128)(2,1)S(1)}, bf16[8,64,1536]{2,1,0:T(8,128)(2,1)S(1)}) custom-call(f32[2,4]{1,0:T(2,128)S(1)} %copy-done.1), custom_call_target="tpu_custom_call" | custom-call | flops 10 | bytes 10 | tf_op jit(solution)/shard_map/pallas_call | solution.py:520
  12.2 0.0 collective-permute-done.2.corner_
  12.2 0.0 collective-permute-done.1.beside_
  12.2 0.0 collective-permute-done.3.came
  12.3 1.4 %collective-permute-start.4 = (f32[144,128]{1,0:T(8,128)S(1)}, f32[144,128]{1,0:T(8,128)S(1)}, u32[]{:S(2)}, u32[]{:S(2)}) collective-permute-start(f32[144,128]{1,0:T(8,128)S(1)} %get-tuple-element.76), channel_id=1, source_target_pairs={{0,2},{1,3},{2,0},{3,1},{4,6},{5,7},{6,4},{7,5},{8,10},{9,11},{10,... | collective-permute-start | bytes 221192 | tf_op jit(solution)/shard_map/ppermute | solution.py:74
  13.6 2.3 %collective-permute-start.5 = (f32[144,128]{1,0:T(8,128)S(1)}, f32[144,128]{1,0:T(8,128)S(1)}, u32[]{:S(2)}, u32[]{:S(2)}) collective-permute-start(f32[144,128]{1,0:T(8,128)S(1)} %get-tuple-element.77), channel_id=1, source_target_pairs={{0,4},{1,5},{2,6},{3,7},{4,0},{5,1},{6,2},{7,3},{8,12},{9,13},{10,... | collective-permute-start | bytes 221192 | tf_op jit(solution)/shard_map/ppermute | solution.py:74
  16.0 3.3 %shard_map.77 = (f32[96,1,8,128]{3,2,1,0:T(8,128)S(1)}, f32[1,97,12,8,128]{4,3,2,1,0:T(8,128)S(1)}, f32[1,97,12,8,128]{4,3,2,1,0:T(8,128)S(1)}, f32[1,97,12,8,12...) custom-call(s32[1]{0:T(128)} %bitcast.1.index, f32[2,4,768]{2,1,0:T(4,128)} %lat_length.3, f32[8,96,1536]{2,1,0:T(8,128)} %bitcast.5), custom_call_target="tpu_custom_call" | custom-call | flops 10 | bytes 10 | tf_op jit(solution)/shard_map/pallas_call | solution.py:271
  19.3 0.7 shard_map.76
  20.0 0.9 collective-permute-done.6.rest_3_
  21.0 12.1 %shard_map.78 = (f32[12,8,96,128]{3,2,1,0:T(8,128)S(1)}, f32[192,128]{1,0:T(8,128)S(1)}, f32[192,128]{1,0:T(8,128)S(1)}, f32[1,97,12,8,128]{4,3,2,1,0:T(8,128)S(...) custom-call(s32[1]{0:T(128)} %bitcast.1.index, ...), custom_call_target="tpu_custom_call", output_to_operand_aliasing={{3}: (6, {}), {4}: (7, {}), {5}: (8, {}), {6}: (9, {})} | custom-call | flops 10 | bytes 10 | tf_op jit(solution)/shard_map/pallas_call | solution.py:396
  33.1 9.6 %collective-permute-start.7 = (f32[192,128]{1,0:T(8,128)S(1)}, f32[192,128]{1,0:T(8,128)S(1)}, u32[]{:S(2)}, u32[]{:S(2)}) collective-permute-start(f32[192,128]{1,0:T(8,128)S(1)} %get-tuple-element.89), channel_id=1, source_target_pairs={{0,1},{1,0},{2,3},{3,2},{4,5},{5,4},{6,7},{7,6},{8,9},{9,8},{10,11... | collective-permute-start | bytes 294920 | tf_op jit(solution)/shard_map/ppermute | solution.py:74
  42.7 2.5 %shard_map.79 = (f32[2,2,96,1536]{3,2,1,0:T(8,128)S(1)}, f32[2,96,1536]{2,1,0:T(8,128)S(1)}, f32[2,96,1536]{2,1,0:T(8,128)S(1)}) custom-call(f32[12,8,96,128]{3,2,1,0:T(8,128)S(1)} %get-tuple-element.90.swept, bf16[8,256,256]{2,1,0:T(8,128)(2,1)S(1)} %get-tuple-element.64.near_high, bf16[8,256,256]{2,1,0:T(8,128)(2,1)S(1)} %get-tuple-element.71.near_low, ...), custom_call_target="tpu_custom_call" | custom-call | flops 10 | bytes 10 | tf_op jit(solution)/shard_map/pallas_call | solution.py:592
  45.1 2.9 %collective-permute-start.8 = (f32[2,96,1536]{2,1,0:T(8,128)S(1)}, f32[2,96,1536]{2,1,0:T(8,128)S(1)}, u32[]{:S(2)}, u32[]{:S(2)}) collective-permute-start(f32[2,96,1536]{2,1,0:T(8,128)S(1)} %get-tuple-element.93), channel_id=1, source_target_pairs={{0,8},{8,0},{16,24},{24,16},{1,9},{9,1},{17,25},{25,17},{2,10},{10... | collective-permute-start | bytes 3538952 | tf_op jit(solution)/shard_map/ppermute | solution.py:954
  48.1 1.5 %shard_map.80 = (f32[128,128]{1,0:T(8,128)S(1)}, f32[4,128]{1,0:T(4,128)S(1)}) custom-call(s32[1]{0:T(128)} %bitcast.1.index, f32[2,4,768]{2,1,0:T(4,128)S(1)} %copy-done), custom_call_target="tpu_custom_call" | custom-call | flops 10 | bytes 10 | tf_op jit(solution)/shard_map/pallas_call | solution.py:447
  49.6 2.5 %shard_map.81 = (f32[2,2,96,1536]{3,2,1,0:T(8,128)S(1)}, f32[2,96,1536]{2,1,0:T(8,128)S(1)}, f32[2,96,1536]{2,1,0:T(8,128)S(1)}) custom-call(f32[12,8,96,128]{3,2,1,0:T(8,128)S(1)} %get-tuple-element.90.swept, bf16[8,256,256]{2,1,0:T(8,128)(2,1)S(1)} %get-tuple-element.64.near_high, bf16[8,256,256]{2,1,0:T(8,128)(2,1)S(1)} %get-tuple-element.71.near_low, ...), custom_call_target="tpu_custom_call" | custom-call | flops 10 | bytes 10 | tf_op jit(solution)/shard_map/pallas_call | solution.py:592
  52.1 0.1 collective-permute-start.9
  52.2 0.1 shard_map.82
  52.4 0.0 copy-start.2
  52.4 3.5 %collective-permute-start.19 = (f32[2,96,1536]{2,1,0:T(8,128)S(1)}, f32[2,96,1536]{2,1,0:T(8,128)S(1)}, u32[]{:S(2)}, u32[]{:S(2)}) collective-permute-start(f32[2,96,1536]{2,1,0:T(8,128)S(1)} %shard_map.82), channel_id=1, source_target_pairs={{0,0},{8,16},{16,8},{24,24},{1,1},{9,17},{17,9},{25,25},{2,2},{10,... | collective-permute-start | bytes 3538952 | tf_op jit(solution)/shard_map/ppermute | solution.py:960
  55.9 0.1 shard_map.84
  56.1 2.5 %collective-permute-start.21 = (f32[2,96,1536]{2,1,0:T(8,128)S(1)}, f32[2,96,1536]{2,1,0:T(8,128)S(1)}, u32[]{:S(2)}, u32[]{:S(2)}) collective-permute-start(f32[2,96,1536]{2,1,0:T(8,128)S(1)} %shard_map.84), channel_id=1, source_target_pairs={{0,0},{8,16},{16,8},{24,24},{1,1},{9,17},{17,9},{25,25},{2,2},{10,... | collective-permute-start | bytes 3538952 | tf_op jit(solution)/shard_map/ppermute | solution.py:960
  58.5 1.8 %collective-permute-start.10 = (f32[96,128]{1,0:T(8,128)S(1)}, f32[96,128]{1,0:T(8,128)S(1)}, u32[]{:S(2)}, u32[]{:S(2)}) collective-permute-start(f32[96,128]{1,0:T(8,128)S(1)} %get-tuple-element.99), channel_id=1, source_target_pairs={{0,2},{1,3},{2,0},{3,1},{4,6},{5,7},{6,4},{7,5},{8,10},{9,11},{10,... | collective-permute-start | bytes 147464 | tf_op jit(solution)/shard_map/ppermute | solution.py:74
  60.4 2.2 %collective-permute-start.12 = (f32[96,128]{1,0:T(8,128)S(1)}, f32[96,128]{1,0:T(8,128)S(1)}, u32[]{:S(2)}, u32[]{:S(2)}) collective-permute-start(f32[96,128]{1,0:T(8,128)S(1)} %get-tuple-element.101), channel_id=1, source_target_pairs={{0,6},{1,7},{2,4},{3,5},{4,2},{5,3},{6,0},{7,1},{8,14},{9,15},{10,... | collective-permute-start | bytes 147464 | tf_op jit(solution)/shard_map/ppermute | solution.py:74
  62.5 2.8 %collective-permute-done.11.rest_2_ = f32[96,128]{1,0:T(8,128)S(1)} collective-permute-done((f32[96,128]{1,0:T(8,128)S(1)}, f32[96,128]{1,0:T(8,128)S(1)}, u32[]{:S(2)}, u32[]{:S(2)}) %collective-permute-start.11) | collective-permute-done | bytes 49184 | tf_op jit(solution)/shard_map/ppermute | solution.py:74
  65.3 1.4 %shard_map.85 = (f32[224,128]{1,0:T(8,128)S(1)}, f32[224,128]{1,0:T(8,128)S(1)}) custom-call(s32[1]{0:T(128)} %bitcast.1.index, f32[2,4]{1,0:T(2,128)S(1)} %copy-done.2, f32[4,128]{1,0:T(4,128)S(1)} %get-tuple-element.86.leaving, f32[128,128]{1,0:T(8,128)S(1)} %get-tuple-element.87.inside, f32[96,128]{1,0:T(8,128)S(1)} %get-tuple-element.98.rest_0_, ...), custom_call_target="tpu_custom_call" | custom-call | flops 10 | bytes 10 | tf_op jit(solution)/shard_map/pallas_call | solution.py:692
  66.7 1.4 %collective-permute-start.13 = (f32[224,128]{1,0:T(8,128)S(1)}, f32[224,128]{1,0:T(8,128)S(1)}, u32[]{:S(2)}, u32[]{:S(2)}) collective-permute-start(f32[224,128]{1,0:T(8,128)S(1)} %get-tuple-element.103), channel_id=1, source_target_pairs={{0,1},{1,0},{2,3},{3,2},{4,5},{5,4},{6,7},{7,6},{8,9},{9,8},{10,11... | collective-permute-start | bytes 344072 | tf_op jit(solution)/shard_map/ppermute | solution.py:74
  68.1 3.1 %collective-permute-done.13.came = f32[224,128]{1,0:T(8,128)S(1)} collective-permute-done((f32[224,128]{1,0:T(8,128)S(1)}, f32[224,128]{1,0:T(8,128)S(1)}, u32[]{:S(2)}, u32[]{:S(2)}) %collective-permute-start.13) | collective-permute-done | bytes 114720 | tf_op jit(solution)/shard_map/ppermute | solution.py:74
  71.3 0.8 collective-permute-start.14
  72.1 2.2 %collective-permute-start.15 = (f32[112,128]{1,0:T(8,128)S(1)}, f32[112,128]{1,0:T(8,128)S(1)}, u32[]{:S(2)}, u32[]{:S(2)}) collective-permute-start(f32[112,128]{1,0:T(8,128)S(1)} %get-tuple-element.106), channel_id=1, source_target_pairs={{0,4},{1,5},{2,6},{3,7},{4,0},{5,1},{6,2},{7,3},{8,12},{9,13},{10,... | collective-permute-start | bytes 172040 | tf_op jit(solution)/shard_map/ppermute | solution.py:74
  74.3 0.6 collective-permute-start.16
  74.9 2.0 %collective-permute-done.15.rest_2_ = f32[112,128]{1,0:T(8,128)S(1)} collective-permute-done((f32[112,128]{1,0:T(8,128)S(1)}, f32[112,128]{1,0:T(8,128)S(1)}, u32[]{:S(2)}, u32[]{:S(2)}) %collective-permute-start.15) | collective-permute-done | bytes 57376 | tf_op jit(solution)/shard_map/ppermute | solution.py:74
  76.9 2.3 %collective-permute-done.16.rest_3_ = f32[112,128]{1,0:T(8,128)S(1)} collective-permute-done((f32[112,128]{1,0:T(8,128)S(1)}, f32[112,128]{1,0:T(8,128)S(1)}, u32[]{:S(2)}, u32[]{:S(2)}) %collective-permute-start.16) | collective-permute-done | bytes 57376 | tf_op jit(solution)/shard_map/ppermute | solution.py:74
  79.2 2.1 %collective-permute-start.20 = (f32[2,96,1536]{2,1,0:T(8,128)S(1)}, f32[2,96,1536]{2,1,0:T(8,128)S(1)}, u32[]{:S(2)}, u32[]{:S(2)}) collective-permute-start(f32[2,96,1536]{2,1,0:T(8,128)S(1)} %collective-permute-done.19.met), channel_id=1, source_target_pairs={{0,8},{8,0},{16,24},{24,16},{1,9},{9,1},{17,25},{25,17},{2,10},{10... | collective-permute-start | bytes 3538952 | tf_op jit(solution)/shard_map/ppermute | solution.py:978
  81.4 1.2 %collective-permute-done.21.met = f32[2,96,1536]{2,1,0:T(8,128)S(1)} collective-permute-done((f32[2,96,1536]{2,1,0:T(8,128)S(1)}, f32[2,96,1536]{2,1,0:T(8,128)S(1)}, u32[]{:S(2)}, u32[]{:S(2)}) %collective-permute-start.21) | collective-permute-done | bytes 1179680 | tf_op jit(solution)/shard_map/ppermute | solution.py:960
  82.5 1.7 %collective-permute-start.17 = (f32[448,128]{1,0:T(8,128)S(1)}, f32[448,128]{1,0:T(8,128)S(1)}, u32[]{:S(2)}, u32[]{:S(2)}) collective-permute-start(f32[448,128]{1,0:T(8,128)S(1)} %shard_map.87.rest_0_), channel_id=1, source_target_pairs={{0,16},{16,0},{8,24},{24,8},{1,17},{17,1},{9,25},{25,9},{2,18},{18... | collective-permute-start | bytes 688136 | tf_op jit(solution)/shard_map/ppermute | solution.py:973
  84.3 0.3 collective-permute-start.18
  84.5 1.1 %shard_map.88.rest_4_ = f32[2,2,96,1536]{3,2,1,0:T(8,128)S(1)} custom-call(f32[2,2,96,1536]{3,2,1,0:T(8,128)S(1)} %get-tuple-element.108.own, f32[2,96,1536]{2,1,0:T(8,128)S(1)} %collective-permute-done.8.near, f32[2,96,1536]{2,1,0:T(8,128)S(1)} %collective-permute-done.20.far, f32[2,96,1536]{2,1,0:T(8,128)S(1)} %collective-permute-done.19.met, ...), custom_call_target="tpu_custom_call" | custom-call | flops 10 | bytes 10 | tf_op jit(solution)/shard_map/pallas_call | solution.py:865
  85.6 1.0 %shard_map.89.rest_5_ = f32[2,2,96,1536]{3,2,1,0:T(8,128)S(1)} custom-call(f32[2,2,96,1536]{3,2,1,0:T(8,128)S(1)} %get-tuple-element.110.own, f32[2,96,1536]{2,1,0:T(8,128)S(1)} %collective-permute-done.9.near, f32[2,96,1536]{2,1,0:T(8,128)S(1)} %collective-permute-done.22.far, f32[2,96,1536]{2,1,0:T(8,128)S(1)} %collective-permute-done.21.met, ...), custom_call_target="tpu_custom_call" | custom-call | flops 10 | bytes 10 | tf_op jit(solution)/shard_map/pallas_call | solution.py:865
  86.6 3.2 %collective-permute-done.17.rest_1_ = f32[448,128]{1,0:T(8,128)S(1)} collective-permute-done((f32[448,128]{1,0:T(8,128)S(1)}, f32[448,128]{1,0:T(8,128)S(1)}, u32[]{:S(2)}, u32[]{:S(2)}) %collective-permute-start.17) | collective-permute-done | bytes 229408 | tf_op jit(solution)/shard_map/ppermute | solution.py:973
  89.8 1.1 %collective-permute-start.23 = (f32[448,128]{1,0:T(8,128)S(1)}, f32[448,128]{1,0:T(8,128)S(1)}, u32[]{:S(2)}, u32[]{:S(2)}) collective-permute-start(f32[448,128]{1,0:T(8,128)S(1)} %collective-permute-done.17.rest_1_), channel_id=1, source_target_pairs={{0,8},{8,0},{16,24},{24,16},{1,9},{9,1},{17,25},{25,17},{2,10},{10... | collective-permute-start | bytes 688136 | tf_op jit(solution)/shard_map/ppermute | solution.py:980
  90.8 1.1 %collective-permute-done.23.rest_3_ = f32[448,128]{1,0:T(8,128)S(1)} collective-permute-done((f32[448,128]{1,0:T(8,128)S(1)}, f32[448,128]{1,0:T(8,128)S(1)}, u32[]{:S(2)}, u32[]{:S(2)}) %collective-permute-start.23) | collective-permute-done | bytes 229408 | tf_op jit(solution)/shard_map/ppermute | solution.py:980
  91.9 2.5 %shard_map.90 = f32[2,4,96,1536]{3,2,1,0:T(8,128)} custom-call(f32[2,4,8,128]{3,2,1,0:T(8,128)S(1)} %get-tuple-element.68.mix, f32[448,128]{1,0:T(8,128)S(1)} %shard_map.87.rest_0_, f32[448,128]{1,0:T(8,128)S(1)} %collective-permute-done.17.rest_1_, f32[448,128]{1,0:T(8,128)S(1)} %collective-permute-done.18.rest_2_, ...), custom_call_target="tpu_custom_call" | custom-call | flops 10 | bytes 10 | tf_op jit(solution)/shard_map/pallas_call | solution.py:925
  (26 shorter events, 0.1 us)
Async XLA Ops:
  4.2 8.1 %collective-permute-start.3 = (f32[288,128]{1,0:T(8,128)S(1)}, f32[288,128]{1,0:T(8,128)S(1)}, u32[]{:S(2)}, u32[]{:S(2)}) collective-permute-start(f32[288,128]{1,0:T(8,128)S(1)} %get-tuple-element.61), channel_id=1, source_target_pairs={{0,1},{1,0},{2,3},{3,2},{4,5},{5,4},{6,7},{7,6},{8,9},{9,8},{10,11... | collective-permute-start | bytes 442376 | tf_op jit(solution)/shard_map/ppermute | solution.py:74
  6.3 5.9 %collective-permute-start.2 = (f32[2,4]{1,0:T(2,128)}, f32[2,4]{1,0:T(2,128)S(1)}, u32[]{:S(2)}, u32[]{:S(2)}) collective-permute-start(f32[2,4]{1,0:T(2,128)} %own), channel_id=1, source_target_pairs={{0,24},{24,0},{8,16},{16,8},{1,25},{25,1},{9,17},{17,9},{2,26},{26... | collective-permute-start | bytes 104 | tf_op jit(solution)/shard_map/ppermute | solution.py:1063
  8.4 3.9 %collective-permute-start.1 = (f32[2,4]{1,0:T(2,128)}, f32[2,4]{1,0:T(2,128)S(1)}, u32[]{:S(2)}, u32[]{:S(2)}) collective-permute-start(f32[2,4]{1,0:T(2,128)} %own), channel_id=1, source_target_pairs={{0,8},{8,0},{16,24},{24,16},{1,9},{9,1},{17,25},{25,17},{2,10},{10... | collective-permute-start | bytes 104 | tf_op jit(solution)/shard_map/ppermute | solution.py:1063
  8.4 3.9 %collective-permute-start = (f32[2,4]{1,0:T(2,128)}, f32[2,4]{1,0:T(2,128)S(1)}, u32[]{:S(2)}, u32[]{:S(2)}) collective-permute-start(f32[2,4]{1,0:T(2,128)} %own), channel_id=1, source_target_pairs={{0,16},{16,0},{8,24},{24,8},{1,17},{17,1},{9,25},{25,9},{2,18},{18... | collective-permute-start | bytes 104 | tf_op jit(solution)/shard_map/ppermute | solution.py:1063
  8.6 0.7 copy-start.1
  12.3 7.7 %collective-permute-start.4 = (f32[144,128]{1,0:T(8,128)S(1)}, f32[144,128]{1,0:T(8,128)S(1)}, u32[]{:S(2)}, u32[]{:S(2)}) collective-permute-start(f32[144,128]{1,0:T(8,128)S(1)} %get-tuple-element.76), channel_id=1, source_target_pairs={{0,2},{1,3},{2,0},{3,1},{4,6},{5,7},{6,4},{7,5},{8,10},{9,11},{10,... | collective-permute-start | bytes 221192 | tf_op jit(solution)/shard_map/ppermute | solution.py:74
  13.6 6.4 %collective-permute-start.5 = (f32[144,128]{1,0:T(8,128)S(1)}, f32[144,128]{1,0:T(8,128)S(1)}, u32[]{:S(2)}, u32[]{:S(2)}) collective-permute-start(f32[144,128]{1,0:T(8,128)S(1)} %get-tuple-element.77), channel_id=1, source_target_pairs={{0,4},{1,5},{2,6},{3,7},{4,0},{5,1},{6,2},{7,3},{8,12},{9,13},{10,... | collective-permute-start | bytes 221192 | tf_op jit(solution)/shard_map/ppermute | solution.py:74
  16.0 5.0 %collective-permute-start.6 = (f32[144,128]{1,0:T(8,128)S(1)}, f32[144,128]{1,0:T(8,128)S(1)}, u32[]{:S(2)}, u32[]{:S(2)}) collective-permute-start(f32[144,128]{1,0:T(8,128)S(1)} %get-tuple-element.78), channel_id=1, source_target_pairs={{0,6},{1,7},{2,4},{3,5},{4,2},{5,3},{6,0},{7,1},{8,14},{9,15},{10,... | collective-permute-start | bytes 221192 | tf_op jit(solution)/shard_map/ppermute | solution.py:74
  16.0 3.3 %copy-start.3 = (f32[2,4]{1,0:T(2,128)S(1)}, f32[2,4]{1,0:T(2,128)}, u32[]{:S(2)}) copy-start(f32[2,4]{1,0:T(2,128)} %own) | copy-start | bytes 100
  33.1 16.6 %collective-permute-start.7 = (f32[192,128]{1,0:T(8,128)S(1)}, f32[192,128]{1,0:T(8,128)S(1)}, u32[]{:S(2)}, u32[]{:S(2)}) collective-permute-start(f32[192,128]{1,0:T(8,128)S(1)} %get-tuple-element.89), channel_id=1, source_target_pairs={{0,1},{1,0},{2,3},{3,2},{4,5},{5,4},{6,7},{7,6},{8,9},{9,8},{10,11... | collective-permute-start | bytes 294920 | tf_op jit(solution)/shard_map/ppermute | solution.py:74
  42.7 5.4 %copy-start = (f32[2,4,768]{2,1,0:T(4,128)S(1)}, f32[2,4,768]{2,1,0:T(4,128)}, u32[]{:S(2)}) copy-start(f32[2,4,768]{2,1,0:T(4,128)} %lat_length.3) | copy-start | bytes 73732
  45.1 7.1 %collective-permute-start.8 = (f32[2,96,1536]{2,1,0:T(8,128)S(1)}, f32[2,96,1536]{2,1,0:T(8,128)S(1)}, u32[]{:S(2)}, u32[]{:S(2)}) collective-permute-start(f32[2,96,1536]{2,1,0:T(8,128)S(1)} %get-tuple-element.93), channel_id=1, source_target_pairs={{0,8},{8,0},{16,24},{24,16},{1,9},{9,1},{17,25},{25,17},{2,10},{10... | collective-permute-start | bytes 3538952 | tf_op jit(solution)/shard_map/ppermute | solution.py:954
  52.1 3.8 %collective-permute-start.9 = (f32[2,96,1536]{2,1,0:T(8,128)S(1)}, f32[2,96,1536]{2,1,0:T(8,128)S(1)}, u32[]{:S(2)}, u32[]{:S(2)}) collective-permute-start(f32[2,96,1536]{2,1,0:T(8,128)S(1)} %get-tuple-element.97), channel_id=1, source_target_pairs={{0,8},{8,0},{16,24},{24,16},{1,9},{9,1},{17,25},{25,17},{2,10},{10... | collective-permute-start | bytes 3538952 | tf_op jit(solution)/shard_map/ppermute | solution.py:954
  52.4 13.0 %copy-start.2 = (f32[2,4]{1,0:T(2,128)S(1)}, f32[2,4]{1,0:T(2,128)}, u32[]{:S(2)}) copy-start(f32[2,4]{1,0:T(2,128)} %lon_length.2) | copy-start | bytes 100
  52.4 26.9 %collective-permute-start.19 = (f32[2,96,1536]{2,1,0:T(8,128)S(1)}, f32[2,96,1536]{2,1,0:T(8,128)S(1)}, u32[]{:S(2)}, u32[]{:S(2)}) collective-permute-start(f32[2,96,1536]{2,1,0:T(8,128)S(1)} %shard_map.82), channel_id=1, source_target_pairs={{0,0},{8,16},{16,8},{24,24},{1,1},{9,17},{17,9},{25,25},{2,2},{10,... | collective-permute-start | bytes 3538952 | tf_op jit(solution)/shard_map/ppermute | solution.py:960
  56.1 26.5 %collective-permute-start.21 = (f32[2,96,1536]{2,1,0:T(8,128)S(1)}, f32[2,96,1536]{2,1,0:T(8,128)S(1)}, u32[]{:S(2)}, u32[]{:S(2)}) collective-permute-start(f32[2,96,1536]{2,1,0:T(8,128)S(1)} %shard_map.84), channel_id=1, source_target_pairs={{0,0},{8,16},{16,8},{24,24},{1,1},{9,17},{17,9},{25,25},{2,2},{10,... | collective-permute-start | bytes 3538952 | tf_op jit(solution)/shard_map/ppermute | solution.py:960
  58.5 4.0 %collective-permute-start.10 = (f32[96,128]{1,0:T(8,128)S(1)}, f32[96,128]{1,0:T(8,128)S(1)}, u32[]{:S(2)}, u32[]{:S(2)}) collective-permute-start(f32[96,128]{1,0:T(8,128)S(1)} %get-tuple-element.99), channel_id=1, source_target_pairs={{0,2},{1,3},{2,0},{3,1},{4,6},{5,7},{6,4},{7,5},{8,10},{9,11},{10,... | collective-permute-start | bytes 147464 | tf_op jit(solution)/shard_map/ppermute | solution.py:74
  60.4 5.0 %collective-permute-start.11 = (f32[96,128]{1,0:T(8,128)S(1)}, f32[96,128]{1,0:T(8,128)S(1)}, u32[]{:S(2)}, u32[]{:S(2)}) collective-permute-start(f32[96,128]{1,0:T(8,128)S(1)} %get-tuple-element.100), channel_id=1, source_target_pairs={{0,4},{1,5},{2,6},{3,7},{4,0},{5,1},{6,2},{7,3},{8,12},{9,13},{10,... | collective-permute-start | bytes 147464 | tf_op jit(solution)/shard_map/ppermute | solution.py:74
  60.4 5.0 %collective-permute-start.12 = (f32[96,128]{1,0:T(8,128)S(1)}, f32[96,128]{1,0:T(8,128)S(1)}, u32[]{:S(2)}, u32[]{:S(2)}) collective-permute-start(f32[96,128]{1,0:T(8,128)S(1)} %get-tuple-element.101), channel_id=1, source_target_pairs={{0,6},{1,7},{2,4},{3,5},{4,2},{5,3},{6,0},{7,1},{8,14},{9,15},{10,... | collective-permute-start | bytes 147464 | tf_op jit(solution)/shard_map/ppermute | solution.py:74
  66.7 4.6 %collective-permute-start.13 = (f32[224,128]{1,0:T(8,128)S(1)}, f32[224,128]{1,0:T(8,128)S(1)}, u32[]{:S(2)}, u32[]{:S(2)}) collective-permute-start(f32[224,128]{1,0:T(8,128)S(1)} %get-tuple-element.103), channel_id=1, source_target_pairs={{0,1},{1,0},{2,3},{3,2},{4,5},{5,4},{6,7},{7,6},{8,9},{9,8},{10,11... | collective-permute-start | bytes 344072 | tf_op jit(solution)/shard_map/ppermute | solution.py:74
  71.3 3.6 %collective-permute-start.14 = (f32[112,128]{1,0:T(8,128)S(1)}, f32[112,128]{1,0:T(8,128)S(1)}, u32[]{:S(2)}, u32[]{:S(2)}) collective-permute-start(f32[112,128]{1,0:T(8,128)S(1)} %get-tuple-element.105), channel_id=1, source_target_pairs={{0,2},{1,3},{2,0},{3,1},{4,6},{5,7},{6,4},{7,5},{8,10},{9,11},{10,... | collective-permute-start | bytes 172040 | tf_op jit(solution)/shard_map/ppermute | solution.py:74
  72.1 4.8 %collective-permute-start.15 = (f32[112,128]{1,0:T(8,128)S(1)}, f32[112,128]{1,0:T(8,128)S(1)}, u32[]{:S(2)}, u32[]{:S(2)}) collective-permute-start(f32[112,128]{1,0:T(8,128)S(1)} %get-tuple-element.106), channel_id=1, source_target_pairs={{0,4},{1,5},{2,6},{3,7},{4,0},{5,1},{6,2},{7,3},{8,12},{9,13},{10,... | collective-permute-start | bytes 172040 | tf_op jit(solution)/shard_map/ppermute | solution.py:74
  74.3 4.9 %collective-permute-start.16 = (f32[112,128]{1,0:T(8,128)S(1)}, f32[112,128]{1,0:T(8,128)S(1)}, u32[]{:S(2)}, u32[]{:S(2)}) collective-permute-start(f32[112,128]{1,0:T(8,128)S(1)} %get-tuple-element.107), channel_id=1, source_target_pairs={{0,6},{1,7},{2,4},{3,5},{4,2},{5,3},{6,0},{7,1},{8,14},{9,15},{10,... | collective-permute-start | bytes 172040 | tf_op jit(solution)/shard_map/ppermute | solution.py:74
  79.2 5.3 %collective-permute-start.20 = (f32[2,96,1536]{2,1,0:T(8,128)S(1)}, f32[2,96,1536]{2,1,0:T(8,128)S(1)}, u32[]{:S(2)}, u32[]{:S(2)}) collective-permute-start(f32[2,96,1536]{2,1,0:T(8,128)S(1)} %collective-permute-done.19.met), channel_id=1, source_target_pairs={{0,8},{8,0},{16,24},{24,16},{1,9},{9,1},{17,25},{25,17},{2,10},{10... | collective-permute-start | bytes 3538952 | tf_op jit(solution)/shard_map/ppermute | solution.py:978
  82.5 3.1 %collective-permute-start.22 = (f32[2,96,1536]{2,1,0:T(8,128)S(1)}, f32[2,96,1536]{2,1,0:T(8,128)S(1)}, u32[]{:S(2)}, u32[]{:S(2)}) collective-permute-start(f32[2,96,1536]{2,1,0:T(8,128)S(1)} %collective-permute-done.21.met), channel_id=1, source_target_pairs={{0,8},{8,0},{16,24},{24,16},{1,9},{9,1},{17,25},{25,17},{2,10},{10... | collective-permute-start | bytes 3538952 | tf_op jit(solution)/shard_map/ppermute | solution.py:978
  82.5 7.2 %collective-permute-start.17 = (f32[448,128]{1,0:T(8,128)S(1)}, f32[448,128]{1,0:T(8,128)S(1)}, u32[]{:S(2)}, u32[]{:S(2)}) collective-permute-start(f32[448,128]{1,0:T(8,128)S(1)} %shard_map.87.rest_0_), channel_id=1, source_target_pairs={{0,16},{16,0},{8,24},{24,8},{1,17},{17,1},{9,25},{25,9},{2,18},{18... | collective-permute-start | bytes 688136 | tf_op jit(solution)/shard_map/ppermute | solution.py:973
  84.3 6.6 %collective-permute-start.18 = (f32[448,128]{1,0:T(8,128)S(1)}, f32[448,128]{1,0:T(8,128)S(1)}, u32[]{:S(2)}, u32[]{:S(2)}) collective-permute-start(f32[448,128]{1,0:T(8,128)S(1)} %shard_map.87.rest_0_), channel_id=1, source_target_pairs={{0,8},{8,0},{16,24},{24,16},{1,9},{9,1},{17,25},{25,17},{2,10},{10... | collective-permute-start | bytes 688136 | tf_op jit(solution)/shard_map/ppermute | solution.py:974
  89.8 2.2 %collective-permute-start.23 = (f32[448,128]{1,0:T(8,128)S(1)}, f32[448,128]{1,0:T(8,128)S(1)}, u32[]{:S(2)}, u32[]{:S(2)}) collective-permute-start(f32[448,128]{1,0:T(8,128)S(1)} %collective-permute-done.17.rest_1_), channel_id=1, source_target_pairs={{0,8},{8,0},{16,24},{24,16},{1,9},{9,1},{17,25},{25,17},{2,10},{10... | collective-permute-start | bytes 688136 | tf_op jit(solution)/shard_map/ppermute | solution.py:980

commit v7 on v6

--- a/solution.py
+++ b/solution.py
@@ -147,7 +147,7 @@
             sorted_[block, tile] = moved[tile * SUBLANES : (tile + 1) * SUBLANES]
         return carry
 
-    lax.fori_loop(0, block_count, sort_block, 0, unroll=8)
+    lax.fori_loop(0, block_count, sort_block, 0, unroll=16)
     copy.wait()
 
     def join_block(block, ends):
@@ -167,7 +167,7 @@
             joined[sub, chunk + 1, tile] = turned
         return tuple(following)
 
-    ends = lax.fori_loop(0, block_count, join_block, (jnp.int32(0),) * sub_count, unroll=2)
+    ends = lax.fori_loop(0, block_count, join_block, (jnp.int32(0),) * sub_count, unroll=8)
     word_row = chunk_count * group_count
     word_rows = packed.shape[1] - word_row
     for sub in range(sub_count):
@@ -318,6 +318,14 @@
         def more(chunk):
             last = jnp.minimum(chunk, chunk_count - 1)
             return (chunk < chunk_count) & (words[first + last, 0] < 8 * strip)
+
+        def two_more(chunk):
+            last = jnp.minimum(chunk + 1, chunk_count - 1)
+            return (chunk + 1 < chunk_count) & (words[first + last, 0] < 8 * strip)
+
+        def two_chunks(chunk):
+            one_chunk(chunk)
+            return one_chunk(chunk + 1)
 
         def one_chunk(chunk):
             blocks = [
@@ -339,7 +347,8 @@
                     total[tile, at, :] = total[tile, at, :] + value
             return chunk + 1
 
-        lax.while_loop(more, one_chunk, jnp.int32(0))
+        done = lax.while_loop(two_more, two_chunks, jnp.int32(0))
+        lax.while_loop(more, one_chunk, done)
         return carry
 
     flat = [total.reshape(tiles, -1, LANES) for total in totals]
@@ -402,7 +411,7 @@
         out_specs=[VMEM] * (1 + len(away) + CHAINS),
         scratch_shapes=[
             pltpu.VMEM((sub_count, rows, LANES), f32),
-            pltpu.VMEM((group_count * exit_rows, LANES), f32),
+            pltpu.VMEM(((group_count + 1) * exit_rows, LANES), f32),
             pltpu.VMEM((sub_count * word_rows, LANES), i32),
             pltpu.SMEM((sub_count * word_rows, LANES), i32),
             pltpu.SemaphoreType.DMA((sub_count,)),
@@ -663,7 +672,7 @@
         ]
         pieces.append(jnp.concatenate(pair, axis=1))
     pieces = circle(pieces, *[weight[0] for weight in weights])
-    message_rows = out.shape[0] // sub_count
+    message_rows = rows + 8
     for at, piece in enumerate(pieces):
         for k in range(2):
             for turn in range(4):
@@ -695,8 +704,8 @@
         out_specs=[VMEM] * len(away),
         scratch_shapes=[
             pltpu.VMEM((sub_count, rows, LANES), f32),
-            pltpu.VMEM((sub_count * message_rows, LANES), f32),
-            pltpu.VMEM((sub_count * rows, LANES), f32),
+            pltpu.VMEM(((sub_count + 1) * message_rows, LANES), f32),
+            pltpu.VMEM(((sub_count + 1) * rows, LANES), f32),
         ]
         + [pltpu.VMEM((1,) + shape, bf16) for shape in weight_shapes(column_total)],
         out_shape=[
@@ -877,7 +886,7 @@
     messages, dense = dense[:4], dense[4:]
     _, _, row_count, column_total = dense[0].shape
     column_count = column_total // LANES
-    stride = message.shape[0] // SUBLANES
+    stride = messages[0].shape[0] // SUBLANES
     copies = []
     for chunk, variables in enumerate(CHUNKS):
         for place, variable in enumerate(variables):
@@ -929,7 +938,7 @@
         out_shape=pltpu.HBM((2, 4, row_count, column_total), f32),
         scratch_shapes=[
             pltpu.VMEM((4, 2, row_count, column_total), f32),
-            pltpu.VMEM(messages[0].shape, f32),
+            pltpu.VMEM((messages[0].shape[0] * 9 // 8, LANES), f32),
             pltpu.SemaphoreType.DMA((8,)),
         ],
         compiler_params=params(12),

time: 95 us -> 94.2 us (level)
  starting transfers between devices: 40.9 us -> 30.9 us
  Pallas kernels: 36 us -> 44.5 us
    ppermute x12, starting transfers between devices: 24.4 us -> 14.5 us  [move(): return lax.ppermute(part, 'sub', [(at, at ^ k) for at in range(sub_count)])]
    pallas_call x1, Pallas kernels: 12.1 us -> 21.4 us  [deposit_and_sweep(): pl.pallas_call(functools.partial(deposit_kernel, sizes), out_shape=[pltpu...]
  transfers between devices with their start and end apart: 24 -> 24, of which waited for: 8 -> 10; matrix products, arithmetic and copies ran while one was open for 0% -> 0% of each run, Pallas kernels for 18% -> 18%
where the time goes in v7:
time: 94.2 us; the launch traced here: 93.6 us
  Pallas kernels  44.5 us (47%)
  starting transfers between devices  30.9 us (33%)
  waiting for transfers between devices  17.1 us (18%)
    pallas_call x1, Pallas kernels, deposit_and_sweep(): pl.pallas_call(functools.partial(deposit_kernel, sizes), out_shape=[pltpu...  21.4 us
    ppermute x12, starting transfers between devices, move(): return lax.ppermute(part, 'sub', [(at, at ^ k) for at in range(sub_count)])  14.5 us
    ppermute x12, waiting for transfers between devices, move(): return lax.ppermute(part, 'sub', [(at, at ^ k) for at in range(sub_count)])  10.9 us
    ppermute x2, starting transfers between devices, cross_some(): mets.append(lax.ppermute(total, 'band', MIDDLE))  5.88 us
    pallas_call x2, Pallas kernels, longitude_pair(): pl.pallas_call(functools.partial(pair_kernel, variables), in_specs=[VMEM]...  4.97 us
    pallas_call x1, Pallas kernels, pack_observations(): pl.pallas_call(functools.partial(pack_kernel, (sub_count, group_count, ch...  3.33 us
    pallas_call x1, Pallas kernels, make_ready(): pl.pallas_call(functools.partial(ready_kernel, sizes), in_specs=[SMEM, HB...  3.33 us
    ppermute x2, starting transfers between devices, filter_some(): nears.append(lax.ppermute(sent, 'band', SWAP))  3.22 us
  transfers between devices with their start and end apart: 24, of which 10 were waited for; matrix products, arithmetic and copies ran while one was open for 0% of the time, Pallas kernels for 18%

profile of v7, /device:TPU:1, one launch (start us, length us, event | category | flops | bytes accessed | tf_op | source)
XLA Modules:
  0.0 93.6 jit_solution(11528165093847247397)
XLA Ops:
  0.0 3.3 %shard_map.73 = (f32[288,128]{1,0:T(8,128)S(1)}, f32[288,128]{1,0:T(8,128)S(1)}) custom-call(s32[1]{0:T(128)} %bitcast.1.index, s32[32,128]{1,0:T(8,128)} %bitcast.6, s32[32,128]{1,0:T(8,128)} %bitcast.7, f32[2,4,4096]{2,1,0:T(4,128)} %values.1), custom_call_target="tpu_custom_call" | custom-call | flops 10 | bytes 10 | tf_op jit(solution)/shard_map/pallas_call | solution.py:198
  3.3 2.1 %collective-permute-start.3 = (f32[288,128]{1,0:T(8,128)S(1)}, f32[288,128]{1,0:T(8,128)S(1)}, u32[]{:S(2)}, u32[]{:S(2)}) collective-permute-start(f32[288,128]{1,0:T(8,128)S(1)} %get-tuple-element.61), channel_id=1, source_target_pairs={{0,1},{1,0},{2,3},{3,2},{4,5},{5,4},{6,7},{7,6},{8,9},{9,8},{10,11... | collective-permute-start | bytes 442376 | tf_op jit(solution)/shard_map/ppermute | solution.py:74
  5.5 2.1 %collective-permute-start.2 = (f32[2,4]{1,0:T(2,128)}, f32[2,4]{1,0:T(2,128)S(1)}, u32[]{:S(2)}, u32[]{:S(2)}) collective-permute-start(f32[2,4]{1,0:T(2,128)} %own), channel_id=1, source_target_pairs={{0,24},{24,0},{8,16},{16,8},{1,25},{25,1},{9,17},{17,9},{2,26},{26... | collective-permute-start | bytes 104 | tf_op jit(solution)/shard_map/ppermute | solution.py:1072
  7.5 0.2 collective-permute-start
  7.8 0.7 copy-done.1
  8.4 2.9 %shard_map.74 = (bf16[8,256,256]{2,1,0:T(8,128)(2,1)S(1)}, bf16[8,256,256]{2,1,0:T(8,128)(2,1)S(1)}, bf16[8,256,256]{2,1,0:T(8,128)(2,1)S(1)}, bf16[8,64,1536]{2,1,0:T(8,128)(2,1)S(1)}) custom-call(f32[2,4]{1,0:T(2,128)S(1)} %copy-done.1), custom_call_target="tpu_custom_call" | custom-call | flops 10 | bytes 10 | tf_op jit(solution)/shard_map/pallas_call | solution.py:529
  11.5 1.4 %collective-permute-start.4 = (f32[144,128]{1,0:T(8,128)S(1)}, f32[144,128]{1,0:T(8,128)S(1)}, u32[]{:S(2)}, u32[]{:S(2)}) collective-permute-start(f32[144,128]{1,0:T(8,128)S(1)} %get-tuple-element.76), channel_id=1, source_target_pairs={{0,2},{1,3},{2,0},{3,1},{4,6},{5,7},{6,4},{7,5},{8,10},{9,11},{10,... | collective-permute-start | bytes 221192 | tf_op jit(solution)/shard_map/ppermute | solution.py:74
  12.8 2.3 %collective-permute-start.5 = (f32[144,128]{1,0:T(8,128)S(1)}, f32[144,128]{1,0:T(8,128)S(1)}, u32[]{:S(2)}, u32[]{:S(2)}) collective-permute-start(f32[144,128]{1,0:T(8,128)S(1)} %get-tuple-element.77), channel_id=1, source_target_pairs={{0,4},{1,5},{2,6},{3,7},{4,0},{5,1},{6,2},{7,3},{8,12},{9,13},{10,... | collective-permute-start | bytes 221192 | tf_op jit(solution)/shard_map/ppermute | solution.py:74
  15.1 3.3 %shard_map.77 = (f32[96,1,8,128]{3,2,1,0:T(8,128)S(1)}, f32[1,97,12,8,128]{4,3,2,1,0:T(8,128)S(1)}, f32[1,97,12,8,128]{4,3,2,1,0:T(8,128)S(1)}, f32[1,97,12,8,12...) custom-call(s32[1]{0:T(128)} %bitcast.1.index, f32[2,4,768]{2,1,0:T(4,128)} %lat_length.3, f32[8,96,1536]{2,1,0:T(8,128)} %bitcast.5), custom_call_target="tpu_custom_call" | custom-call | flops 10 | bytes 10 | tf_op jit(solution)/shard_map/pallas_call | solution.py:271
  18.5 0.7 shard_map.76
  19.2 0.9 collective-permute-done.6.rest_3_
  20.1 21.4 %shard_map.78 = (f32[12,8,96,128]{3,2,1,0:T(8,128)S(1)}, f32[192,128]{1,0:T(8,128)S(1)}, f32[192,128]{1,0:T(8,128)S(1)}, f32[1,97,12,8,128]{4,3,2,1,0:T(8,128)S(...) custom-call(s32[1]{0:T(128)} %bitcast.1.index, ...), custom_call_target="tpu_custom_call", output_to_operand_aliasing={{3}: (6, {}), {4}: (7, {}), {5}: (8, {}), {6}: (9, {})} | custom-call | flops 10 | bytes 10 | tf_op jit(solution)/shard_map/pallas_call | solution.py:405
  41.6 0.1 collective-permute-start.7
  41.6 0.0 copy-start
  41.6 2.5 %shard_map.79 = (f32[2,2,96,1536]{3,2,1,0:T(8,128)S(1)}, f32[2,96,1536]{2,1,0:T(8,128)S(1)}, f32[2,96,1536]{2,1,0:T(8,128)S(1)}) custom-call(f32[12,8,96,128]{3,2,1,0:T(8,128)S(1)} %get-tuple-element.90.swept, bf16[8,256,256]{2,1,0:T(8,128)(2,1)S(1)} %get-tuple-element.64.near_high, bf16[8,256,256]{2,1,0:T(8,128)(2,1)S(1)} %get-tuple-element.71.near_low, ...), custom_call_target="tpu_custom_call" | custom-call | flops 10 | bytes 10 | tf_op jit(solution)/shard_map/pallas_call | solution.py:601
  44.1 2.7 %collective-permute-start.8 = (f32[2,96,1536]{2,1,0:T(8,128)S(1)}, f32[2,96,1536]{2,1,0:T(8,128)S(1)}, u32[]{:S(2)}, u32[]{:S(2)}) collective-permute-start(f32[2,96,1536]{2,1,0:T(8,128)S(1)} %get-tuple-element.93), channel_id=1, source_target_pairs={{0,8},{8,0},{16,24},{24,16},{1,9},{9,1},{17,25},{25,17},{2,10},{10... | collective-permute-start | bytes 3538952 | tf_op jit(solution)/shard_map/ppermute | solution.py:963
  46.8 1.5 %shard_map.80 = (f32[128,128]{1,0:T(8,128)S(1)}, f32[4,128]{1,0:T(4,128)S(1)}) custom-call(s32[1]{0:T(128)} %bitcast.1.index, f32[2,4,768]{2,1,0:T(4,128)S(1)} %copy-done), custom_call_target="tpu_custom_call" | custom-call | flops 10 | bytes 10 | tf_op jit(solution)/shard_map/pallas_call | solution.py:456
  48.3 2.5 %shard_map.81 = (f32[2,2,96,1536]{3,2,1,0:T(8,128)S(1)}, f32[2,96,1536]{2,1,0:T(8,128)S(1)}, f32[2,96,1536]{2,1,0:T(8,128)S(1)}) custom-call(f32[12,8,96,128]{3,2,1,0:T(8,128)S(1)} %get-tuple-element.90.swept, bf16[8,256,256]{2,1,0:T(8,128)(2,1)S(1)} %get-tuple-element.64.near_high, bf16[8,256,256]{2,1,0:T(8,128)(2,1)S(1)} %get-tuple-element.71.near_low, ...), custom_call_target="tpu_custom_call" | custom-call | flops 10 | bytes 10 | tf_op jit(solution)/shard_map/pallas_call | solution.py:601
  50.8 0.6 collective-permute-start.9
  51.4 0.1 shard_map.82
  51.5 0.0 copy-start.2
  51.5 3.1 %collective-permute-start.19 = (f32[2,96,1536]{2,1,0:T(8,128)S(1)}, f32[2,96,1536]{2,1,0:T(8,128)S(1)}, u32[]{:S(2)}, u32[]{:S(2)}) collective-permute-start(f32[2,96,1536]{2,1,0:T(8,128)S(1)} %shard_map.82), channel_id=1, source_target_pairs={{0,0},{8,16},{16,8},{24,24},{1,1},{9,17},{17,9},{25,25},{2,2},{10,... | collective-permute-start | bytes 3538952 | tf_op jit(solution)/shard_map/ppermute | solution.py:969
  54.6 0.1 shard_map.84
  54.8 2.8 %collective-permute-start.21 = (f32[2,96,1536]{2,1,0:T(8,128)S(1)}, f32[2,96,1536]{2,1,0:T(8,128)S(1)}, u32[]{:S(2)}, u32[]{:S(2)}) collective-permute-start(f32[2,96,1536]{2,1,0:T(8,128)S(1)} %shard_map.84), channel_id=1, source_target_pairs={{0,0},{8,16},{16,8},{24,24},{1,1},{9,17},{17,9},{25,25},{2,2},{10,... | collective-permute-start | bytes 3538952 | tf_op jit(solution)/shard_map/ppermute | solution.py:969
  57.6 0.1 collective-permute-start.10
  57.7 0.1 collective-permute-start.11
  57.8 3.5 %collective-permute-start.12 = (f32[96,128]{1,0:T(8,128)S(1)}, f32[96,128]{1,0:T(8,128)S(1)}, u32[]{:S(2)}, u32[]{:S(2)}) collective-permute-start(f32[96,128]{1,0:T(8,128)S(1)} %get-tuple-element.101), channel_id=1, source_target_pairs={{0,6},{1,7},{2,4},{3,5},{4,2},{5,3},{6,0},{7,1},{8,14},{9,15},{10,... | collective-permute-start | bytes 147464 | tf_op jit(solution)/shard_map/ppermute | solution.py:74
  61.2 1.0 %collective-permute-done.11.rest_2_ = f32[96,128]{1,0:T(8,128)S(1)} collective-permute-done((f32[96,128]{1,0:T(8,128)S(1)}, f32[96,128]{1,0:T(8,128)S(1)}, u32[]{:S(2)}, u32[]{:S(2)}) %collective-permute-start.11) | collective-permute-done | bytes 49184 | tf_op jit(solution)/shard_map/ppermute | solution.py:74
  62.2 1.1 %collective-permute-done.12.rest_3_ = f32[96,128]{1,0:T(8,128)S(1)} collective-permute-done((f32[96,128]{1,0:T(8,128)S(1)}, f32[96,128]{1,0:T(8,128)S(1)}, u32[]{:S(2)}, u32[]{:S(2)}) %collective-permute-start.12) | collective-permute-done | bytes 49184 | tf_op jit(solution)/shard_map/ppermute | solution.py:74
  63.3 1.4 %shard_map.85 = (f32[224,128]{1,0:T(8,128)S(1)}, f32[224,128]{1,0:T(8,128)S(1)}) custom-call(s32[1]{0:T(128)} %bitcast.1.index, f32[2,4]{1,0:T(2,128)S(1)} %copy-done.2, f32[4,128]{1,0:T(4,128)S(1)} %get-tuple-element.86.leaving, f32[128,128]{1,0:T(8,128)S(1)} %get-tuple-element.87.inside, f32[96,128]{1,0:T(8,128)S(1)} %get-tuple-element.98.rest_0_, ...), custom_call_target="tpu_custom_call" | custom-call | flops 10 | bytes 10 | tf_op jit(solution)/shard_map/pallas_call | solution.py:701
  64.7 1.4 %collective-permute-start.13 = (f32[224,128]{1,0:T(8,128)S(1)}, f32[224,128]{1,0:T(8,128)S(1)}, u32[]{:S(2)}, u32[]{:S(2)}) collective-permute-start(f32[224,128]{1,0:T(8,128)S(1)} %get-tuple-element.103), channel_id=1, source_target_pairs={{0,1},{1,0},{2,3},{3,2},{4,5},{5,4},{6,7},{7,6},{8,9},{9,8},{10,11... | collective-permute-start | bytes 344072 | tf_op jit(solution)/shard_map/ppermute | solution.py:74
  66.1 3.0 %collective-permute-done.13.came = f32[224,128]{1,0:T(8,128)S(1)} collective-permute-done((f32[224,128]{1,0:T(8,128)S(1)}, f32[224,128]{1,0:T(8,128)S(1)}, u32[]{:S(2)}, u32[]{:S(2)}) %collective-permute-start.13) | collective-permute-done | bytes 114720 | tf_op jit(solution)/shard_map/ppermute | solution.py:74
  69.2 0.1 collective-permute-start.14
  69.3 3.4 %collective-permute-start.15 = (f32[112,128]{1,0:T(8,128)S(1)}, f32[112,128]{1,0:T(8,128)S(1)}, u32[]{:S(2)}, u32[]{:S(2)}) collective-permute-start(f32[112,128]{1,0:T(8,128)S(1)} %get-tuple-element.106), channel_id=1, source_target_pairs={{0,4},{1,5},{2,6},{3,7},{4,0},{5,1},{6,2},{7,3},{8,12},{9,13},{10,... | collective-permute-start | bytes 172040 | tf_op jit(solution)/shard_map/ppermute | solution.py:74
  72.6 0.2 collective-permute-start.16
  72.8 1.6 %collective-permute-done.15.rest_2_ = f32[112,128]{1,0:T(8,128)S(1)} collective-permute-done((f32[112,128]{1,0:T(8,128)S(1)}, f32[112,128]{1,0:T(8,128)S(1)}, u32[]{:S(2)}, u32[]{:S(2)}) %collective-permute-start.15) | collective-permute-done | bytes 57376 | tf_op jit(solution)/shard_map/ppermute | solution.py:74
  74.4 3.2 %collective-permute-done.16.rest_3_ = f32[112,128]{1,0:T(8,128)S(1)} collective-permute-done((f32[112,128]{1,0:T(8,128)S(1)}, f32[112,128]{1,0:T(8,128)S(1)}, u32[]{:S(2)}, u32[]{:S(2)}) %collective-permute-start.16) | collective-permute-done | bytes 57376 | tf_op jit(solution)/shard_map/ppermute | solution.py:74
  77.6 2.1 %collective-permute-start.20 = (f32[2,96,1536]{2,1,0:T(8,128)S(1)}, f32[2,96,1536]{2,1,0:T(8,128)S(1)}, u32[]{:S(2)}, u32[]{:S(2)}) collective-permute-start(f32[2,96,1536]{2,1,0:T(8,128)S(1)} %collective-permute-done.19.met), channel_id=1, source_target_pairs={{0,8},{8,0},{16,24},{24,16},{1,9},{9,1},{17,25},{25,17},{2,10},{10... | collective-permute-start | bytes 3538952 | tf_op jit(solution)/shard_map/ppermute | solution.py:987
  79.7 2.0 %collective-permute-done.21.met = f32[2,96,1536]{2,1,0:T(8,128)S(1)} collective-permute-done((f32[2,96,1536]{2,1,0:T(8,128)S(1)}, f32[2,96,1536]{2,1,0:T(8,128)S(1)}, u32[]{:S(2)}, u32[]{:S(2)}) %collective-permute-start.21) | collective-permute-done | bytes 1179680 | tf_op jit(solution)/shard_map/ppermute | solution.py:969
  81.7 1.3 %collective-permute-start.17 = (f32[448,128]{1,0:T(8,128)S(1)}, f32[448,128]{1,0:T(8,128)S(1)}, u32[]{:S(2)}, u32[]{:S(2)}) collective-permute-start(f32[448,128]{1,0:T(8,128)S(1)} %shard_map.87.rest_0_), channel_id=1, source_target_pairs={{0,16},{16,0},{8,24},{24,8},{1,17},{17,1},{9,25},{25,9},{2,18},{18... | collective-permute-start | bytes 688136 | tf_op jit(solution)/shard_map/ppermute | solution.py:982
  83.0 0.3 collective-permute-start.18
  83.3 1.1 %shard_map.88.rest_4_ = f32[2,2,96,1536]{3,2,1,0:T(8,128)S(1)} custom-call(f32[2,2,96,1536]{3,2,1,0:T(8,128)S(1)} %get-tuple-element.108.own, f32[2,96,1536]{2,1,0:T(8,128)S(1)} %collective-permute-done.8.near, f32[2,96,1536]{2,1,0:T(8,128)S(1)} %collective-permute-done.20.far, f32[2,96,1536]{2,1,0:T(8,128)S(1)} %collective-permute-done.19.met, ...), custom_call_target="tpu_custom_call" | custom-call | flops 10 | bytes 10 | tf_op jit(solution)/shard_map/pallas_call | solution.py:874
  84.3 0.2 collective-permute-done.22.far
  84.6 1.0 %shard_map.89.rest_5_ = f32[2,2,96,1536]{3,2,1,0:T(8,128)S(1)} custom-call(f32[2,2,96,1536]{3,2,1,0:T(8,128)S(1)} %get-tuple-element.110.own, f32[2,96,1536]{2,1,0:T(8,128)S(1)} %collective-permute-done.9.near, f32[2,96,1536]{2,1,0:T(8,128)S(1)} %collective-permute-done.22.far, f32[2,96,1536]{2,1,0:T(8,128)S(1)} %collective-permute-done.21.met, ...), custom_call_target="tpu_custom_call" | custom-call | flops 10 | bytes 10 | tf_op jit(solution)/shard_map/pallas_call | solution.py:874
  85.5 2.9 %collective-permute-done.17.rest_1_ = f32[448,128]{1,0:T(8,128)S(1)} collective-permute-done((f32[448,128]{1,0:T(8,128)S(1)}, f32[448,128]{1,0:T(8,128)S(1)}, u32[]{:S(2)}, u32[]{:S(2)}) %collective-permute-start.17) | collective-permute-done | bytes 229408 | tf_op jit(solution)/shard_map/ppermute | solution.py:982
  88.4 1.4 %collective-permute-start.23 = (f32[448,128]{1,0:T(8,128)S(1)}, f32[448,128]{1,0:T(8,128)S(1)}, u32[]{:S(2)}, u32[]{:S(2)}) collective-permute-start(f32[448,128]{1,0:T(8,128)S(1)} %collective-permute-done.17.rest_1_), channel_id=1, source_target_pairs={{0,8},{8,0},{16,24},{24,16},{1,9},{9,1},{17,25},{25,17},{2,10},{10... | collective-permute-start | bytes 688136 | tf_op jit(solution)/shard_map/ppermute | solution.py:989
  89.7 1.1 %collective-permute-done.23.rest_3_ = f32[448,128]{1,0:T(8,128)S(1)} collective-permute-done((f32[448,128]{1,0:T(8,128)S(1)}, f32[448,128]{1,0:T(8,128)S(1)}, u32[]{:S(2)}, u32[]{:S(2)}) %collective-permute-start.23) | collective-permute-done | bytes 229408 | tf_op jit(solution)/shard_map/ppermute | solution.py:989
  90.8 2.5 %shard_map.90 = f32[2,4,96,1536]{3,2,1,0:T(8,128)} custom-call(f32[2,4,8,128]{3,2,1,0:T(8,128)S(1)} %get-tuple-element.68.mix, f32[448,128]{1,0:T(8,128)S(1)} %shard_map.87.rest_0_, f32[448,128]{1,0:T(8,128)S(1)} %collective-permute-done.17.rest_1_, f32[448,128]{1,0:T(8,128)S(1)} %collective-permute-done.18.rest_2_, ...), custom_call_target="tpu_custom_call" | custom-call | flops 10 | bytes 10 | tf_op jit(solution)/shard_map/pallas_call | solution.py:934
  (26 shorter events, 0.1 us)
Async XLA Ops:
  3.3 8.1 %collective-permute-start.3 = (f32[288,128]{1,0:T(8,128)S(1)}, f32[288,128]{1,0:T(8,128)S(1)}, u32[]{:S(2)}, u32[]{:S(2)}) collective-permute-start(f32[288,128]{1,0:T(8,128)S(1)} %get-tuple-element.61), channel_id=1, source_target_pairs={{0,1},{1,0},{2,3},{3,2},{4,5},{5,4},{6,7},{7,6},{8,9},{9,8},{10,11... | collective-permute-start | bytes 442376 | tf_op jit(solution)/shard_map/ppermute | solution.py:74
  5.5 5.9 %collective-permute-start.2 = (f32[2,4]{1,0:T(2,128)}, f32[2,4]{1,0:T(2,128)S(1)}, u32[]{:S(2)}, u32[]{:S(2)}) collective-permute-start(f32[2,4]{1,0:T(2,128)} %own), channel_id=1, source_target_pairs={{0,24},{24,0},{8,16},{16,8},{1,25},{25,1},{9,17},{17,9},{2,26},{26... | collective-permute-start | bytes 104 | tf_op jit(solution)/shard_map/ppermute | solution.py:1072
  7.5 3.9 %collective-permute-start.1 = (f32[2,4]{1,0:T(2,128)}, f32[2,4]{1,0:T(2,128)S(1)}, u32[]{:S(2)}, u32[]{:S(2)}) collective-permute-start(f32[2,4]{1,0:T(2,128)} %own), channel_id=1, source_target_pairs={{0,8},{8,0},{16,24},{24,16},{1,9},{9,1},{17,25},{25,17},{2,10},{10... | collective-permute-start | bytes 104 | tf_op jit(solution)/shard_map/ppermute | solution.py:1072
  7.5 3.9 %collective-permute-start = (f32[2,4]{1,0:T(2,128)}, f32[2,4]{1,0:T(2,128)S(1)}, u32[]{:S(2)}, u32[]{:S(2)}) collective-permute-start(f32[2,4]{1,0:T(2,128)} %own), channel_id=1, source_target_pairs={{0,16},{16,0},{8,24},{24,8},{1,17},{17,1},{9,25},{25,9},{2,18},{18... | collective-permute-start | bytes 104 | tf_op jit(solution)/shard_map/ppermute | solution.py:1072
  7.8 0.7 copy-start.1
  11.5 7.7 %collective-permute-start.4 = (f32[144,128]{1,0:T(8,128)S(1)}, f32[144,128]{1,0:T(8,128)S(1)}, u32[]{:S(2)}, u32[]{:S(2)}) collective-permute-start(f32[144,128]{1,0:T(8,128)S(1)} %get-tuple-element.76), channel_id=1, source_target_pairs={{0,2},{1,3},{2,0},{3,1},{4,6},{5,7},{6,4},{7,5},{8,10},{9,11},{10,... | collective-permute-start | bytes 221192 | tf_op jit(solution)/shard_map/ppermute | solution.py:74
  12.8 6.4 %collective-permute-start.5 = (f32[144,128]{1,0:T(8,128)S(1)}, f32[144,128]{1,0:T(8,128)S(1)}, u32[]{:S(2)}, u32[]{:S(2)}) collective-permute-start(f32[144,128]{1,0:T(8,128)S(1)} %get-tuple-element.77), channel_id=1, source_target_pairs={{0,4},{1,5},{2,6},{3,7},{4,0},{5,1},{6,2},{7,3},{8,12},{9,13},{10,... | collective-permute-start | bytes 221192 | tf_op jit(solution)/shard_map/ppermute | solution.py:74
  15.1 5.0 %collective-permute-start.6 = (f32[144,128]{1,0:T(8,128)S(1)}, f32[144,128]{1,0:T(8,128)S(1)}, u32[]{:S(2)}, u32[]{:S(2)}) collective-permute-start(f32[144,128]{1,0:T(8,128)S(1)} %get-tuple-element.78), channel_id=1, source_target_pairs={{0,6},{1,7},{2,4},{3,5},{4,2},{5,3},{6,0},{7,1},{8,14},{9,15},{10,... | collective-permute-start | bytes 221192 | tf_op jit(solution)/shard_map/ppermute | solution.py:74
  15.1 3.3 %copy-start.3 = (f32[2,4]{1,0:T(2,128)S(1)}, f32[2,4]{1,0:T(2,128)}, u32[]{:S(2)}) copy-start(f32[2,4]{1,0:T(2,128)} %own) | copy-start | bytes 100
  41.6 6.8 %collective-permute-start.7 = (f32[192,128]{1,0:T(8,128)S(1)}, f32[192,128]{1,0:T(8,128)S(1)}, u32[]{:S(2)}, u32[]{:S(2)}) collective-permute-start(f32[192,128]{1,0:T(8,128)S(1)} %get-tuple-element.89), channel_id=1, source_target_pairs={{0,1},{1,0},{2,3},{3,2},{4,5},{5,4},{6,7},{7,6},{8,9},{9,8},{10,11... | collective-permute-start | bytes 294920 | tf_op jit(solution)/shard_map/ppermute | solution.py:74
  41.6 5.2 %copy-start = (f32[2,4,768]{2,1,0:T(4,128)S(1)}, f32[2,4,768]{2,1,0:T(4,128)}, u32[]{:S(2)}) copy-start(f32[2,4,768]{2,1,0:T(4,128)} %lat_length.3) | copy-start | bytes 73732
  44.1 7.3 %collective-permute-start.8 = (f32[2,96,1536]{2,1,0:T(8,128)S(1)}, f32[2,96,1536]{2,1,0:T(8,128)S(1)}, u32[]{:S(2)}, u32[]{:S(2)}) collective-permute-start(f32[2,96,1536]{2,1,0:T(8,128)S(1)} %get-tuple-element.93), channel_id=1, source_target_pairs={{0,8},{8,0},{16,24},{24,16},{1,9},{9,1},{17,25},{25,17},{2,10},{10... | collective-permute-start | bytes 3538952 | tf_op jit(solution)/shard_map/ppermute | solution.py:963
  50.8 3.8 %collective-permute-start.9 = (f32[2,96,1536]{2,1,0:T(8,128)S(1)}, f32[2,96,1536]{2,1,0:T(8,128)S(1)}, u32[]{:S(2)}, u32[]{:S(2)}) collective-permute-start(f32[2,96,1536]{2,1,0:T(8,128)S(1)} %get-tuple-element.97), channel_id=1, source_target_pairs={{0,8},{8,0},{16,24},{24,16},{1,9},{9,1},{17,25},{25,17},{2,10},{10... | collective-permute-start | bytes 3538952 | tf_op jit(solution)/shard_map/ppermute | solution.py:963
  51.5 11.8 %copy-start.2 = (f32[2,4]{1,0:T(2,128)S(1)}, f32[2,4]{1,0:T(2,128)}, u32[]{:S(2)}) copy-start(f32[2,4]{1,0:T(2,128)} %lon_length.2) | copy-start | bytes 100
  51.5 26.1 %collective-permute-start.19 = (f32[2,96,1536]{2,1,0:T(8,128)S(1)}, f32[2,96,1536]{2,1,0:T(8,128)S(1)}, u32[]{:S(2)}, u32[]{:S(2)}) collective-permute-start(f32[2,96,1536]{2,1,0:T(8,128)S(1)} %shard_map.82), channel_id=1, source_target_pairs={{0,0},{8,16},{16,8},{24,24},{1,1},{9,17},{17,9},{25,25},{2,2},{10,... | collective-permute-start | bytes 3538952 | tf_op jit(solution)/shard_map/ppermute | solution.py:969
  54.8 26.9 %collective-permute-start.21 = (f32[2,96,1536]{2,1,0:T(8,128)S(1)}, f32[2,96,1536]{2,1,0:T(8,128)S(1)}, u32[]{:S(2)}, u32[]{:S(2)}) collective-permute-start(f32[2,96,1536]{2,1,0:T(8,128)S(1)} %shard_map.84), channel_id=1, source_target_pairs={{0,0},{8,16},{16,8},{24,24},{1,1},{9,17},{17,9},{25,25},{2,2},{10,... | collective-permute-start | bytes 3538952 | tf_op jit(solution)/shard_map/ppermute | solution.py:969
  57.6 3.6 %collective-permute-start.10 = (f32[96,128]{1,0:T(8,128)S(1)}, f32[96,128]{1,0:T(8,128)S(1)}, u32[]{:S(2)}, u32[]{:S(2)}) collective-permute-start(f32[96,128]{1,0:T(8,128)S(1)} %get-tuple-element.99), channel_id=1, source_target_pairs={{0,2},{1,3},{2,0},{3,1},{4,6},{5,7},{6,4},{7,5},{8,10},{9,11},{10,... | collective-permute-start | bytes 147464 | tf_op jit(solution)/shard_map/ppermute | solution.py:74
  57.7 4.5 %collective-permute-start.11 = (f32[96,128]{1,0:T(8,128)S(1)}, f32[96,128]{1,0:T(8,128)S(1)}, u32[]{:S(2)}, u32[]{:S(2)}) collective-permute-start(f32[96,128]{1,0:T(8,128)S(1)} %get-tuple-element.100), channel_id=1, source_target_pairs={{0,4},{1,5},{2,6},{3,7},{4,0},{5,1},{6,2},{7,3},{8,12},{9,13},{10,... | collective-permute-start | bytes 147464 | tf_op jit(solution)/shard_map/ppermute | solution.py:74
  57.8 5.6 %collective-permute-start.12 = (f32[96,128]{1,0:T(8,128)S(1)}, f32[96,128]{1,0:T(8,128)S(1)}, u32[]{:S(2)}, u32[]{:S(2)}) collective-permute-start(f32[96,128]{1,0:T(8,128)S(1)} %get-tuple-element.101), channel_id=1, source_target_pairs={{0,6},{1,7},{2,4},{3,5},{4,2},{5,3},{6,0},{7,1},{8,14},{9,15},{10,... | collective-permute-start | bytes 147464 | tf_op jit(solution)/shard_map/ppermute | solution.py:74
  64.7 4.5 %collective-permute-start.13 = (f32[224,128]{1,0:T(8,128)S(1)}, f32[224,128]{1,0:T(8,128)S(1)}, u32[]{:S(2)}, u32[]{:S(2)}) collective-permute-start(f32[224,128]{1,0:T(8,128)S(1)} %get-tuple-element.103), channel_id=1, source_target_pairs={{0,1},{1,0},{2,3},{3,2},{4,5},{5,4},{6,7},{7,6},{8,9},{9,8},{10,11... | collective-permute-start | bytes 344072 | tf_op jit(solution)/shard_map/ppermute | solution.py:74
  69.2 3.6 %collective-permute-start.14 = (f32[112,128]{1,0:T(8,128)S(1)}, f32[112,128]{1,0:T(8,128)S(1)}, u32[]{:S(2)}, u32[]{:S(2)}) collective-permute-start(f32[112,128]{1,0:T(8,128)S(1)} %get-tuple-element.105), channel_id=1, source_target_pairs={{0,2},{1,3},{2,0},{3,1},{4,6},{5,7},{6,4},{7,5},{8,10},{9,11},{10,... | collective-permute-start | bytes 172040 | tf_op jit(solution)/shard_map/ppermute | solution.py:74
  69.3 5.1 %collective-permute-start.15 = (f32[112,128]{1,0:T(8,128)S(1)}, f32[112,128]{1,0:T(8,128)S(1)}, u32[]{:S(2)}, u32[]{:S(2)}) collective-permute-start(f32[112,128]{1,0:T(8,128)S(1)} %get-tuple-element.106), channel_id=1, source_target_pairs={{0,4},{1,5},{2,6},{3,7},{4,0},{5,1},{6,2},{7,3},{8,12},{9,13},{10,... | collective-permute-start | bytes 172040 | tf_op jit(solution)/shard_map/ppermute | solution.py:74
  72.6 4.9 %collective-permute-start.16 = (f32[112,128]{1,0:T(8,128)S(1)}, f32[112,128]{1,0:T(8,128)S(1)}, u32[]{:S(2)}, u32[]{:S(2)}) collective-permute-start(f32[112,128]{1,0:T(8,128)S(1)} %get-tuple-element.107), channel_id=1, source_target_pairs={{0,6},{1,7},{2,4},{3,5},{4,2},{5,3},{6,0},{7,1},{8,14},{9,15},{10,... | collective-permute-start | bytes 172040 | tf_op jit(solution)/shard_map/ppermute | solution.py:74
  77.6 5.7 %collective-permute-start.20 = (f32[2,96,1536]{2,1,0:T(8,128)S(1)}, f32[2,96,1536]{2,1,0:T(8,128)S(1)}, u32[]{:S(2)}, u32[]{:S(2)}) collective-permute-start(f32[2,96,1536]{2,1,0:T(8,128)S(1)} %collective-permute-done.19.met), channel_id=1, source_target_pairs={{0,8},{8,0},{16,24},{24,16},{1,9},{9,1},{17,25},{25,17},{2,10},{10... | collective-permute-start | bytes 3538952 | tf_op jit(solution)/shard_map/ppermute | solution.py:987
  81.7 2.8 %collective-permute-start.22 = (f32[2,96,1536]{2,1,0:T(8,128)S(1)}, f32[2,96,1536]{2,1,0:T(8,128)S(1)}, u32[]{:S(2)}, u32[]{:S(2)}) collective-permute-start(f32[2,96,1536]{2,1,0:T(8,128)S(1)} %collective-permute-done.21.met), channel_id=1, source_target_pairs={{0,8},{8,0},{16,24},{24,16},{1,9},{9,1},{17,25},{25,17},{2,10},{10... | collective-permute-start | bytes 3538952 | tf_op jit(solution)/shard_map/ppermute | solution.py:987
  81.7 6.7 %collective-permute-start.17 = (f32[448,128]{1,0:T(8,128)S(1)}, f32[448,128]{1,0:T(8,128)S(1)}, u32[]{:S(2)}, u32[]{:S(2)}) collective-permute-start(f32[448,128]{1,0:T(8,128)S(1)} %shard_map.87.rest_0_), channel_id=1, source_target_pairs={{0,16},{16,0},{8,24},{24,8},{1,17},{17,1},{9,25},{25,9},{2,18},{18... | collective-permute-start | bytes 688136 | tf_op jit(solution)/shard_map/ppermute | solution.py:982
  83.0 6.8 %collective-permute-start.18 = (f32[448,128]{1,0:T(8,128)S(1)}, f32[448,128]{1,0:T(8,128)S(1)}, u32[]{:S(2)}, u32[]{:S(2)}) collective-permute-start(f32[448,128]{1,0:T(8,128)S(1)} %shard_map.87.rest_0_), channel_id=1, source_target_pairs={{0,8},{8,0},{16,24},{24,16},{1,9},{9,1},{17,25},{25,17},{2,10},{10... | collective-permute-start | bytes 688136 | tf_op jit(solution)/shard_map/ppermute | solution.py:983
  88.4 2.5 %collective-permute-start.23 = (f32[448,128]{1,0:T(8,128)S(1)}, f32[448,128]{1,0:T(8,128)S(1)}, u32[]{:S(2)}, u32[]{:S(2)}) collective-permute-start(f32[448,128]{1,0:T(8,128)S(1)} %collective-permute-done.17.rest_1_), channel_id=1, source_target_pairs={{0,8},{8,0},{16,24},{24,16},{1,9},{9,1},{17,25},{25,17},{2,10},{10... | collective-permute-start | bytes 688136 | tf_op jit(solution)/shard_map/ppermute | solution.py:989

commit v8 on v7

--- a/solution.py
+++ b/solution.py
@@ -953,7 +953,7 @@
 MIDDLE = [(0, 0), (1, 2), (2, 1), (3, 3)]
 
 
-def four_bands(swept, weights, exits, units, chain, gather, table, mix):
+def four_bands(swept, weights, exits, response, chain, gather, table, mix):
     owns, parts, nears, mets = [], [], [], []
 
     def filter_some(at, *earlier):
@@ -969,11 +969,10 @@
         mets.append(lax.ppermute(total, "band", MIDDLE))
         return total
 
-    first = filter_some(0)
-    response = units(first)
+    filter_some(0)
 
     def before_second_stage(came):
-        return (cross_some(0, filter_some(1, came, *response)),)
+        return (cross_some(0, filter_some(1, came)),)
 
     exits = exchange(exits, 8, before_second_stage)
     mark = cross_some(1, exits[0])
@@ -1034,10 +1033,10 @@
     )
 
 
-def any_bands(swept, weights, exits, units, chain, gather, vert_length):
+def any_bands(swept, weights, exits, response, chain, gather, vert_length):
     column_count, group_count, row_count, _ = swept.shape
     sub_count = lax.axis_size("sub")
-    chained = chain(exchange(exits, sub_count), units())
+    chained = chain(exchange(exits, sub_count), response)
     messages = gather(exchange(chained, sub_count))
     (values,) = longitude(swept, weights, group_count, 0, 1)
     messages = messages.reshape(group_count, -1, LANES)
@@ -1080,6 +1079,7 @@
         ready.append(table)
 
     sizes = (sub_count, group_count, row_count, column_count, chunk_count, strip)
+    response = unit_responses(after(index, got[0]), lat_length, sub_count, row_count)
     decay, *totals = make_ready(
         after(index, got[0]),
         lat_length,
@@ -1087,12 +1087,8 @@
         sizes,
     )
     swept, *exits = deposit_and_sweep(
-        index, decay, totals, [after(got[0], *ready)] + got[1:], sizes
+        index, decay, totals, [after(got[0], *ready, *response)] + got[1:], sizes
     )
-
-    def units(*earlier):
-        start = after(index, swept, *earlier)
-        return unit_responses(start, lat_length, sub_count, row_count)
 
     def chain(arrived, response):
         inside, leaving = response
@@ -1102,8 +1098,8 @@
         return gather_messages(arriving_layout(sub_count), index, parts)
 
     if two_chips:
-        return four_bands(swept, weights, exits, units, chain, gather, table, mix)
-    return any_bands(swept, weights, exits, units, chain, gather, vert_length)
+        return four_bands(swept, weights, exits, response, chain, gather, table, mix)
+    return any_bands(swept, weights, exits, response, chain, gather, vert_length)
 
 
 def solution(mesh):

time: 94.2 us -> 92.8 us (0.985); the launches traced: 93.6 us -> 93.2 us
  starting transfers between devices: 30.9 us -> 42.5 us
  Pallas kernels: 44.5 us -> 33.1 us
  waiting for transfers between devices: 17.1 us -> 15.8 us
    pallas_call x1, Pallas kernels: 21.4 us -> 10.1 us  [deposit_and_sweep(): pl.pallas_call(functools.partial(deposit_kernel, sizes), out_shape=[pltpu...]
    ppermute x12, starting transfers between devices: 14.5 us -> 25 us  [move(): return lax.ppermute(part, 'sub', [(at, at ^ k) for at in range(sub_count)])]
    ppermute x2, waiting for transfers between devices: 2.03 us -> 0.01 us  [cross_some(): mets.append(lax.ppermute(total, 'band', MIDDLE))]
    ppermute x12, waiting for transfers between devices: 10.9 us -> 12 us  [move(): return lax.ppermute(part, 'sub', [(at, at ^ k) for at in range(sub_count)])]
    ppermute x1, waiting for transfers between devices: 2.86 us -> 1.8 us  [four_bands(): across = lax.ppermute(messages, 'band', CROSS)]
  transfers between devices with their start and end apart: 24 -> 24, of which waited for: 10 -> 9; matrix products, arithmetic and copies ran while one was open for 0% -> 0% of each run, Pallas kernels for 18% -> 18%
where the time goes in v8:
time: 92.8 us; the launch traced here: 93.2 us
  starting transfers between devices  42.5 us (46%)
  Pallas kernels  33.1 us (36%)
  waiting for transfers between devices  15.8 us (17%)
  local copies, waits for them, and re-layouts  1.43 us (2%)
    ppermute x12, starting transfers between devices, move(): return lax.ppermute(part, 'sub', [(at, at ^ k) for at in range(sub_count)])  25 us
    ppermute x12, waiting for transfers between devices, move(): return lax.ppermute(part, 'sub', [(at, at ^ k) for at in range(sub_count)])  12 us
    pallas_call x1, Pallas kernels, deposit_and_sweep(): pl.pallas_call(functools.partial(deposit_kernel, sizes), out_shape=[pltpu...  10.1 us
    ppermute x2, starting transfers between devices, cross_some(): mets.append(lax.ppermute(total, 'band', MIDDLE))  5.87 us
    pallas_call x2, Pallas kernels, longitude_pair(): pl.pallas_call(functools.partial(pair_kernel, variables), in_specs=[VMEM]...  4.97 us
    pallas_call x1, Pallas kernels, pack_observations(): pl.pallas_call(functools.partial(pack_kernel, (sub_count, group_count, ch...  3.33 us
    ppermute x2, starting transfers between devices, filter_some(): nears.append(lax.ppermute(sent, 'band', SWAP))  3.33 us
    pallas_call x1, Pallas kernels, make_ready(): pl.pallas_call(functools.partial(ready_kernel, sizes), in_specs=[SMEM, HB...  3.33 us
  transfers between devices with their start and end apart: 24, of which 9 were waited for; matrix products, arithmetic and copies ran while one was open for 0% of the time, Pallas kernels for 18%

profile of v8, /device:TPU:1, one launch (start us, length us, event | category | flops | bytes accessed | tf_op | source)
XLA Modules:
  0.0 93.2 jit_solution(11524783492192788857)
XLA Ops:
  0.0 3.3 %shard_map.73 = (f32[288,128]{1,0:T(8,128)S(1)}, f32[288,128]{1,0:T(8,128)S(1)}) custom-call(s32[1]{0:T(128)} %bitcast.1.index, s32[32,128]{1,0:T(8,128)} %bitcast.6, s32[32,128]{1,0:T(8,128)} %bitcast.7, f32[2,4,4096]{2,1,0:T(4,128)} %values.1), custom_call_target="tpu_custom_call" | custom-call | flops 10 | bytes 10 | tf_op jit(solution)/shard_map/pallas_call | solution.py:198
  3.3 2.1 %collective-permute-start.3 = (f32[288,128]{1,0:T(8,128)S(1)}, f32[288,128]{1,0:T(8,128)S(1)}, u32[]{:S(2)}, u32[]{:S(2)}) collective-permute-start(f32[288,128]{1,0:T(8,128)S(1)} %get-tuple-element.60), channel_id=1, source_target_pairs={{0,1},{1,0},{2,3},{3,2},{4,5},{5,4},{6,7},{7,6},{8,9},{9,8},{10,11... | collective-permute-start | bytes 442376 | tf_op jit(solution)/shard_map/ppermute | solution.py:74
  5.5 2.1 %collective-permute-start.2 = (f32[2,4]{1,0:T(2,128)}, f32[2,4]{1,0:T(2,128)S(1)}, u32[]{:S(2)}, u32[]{:S(2)}) collective-permute-start(f32[2,4]{1,0:T(2,128)} %own), channel_id=1, source_target_pairs={{0,24},{24,0},{8,16},{16,8},{1,25},{25,1},{9,17},{17,9},{2,26},{26... | collective-permute-start | bytes 104 | tf_op jit(solution)/shard_map/ppermute | solution.py:1071
  7.5 0.2 collective-permute-start
  7.8 0.7 copy-done.1
  8.4 2.9 %shard_map.74 = (bf16[8,256,256]{2,1,0:T(8,128)(2,1)S(1)}, bf16[8,256,256]{2,1,0:T(8,128)(2,1)S(1)}, bf16[8,256,256]{2,1,0:T(8,128)(2,1)S(1)}, bf16[8,64,1536]{2,1,0:T(8,128)(2,1)S(1)}) custom-call(f32[2,4]{1,0:T(2,128)S(1)} %copy-done.1), custom_call_target="tpu_custom_call" | custom-call | flops 10 | bytes 10 | tf_op jit(solution)/shard_map/pallas_call | solution.py:529
  11.5 1.4 %collective-permute-start.4 = (f32[144,128]{1,0:T(8,128)S(1)}, f32[144,128]{1,0:T(8,128)S(1)}, u32[]{:S(2)}, u32[]{:S(2)}) collective-permute-start(f32[144,128]{1,0:T(8,128)S(1)} %get-tuple-element.77), channel_id=1, source_target_pairs={{0,2},{1,3},{2,0},{3,1},{4,6},{5,7},{6,4},{7,5},{8,10},{9,11},{10,... | collective-permute-start | bytes 221192 | tf_op jit(solution)/shard_map/ppermute | solution.py:74
  12.8 2.3 %collective-permute-start.5 = (f32[144,128]{1,0:T(8,128)S(1)}, f32[144,128]{1,0:T(8,128)S(1)}, u32[]{:S(2)}, u32[]{:S(2)}) collective-permute-start(f32[144,128]{1,0:T(8,128)S(1)} %get-tuple-element.78), channel_id=1, source_target_pairs={{0,4},{1,5},{2,6},{3,7},{4,0},{5,1},{6,2},{7,3},{8,12},{9,13},{10,... | collective-permute-start | bytes 221192 | tf_op jit(solution)/shard_map/ppermute | solution.py:74
  15.1 0.7 copy-done
  15.9 1.5 %shard_map.77 = (f32[128,128]{1,0:T(8,128)S(1)}, f32[4,128]{1,0:T(4,128)S(1)}) custom-call(s32[1]{0:T(128)} %bitcast.1.index, f32[2,4,768]{2,1,0:T(4,128)S(1)} %copy-done), custom_call_target="tpu_custom_call" | custom-call | flops 10 | bytes 10 | tf_op jit(solution)/shard_map/pallas_call | solution.py:456
  17.4 0.0 copy-start.3
  17.4 3.3 %shard_map.78 = (f32[96,1,8,128]{3,2,1,0:T(8,128)S(1)}, f32[1,97,12,8,128]{4,3,2,1,0:T(8,128)S(1)}, f32[1,97,12,8,128]{4,3,2,1,0:T(8,128)S(1)}, f32[1,97,12,8,12...) custom-call(s32[1]{0:T(128)} %bitcast.1.index, f32[2,4,768]{2,1,0:T(4,128)} %lat_length.3, f32[8,96,1536]{2,1,0:T(8,128)} %bitcast.5), custom_call_target="tpu_custom_call" | custom-call | flops 10 | bytes 10 | tf_op jit(solution)/shard_map/pallas_call | solution.py:271
  20.8 0.7 shard_map.76
  21.5 10.1 %shard_map.79 = (f32[12,8,96,128]{3,2,1,0:T(8,128)S(1)}, f32[192,128]{1,0:T(8,128)S(1)}, f32[192,128]{1,0:T(8,128)S(1)}, f32[1,97,12,8,128]{4,3,2,1,0:T(8,128)S(...) custom-call(s32[1]{0:T(128)} %bitcast.1.index, ...), custom_call_target="tpu_custom_call", output_to_operand_aliasing={{3}: (6, {}), {4}: (7, {}), {5}: (8, {}), {6}: (9, {})} | custom-call | flops 10 | bytes 10 | tf_op jit(solution)/shard_map/pallas_call | solution.py:405
  31.6 0.5 collective-permute-start.7
  32.0 2.5 %shard_map.80 = (f32[2,2,96,1536]{3,2,1,0:T(8,128)S(1)}, f32[2,96,1536]{2,1,0:T(8,128)S(1)}, f32[2,96,1536]{2,1,0:T(8,128)S(1)}) custom-call(f32[12,8,96,128]{3,2,1,0:T(8,128)S(1)} %get-tuple-element.88.swept, bf16[8,256,256]{2,1,0:T(8,128)(2,1)S(1)} %get-tuple-element.63.near_high, bf16[8,256,256]{2,1,0:T(8,128)(2,1)S(1)} %get-tuple-element.72.near_low, ...), custom_call_target="tpu_custom_call" | custom-call | flops 10 | bytes 10 | tf_op jit(solution)/shard_map/pallas_call | solution.py:601
  34.5 1.7 %collective-permute-start.8 = (f32[2,96,1536]{2,1,0:T(8,128)S(1)}, f32[2,96,1536]{2,1,0:T(8,128)S(1)}, u32[]{:S(2)}, u32[]{:S(2)}) collective-permute-start(f32[2,96,1536]{2,1,0:T(8,128)S(1)} %get-tuple-element.91), channel_id=1, source_target_pairs={{0,8},{8,0},{16,24},{24,16},{1,9},{9,1},{17,25},{25,17},{2,10},{10... | collective-permute-start | bytes 3538952 | tf_op jit(solution)/shard_map/ppermute | solution.py:963
  36.2 2.5 %shard_map.81 = (f32[2,2,96,1536]{3,2,1,0:T(8,128)S(1)}, f32[2,96,1536]{2,1,0:T(8,128)S(1)}, f32[2,96,1536]{2,1,0:T(8,128)S(1)}) custom-call(f32[12,8,96,128]{3,2,1,0:T(8,128)S(1)} %get-tuple-element.88.swept, bf16[8,256,256]{2,1,0:T(8,128)(2,1)S(1)} %get-tuple-element.63.near_high, bf16[8,256,256]{2,1,0:T(8,128)(2,1)S(1)} %get-tuple-element.72.near_low, ...), custom_call_target="tpu_custom_call" | custom-call | flops 10 | bytes 10 | tf_op jit(solution)/shard_map/pallas_call | solution.py:601
  38.7 1.6 %collective-permute-start.9 = (f32[2,96,1536]{2,1,0:T(8,128)S(1)}, f32[2,96,1536]{2,1,0:T(8,128)S(1)}, u32[]{:S(2)}, u32[]{:S(2)}) collective-permute-start(f32[2,96,1536]{2,1,0:T(8,128)S(1)} %get-tuple-element.95), channel_id=1, source_target_pairs={{0,8},{8,0},{16,24},{24,16},{1,9},{9,1},{17,25},{25,17},{2,10},{10... | collective-permute-start | bytes 3538952 | tf_op jit(solution)/shard_map/ppermute | solution.py:963
  40.4 0.1 shard_map.82
  40.5 0.0 copy-start.2
  40.5 3.1 %collective-permute-start.19 = (f32[2,96,1536]{2,1,0:T(8,128)S(1)}, f32[2,96,1536]{2,1,0:T(8,128)S(1)}, u32[]{:S(2)}, u32[]{:S(2)}) collective-permute-start(f32[2,96,1536]{2,1,0:T(8,128)S(1)} %shard_map.82), channel_id=1, source_target_pairs={{0,0},{8,16},{16,8},{24,24},{1,1},{9,17},{17,9},{25,25},{2,2},{10,... | collective-permute-start | bytes 3538952 | tf_op jit(solution)/shard_map/ppermute | solution.py:969
  43.6 0.1 shard_map.84
  43.7 2.8 %collective-permute-start.21 = (f32[2,96,1536]{2,1,0:T(8,128)S(1)}, f32[2,96,1536]{2,1,0:T(8,128)S(1)}, u32[]{:S(2)}, u32[]{:S(2)}) collective-permute-start(f32[2,96,1536]{2,1,0:T(8,128)S(1)} %shard_map.84), channel_id=1, source_target_pairs={{0,0},{8,16},{16,8},{24,24},{1,1},{9,17},{17,9},{25,25},{2,2},{10,... | collective-permute-start | bytes 3538952 | tf_op jit(solution)/shard_map/ppermute | solution.py:969
  46.6 1.7 %collective-permute-start.10 = (f32[96,128]{1,0:T(8,128)S(1)}, f32[96,128]{1,0:T(8,128)S(1)}, u32[]{:S(2)}, u32[]{:S(2)}) collective-permute-start(f32[96,128]{1,0:T(8,128)S(1)} %get-tuple-element.97), channel_id=1, source_target_pairs={{0,2},{1,3},{2,0},{3,1},{4,6},{5,7},{6,4},{7,5},{8,10},{9,11},{10,... | collective-permute-start | bytes 147464 | tf_op jit(solution)/shard_map/ppermute | solution.py:74
  48.3 13.3 %collective-permute-start.11 = (f32[96,128]{1,0:T(8,128)S(1)}, f32[96,128]{1,0:T(8,128)S(1)}, u32[]{:S(2)}, u32[]{:S(2)}) collective-permute-start(f32[96,128]{1,0:T(8,128)S(1)} %get-tuple-element.98), channel_id=1, source_target_pairs={{0,4},{1,5},{2,6},{3,7},{4,0},{5,1},{6,2},{7,3},{8,12},{9,13},{10,... | collective-permute-start | bytes 147464 | tf_op jit(solution)/shard_map/ppermute | solution.py:74
  61.6 2.2 %collective-permute-done.11.rest_2_ = f32[96,128]{1,0:T(8,128)S(1)} collective-permute-done((f32[96,128]{1,0:T(8,128)S(1)}, f32[96,128]{1,0:T(8,128)S(1)}, u32[]{:S(2)}, u32[]{:S(2)}) %collective-permute-start.11) | collective-permute-done | bytes 49184 | tf_op jit(solution)/shard_map/ppermute | solution.py:74
  63.8 2.5 %collective-permute-done.12.rest_3_ = f32[96,128]{1,0:T(8,128)S(1)} collective-permute-done((f32[96,128]{1,0:T(8,128)S(1)}, f32[96,128]{1,0:T(8,128)S(1)}, u32[]{:S(2)}, u32[]{:S(2)}) %collective-permute-start.12) | collective-permute-done | bytes 49184 | tf_op jit(solution)/shard_map/ppermute | solution.py:74
  66.3 1.4 %shard_map.85 = (f32[224,128]{1,0:T(8,128)S(1)}, f32[224,128]{1,0:T(8,128)S(1)}) custom-call(s32[1]{0:T(128)} %bitcast.1.index, f32[2,4]{1,0:T(2,128)S(1)} %copy-done.2, f32[4,128]{1,0:T(4,128)S(1)} %get-tuple-element.69.leaving, f32[128,128]{1,0:T(8,128)S(1)} %get-tuple-element.70.inside, f32[96,128]{1,0:T(8,128)S(1)} %get-tuple-element.96.rest_0_, ...), custom_call_target="tpu_custom_call" | custom-call | flops 10 | bytes 10 | tf_op jit(solution)/shard_map/pallas_call | solution.py:701
  67.7 0.1 collective-permute-start.13
  67.8 4.9 %collective-permute-done.13.came = f32[224,128]{1,0:T(8,128)S(1)} collective-permute-done((f32[224,128]{1,0:T(8,128)S(1)}, f32[224,128]{1,0:T(8,128)S(1)}, u32[]{:S(2)}, u32[]{:S(2)}) %collective-permute-start.13) | collective-permute-done | bytes 114720 | tf_op jit(solution)/shard_map/ppermute | solution.py:74
  72.7 0.1 collective-permute-start.14
  72.8 0.4 collective-permute-start.15
  73.2 3.1 %collective-permute-start.16 = (f32[112,128]{1,0:T(8,128)S(1)}, f32[112,128]{1,0:T(8,128)S(1)}, u32[]{:S(2)}, u32[]{:S(2)}) collective-permute-start(f32[112,128]{1,0:T(8,128)S(1)} %get-tuple-element.105), channel_id=1, source_target_pairs={{0,6},{1,7},{2,4},{3,5},{4,2},{5,3},{6,0},{7,1},{8,14},{9,15},{10,... | collective-permute-start | bytes 172040 | tf_op jit(solution)/shard_map/ppermute | solution.py:74
  76.3 0.6 collective-permute-done.15.rest_2_
  76.9 1.8 %collective-permute-done.16.rest_3_ = f32[112,128]{1,0:T(8,128)S(1)} collective-permute-done((f32[112,128]{1,0:T(8,128)S(1)}, f32[112,128]{1,0:T(8,128)S(1)}, u32[]{:S(2)}, u32[]{:S(2)}) %collective-permute-start.16) | collective-permute-done | bytes 57376 | tf_op jit(solution)/shard_map/ppermute | solution.py:74
  78.7 2.5 %collective-permute-start.20 = (f32[2,96,1536]{2,1,0:T(8,128)S(1)}, f32[2,96,1536]{2,1,0:T(8,128)S(1)}, u32[]{:S(2)}, u32[]{:S(2)}) collective-permute-start(f32[2,96,1536]{2,1,0:T(8,128)S(1)} %collective-permute-done.19.met), channel_id=1, source_target_pairs={{0,8},{8,0},{16,24},{24,16},{1,9},{9,1},{17,25},{25,17},{2,10},{10... | collective-permute-start | bytes 3538952 | tf_op jit(solution)/shard_map/ppermute | solution.py:986
  81.2 0.1 collective-permute-start.22
  81.3 1.5 %collective-permute-start.17 = (f32[448,128]{1,0:T(8,128)S(1)}, f32[448,128]{1,0:T(8,128)S(1)}, u32[]{:S(2)}, u32[]{:S(2)}) collective-permute-start(f32[448,128]{1,0:T(8,128)S(1)} %shard_map.87.rest_0_), channel_id=1, source_target_pairs={{0,16},{16,0},{8,24},{24,8},{1,17},{17,1},{9,25},{25,9},{2,18},{18... | collective-permute-start | bytes 688136 | tf_op jit(solution)/shard_map/ppermute | solution.py:981
  82.8 0.7 collective-permute-start.18
  83.5 0.2 collective-permute-done.20.far
  83.7 1.1 %shard_map.88.rest_4_ = f32[2,2,96,1536]{3,2,1,0:T(8,128)S(1)} custom-call(f32[2,2,96,1536]{3,2,1,0:T(8,128)S(1)} %get-tuple-element.106.own, f32[2,96,1536]{2,1,0:T(8,128)S(1)} %collective-permute-done.8.near, f32[2,96,1536]{2,1,0:T(8,128)S(1)} %collective-permute-done.20.far, f32[2,96,1536]{2,1,0:T(8,128)S(1)} %collective-permute-done.19.met, ...), custom_call_target="tpu_custom_call" | custom-call | flops 10 | bytes 10 | tf_op jit(solution)/shard_map/pallas_call | solution.py:874
  84.8 0.6 collective-permute-done.22.far
  85.4 1.0 %shard_map.89.rest_5_ = f32[2,2,96,1536]{3,2,1,0:T(8,128)S(1)} custom-call(f32[2,2,96,1536]{3,2,1,0:T(8,128)S(1)} %get-tuple-element.108.own, f32[2,96,1536]{2,1,0:T(8,128)S(1)} %collective-permute-done.9.near, f32[2,96,1536]{2,1,0:T(8,128)S(1)} %collective-permute-done.22.far, f32[2,96,1536]{2,1,0:T(8,128)S(1)} %collective-permute-done.21.met, ...), custom_call_target="tpu_custom_call" | custom-call | flops 10 | bytes 10 | tf_op jit(solution)/shard_map/pallas_call | solution.py:874
  86.4 1.8 %collective-permute-done.17.rest_1_ = f32[448,128]{1,0:T(8,128)S(1)} collective-permute-done((f32[448,128]{1,0:T(8,128)S(1)}, f32[448,128]{1,0:T(8,128)S(1)}, u32[]{:S(2)}, u32[]{:S(2)}) %collective-permute-start.17) | collective-permute-done | bytes 229408 | tf_op jit(solution)/shard_map/ppermute | solution.py:981
  88.2 1.2 %collective-permute-start.23 = (f32[448,128]{1,0:T(8,128)S(1)}, f32[448,128]{1,0:T(8,128)S(1)}, u32[]{:S(2)}, u32[]{:S(2)}) collective-permute-start(f32[448,128]{1,0:T(8,128)S(1)} %collective-permute-done.17.rest_1_), channel_id=1, source_target_pairs={{0,8},{8,0},{16,24},{24,16},{1,9},{9,1},{17,25},{25,17},{2,10},{10... | collective-permute-start | bytes 688136 | tf_op jit(solution)/shard_map/ppermute | solution.py:988
  89.4 1.1 %collective-permute-done.23.rest_3_ = f32[448,128]{1,0:T(8,128)S(1)} collective-permute-done((f32[448,128]{1,0:T(8,128)S(1)}, f32[448,128]{1,0:T(8,128)S(1)}, u32[]{:S(2)}, u32[]{:S(2)}) %collective-permute-start.23) | collective-permute-done | bytes 229408 | tf_op jit(solution)/shard_map/ppermute | solution.py:988
  90.5 2.5 %shard_map.90 = f32[2,4,96,1536]{3,2,1,0:T(8,128)} custom-call(f32[2,4,8,128]{3,2,1,0:T(8,128)S(1)} %get-tuple-element.67.mix, f32[448,128]{1,0:T(8,128)S(1)} %shard_map.87.rest_0_, f32[448,128]{1,0:T(8,128)S(1)} %collective-permute-done.17.rest_1_, f32[448,128]{1,0:T(8,128)S(1)} %collective-permute-done.18.rest_2_, ...), custom_call_target="tpu_custom_call" | custom-call | flops 10 | bytes 10 | tf_op jit(solution)/shard_map/pallas_call | solution.py:934
  (26 shorter events, 0.1 us)
Async XLA Ops:
  3.3 8.1 %collective-permute-start.3 = (f32[288,128]{1,0:T(8,128)S(1)}, f32[288,128]{1,0:T(8,128)S(1)}, u32[]{:S(2)}, u32[]{:S(2)}) collective-permute-start(f32[288,128]{1,0:T(8,128)S(1)} %get-tuple-element.60), channel_id=1, source_target_pairs={{0,1},{1,0},{2,3},{3,2},{4,5},{5,4},{6,7},{7,6},{8,9},{9,8},{10,11... | collective-permute-start | bytes 442376 | tf_op jit(solution)/shard_map/ppermute | solution.py:74
  5.5 5.9 %collective-permute-start.2 = (f32[2,4]{1,0:T(2,128)}, f32[2,4]{1,0:T(2,128)S(1)}, u32[]{:S(2)}, u32[]{:S(2)}) collective-permute-start(f32[2,4]{1,0:T(2,128)} %own), channel_id=1, source_target_pairs={{0,24},{24,0},{8,16},{16,8},{1,25},{25,1},{9,17},{17,9},{2,26},{26... | collective-permute-start | bytes 104 | tf_op jit(solution)/shard_map/ppermute | solution.py:1071
  7.5 3.9 %collective-permute-start.1 = (f32[2,4]{1,0:T(2,128)}, f32[2,4]{1,0:T(2,128)S(1)}, u32[]{:S(2)}, u32[]{:S(2)}) collective-permute-start(f32[2,4]{1,0:T(2,128)} %own), channel_id=1, source_target_pairs={{0,8},{8,0},{16,24},{24,16},{1,9},{9,1},{17,25},{25,17},{2,10},{10... | collective-permute-start | bytes 104 | tf_op jit(solution)/shard_map/ppermute | solution.py:1071
  7.5 3.9 %collective-permute-start = (f32[2,4]{1,0:T(2,128)}, f32[2,4]{1,0:T(2,128)S(1)}, u32[]{:S(2)}, u32[]{:S(2)}) collective-permute-start(f32[2,4]{1,0:T(2,128)} %own), channel_id=1, source_target_pairs={{0,16},{16,0},{8,24},{24,8},{1,17},{17,1},{9,25},{25,9},{2,18},{18... | collective-permute-start | bytes 104 | tf_op jit(solution)/shard_map/ppermute | solution.py:1071
  7.8 0.7 copy-start.1
  11.5 10.0 %collective-permute-start.4 = (f32[144,128]{1,0:T(8,128)S(1)}, f32[144,128]{1,0:T(8,128)S(1)}, u32[]{:S(2)}, u32[]{:S(2)}) collective-permute-start(f32[144,128]{1,0:T(8,128)S(1)} %get-tuple-element.77), channel_id=1, source_target_pairs={{0,2},{1,3},{2,0},{3,1},{4,6},{5,7},{6,4},{7,5},{8,10},{9,11},{10,... | collective-permute-start | bytes 221192 | tf_op jit(solution)/shard_map/ppermute | solution.py:74
  12.8 8.6 %collective-permute-start.5 = (f32[144,128]{1,0:T(8,128)S(1)}, f32[144,128]{1,0:T(8,128)S(1)}, u32[]{:S(2)}, u32[]{:S(2)}) collective-permute-start(f32[144,128]{1,0:T(8,128)S(1)} %get-tuple-element.78), channel_id=1, source_target_pairs={{0,4},{1,5},{2,6},{3,7},{4,0},{5,1},{6,2},{7,3},{8,12},{9,13},{10,... | collective-permute-start | bytes 221192 | tf_op jit(solution)/shard_map/ppermute | solution.py:74
  15.1 6.4 %collective-permute-start.6 = (f32[144,128]{1,0:T(8,128)S(1)}, f32[144,128]{1,0:T(8,128)S(1)}, u32[]{:S(2)}, u32[]{:S(2)}) collective-permute-start(f32[144,128]{1,0:T(8,128)S(1)} %get-tuple-element.79), channel_id=1, source_target_pairs={{0,6},{1,7},{2,4},{3,5},{4,2},{5,3},{6,0},{7,1},{8,14},{9,15},{10,... | collective-permute-start | bytes 221192 | tf_op jit(solution)/shard_map/ppermute | solution.py:74
  15.1 0.7 copy-start
  17.4 3.4 %copy-start.3 = (f32[2,4]{1,0:T(2,128)S(1)}, f32[2,4]{1,0:T(2,128)}, u32[]{:S(2)}) copy-start(f32[2,4]{1,0:T(2,128)} %own) | copy-start | bytes 100
  31.6 4.7 %collective-permute-start.7 = (f32[192,128]{1,0:T(8,128)S(1)}, f32[192,128]{1,0:T(8,128)S(1)}, u32[]{:S(2)}, u32[]{:S(2)}) collective-permute-start(f32[192,128]{1,0:T(8,128)S(1)} %get-tuple-element.87), channel_id=1, source_target_pairs={{0,1},{1,0},{2,3},{3,2},{4,5},{5,4},{6,7},{7,6},{8,9},{9,8},{10,11... | collective-permute-start | bytes 294920 | tf_op jit(solution)/shard_map/ppermute | solution.py:74
  34.5 5.8 %collective-permute-start.8 = (f32[2,96,1536]{2,1,0:T(8,128)S(1)}, f32[2,96,1536]{2,1,0:T(8,128)S(1)}, u32[]{:S(2)}, u32[]{:S(2)}) collective-permute-start(f32[2,96,1536]{2,1,0:T(8,128)S(1)} %get-tuple-element.91), channel_id=1, source_target_pairs={{0,8},{8,0},{16,24},{24,16},{1,9},{9,1},{17,25},{25,17},{2,10},{10... | collective-permute-start | bytes 3538952 | tf_op jit(solution)/shard_map/ppermute | solution.py:963
  38.7 4.9 %collective-permute-start.9 = (f32[2,96,1536]{2,1,0:T(8,128)S(1)}, f32[2,96,1536]{2,1,0:T(8,128)S(1)}, u32[]{:S(2)}, u32[]{:S(2)}) collective-permute-start(f32[2,96,1536]{2,1,0:T(8,128)S(1)} %get-tuple-element.95), channel_id=1, source_target_pairs={{0,8},{8,0},{16,24},{24,16},{1,9},{9,1},{17,25},{25,17},{2,10},{10... | collective-permute-start | bytes 3538952 | tf_op jit(solution)/shard_map/ppermute | solution.py:963
  40.5 25.9 %copy-start.2 = (f32[2,4]{1,0:T(2,128)S(1)}, f32[2,4]{1,0:T(2,128)}, u32[]{:S(2)}) copy-start(f32[2,4]{1,0:T(2,128)} %lon_length.2) | copy-start | bytes 100
  40.5 38.2 %collective-permute-start.19 = (f32[2,96,1536]{2,1,0:T(8,128)S(1)}, f32[2,96,1536]{2,1,0:T(8,128)S(1)}, u32[]{:S(2)}, u32[]{:S(2)}) collective-permute-start(f32[2,96,1536]{2,1,0:T(8,128)S(1)} %shard_map.82), channel_id=1, source_target_pairs={{0,0},{8,16},{16,8},{24,24},{1,1},{9,17},{17,9},{25,25},{2,2},{10,... | collective-permute-start | bytes 3538952 | tf_op jit(solution)/shard_map/ppermute | solution.py:969
  43.7 37.5 %collective-permute-start.21 = (f32[2,96,1536]{2,1,0:T(8,128)S(1)}, f32[2,96,1536]{2,1,0:T(8,128)S(1)}, u32[]{:S(2)}, u32[]{:S(2)}) collective-permute-start(f32[2,96,1536]{2,1,0:T(8,128)S(1)} %shard_map.84), channel_id=1, source_target_pairs={{0,0},{8,16},{16,8},{24,24},{1,1},{9,17},{17,9},{25,25},{2,2},{10,... | collective-permute-start | bytes 3538952 | tf_op jit(solution)/shard_map/ppermute | solution.py:969
  46.6 15.1 %collective-permute-start.10 = (f32[96,128]{1,0:T(8,128)S(1)}, f32[96,128]{1,0:T(8,128)S(1)}, u32[]{:S(2)}, u32[]{:S(2)}) collective-permute-start(f32[96,128]{1,0:T(8,128)S(1)} %get-tuple-element.97), channel_id=1, source_target_pairs={{0,2},{1,3},{2,0},{3,1},{4,6},{5,7},{6,4},{7,5},{8,10},{9,11},{10,... | collective-permute-start | bytes 147464 | tf_op jit(solution)/shard_map/ppermute | solution.py:74
  48.3 15.6 %collective-permute-start.11 = (f32[96,128]{1,0:T(8,128)S(1)}, f32[96,128]{1,0:T(8,128)S(1)}, u32[]{:S(2)}, u32[]{:S(2)}) collective-permute-start(f32[96,128]{1,0:T(8,128)S(1)} %get-tuple-element.98), channel_id=1, source_target_pairs={{0,4},{1,5},{2,6},{3,7},{4,0},{5,1},{6,2},{7,3},{8,12},{9,13},{10,... | collective-permute-start | bytes 147464 | tf_op jit(solution)/shard_map/ppermute | solution.py:74
  61.6 4.7 %collective-permute-start.12 = (f32[96,128]{1,0:T(8,128)S(1)}, f32[96,128]{1,0:T(8,128)S(1)}, u32[]{:S(2)}, u32[]{:S(2)}) collective-permute-start(f32[96,128]{1,0:T(8,128)S(1)} %get-tuple-element.99), channel_id=1, source_target_pairs={{0,6},{1,7},{2,4},{3,5},{4,2},{5,3},{6,0},{7,1},{8,14},{9,15},{10,... | collective-permute-start | bytes 147464 | tf_op jit(solution)/shard_map/ppermute | solution.py:74
  67.7 5.0 %collective-permute-start.13 = (f32[224,128]{1,0:T(8,128)S(1)}, f32[224,128]{1,0:T(8,128)S(1)}, u32[]{:S(2)}, u32[]{:S(2)}) collective-permute-start(f32[224,128]{1,0:T(8,128)S(1)} %get-tuple-element.101), channel_id=1, source_target_pairs={{0,1},{1,0},{2,3},{3,2},{4,5},{5,4},{6,7},{7,6},{8,9},{9,8},{10,11... | collective-permute-start | bytes 344072 | tf_op jit(solution)/shard_map/ppermute | solution.py:74
  72.7 3.6 %collective-permute-start.14 = (f32[112,128]{1,0:T(8,128)S(1)}, f32[112,128]{1,0:T(8,128)S(1)}, u32[]{:S(2)}, u32[]{:S(2)}) collective-permute-start(f32[112,128]{1,0:T(8,128)S(1)} %get-tuple-element.103), channel_id=1, source_target_pairs={{0,2},{1,3},{2,0},{3,1},{4,6},{5,7},{6,4},{7,5},{8,10},{9,11},{10,... | collective-permute-start | bytes 172040 | tf_op jit(solution)/shard_map/ppermute | solution.py:74
  72.8 4.1 %collective-permute-start.15 = (f32[112,128]{1,0:T(8,128)S(1)}, f32[112,128]{1,0:T(8,128)S(1)}, u32[]{:S(2)}, u32[]{:S(2)}) collective-permute-start(f32[112,128]{1,0:T(8,128)S(1)} %get-tuple-element.104), channel_id=1, source_target_pairs={{0,4},{1,5},{2,6},{3,7},{4,0},{5,1},{6,2},{7,3},{8,12},{9,13},{10,... | collective-permute-start | bytes 172040 | tf_op jit(solution)/shard_map/ppermute | solution.py:74
  73.2 5.5 %collective-permute-start.16 = (f32[112,128]{1,0:T(8,128)S(1)}, f32[112,128]{1,0:T(8,128)S(1)}, u32[]{:S(2)}, u32[]{:S(2)}) collective-permute-start(f32[112,128]{1,0:T(8,128)S(1)} %get-tuple-element.105), channel_id=1, source_target_pairs={{0,6},{1,7},{2,4},{3,5},{4,2},{5,3},{6,0},{7,1},{8,14},{9,15},{10,... | collective-permute-start | bytes 172040 | tf_op jit(solution)/shard_map/ppermute | solution.py:74
  78.7 5.0 %collective-permute-start.20 = (f32[2,96,1536]{2,1,0:T(8,128)S(1)}, f32[2,96,1536]{2,1,0:T(8,128)S(1)}, u32[]{:S(2)}, u32[]{:S(2)}) collective-permute-start(f32[2,96,1536]{2,1,0:T(8,128)S(1)} %collective-permute-done.19.met), channel_id=1, source_target_pairs={{0,8},{8,0},{16,24},{24,16},{1,9},{9,1},{17,25},{25,17},{2,10},{10... | collective-permute-start | bytes 3538952 | tf_op jit(solution)/shard_map/ppermute | solution.py:986
  81.2 4.2 %collective-permute-start.22 = (f32[2,96,1536]{2,1,0:T(8,128)S(1)}, f32[2,96,1536]{2,1,0:T(8,128)S(1)}, u32[]{:S(2)}, u32[]{:S(2)}) collective-permute-start(f32[2,96,1536]{2,1,0:T(8,128)S(1)} %collective-permute-done.21.met), channel_id=1, source_target_pairs={{0,8},{8,0},{16,24},{24,16},{1,9},{9,1},{17,25},{25,17},{2,10},{10... | collective-permute-start | bytes 3538952 | tf_op jit(solution)/shard_map/ppermute | solution.py:986
  81.3 6.8 %collective-permute-start.17 = (f32[448,128]{1,0:T(8,128)S(1)}, f32[448,128]{1,0:T(8,128)S(1)}, u32[]{:S(2)}, u32[]{:S(2)}) collective-permute-start(f32[448,128]{1,0:T(8,128)S(1)} %shard_map.87.rest_0_), channel_id=1, source_target_pairs={{0,16},{16,0},{8,24},{24,8},{1,17},{17,1},{9,25},{25,9},{2,18},{18... | collective-permute-start | bytes 688136 | tf_op jit(solution)/shard_map/ppermute | solution.py:981
  82.8 6.6 %collective-permute-start.18 = (f32[448,128]{1,0:T(8,128)S(1)}, f32[448,128]{1,0:T(8,128)S(1)}, u32[]{:S(2)}, u32[]{:S(2)}) collective-permute-start(f32[448,128]{1,0:T(8,128)S(1)} %shard_map.87.rest_0_), channel_id=1, source_target_pairs={{0,8},{8,0},{16,24},{24,16},{1,9},{9,1},{17,25},{25,17},{2,10},{10... | collective-permute-start | bytes 688136 | tf_op jit(solution)/shard_map/ppermute | solution.py:982
  88.2 2.3 %collective-permute-start.23 = (f32[448,128]{1,0:T(8,128)S(1)}, f32[448,128]{1,0:T(8,128)S(1)}, u32[]{:S(2)}, u32[]{:S(2)}) collective-permute-start(f32[448,128]{1,0:T(8,128)S(1)} %collective-permute-done.17.rest_1_), channel_id=1, source_target_pairs={{0,8},{8,0},{16,24},{24,16},{1,9},{9,1},{17,25},{25,17},{2,10},{10... | collective-permute-start | bytes 688136 | tf_op jit(solution)/shard_map/ppermute | solution.py:988
